TPU v7x, 512 devices: a whole 4x8x8 slice. The times are simulated.
512 devices in a mesh: seq: 64 (over z, x, core), head: 8 (over y).
Axes of the slice: x: 4, y: 8, z: 8, core: 2. Of those that a mesh axis runs over, the one named last changes fastest.
Arguments:
- input_x: bfloat16 [16384, 4096], P('seq', 'head'), may hold values from -6 to 6
- input_z: bfloat16 [16384, 4096], P('seq', 'head'), may hold values from -6 to 6
- input_b: bfloat16 [16384, 128], P('seq'), may hold values from -6 to 6
- input_c: bfloat16 [16384, 128], P('seq'), may hold values from -6 to 6
- step_raw: float32 [16384, 64], P('seq', 'head'), may hold values from -8 to 2
- doc_starts: int32 [16384], P('seq'), may hold values from 0 to 1, as said below
- log_rate: float32 [64], P('head'), may hold values from -9.5 to 2.5
- step_bias: float32 [64], P('head'), may hold values from -0.5 to 0.5
- skip_gain: float32 [64], P('head'), may hold values from 0.5 to 1.5
- norm_gain: float32 [4096], P('head'), may hold values from 0.1 to 1.9
- out_weight: bfloat16 [4096, 4096], P('head'), may hold values from -0.125 to 0.125
Outputs:
- mixed: bfloat16 [16384, 4096], P('seq', 'head')
Inputs may be any that keep to these rules, and one draw needn't show every extreme that they name: `doc_starts`: the first token of the context always carries a document start. Some document start lies within the first 4096 tokens such that the 12288 tokens after it carry no document start.
All inputs are finite; a program needn't handle non-finite values.
Results may differ from a plain program's by a relative error of at most 0.019.
Values may be sent and summed in bfloat16 or wider, within the bound.
No kernel may reach another device: no remote copies, remote signals or barrier semaphores. Data moves between devices by JAX's collectives and lax.ppermute only.
A program may use at most 128 MiB of HBM per device.

v0:
```python
import jax
import jax.numpy as jnp
from jax import lax
from jax.sharding import PartitionSpec as P

SPAN = 256


def carried_in(value, axis, join, neutral):
    count, mine = (lax.axis_size(axis), lax.axis_index(axis))
    pieces = jax.tree.map(lambda part: lax.all_gather(part, axis), value)
    so_far = jax.tree.map(
        lambda part, zero: jnp.full_like(part, 0) + jnp.asarray(zero, part.dtype), value, neutral
    )

    def turn(position, so_far):
        longer = join(so_far, jax.tree.map(lambda part: part[position], pieces))
        return jax.tree.map(lambda new, old: jnp.where(position < mine, new, old), longer, so_far)

    return lax.fori_loop(0, count - 1, turn, so_far)


def span_parts(pieces, rate_values):
    x_block, b_block, c_block, dt_block, flag_block = pieces
    log_steps = dt_block * rate_values[None, :]
    running = jnp.cumsum(log_steps, axis=0)
    resets = jnp.cumsum(flag_block, axis=0)
    positions = jnp.arange(flag_block.shape[0])
    allowed = (positions[:, None] >= positions[None, :]) & (resets[:, None] == resets[None, :])
    running_t = running.T
    spread = running_t[:, :, None] - running_t[:, None, :]
    decays = jnp.where(allowed[None], jnp.exp(jnp.where(allowed[None], spread, 0.0)), 0.0)
    scores = jnp.dot(c_block, b_block.T, preferred_element_type=jnp.float32)
    mixing = (scores[None] * decays * dt_block.T[:, None, :]).astype(jnp.bfloat16)
    intra_out = jnp.einsum("hts,shp->thp", mixing, x_block, preferred_element_type=jnp.float32)
    living = resets == resets[-1]
    weights = jnp.where(living[:, None], jnp.exp(running[-1][None, :] - running), 0.0) * dt_block
    scaled = (weights[:, :, None] * x_block.astype(jnp.float32)).astype(jnp.bfloat16)
    states = jnp.einsum("shp,sn->hpn", scaled, b_block, preferred_element_type=jnp.float32)
    through = jnp.where(resets[-1] == 0, jnp.exp(running[-1]), 0.0)
    opening = jnp.where((resets == 0)[:, None], jnp.exp(running), 0.0)
    return (intra_out, states, through, opening)


def combine(earlier, later_one):
    early_keep, early_state = earlier
    late_keep, late_state = later_one
    return (early_keep * late_keep, late_keep[:, None, None] * early_state + late_state)


def body(
    input_x,
    input_z,
    input_b,
    input_c,
    step_raw,
    doc_starts,
    log_rate,
    step_bias,
    skip_gain,
    norm_gain,
    out_weight,
):
    tokens = input_x.shape[0]
    head_count = log_rate.shape[0]
    head_width = input_x.shape[1] // head_count
    state_width = input_b.shape[1]
    blocks = tokens // SPAN
    step_dt = jax.nn.softplus(step_raw + step_bias[None, :])
    rate_values = -jnp.exp(log_rate)
    x_blocks = input_x.reshape(blocks, SPAN, head_count, head_width)
    b_blocks = input_b.reshape(blocks, SPAN, state_width)
    c_blocks = input_c.reshape(blocks, SPAN, state_width)
    dt_blocks = step_dt.reshape(blocks, SPAN, head_count)
    flag_blocks = doc_starts.reshape(blocks, SPAN)
    intra_out, states, through, opening = lax.map(
        lambda pieces: span_parts(pieces, rate_values),
        (x_blocks, b_blocks, c_blocks, dt_blocks, flag_blocks),
    )

    def advance(carried, element):
        retained, state_now = carried
        through_one, state_one = element
        return (
            (retained * through_one, through_one[:, None, None] * state_now + state_one),
            (retained, state_now),
        )

    empty_state = jnp.zeros((head_count, head_width, state_width), jnp.float32)
    ones_keep = jnp.ones((head_count,), jnp.float32)
    device_sum, relative = lax.scan(advance, (ones_keep, empty_state), (through, states))
    device_keep, device_state = device_sum
    rel_keep, rel_state = relative
    incoming = carried_in((device_keep, device_state), "seq", combine, (ones_keep, empty_state))[1]
    entries = rel_keep[:, :, None, None] * incoming[None] + rel_state
    entry_bf = entries.astype(jnp.bfloat16)
    carried_out = (
        jnp.einsum("ctn,chpn->cthp", c_blocks, entry_bf, preferred_element_type=jnp.float32)
        * opening[:, :, :, None]
    )
    ys = intra_out + carried_out + skip_gain[None, None, :, None] * x_blocks.astype(jnp.float32)
    ys = ys.reshape(tokens, head_count * head_width)
    gated_out = ys * jax.nn.silu(input_z.astype(jnp.float32))
    local_squares = jnp.sum(gated_out * gated_out, axis=1)
    totals = lax.psum(local_squares, "head")
    mean_square = totals / (gated_out.shape[1] * lax.axis_size("head"))
    normed = (gated_out * lax.rsqrt(mean_square + 1e-05)[:, None] * norm_gain[None, :]).astype(
        jnp.bfloat16
    )
    summed = lax.psum_scatter(
        lax.dot_general(
            out_weight, normed, (((0,), (1,)), ((), ())), preferred_element_type=jnp.float32
        ).astype(jnp.bfloat16),
        "head",
        scatter_dimension=0,
        tiled=True,
    ).astype(jnp.float32)
    return summed.T.astype(jnp.bfloat16)


def solution(mesh):
    in_specs = (
        P("seq", "head"),
        P("seq", "head"),
        P("seq", None),
        P("seq", None),
        P("seq", "head"),
        P("seq"),
        P("head"),
        P("head"),
        P("head"),
        P("head"),
        P("head", None),
    )
    out_specs = P("seq", "head")
    return jax.shard_map(body, mesh=mesh, in_specs=in_specs, out_specs=out_specs, check_vma=False)
```

profile of v0, /device:TPU:8, one launch (start us, length us, event | category | flops | bytes accessed | tf_op | source)
XLA Modules:
  0.0 264.6 jit_solution(5867264403067885821)
XLA Ops:
  13.1 1.1 copy.16
  14.2 1.8 convolution_add_fusion
  16.0 45.0 %all-gather.1 = f32[64,1,8]{2,1,0:T(1,128)S(1)} all-gather(f32[1,1,8]{2,1,0:T(1,128)S(1)} %bitcast.60), channel_id=1, replica_groups=mesh['seq'=64,'head'=8] {'seq'}, dimensions={0}, use_global_device_ids=true | all-gather | bytes 2080 | tf_op jit(solution)/shard_map/all_gather | solution.py:11
  62.3 64.3 %all-gather.4.cloned.1.call-done = f32[512,64,128]{2,1,0:T(8,128)} async-done(((f32[8,64,128]{2,1,0:T(8,128)}), f32[512,64,128]{2,1,0:T(8,128)}) %all-gather.4.cloned.1.call-update) | async-done | bytes 16777232 | tf_op jit(solution)/shard_map/all_gather | solution.py:11
  126.6 68.9 %while.9 = (s32[]{:T(128)}, f32[8,64,128]{2,1,0:T(8,128)S(1)}, s32[]{:T(128)}, f32[64,8]{1,0:T(8,128)S(1)}, f32[64,8,64,128]{3,2,1,0:T(8,128)}, /*index=5*/s32[]{:T(128)}, s32[]{:T(128)}) while((s32[]{:T(128)}, f32[8,64,128]{2,1,0:T(8,128)S(1)}, s32[]{:T(128)}, f32[64,8]{1,0:T(8,128)S(1)}, f32[64,8,64,128]{3,2,1,0:T(8,128)}, ...), condition=%wide.region_5.6_spmd.clone, body=%wide.region_4.5_spmd.clone.sunk | while | flops 262148 | bytes 786633 | solution.py:20
  126.6 1.1 fusion.34
  127.7 1.1 fusion.34
  128.8 1.1 fusion.34
  129.9 1.1 fusion.34
  131.0 1.1 fusion.34
  132.1 1.1 fusion.34
  133.2 1.1 fusion.34
  134.3 1.1 fusion.34
  135.4 1.1 fusion.34
  136.5 1.1 fusion.34
  137.6 1.1 fusion.34
  138.7 1.1 fusion.34
  139.8 1.1 fusion.34
  140.9 1.1 fusion.34
  142.0 1.1 fusion.34
  143.1 1.1 fusion.34
  144.1 1.1 fusion.34
  145.2 1.1 fusion.34
  146.3 1.1 fusion.34
  147.4 1.1 fusion.34
  148.5 1.1 fusion.34
  149.6 1.1 fusion.34
  150.7 1.1 fusion.34
  151.8 1.1 fusion.34
  152.9 1.1 fusion.34
  154.0 1.1 fusion.34
  155.1 1.1 fusion.34
  156.2 1.1 fusion.34
  157.3 1.1 fusion.34
  158.4 1.1 fusion.34
  159.5 1.1 fusion.34
  160.6 1.1 fusion.34
  161.7 1.1 fusion.34
  162.7 1.1 fusion.34
  163.8 1.1 fusion.34
  164.9 1.1 fusion.34
  166.0 1.1 fusion.34
  167.1 1.1 fusion.34
  168.2 1.1 fusion.34
  169.3 1.1 fusion.34
  170.4 1.1 fusion.34
  171.5 1.1 fusion.34
  172.6 1.1 fusion.34
  173.7 1.1 fusion.34
  174.8 1.1 fusion.34
  175.9 1.1 fusion.34
  177.0 1.1 fusion.34
  178.1 1.1 fusion.34
  179.2 1.1 fusion.34
  181.3 1.1 fusion.34
  183.5 1.1 fusion.34
  185.7 1.1 fusion.34
  187.9 1.1 fusion.34
  190.1 1.1 fusion.34
  192.3 1.1 fusion.34
  194.5 1.1 fusion.34
  197.1 15.7 %psum.7 = f32[256]{0:T(256)S(1)} all-reduce(f32[256]{0:T(256)S(1)} %multiply_reduce_fusion), channel_id=1, replica_groups=mesh['seq'=64,'head'=8] {'head'}, use_global_device_ids=true, to_apply=%region_7.8 | all-reduce | flops 256 | bytes 2048 | tf_op jit(solution)/shard_map/psum | solution.py:105
  212.8 4.9 %fusion.1 = bf16[4096,256]{0,1:T(8,128)(2,1)} fusion(bf16[512,4096]{1,0:T(8,128)(2,1)} %param.23, f32[512]{0:T(512)S(1)} %copy-done.2, f32[256]{0:T(256)S(1)} %add_rsqrt_fusion, f32[256,512]{1,0:T(8,128)S(1)} %copy.17, bf16[256,512]{1,0:T(8,128)(2,1)S(1)} %copy-done.1), kind=kOutput, calls=%fused_computation.4 | convolution fusion | flops 1075970048 | bytes 7080960 | tf_op jit(solution)/shard_map/dot_general | solution.py:111
  217.8 40.0 %reduce-scatter.2.cloned.1.call-done = bf16[512,256]{0,1:T(8,128)(2,1)} async-done(((bf16[4096,256]{0,1:T(8,128)(2,1)}), bf16[512,256]{0,1:T(8,128)(2,1)}) %reduce-scatter.2.cloned.1.call-update) | async-done | bytes 262160 | tf_op jit(solution)/shard_map/reduce_scatter | solution.py:110
  (108 shorter events, 16.6 us)
Async XLA Ops:
  6.5 54.7 %copy-start = (bf16[256,128]{1,0:T(8,128)(2,1)S(1)}, bf16[256,128]{1,0:T(8,128)(2,1)}, u32[]{:S(2)}) copy-start(bf16[256,128]{1,0:T(8,128)(2,1)} %param.16) | copy-start | bytes 196612
  6.5 120.1 %all-gather.4.cloned.1.call-start = ((), (), s32[]{:S(2)}) async-start(), calls=%async_computation.2 | async-start | bytes 17039360 | tf_op jit(solution)/shard_map/all_gather | solution.py:11
  16.0 241.8 %reduce-scatter.2.cloned.1.call-start = ((), (), s32[]{:S(2)}) async-start(), calls=%async_computation.1 | async-start | bytes 2359296 | tf_op jit(solution)/shard_map/reduce_scatter | solution.py:110
  126.6 69.2 %copy-start.3 = (f32[8]{0:T(128)S(1)}, f32[8]{0:T(128)}, u32[]{:S(2)}) copy-start(f32[8]{0:T(128)} %param.21) | copy-start | bytes 100
  195.8 1.1 copy-start.1
  195.8 17.0 %copy-start.2 = (f32[512]{0:T(512)S(1)}, f32[512]{0:T(512)}, u32[]{:S(2)}) copy-start(f32[512]{0:T(512)} %param.22) | copy-start | bytes 6148
Sparse Core Ops, SparseCore 0:
  16.1 110.4 all-gather.3
  217.9 39.7 reduce-scatter.1
where the time goes:
time: 267 us; the launch traced here: 265 us
  waiting for transfers between devices  104 us (39%)
  other arithmetic  71.7 us (27%)
  blocking collectives  60.7 us (23%)
  between operations  14.2 us (5%)
  matrix products  8.77 us (3%)
  local copies, waits for them, and re-layouts  2.83 us (1%)
    select_n x63, other arithmetic, turn(): jnp.where(position < mine, new, old)  66.3 us
    all_gather x1, waiting for transfers between devices, carried_in(): pieces = jax.tree.map(lambda part: lax.all_gather(part, axis), value)  64.3 us
    all_gather x1, blocking collectives, carried_in(): pieces = jax.tree.map(lambda part: lax.all_gather(part, axis), value)  45 us
    reduce_scatter x1, waiting for transfers between devices, body(): lax.psum_scatter(lax.dot_general(out_weight, normed, (((0,), (1,)), ((),...  40 us
    psum x1, blocking collectives, body(): totals = lax.psum(local_squares, 'head')  15.7 us
  transfers between devices with their start and end apart: 2, of which 2 were waited for; matrix products, arithmetic and copies ran while one was open for 0% of the time, Pallas kernels for 0%

commit v1 on v0

v1 whole, which is shorter than its diff:
```python
import jax
import jax.numpy as jnp
from jax import lax
from jax.experimental import pallas as pl
from jax.experimental.pallas import tpu as pltpu
from jax.sharding import PartitionSpec as P

SPAN = 256
N_ROW = 8
PAD = 16
F32, BF16 = (jnp.float32, jnp.bfloat16)
VMEM = pl.BlockSpec(memory_space=pltpu.VMEM)
SMEM = pl.BlockSpec(memory_space=pltpu.SMEM)


def column_of(ref, shape):
    rows = lax.broadcasted_iota(jnp.int32, shape, 0)
    out = jnp.zeros(shape, F32)
    for h in range(shape[0]):
        out = jnp.where(rows == h, ref[h], out)
    return out


def running_sum(rows):
    lanes = lax.broadcasted_iota(jnp.int32, rows.shape, 1)
    step = 1
    while step < rows.shape[1]:
        rows = rows + jnp.where(lanes >= step, pltpu.roll(rows, step, 1), 0.0)
        step *= 2
    return rows


def keep_rows(keep):
    high = keep.astype(BF16).astype(F32)
    middle = (keep - high).astype(BF16).astype(F32)
    low = keep - high - middle
    rows = lax.broadcasted_iota(jnp.int32, (PAD, keep.shape[1]), 0)
    out = jnp.where(rows == 0, high, jnp.where(rows == 1, middle, jnp.where(rows == 2, low, 0.0)))
    return out.astype(BF16)


def piece(ref, index, state_rows):
    state = ref[index, :state_rows, :].astype(F32)
    keep = jnp.sum(ref[index, state_rows:, :].astype(F32), axis=0, keepdims=True)
    return state, keep


def state_kernel(log_rate, bias, raw_ref, flag_ref, x_ref, b_ref, out_ref, rows_ref, cols_ref):
    heads, tokens = raw_ref.shape
    width = x_ref.shape[1] // heads
    raw = raw_ref[...]
    dt = jax.nn.softplus(raw + column_of(bias, raw.shape))
    rate = -jnp.exp(column_of(log_rate, raw.shape))
    flags = jnp.broadcast_to(flag_ref[...].astype(F32), raw.shape)
    sums = running_sum(jnp.concatenate([rate * dt, flags], axis=0))
    running, resets = (sums[:heads], sums[heads:])
    run_last = jnp.broadcast_to(running[:, tokens - 1 :], raw.shape)
    reset_last = jnp.broadcast_to(resets[:, tokens - 1 :], raw.shape)
    weights = jnp.where(resets == reset_last, jnp.exp(run_last - running), 0.0) * dt
    opening = jnp.where(resets == 0.0, jnp.exp(running), 0.0)
    rows = jnp.concatenate([running, dt, resets, opening, weights], axis=0)
    rows_ref[...] = rows
    cols = jnp.concatenate([rows, jnp.zeros((128 - rows.shape[0], tokens), F32)], axis=0).T
    cols_ref[...] = cols
    through = jnp.where(reset_last == 0.0, jnp.exp(run_last), 0.0)
    spread = jnp.concatenate(
        [
            jnp.broadcast_to(cols[:, 4 * heads + h : 4 * heads + h + 1], (tokens, width))
            for h in range(heads)
        ],
        axis=1,
    )
    scaled = (spread * x_ref[...].astype(F32)).astype(BF16)
    states = lax.dot_general(scaled, b_ref[...], (((0,), (0,)), ((), ())), preferred_element_type=F32)
    for h in range(heads):
        out_ref[h, :width, :] = states[h * width : (h + 1) * width].astype(BF16)
        out_ref[h, width:, :] = keep_rows(through[h : h + 1, :128])


def intra_kernel(skip, rows_ref, cols_ref, x_ref, z_ref, b_ref, c_ref, own_ref, open_ref):
    tokens = x_ref.shape[0]
    heads = skip.shape[0]
    width = x_ref.shape[1] // heads
    scores = lax.dot_general(c_ref[...], b_ref[...], (((1,), (1,)), ((), ())), preferred_element_type=F32)
    reset_row = rows_ref[2 * heads : 2 * heads + 1, :]
    reset_col = cols_ref[:, 2 * heads : 2 * heads + 1]
    later = lax.broadcasted_iota(jnp.int32, scores.shape, 0)
    earlier = lax.broadcasted_iota(jnp.int32, scores.shape, 1)
    allowed = (later >= earlier) & (reset_col == reset_row)
    scores = jnp.where(allowed, scores, 0.0)
    for h in range(heads):
        span = slice(h * width, (h + 1) * width)
        spread = cols_ref[:, h : h + 1] - rows_ref[h : h + 1, :]
        decays = jnp.exp(jnp.where(allowed, spread, 0.0))
        mixing = (scores * decays * rows_ref[heads + h : heads + h + 1, :]).astype(BF16)
        x_h = x_ref[:, span]
        out = jnp.dot(mixing, x_h, preferred_element_type=F32) + skip[h] * x_h.astype(F32)
        v = z_ref[:, span].astype(F32)
        gate = v / (1.0 + jnp.exp(-v))
        own_ref[:, span] = out * gate
        open_ref[:, span] = gate * cols_ref[:, 3 * heads + h : 3 * heads + h + 1]


def plane_kernel(got_ref, out_ref):
    count, rows, lanes = got_ref.shape
    state_rows = rows - PAD
    total, keep = piece(got_ref, 0, state_rows)
    for i in range(1, count):
        state, factor = piece(got_ref, i, state_rows)
        total = factor * total + state
        keep = keep * factor
    total, keep = (total.astype(BF16), keep_rows(keep))
    for i in range(out_ref.shape[0]):
        out_ref[i, :state_rows, :] = total
        out_ref[i, state_rows:, :] = keep


def entry_kernel(plane, got_ref, planes_ref, out_ref):
    count, rows, lanes = got_ref.shape
    state_rows = rows - PAD
    mine = plane[0]
    entry = jnp.zeros((state_rows, lanes), F32)
    for i in range(planes_ref.shape[0] - 1):
        state, factor = piece(planes_ref, i, state_rows)
        entry = jnp.where(i < mine, factor * entry + state, entry)
    out_ref[0] = entry.astype(BF16)
    for i in range(count - 1):
        state, factor = piece(got_ref, i, state_rows)
        entry = factor * entry + state
        out_ref[i + 1] = entry.astype(BF16)


def project_kernel(entry_ref, c_ref, own_ref, open_ref, gain_ref, w_ref, out_ref, square_ref):
    heads, width, lanes = entry_ref.shape
    entries = entry_ref[...].reshape(heads * width, lanes)
    carried = lax.dot_general(c_ref[...], entries, (((1,), (1,)), ((), ())), preferred_element_type=F32)
    gated = own_ref[...] + open_ref[...] * carried
    tokens = gated.shape[0]
    squares = jnp.sum(gated * gated, axis=1, keepdims=True)
    square_ref[...] = jnp.broadcast_to(squares, (tokens, 128)).T[:1]
    gated = (gated * gain_ref[...]).astype(BF16)
    groups, _, features = out_ref.shape
    for g in range(groups):
        out_ref[g] = jnp.dot(
            gated, w_ref[:, g * features : (g + 1) * features], preferred_element_type=F32
        ).astype(BF16)


def scale_kernel(inner, summed_ref, square_ref, out_ref):
    tokens, features = out_ref.shape
    factor = lax.rsqrt(square_ref[...] * (1.0 / inner) + 1e-05)
    factor = jnp.broadcast_to(factor, (128, tokens)).T
    for i in range(features // 128):
        span = slice(i * 128, (i + 1) * 128)
        out_ref[:, span] = (summed_ref[:, span].astype(F32) * factor).astype(BF16)


def call(kernel, ins, outs, args, flops=0, moved=0, limit=None):
    return pl.pallas_call(
        kernel,
        in_specs=ins,
        out_specs=[VMEM] * len(outs),
        out_shape=[jax.ShapeDtypeStruct(*o) for o in outs],
        cost_estimate=pl.CostEstimate(flops=flops, bytes_accessed=moved, transcendentals=0),
        compiler_params=pltpu.CompilerParams(vmem_limit_bytes=limit or 16 * 2**20),
    )(*args)


def body(
    input_x, input_z, input_b, input_c, step_raw, doc_starts, log_rate, step_bias, skip_gain, norm_gain, out_weight
):
    tokens, channels = input_x.shape
    heads = log_rate.shape[0]
    width = channels // heads
    state_width = input_b.shape[1]
    devices = lax.axis_size("seq")
    parts = lax.axis_size("head")
    planes = devices // N_ROW
    in_plane = [[p * N_ROW + i for i in range(N_ROW)] for p in range(planes)]
    across = [[p * N_ROW + i for p in range(planes)] for i in range(N_ROW)]
    sent = (width + PAD, state_width)

    pieces, rows, cols = call(
        state_kernel,
        [SMEM, SMEM] + [VMEM] * 4,
        [((heads, *sent), BF16), ((5 * heads, tokens), F32), ((tokens, 128), F32)],
        (log_rate, step_bias, step_raw.T, doc_starts.reshape(1, tokens), input_x, input_b),
        flops=2 * tokens * channels * state_width,
        moved=2 * tokens * channels,
    )
    got = lax.all_to_all(pieces, "seq", 0, 0, axis_index_groups=in_plane)
    own, opened = call(
        intra_kernel,
        [SMEM] + [VMEM] * 6,
        [((tokens, channels), F32)] * 2,
        (skip_gain, rows, cols, input_x, input_z, input_b, input_c),
        flops=2 * tokens * tokens * channels,
        moved=12 * tokens * channels,
    )
    (totals,) = call(plane_kernel, [VMEM], [((planes, *sent), BF16)], (got,), moved=2**19)
    got_planes = lax.all_to_all(totals, "seq", 0, 0, axis_index_groups=across)
    plane = lax.div(lax.axis_index("seq"), N_ROW).reshape(1)
    (entries,) = call(
        entry_kernel, [SMEM, VMEM, VMEM], [((N_ROW, width, state_width), BF16)], (plane, got, got_planes), moved=2**19
    )
    entries = lax.all_to_all(entries, "seq", 0, 0, axis_index_groups=in_plane)
    partial, squares = call(
        project_kernel,
        [VMEM] * 6,
        [((parts, tokens, out_weight.shape[1] // parts), BF16), ((1, tokens), F32)],
        (entries, input_c, own, opened, norm_gain.reshape(1, channels), out_weight),
        flops=2 * tokens * channels * out_weight.shape[1],
        moved=8 * 2**20,
        limit=32 * 2**20,
    )
    summed = lax.psum_scatter(partial, "head", scatter_dimension=0, tiled=False)
    squares = lax.psum(squares, "head")
    (out,) = call(
        lambda *refs: scale_kernel(channels * parts, *refs),
        [VMEM] * 2,
        [(summed.shape, BF16)],
        (summed, squares),
        moved=2**19,
    )
    return out


def solution(mesh):
    in_specs = (
        P("seq", "head"),
        P("seq", "head"),
        P("seq", None),
        P("seq", None),
        P("seq", "head"),
        P("seq"),
        P("head"),
        P("head"),
        P("head"),
        P("head"),
        P("head", None),
    )
    out_specs = P("seq", "head")
    return jax.shard_map(body, mesh=mesh, in_specs=in_specs, out_specs=out_specs, check_vma=False)
```

time: 267 us -> 112 us (0.42)
  the two profiles are of different devices: /device:TPU:8 before, /device:TPU:24 now
where the time goes in v1:
time: 112 us; the launch traced here: 111 us
  waiting for transfers between devices  34.9 us (31%)
  blocking collectives  26.3 us (23%)
  starting transfers between devices  13.7 us (12%)
  between operations  13.5 us (12%)
  local copies, waits for them, and re-layouts  13.4 us (12%)
  Pallas kernels  9.16 us (8%)
    reduce_scatter x1, waiting for transfers between devices, body(): summed = lax.psum_scatter(partial, 'head', scatter_dimension=0, tiled=False)  25.4 us
    psum x1, blocking collectives, body(): squares = lax.psum(squares, 'head')  15.7 us
    unnamed x30, local copies, waits for them, and re-layouts  13.4 us
    all_to_all x1, blocking collectives, body(): got = lax.all_to_all(pieces, 'seq', 0, 0, axis_index_groups=in_plane)  10.6 us
    all_to_all x1, starting transfers between devices, body(): got_planes = lax.all_to_all(totals, 'seq', 0, 0, axis_index_groups=across)  10.3 us
    all_to_all x1, waiting for transfers between devices, body(): got_planes = lax.all_to_all(totals, 'seq', 0, 0, axis_index_groups=across)  9.54 us
    pallas_call x6, Pallas kernels, call(): pl.pallas_call(kernel, in_specs=ins, out_specs=[VMEM] * len(outs), out_sh...  9.16 us
    all_to_all x1, starting transfers between devices, body(): entries = lax.all_to_all(entries, 'seq', 0, 0, axis_index_groups=in_plane)  3.37 us
  transfers between devices with their start and end apart: 3, of which 2 were waited for; matrix products, arithmetic and copies ran while one was open for 0% of the time, Pallas kernels for 2%

profile of v1, /device:TPU:24, one launch (start us, length us, event | category | flops | bytes accessed | tf_op | source)
XLA Modules:
  0.0 111.0 jit_solution(11278547769055296827)
XLA Ops:
  6.5 0.0 copy-start.1
  6.5 0.9 copy-done.1
  7.5 0.0 copy-start.6
  7.5 0.8 copy-done.6
  8.3 0.0 copy-start.9
  8.3 0.7 copy-done.9
  9.0 0.0 copy-start.11
  9.0 0.7 copy-done.11
  9.7 0.0 copy-start.12
  9.7 0.7 copy-done.12
  10.4 0.0 copy-start.13
  10.4 0.7 copy-done.13
  11.0 1.9 %shard_map.109 = (bf16[8,80,128]{2,1,0:T(8,128)(2,1)S(1)}, f32[40,256]{1,0:T(8,128)S(1)}, f32[256,128]{1,0:T(8,128)S(1)}) custom-call(f32[8]{0:T(128)S(1)} %copy-done.12, f32[8]{0:T(128)S(1)} %copy-done.13, f32[8,256]{1,0:T(8,128)S(1)} %bitcast.6, s32[1,256]{1,0:T(1,128)S(1)} %bitcast.8, bf16[256,512]{1,0:T(8,128)(2,1)S(1)} %copy-done.1, ...), custom_call_target="tpu_custom_call" | custom-call | flops 33554432 | bytes 262144 | tf_op jit(solution)/shard_map/pallas_call | solution.py:159
  12.9 10.6 %all_to_all.15.got_ref = bf16[8,80,128]{2,1,0:T(8,128)(2,1)S(1)} all-to-all(bf16[8,80,128]{2,1,0:T(8,128)(2,1)S(1)} %get-tuple-element.12), channel_id=1, replica_groups={{0,8,16,24,32,40,48,56},{64,72,80,88,96,104,112,120},{128,136,144,152,1..., dimensions={0} | all-to-all | bytes 327680 | tf_op jit(solution)/shard_map/all_to_all | solution.py:191
  23.5 0.7 shard_map.110
  24.2 10.3 %all-to-all-start.1 = ((bf16[8,80,128]{2,1,0:T(8,128)(2,1)}), bf16[8,80,128]{2,1,0:T(8,128)(2,1)S(1)}, u32[]{:S(2)}, u32[]{:S(2)}) async-start(bf16[8,80,128]{2,1,0:T(8,128)(2,1)} %shard_map.110), calls=%async_computation.1 | async-start | bytes 327680 | tf_op jit(solution)/shard_map/all_to_all | solution.py:201
  34.5 9.5 %all-to-all-done.1.planes_ref = bf16[8,80,128]{2,1,0:T(8,128)(2,1)S(1)} async-done(((bf16[8,80,128]{2,1,0:T(8,128)(2,1)}), bf16[8,80,128]{2,1,0:T(8,128)(2,1)S(1)}, u32[]{:S(2)}, u32[]{:S(2)}) %all-to-all-start.1) | async-done | bytes 163872 | tf_op jit(solution)/shard_map/all_to_all | solution.py:201
  44.0 0.7 shard_map.111
  44.8 3.4 %all-to-all-start.2 = ((bf16[8,64,128]{2,1,0:T(8,128)(2,1)}), bf16[8,64,128]{2,1,0:T(8,128)(2,1)S(1)}, u32[]{:S(2)}, u32[]{:S(2)}) async-start(bf16[8,64,128]{2,1,0:T(8,128)(2,1)} %shard_map.111), calls=%async_computation.2 | async-start | bytes 262144 | tf_op jit(solution)/shard_map/all_to_all | solution.py:206
  48.2 0.0 reduce-scatter.2.cloned.1.call-start
  48.2 0.0 copy-start.2
  48.2 0.9 copy-done.2
  49.2 0.0 copy-start.3
  49.2 0.8 copy-done.3
  50.0 0.0 copy-start.7
  50.0 0.8 copy-done.7
  50.8 0.0 copy-start.8
  50.8 0.9 copy-done.8
  51.8 0.0 copy-start.14
  51.8 0.7 copy-done.14
  52.4 2.2 %shard_map.112 = (f32[256,512]{1,0:T(8,128)S(1)}, f32[256,512]{1,0:T(8,128)S(1)}) custom-call(f32[8]{0:T(128)S(1)} %copy-done.14, f32[40,256]{1,0:T(8,128)S(1)} %get-tuple-element.13.rows_ref, f32[256,128]{1,0:T(8,128)S(1)} %get-tuple-element.14.cols_ref, bf16[256,512]{1,0:T(8,128)(2,1)S(1)} %copy-done.2, bf16[256,512]{1,0:T(8,128)(2,1)S(1)} %copy-done.8, ...), custom_call_target="tpu_custom_call" | custom-call | flops 67108864 | bytes 1572864 | tf_op jit(solution)/shard_map/pallas_call | solution.py:159
  54.7 0.0 all-to-all-done.2.entry_ref
  54.7 0.0 copy-start
  54.7 2.2 %copy-done = bf16[512,4096]{1,0:T(8,128)(2,1)S(1)} copy-done((bf16[512,4096]{1,0:T(8,128)(2,1)S(1)}, bf16[512,4096]{1,0:T(8,128)(2,1)}, u32[]{:S(2)}) %copy-start) | copy-done | bytes 4194328
  56.9 0.0 copy-start.4
  56.9 0.8 copy-done.4
  57.7 0.0 copy-start.10
  57.7 0.7 copy-done.10
  58.4 2.8 %shard_map.113 = (bf16[8,256,512]{2,1,0:T(8,128)(2,1)}, f32[1,256]{1,0:T(1,128)S(1)}) custom-call(bf16[8,64,128]{2,1,0:T(8,128)(2,1)S(1)} %all-to-all-done.2.entry_ref, bf16[256,128]{1,0:T(8,128)(2,1)S(1)} %copy-done.4, f32[256,512]{1,0:T(8,128)S(1)} %get-tuple-element.15.own_ref, f32[256,512]{1,0:T(8,128)S(1)} %get-tuple-element.16.open_ref, ...), custom_call_target="tpu_custom_call" | custom-call | flops 1073741824 | bytes 8388608 | tf_op jit(solution)/shard_map/pallas_call | solution.py:159
  61.2 0.0 reduce-scatter.2.cloned.1.call-update
  61.2 15.7 %psum.7.refs_1_ = f32[1,256]{1,0:T(1,128)S(1)} all-reduce(f32[1,256]{1,0:T(1,128)S(1)} %get-tuple-element.18), channel_id=1, replica_groups=mesh['seq'=64,'head'=8] {'head'}, use_global_device_ids=true, to_apply=%region_1.0 | all-reduce | flops 256 | bytes 2048 | tf_op jit(solution)/shard_map/psum | solution.py:217
  77.0 25.4 %reduce-scatter.2.cloned.1.call-done = bf16[1,256,512]{2,1,0:T(8,128)(2,1)} async-done(((bf16[8,256,512]{2,1,0:T(8,128)(2,1)}), bf16[1,256,512]{2,1,0:T(8,128)(2,1)}) %reduce-scatter.2.cloned.1.call-update) | async-done | bytes 262160 | tf_op jit(solution)/shard_map/reduce_scatter | solution.py:216
  102.3 0.0 copy-start.5
  102.3 0.9 copy-done.5
  103.3 0.8 shard_map.114
Async XLA Ops:
  6.5 0.9 copy-start.1
  7.5 0.8 copy-start.6
  8.3 0.7 copy-start.9
  9.0 0.7 copy-start.11
  9.7 0.7 copy-start.12
  10.4 0.7 copy-start.13
  24.2 19.9 %all-to-all-start.1 = ((bf16[8,80,128]{2,1,0:T(8,128)(2,1)}), bf16[8,80,128]{2,1,0:T(8,128)(2,1)S(1)}, u32[]{:S(2)}, u32[]{:S(2)}) async-start(bf16[8,80,128]{2,1,0:T(8,128)(2,1)} %shard_map.110), calls=%async_computation.1 | async-start | bytes 327680 | tf_op jit(solution)/shard_map/all_to_all | solution.py:201
  44.8 9.9 %all-to-all-start.2 = ((bf16[8,64,128]{2,1,0:T(8,128)(2,1)}), bf16[8,64,128]{2,1,0:T(8,128)(2,1)S(1)}, u32[]{:S(2)}, u32[]{:S(2)}) async-start(bf16[8,64,128]{2,1,0:T(8,128)(2,1)} %shard_map.111), calls=%async_computation.2 | async-start | bytes 262144 | tf_op jit(solution)/shard_map/all_to_all | solution.py:206
  48.2 54.2 %reduce-scatter.2.cloned.1.call-start = ((), (), s32[]{:S(2)}) async-start(), calls=%async_computation.4 | async-start | bytes 2359296 | tf_op jit(solution)/shard_map/reduce_scatter | solution.py:216
  48.2 1.0 copy-start.2
  49.2 0.8 copy-start.3
  50.0 0.8 copy-start.7
  50.8 0.9 copy-start.8
  51.8 0.7 copy-start.14
  54.7 2.2 %copy-start = (bf16[512,4096]{1,0:T(8,128)(2,1)S(1)}, bf16[512,4096]{1,0:T(8,128)(2,1)}, u32[]{:S(2)}) copy-start(bf16[512,4096]{1,0:T(8,128)(2,1)} %w_ref.1) | copy-start | bytes 12582916
  56.9 0.8 copy-start.4
  57.7 0.7 copy-start.10
  102.3 0.9 copy-start.5
Sparse Core Ops, SparseCore 0:
  61.3 40.9 reduce-scatter.1

commit v2 on v1

--- a/solution.py
+++ b/solution.py
@@ -11,14 +11,22 @@
 F32, BF16 = (jnp.float32, jnp.bfloat16)
 VMEM = pl.BlockSpec(memory_space=pltpu.VMEM)
 SMEM = pl.BlockSpec(memory_space=pltpu.SMEM)
-
-
-def column_of(ref, shape):
-    rows = lax.broadcasted_iota(jnp.int32, shape, 0)
-    out = jnp.zeros(shape, F32)
-    for h in range(shape[0]):
-        out = jnp.where(rows == h, ref[h], out)
-    return out
+HBM = pl.BlockSpec(memory_space=pltpu.HBM)
+ANY = pl.BlockSpec(memory_space=pl.ANY)
+
+
+def column_of(row, shape):
+    count = shape[0]
+    spread = jnp.broadcast_to(row, (count, count))
+    same = lax.broadcasted_iota(jnp.int32, spread.shape, 0) == lax.broadcasted_iota(jnp.int32, spread.shape, 1)
+    return jnp.broadcast_to(jnp.sum(jnp.where(same, spread, 0.0), axis=1, keepdims=True), shape)
+
+
+def fetch(sources, targets, sems):
+    copies = [pltpu.make_async_copy(s, t, sems.at[i]) for i, (s, t) in enumerate(zip(sources, targets))]
+    for copy in copies:
+        copy.start()
+    return copies
 
 
 def running_sum(rows):
@@ -45,12 +53,17 @@
     return state, keep
 
 
-def state_kernel(log_rate, bias, raw_ref, flag_ref, x_ref, b_ref, out_ref, rows_ref, cols_ref):
+def state_kernel(*refs):
+    (log_rate, bias, raw_ref, flag_ref, b_ref, x_ref) = refs[9:15]
+    out_ref, rows_ref, cols_ref = refs[6:9]
+    copies = fetch(refs[:6], refs[9:15], refs[15])
+    for copy in copies[:4]:
+        copy.wait()
     heads, tokens = raw_ref.shape
     width = x_ref.shape[1] // heads
     raw = raw_ref[...]
-    dt = jax.nn.softplus(raw + column_of(bias, raw.shape))
-    rate = -jnp.exp(column_of(log_rate, raw.shape))
+    dt = jax.nn.softplus(raw + column_of(bias[...], raw.shape))
+    rate = -jnp.exp(column_of(log_rate[...], raw.shape))
     flags = jnp.broadcast_to(flag_ref[...].astype(F32), raw.shape)
     sums = running_sum(jnp.concatenate([rate * dt, flags], axis=0))
     running, resets = (sums[:heads], sums[heads:])
@@ -70,6 +83,8 @@
         ],
         axis=1,
     )
+    for copy in copies[4:]:
+        copy.wait()
     scaled = (spread * x_ref[...].astype(F32)).astype(BF16)
     states = lax.dot_general(scaled, b_ref[...], (((0,), (0,)), ((), ())), preferred_element_type=F32)
     for h in range(heads):
@@ -77,10 +92,16 @@
         out_ref[h, width:, :] = keep_rows(through[h : h + 1, :128])
 
 
-def intra_kernel(skip, rows_ref, cols_ref, x_ref, z_ref, b_ref, c_ref, own_ref, open_ref):
+def intra_kernel(*refs):
+    own_ref, open_ref, done_ref = refs[7:10]
+    c_ref, b_ref, rows_ref, cols_ref, skip_ref, x_ref, z_ref = refs[10:17]
+    for copy in fetch(refs[:7], refs[10:17], refs[17]):
+        copy.wait()
+    done_ref[...] = jnp.zeros_like(done_ref)
     tokens = x_ref.shape[0]
-    heads = skip.shape[0]
+    heads = skip_ref.shape[1]
     width = x_ref.shape[1] // heads
+    skip = skip_ref[...]
     scores = lax.dot_general(c_ref[...], b_ref[...], (((1,), (1,)), ((), ())), preferred_element_type=F32)
     reset_row = rows_ref[2 * heads : 2 * heads + 1, :]
     reset_col = cols_ref[:, 2 * heads : 2 * heads + 1]
@@ -94,14 +115,14 @@
         decays = jnp.exp(jnp.where(allowed, spread, 0.0))
         mixing = (scores * decays * rows_ref[heads + h : heads + h + 1, :]).astype(BF16)
         x_h = x_ref[:, span]
-        out = jnp.dot(mixing, x_h, preferred_element_type=F32) + skip[h] * x_h.astype(F32)
+        out = jnp.dot(mixing, x_h, preferred_element_type=F32) + skip[:, h : h + 1] * x_h.astype(F32)
         v = z_ref[:, span].astype(F32)
         gate = v / (1.0 + jnp.exp(-v))
         own_ref[:, span] = out * gate
         open_ref[:, span] = gate * cols_ref[:, 3 * heads + h : 3 * heads + h + 1]
 
 
-def plane_kernel(got_ref, out_ref):
+def plane_kernel(after_ref, got_ref, out_ref):
     count, rows, lanes = got_ref.shape
     state_rows = rows - PAD
     total, keep = piece(got_ref, 0, state_rows)
@@ -130,37 +151,46 @@
         out_ref[i + 1] = entry.astype(BF16)
 
 
-def project_kernel(entry_ref, c_ref, own_ref, open_ref, gain_ref, w_ref, out_ref, square_ref):
+def project_kernel(*refs):
+    out_ref, square_ref = refs[6:8]
+    entry_ref, c_ref, own_ref, open_ref, gain_ref, w_ref = refs[8:14]
+    groups, tokens, features = out_ref.shape
+    copies = fetch(refs[:5], refs[8:13], refs[14])
+    spans = [slice(g * features, (g + 1) * features) for g in range(groups)]
+    weights = fetch([refs[5].at[:, s] for s in spans], [w_ref.at[:, s] for s in spans], refs[15])
+    for copy in copies:
+        copy.wait()
     heads, width, lanes = entry_ref.shape
     entries = entry_ref[...].reshape(heads * width, lanes)
     carried = lax.dot_general(c_ref[...], entries, (((1,), (1,)), ((), ())), preferred_element_type=F32)
     gated = own_ref[...] + open_ref[...] * carried
-    tokens = gated.shape[0]
     squares = jnp.sum(gated * gated, axis=1, keepdims=True)
     square_ref[...] = jnp.broadcast_to(squares, (tokens, 128)).T[:1]
     gated = (gated * gain_ref[...]).astype(BF16)
-    groups, _, features = out_ref.shape
     for g in range(groups):
-        out_ref[g] = jnp.dot(
-            gated, w_ref[:, g * features : (g + 1) * features], preferred_element_type=F32
-        ).astype(BF16)
-
-
-def scale_kernel(inner, summed_ref, square_ref, out_ref):
+        weights[g].wait()
+        out_ref[g] = jnp.dot(gated, w_ref[:, spans[g]], preferred_element_type=F32).astype(BF16)
+
+
+def scale_kernel(inner, summed_hbm, square_ref, out_ref, summed_ref, sems, _):
+    (copy,) = fetch([summed_hbm], [summed_ref], sems)
     tokens, features = out_ref.shape
     factor = lax.rsqrt(square_ref[...] * (1.0 / inner) + 1e-05)
     factor = jnp.broadcast_to(factor, (128, tokens)).T
+    copy.wait()
     for i in range(features // 128):
         span = slice(i * 128, (i + 1) * 128)
         out_ref[:, span] = (summed_ref[:, span].astype(F32) * factor).astype(BF16)
 
 
-def call(kernel, ins, outs, args, flops=0, moved=0, limit=None):
+def call(kernel, ins, outs, args, fetched=(), flops=0, moved=0, limit=None):
+    scratch = [pltpu.VMEM(a.shape, a.dtype) for a in fetched]
     return pl.pallas_call(
         kernel,
         in_specs=ins,
         out_specs=[VMEM] * len(outs),
         out_shape=[jax.ShapeDtypeStruct(*o) for o in outs],
+        scratch_shapes=scratch + [pltpu.SemaphoreType.DMA((8,))] * 2 * (HBM in ins),
         cost_estimate=pl.CostEstimate(flops=flops, bytes_accessed=moved, transcendentals=0),
         compiler_params=pltpu.CompilerParams(vmem_limit_bytes=limit or 16 * 2**20),
     )(*args)
@@ -173,53 +203,71 @@
     heads = log_rate.shape[0]
     width = channels // heads
     state_width = input_b.shape[1]
-    devices = lax.axis_size("seq")
     parts = lax.axis_size("head")
-    planes = devices // N_ROW
+    planes = lax.axis_size("seq") // N_ROW
     in_plane = [[p * N_ROW + i for i in range(N_ROW)] for p in range(planes)]
     across = [[p * N_ROW + i for p in range(planes)] for i in range(N_ROW)]
     sent = (width + PAD, state_width)
 
+    local = (
+        log_rate.reshape(1, heads),
+        step_bias.reshape(1, heads),
+        step_raw.T,
+        doc_starts.reshape(1, tokens),
+        input_b,
+        input_x,
+    )
     pieces, rows, cols = call(
         state_kernel,
-        [SMEM, SMEM] + [VMEM] * 4,
+        [HBM] * 6,
         [((heads, *sent), BF16), ((5 * heads, tokens), F32), ((tokens, 128), F32)],
-        (log_rate, step_bias, step_raw.T, doc_starts.reshape(1, tokens), input_x, input_b),
+        local,
+        fetched=local,
+        limit=60 * 2**20,
         flops=2 * tokens * channels * state_width,
         moved=2 * tokens * channels,
     )
     got = lax.all_to_all(pieces, "seq", 0, 0, axis_index_groups=in_plane)
-    own, opened = call(
+    skip = skip_gain.reshape(1, heads)
+    gain = norm_gain.reshape(1, channels)
+    near = (input_c, input_b, rows, cols, skip, input_x, input_z)
+    own, opened, done = call(
         intra_kernel,
-        [SMEM] + [VMEM] * 6,
-        [((tokens, channels), F32)] * 2,
-        (skip_gain, rows, cols, input_x, input_z, input_b, input_c),
+        [HBM] * 7,
+        [((tokens, channels), F32)] * 2 + [((8, 128), F32)],
+        near,
+        fetched=near,
         flops=2 * tokens * tokens * channels,
-        moved=12 * tokens * channels,
-    )
-    (totals,) = call(plane_kernel, [VMEM], [((planes, *sent), BF16)], (got,), moved=2**19)
+        moved=8 * 2**20,
+        limit=60 * 2**20,
+    )
+    (totals,) = call(plane_kernel, [ANY, VMEM], [((planes, *sent), BF16)], (done, got), moved=2**19)
     got_planes = lax.all_to_all(totals, "seq", 0, 0, axis_index_groups=across)
     plane = lax.div(lax.axis_index("seq"), N_ROW).reshape(1)
     (entries,) = call(
         entry_kernel, [SMEM, VMEM, VMEM], [((N_ROW, width, state_width), BF16)], (plane, got, got_planes), moved=2**19
     )
     entries = lax.all_to_all(entries, "seq", 0, 0, axis_index_groups=in_plane)
+    last = (entries, input_c, own, opened, gain, out_weight)
     partial, squares = call(
         project_kernel,
-        [VMEM] * 6,
+        [HBM] * 6,
         [((parts, tokens, out_weight.shape[1] // parts), BF16), ((1, tokens), F32)],
-        (entries, input_c, own, opened, norm_gain.reshape(1, channels), out_weight),
+        last,
+        fetched=last,
         flops=2 * tokens * channels * out_weight.shape[1],
         moved=8 * 2**20,
-        limit=32 * 2**20,
+        limit=60 * 2**20,
     )
     summed = lax.psum_scatter(partial, "head", scatter_dimension=0, tiled=False)
     squares = lax.psum(squares, "head")
     (out,) = call(
         lambda *refs: scale_kernel(channels * parts, *refs),
-        [VMEM] * 2,
+        [HBM, VMEM],
         [(summed.shape, BF16)],
         (summed, squares),
+        fetched=(summed,),
+        limit=60 * 2**20,
         moved=2**19,
     )
     return out

time: 112 us -> 106 us (0.946)
  the two profiles are of different devices: /device:TPU:24 before, /device:TPU:4 now
where the time goes in v2:
time: 106 us
  waiting for transfers between devices  33 us (31%)
  blocking collectives  26.7 us (25%)
  Pallas kernels  16.8 us (16%)
  starting transfers between devices  15.2 us (14%)
  between operations  13.5 us (13%)
    reduce_scatter x1, waiting for transfers between devices, body(): summed = lax.psum_scatter(partial, 'head', scatter_dimension=0, tiled=False)  22.9 us
    psum x1, blocking collectives, body(): squares = lax.psum(squares, 'head')  18.3 us
    pallas_call x6, Pallas kernels, call(): pl.pallas_call(kernel, in_specs=ins, out_specs=[VMEM] * len(outs), out_sh...  16.8 us
    all_to_all x1, waiting for transfers between devices, body(): got_planes = lax.all_to_all(totals, 'seq', 0, 0, axis_index_groups=across)  10 us
    all_to_all x1, starting transfers between devices, body(): got = lax.all_to_all(pieces, 'seq', 0, 0, axis_index_groups=in_plane)  9.2 us
    all_to_all x1, blocking collectives, body(): entries = lax.all_to_all(entries, 'seq', 0, 0, axis_index_groups=in_plane)  8.37 us
    all_to_all x1, starting transfers between devices, body(): got_planes = lax.all_to_all(totals, 'seq', 0, 0, axis_index_groups=across)  5.93 us
  transfers between devices with their start and end apart: 3, of which 2 were waited for; matrix products, arithmetic and copies ran while one was open for 0% of the time, Pallas kernels for 4%

profile of v2, /device:TPU:4, one launch (start us, length us, event | category | flops | bytes accessed | tf_op | source)
XLA Modules:
  0.0 105.8 jit_solution(9566339588461940924)
XLA Ops:
  6.5 2.9 %shard_map.109 = (bf16[8,80,128]{2,1,0:T(8,128)(2,1)}, f32[40,256]{1,0:T(8,128)}, f32[256,128]{1,0:T(8,128)}) custom-call(f32[1,8]{1,0:T(1,128)} %bitcast.12, f32[1,8]{1,0:T(1,128)} %bitcast.13, f32[8,256]{1,0:T(8,128)} %bitcast.9, s32[1,256]{1,0:T(1,128)} %bitcast.11, bf16[256,128]{1,0:T(8,128)(2,1)} %refs_1_.2, bf16[256,512]{1,0:T(8,128)(2,1)} %refs_5_.4), custom_call_target="tpu_custom_call" | custom-call | flops 33554432 | bytes 262144 | tf_op jit(solution)/shard_map/pallas_call | solution.py:188
  9.5 9.2 %all-to-all-start = ((bf16[8,80,128]{2,1,0:T(8,128)(2,1)}), bf16[8,80,128]{2,1,0:T(8,128)(2,1)S(1)}, u32[]{:S(2)}, u32[]{:S(2)}) async-start(bf16[8,80,128]{2,1,0:T(8,128)(2,1)} %get-tuple-element.13), calls=%async_computation | async-start | bytes 327680 | tf_op jit(solution)/shard_map/all_to_all | solution.py:230
  18.7 4.0 %shard_map.110 = (f32[256,512]{1,0:T(8,128)}, f32[256,512]{1,0:T(8,128)}, f32[8,128]{1,0:T(8,128)}) custom-call(bf16[256,128]{1,0:T(8,128)(2,1)} %refs_1_.3, bf16[256,128]{1,0:T(8,128)(2,1)} %refs_1_.2, f32[40,256]{1,0:T(8,128)} %get-tuple-element.14.refs_2_, f32[256,128]{1,0:T(8,128)} %get-tuple-element.15.refs_3_, f32[1,8]{1,0:T(1,128)} %bitcast.14, ...), custom_call_target="tpu_custom_call" | custom-call | flops 67108864 | bytes 8388608 | tf_op jit(solution)/shard_map/pallas_call | solution.py:188
  22.7 0.0 all-to-all-done.got_ref
  22.7 0.0 copy-start
  22.7 0.7 copy-done
  23.4 0.7 shard_map.111
  24.1 5.9 %all-to-all-start.1 = ((bf16[8,80,128]{2,1,0:T(8,128)(2,1)}), bf16[8,80,128]{2,1,0:T(8,128)(2,1)S(1)}, u32[]{:S(2)}, u32[]{:S(2)}) async-start(bf16[8,80,128]{2,1,0:T(8,128)(2,1)} %shard_map.111), calls=%async_computation.1 | async-start | bytes 327680 | tf_op jit(solution)/shard_map/all_to_all | solution.py:245
  30.1 0.0 reduce-scatter.2.cloned.1.call-start
  30.1 10.0 %all-to-all-done.1.planes_ref = bf16[8,80,128]{2,1,0:T(8,128)(2,1)S(1)} async-done(((bf16[8,80,128]{2,1,0:T(8,128)(2,1)}), bf16[8,80,128]{2,1,0:T(8,128)(2,1)S(1)}, u32[]{:S(2)}, u32[]{:S(2)}) %all-to-all-start.1) | async-done | bytes 163872 | tf_op jit(solution)/shard_map/all_to_all | solution.py:245
  40.2 0.1 shard_map.112
  40.2 8.4 %all_to_all.15.refs_0_ = bf16[8,64,128]{2,1,0:T(8,128)(2,1)} all-to-all(bf16[8,64,128]{2,1,0:T(8,128)(2,1)S(1)} %shard_map.112), channel_id=1, replica_groups={{0,8,16,24,32,40,48,56},{64,72,80,88,96,104,112,120},{128,136,144,152,1..., dimensions={0} | all-to-all | bytes 262144 | tf_op jit(solution)/shard_map/all_to_all | solution.py:250
  48.6 6.5 %shard_map.113 = (bf16[8,256,512]{2,1,0:T(8,128)(2,1)}, f32[1,256]{1,0:T(1,128)}) custom-call(bf16[8,64,128]{2,1,0:T(8,128)(2,1)} %all_to_all.15.refs_0_, bf16[256,128]{1,0:T(8,128)(2,1)} %refs_1_.3, f32[256,512]{1,0:T(8,128)} %get-tuple-element.17.refs_2_, f32[256,512]{1,0:T(8,128)} %get-tuple-element.18.refs_3_, f32[1,512]{1,0:T(1,128)} %bitcast.10, ...), custom_call_target="tpu_custom_call" | custom-call | flops 1073741824 | bytes 8388608 | tf_op jit(solution)/shard_map/pallas_call | solution.py:188
  55.2 0.0 reduce-scatter.2.cloned.1.call-update
  55.2 18.3 %psum.7.refs_1_ = f32[1,256]{1,0:T(1,128)} all-reduce(f32[1,256]{1,0:T(1,128)} %get-tuple-element.20), channel_id=1, replica_groups=mesh['seq'=64,'head'=8] {'head'}, use_global_device_ids=true, to_apply=%region_1.0 | all-reduce | flops 256 | bytes 2048 | tf_op jit(solution)/shard_map/psum | solution.py:263
  73.5 22.9 %reduce-scatter.2.cloned.1.call-done = bf16[1,256,512]{2,1,0:T(8,128)(2,1)} async-done(((bf16[8,256,512]{2,1,0:T(8,128)(2,1)}), bf16[1,256,512]{2,1,0:T(8,128)(2,1)}) %reduce-scatter.2.cloned.1.call-update) | async-done | bytes 262160 | tf_op jit(solution)/shard_map/reduce_scatter | solution.py:262
  96.4 2.5 %shard_map.114 = bf16[256,512]{1,0:T(8,128)(2,1)} custom-call(bf16[256,512]{1,0:T(8,128)(2,1)} %bitcast.8, f32[1,256]{1,0:T(1,128)} %psum.7.refs_1_), custom_call_target="tpu_custom_call" | custom-call | bytes 524288 | tf_op jit(solution)/shard_map/pallas_call | solution.py:188
Async XLA Ops:
  9.5 13.2 %all-to-all-start = ((bf16[8,80,128]{2,1,0:T(8,128)(2,1)}), bf16[8,80,128]{2,1,0:T(8,128)(2,1)S(1)}, u32[]{:S(2)}, u32[]{:S(2)}) async-start(bf16[8,80,128]{2,1,0:T(8,128)(2,1)} %get-tuple-element.13), calls=%async_computation | async-start | bytes 327680 | tf_op jit(solution)/shard_map/all_to_all | solution.py:230
  22.7 0.7 copy-start
  24.1 16.0 %all-to-all-start.1 = ((bf16[8,80,128]{2,1,0:T(8,128)(2,1)}), bf16[8,80,128]{2,1,0:T(8,128)(2,1)S(1)}, u32[]{:S(2)}, u32[]{:S(2)}) async-start(bf16[8,80,128]{2,1,0:T(8,128)(2,1)} %shard_map.111), calls=%async_computation.1 | async-start | bytes 327680 | tf_op jit(solution)/shard_map/all_to_all | solution.py:245
  30.1 66.4 %reduce-scatter.2.cloned.1.call-start = ((), (), s32[]{:S(2)}) async-start(), calls=%async_computation.4 | async-start | bytes 2359296 | tf_op jit(solution)/shard_map/reduce_scatter | solution.py:262
Sparse Core Ops, SparseCore 0:
  55.3 41.0 reduce-scatter.1

commit v3 on v2

--- a/solution.py
+++ b/solution.py
@@ -152,27 +152,33 @@
 
 
 def project_kernel(*refs):
-    out_ref, square_ref = refs[6:8]
+    out_hbm, square_ref = refs[6:8]
     entry_ref, c_ref, own_ref, open_ref, gain_ref, w_ref = refs[8:14]
+    out_ref, in_sems, w_sems, out_sems = refs[14:]
     groups, tokens, features = out_ref.shape
-    copies = fetch(refs[:5], refs[8:13], refs[14])
+    copies = fetch(refs[:5], refs[8:13], in_sems)
+    for copy in copies:
+        copy.wait()
     spans = [slice(g * features, (g + 1) * features) for g in range(groups)]
-    weights = fetch([refs[5].at[:, s] for s in spans], [w_ref.at[:, s] for s in spans], refs[15])
-    for copy in copies:
-        copy.wait()
+    weights = fetch([refs[5].at[:, s] for s in spans], [w_ref.at[:, s] for s in spans], w_sems)
     heads, width, lanes = entry_ref.shape
     entries = entry_ref[...].reshape(heads * width, lanes)
     carried = lax.dot_general(c_ref[...], entries, (((1,), (1,)), ((), ())), preferred_element_type=F32)
     gated = own_ref[...] + open_ref[...] * carried
+    scaled = (gated * gain_ref[...]).astype(BF16)
+    sent = []
+    for g in range(groups):
+        weights[g].wait()
+        out_ref[g] = jnp.dot(scaled, w_ref[:, spans[g]], preferred_element_type=F32).astype(BF16)
+        sent.append(pltpu.make_async_copy(out_ref.at[g], out_hbm.at[g], out_sems.at[g]))
+        sent[g].start()
     squares = jnp.sum(gated * gated, axis=1, keepdims=True)
     square_ref[...] = jnp.broadcast_to(squares, (tokens, 128)).T[:1]
-    gated = (gated * gain_ref[...]).astype(BF16)
-    for g in range(groups):
-        weights[g].wait()
-        out_ref[g] = jnp.dot(gated, w_ref[:, spans[g]], preferred_element_type=F32).astype(BF16)
-
-
-def scale_kernel(inner, summed_hbm, square_ref, out_ref, summed_ref, sems, _):
+    for copy in sent:
+        copy.wait()
+
+
+def scale_kernel(inner, summed_hbm, square_ref, out_ref, summed_ref, sems, *_):
     (copy,) = fetch([summed_hbm], [summed_ref], sems)
     tokens, features = out_ref.shape
     factor = lax.rsqrt(square_ref[...] * (1.0 / inner) + 1e-05)
@@ -183,16 +189,18 @@
         out_ref[:, span] = (summed_ref[:, span].astype(F32) * factor).astype(BF16)
 
 
-def call(kernel, ins, outs, args, fetched=(), flops=0, moved=0, limit=None):
+def call(kernel, ins, outs, args, fetched=(), staged=(), flops=0, moved=0):
     scratch = [pltpu.VMEM(a.shape, a.dtype) for a in fetched]
+    scratch += [pltpu.VMEM(*a) for a in staged]
+    scratch += [pltpu.SemaphoreType.DMA((8,))] * 3 * (len(fetched) > 0)
     return pl.pallas_call(
         kernel,
         in_specs=ins,
-        out_specs=[VMEM] * len(outs),
+        out_specs=[HBM] * len(staged) + [VMEM] * (len(outs) - len(staged)),
         out_shape=[jax.ShapeDtypeStruct(*o) for o in outs],
-        scratch_shapes=scratch + [pltpu.SemaphoreType.DMA((8,))] * 2 * (HBM in ins),
+        scratch_shapes=scratch,
         cost_estimate=pl.CostEstimate(flops=flops, bytes_accessed=moved, transcendentals=0),
-        compiler_params=pltpu.CompilerParams(vmem_limit_bytes=limit or 16 * 2**20),
+        compiler_params=pltpu.CompilerParams(vmem_limit_bytes=(60 if fetched else 16) * 2**20),
     )(*args)
 
 
@@ -223,7 +231,6 @@
         [((heads, *sent), BF16), ((5 * heads, tokens), F32), ((tokens, 128), F32)],
         local,
         fetched=local,
-        limit=60 * 2**20,
         flops=2 * tokens * channels * state_width,
         moved=2 * tokens * channels,
     )
@@ -239,7 +246,6 @@
         fetched=near,
         flops=2 * tokens * tokens * channels,
         moved=8 * 2**20,
-        limit=60 * 2**20,
     )
     (totals,) = call(plane_kernel, [ANY, VMEM], [((planes, *sent), BF16)], (done, got), moved=2**19)
     got_planes = lax.all_to_all(totals, "seq", 0, 0, axis_index_groups=across)
@@ -249,15 +255,16 @@
     )
     entries = lax.all_to_all(entries, "seq", 0, 0, axis_index_groups=in_plane)
     last = (entries, input_c, own, opened, gain, out_weight)
+    partials = ((parts, tokens, out_weight.shape[1] // parts), BF16)
     partial, squares = call(
         project_kernel,
         [HBM] * 6,
-        [((parts, tokens, out_weight.shape[1] // parts), BF16), ((1, tokens), F32)],
+        [partials, ((1, tokens), F32)],
         last,
         fetched=last,
+        staged=[partials],
         flops=2 * tokens * channels * out_weight.shape[1],
         moved=8 * 2**20,
-        limit=60 * 2**20,
     )
     summed = lax.psum_scatter(partial, "head", scatter_dimension=0, tiled=False)
     squares = lax.psum(squares, "head")
@@ -267,7 +274,6 @@
         [(summed.shape, BF16)],
         (summed, squares),
         fetched=(summed,),
-        limit=60 * 2**20,
         moved=2**19,
     )
     return out

time: 106 us -> 106 us (level)
  no operation moved by 1% of the time
where the time goes in v3:
time: 106 us
  waiting for transfers between devices  32.9 us (31%)
  blocking collectives  26.6 us (25%)
  Pallas kernels  16.8 us (16%)
  starting transfers between devices  15.2 us (14%)
  between operations  13.5 us (13%)
    reduce_scatter x1, waiting for transfers between devices, body(): summed = lax.psum_scatter(partial, 'head', scatter_dimension=0, tiled=False)  22.9 us
    psum x1, blocking collectives, body(): squares = lax.psum(squares, 'head')  18.3 us
    pallas_call x6, Pallas kernels, call(): pl.pallas_call(kernel, in_specs=ins, out_specs=[HBM] * len(staged) + [VME...  16.8 us
    all_to_all x1, waiting for transfers between devices, body(): got_planes = lax.all_to_all(totals, 'seq', 0, 0, axis_index_groups=across)  10 us
    all_to_all x1, starting transfers between devices, body(): got = lax.all_to_all(pieces, 'seq', 0, 0, axis_index_groups=in_plane)  9.2 us
    all_to_all x1, blocking collectives, body(): entries = lax.all_to_all(entries, 'seq', 0, 0, axis_index_groups=in_plane)  8.3 us
    all_to_all x1, starting transfers between devices, body(): got_planes = lax.all_to_all(totals, 'seq', 0, 0, axis_index_groups=across)  5.93 us
  transfers between devices with their start and end apart: 3, of which 2 were waited for; matrix products, arithmetic and copies ran while one was open for 0% of the time, Pallas kernels for 4%

profile of v3, /device:TPU:4, one launch (start us, length us, event | category | flops | bytes accessed | tf_op | source)
XLA Modules:
  0.0 105.6 jit_solution(18289974983957837502)
XLA Ops:
  6.5 3.0 %shard_map.109 = (bf16[8,80,128]{2,1,0:T(8,128)(2,1)}, f32[40,256]{1,0:T(8,128)}, f32[256,128]{1,0:T(8,128)}) custom-call(f32[1,8]{1,0:T(1,128)} %bitcast.12, f32[1,8]{1,0:T(1,128)} %bitcast.13, f32[8,256]{1,0:T(8,128)} %bitcast.9, s32[1,256]{1,0:T(1,128)} %bitcast.11, bf16[256,128]{1,0:T(8,128)(2,1)} %refs_1_.2, bf16[256,512]{1,0:T(8,128)(2,1)} %refs_5_.4), custom_call_target="tpu_custom_call" | custom-call | flops 33554432 | bytes 262144 | tf_op jit(solution)/shard_map/pallas_call | solution.py:196
  9.6 9.2 %all-to-all-start = ((bf16[8,80,128]{2,1,0:T(8,128)(2,1)}), bf16[8,80,128]{2,1,0:T(8,128)(2,1)S(1)}, u32[]{:S(2)}, u32[]{:S(2)}) async-start(bf16[8,80,128]{2,1,0:T(8,128)(2,1)} %get-tuple-element.13), calls=%async_computation | async-start | bytes 327680 | tf_op jit(solution)/shard_map/all_to_all | solution.py:237
  18.8 4.1 %shard_map.110 = (f32[256,512]{1,0:T(8,128)}, f32[256,512]{1,0:T(8,128)}, f32[8,128]{1,0:T(8,128)}) custom-call(bf16[256,128]{1,0:T(8,128)(2,1)} %refs_1_.3, bf16[256,128]{1,0:T(8,128)(2,1)} %refs_1_.2, f32[40,256]{1,0:T(8,128)} %get-tuple-element.14.refs_2_, f32[256,128]{1,0:T(8,128)} %get-tuple-element.15.refs_3_, f32[1,8]{1,0:T(1,128)} %bitcast.14, ...), custom_call_target="tpu_custom_call" | custom-call | flops 67108864 | bytes 8388608 | tf_op jit(solution)/shard_map/pallas_call | solution.py:196
  22.9 0.0 all-to-all-done.got_ref
  22.9 0.0 copy-start
  22.9 0.7 copy-done
  23.6 0.7 shard_map.111
  24.3 5.9 %all-to-all-start.1 = ((bf16[8,80,128]{2,1,0:T(8,128)(2,1)}), bf16[8,80,128]{2,1,0:T(8,128)(2,1)S(1)}, u32[]{:S(2)}, u32[]{:S(2)}) async-start(bf16[8,80,128]{2,1,0:T(8,128)(2,1)} %shard_map.111), calls=%async_computation.1 | async-start | bytes 327680 | tf_op jit(solution)/shard_map/all_to_all | solution.py:251
  30.2 0.0 reduce-scatter.2.cloned.1.call-start
  30.3 10.0 %all-to-all-done.1.planes_ref = bf16[8,80,128]{2,1,0:T(8,128)(2,1)S(1)} async-done(((bf16[8,80,128]{2,1,0:T(8,128)(2,1)}), bf16[8,80,128]{2,1,0:T(8,128)(2,1)S(1)}, u32[]{:S(2)}, u32[]{:S(2)}) %all-to-all-start.1) | async-done | bytes 163872 | tf_op jit(solution)/shard_map/all_to_all | solution.py:251
  40.3 0.1 shard_map.112
  40.4 8.3 %all_to_all.15.refs_0_ = bf16[8,64,128]{2,1,0:T(8,128)(2,1)} all-to-all(bf16[8,64,128]{2,1,0:T(8,128)(2,1)S(1)} %shard_map.112), channel_id=1, replica_groups={{0,8,16,24,32,40,48,56},{64,72,80,88,96,104,112,120},{128,136,144,152,1..., dimensions={0} | all-to-all | bytes 262144 | tf_op jit(solution)/shard_map/all_to_all | solution.py:256
  48.7 6.3 %shard_map.113 = (bf16[8,256,512]{2,1,0:T(8,128)(2,1)}, f32[1,256]{1,0:T(1,128)}) custom-call(bf16[8,64,128]{2,1,0:T(8,128)(2,1)} %all_to_all.15.refs_0_, bf16[256,128]{1,0:T(8,128)(2,1)} %refs_1_.3, f32[256,512]{1,0:T(8,128)} %get-tuple-element.17.refs_2_, f32[256,512]{1,0:T(8,128)} %get-tuple-element.18.refs_3_, f32[1,512]{1,0:T(1,128)} %bitcast.10, ...), custom_call_target="tpu_custom_call" | custom-call | flops 1073741824 | bytes 8388608 | tf_op jit(solution)/shard_map/pallas_call | solution.py:196
  55.0 0.0 reduce-scatter.2.cloned.1.call-update
  55.0 18.3 %psum.7.refs_1_ = f32[1,256]{1,0:T(1,128)} all-reduce(f32[1,256]{1,0:T(1,128)} %get-tuple-element.20), channel_id=1, replica_groups=mesh['seq'=64,'head'=8] {'head'}, use_global_device_ids=true, to_apply=%region_1.0 | all-reduce | flops 256 | bytes 2048 | tf_op jit(solution)/shard_map/psum | solution.py:270
  73.3 22.9 %reduce-scatter.2.cloned.1.call-done = bf16[1,256,512]{2,1,0:T(8,128)(2,1)} async-done(((bf16[8,256,512]{2,1,0:T(8,128)(2,1)}), bf16[1,256,512]{2,1,0:T(8,128)(2,1)}) %reduce-scatter.2.cloned.1.call-update) | async-done | bytes 262160 | tf_op jit(solution)/shard_map/reduce_scatter | solution.py:269
  96.2 2.6 %shard_map.114 = bf16[256,512]{1,0:T(8,128)(2,1)} custom-call(bf16[256,512]{1,0:T(8,128)(2,1)} %bitcast.8, f32[1,256]{1,0:T(1,128)} %psum.7.refs_1_), custom_call_target="tpu_custom_call" | custom-call | bytes 524288 | tf_op jit(solution)/shard_map/pallas_call | solution.py:196
Async XLA Ops:
  9.6 13.3 %all-to-all-start = ((bf16[8,80,128]{2,1,0:T(8,128)(2,1)}), bf16[8,80,128]{2,1,0:T(8,128)(2,1)S(1)}, u32[]{:S(2)}, u32[]{:S(2)}) async-start(bf16[8,80,128]{2,1,0:T(8,128)(2,1)} %get-tuple-element.13), calls=%async_computation | async-start | bytes 327680 | tf_op jit(solution)/shard_map/all_to_all | solution.py:237
  22.9 0.7 copy-start
  24.3 16.0 %all-to-all-start.1 = ((bf16[8,80,128]{2,1,0:T(8,128)(2,1)}), bf16[8,80,128]{2,1,0:T(8,128)(2,1)S(1)}, u32[]{:S(2)}, u32[]{:S(2)}) async-start(bf16[8,80,128]{2,1,0:T(8,128)(2,1)} %shard_map.111), calls=%async_computation.1 | async-start | bytes 327680 | tf_op jit(solution)/shard_map/all_to_all | solution.py:251
  30.2 66.0 %reduce-scatter.2.cloned.1.call-start = ((), (), s32[]{:S(2)}) async-start(), calls=%async_computation.4 | async-start | bytes 2359296 | tf_op jit(solution)/shard_map/reduce_scatter | solution.py:269
Sparse Core Ops, SparseCore 0:
  55.1 41.0 reduce-scatter.1

commit v4 on v2

--- a/solution.py
+++ b/solution.py
@@ -1,3 +1,5 @@
+import functools
+
 import jax
 import jax.numpy as jnp
 from jax import lax
@@ -7,6 +9,8 @@
 
 SPAN = 256
 N_ROW = 8
+N_PART = 8
+NEAR = (3, -3, 2, -2, 1, -1, 0)
 PAD = 16
 F32, BF16 = (jnp.float32, jnp.bfloat16)
 VMEM = pl.BlockSpec(memory_space=pltpu.VMEM)
@@ -151,48 +155,96 @@
         out_ref[i + 1] = entry.astype(BF16)
 
 
-def project_kernel(*refs):
-    out_ref, square_ref = refs[6:8]
-    entry_ref, c_ref, own_ref, open_ref, gain_ref, w_ref = refs[8:14]
-    groups, tokens, features = out_ref.shape
-    copies = fetch(refs[:5], refs[8:13], refs[14])
-    spans = [slice(g * features, (g + 1) * features) for g in range(groups)]
-    weights = fetch([refs[5].at[:, s] for s in spans], [w_ref.at[:, s] for s in spans], refs[15])
-    for copy in copies:
-        copy.wait()
+def bring_kernel(*refs):
+    count = len(refs) // 2 - 1
+    for copy in fetch(refs[1 : count + 1], refs[count + 1 : -1], refs[-1]):
+        copy.wait()
+
+
+def put_squares(ref, squares):
+    high = squares.astype(BF16).astype(F32)
+    middle = (squares - high).astype(BF16).astype(F32)
+    low = squares - high - middle
+    first = jnp.concatenate([high, middle], axis=1)
+    second = jnp.concatenate([low, jnp.zeros_like(low)], axis=1)
+    row = lax.broadcasted_iota(jnp.int32, (PAD, ref.shape[1]), 0)
+    rows = jnp.where(row == 0, first, jnp.where(row == 1, second, 0.0))
+    ref[ref.shape[0] - PAD :, :] = rows.astype(BF16)
+
+
+def get_squares(ref):
+    rows = jnp.sum(ref[ref.shape[0] - PAD :, :].astype(F32), axis=0, keepdims=True)
+    half = ref.shape[1] // 2
+    return rows[:, :half] + rows[:, half:]
+
+
+def columns(w_hbm, me, away, features):
+    place = (me[0] + away + N_PART) % N_PART
+    return w_hbm.at[:, pl.ds(pl.multiple_of(place * features, features), features)]
+
+
+def gate_kernel(me, entry_ref, c_ref, own_ref, open_ref, gain_ref, w_hbm, *refs):
+    scaled_ref, square_ref, right_ref, left_ref, w_ref, sems = refs
     heads, width, lanes = entry_ref.shape
+    tokens = own_ref.shape[0]
+    half = tokens // 2
+    (copy,) = fetch([columns(w_hbm, me, N_PART // 2, w_ref.shape[1])], [w_ref], sems)
     entries = entry_ref[...].reshape(heads * width, lanes)
     carried = lax.dot_general(c_ref[...], entries, (((1,), (1,)), ((), ())), preferred_element_type=F32)
     gated = own_ref[...] + open_ref[...] * carried
+    scaled = (gated * gain_ref[...]).astype(BF16)
+    scaled_ref[...] = scaled
     squares = jnp.sum(gated * gated, axis=1, keepdims=True)
-    square_ref[...] = jnp.broadcast_to(squares, (tokens, 128)).T[:1]
-    gated = (gated * gain_ref[...]).astype(BF16)
-    for g in range(groups):
-        weights[g].wait()
-        out_ref[g] = jnp.dot(gated, w_ref[:, spans[g]], preferred_element_type=F32).astype(BF16)
-
-
-def scale_kernel(inner, summed_hbm, square_ref, out_ref, summed_ref, sems, _):
-    (copy,) = fetch([summed_hbm], [summed_ref], sems)
+    squares = jnp.broadcast_to(squares, (tokens, 128)).T[:1]
+    square_ref[...] = squares
+    first = lax.broadcasted_iota(jnp.int32, squares.shape, 1) < half
+    put_squares(right_ref, jnp.where(first, squares, 0.0))
+    put_squares(left_ref, jnp.where(first, 0.0, squares))
+    copy.wait()
+    far = jnp.dot(scaled, w_ref[...], preferred_element_type=F32).astype(BF16)
+    right_ref[:half] = far[:half]
+    left_ref[:half] = far[half:]
+
+
+def chunks_kernel(me, scaled_ref, w_hbm, out_ref, w_ref, sems):
+    features = out_ref.shape[2]
+    copies = fetch([columns(w_hbm, me, away, features) for away in NEAR], [w_ref.at[i] for i in range(len(NEAR))], sems)
+    for i, copy in enumerate(copies):
+        copy.wait()
+        out_ref[i] = jnp.dot(scaled_ref[...], w_ref[i], preferred_element_type=F32).astype(BF16)
+
+
+def join_kernel(index, from_row, got_ref, chunks_ref, square_ref, out_ref):
+    tokens = chunks_ref.shape[1]
+    count = got_ref.shape[0] - PAD
+    if count < tokens:
+        out_ref[:tokens] = chunks_ref[index]
+    rows = slice(from_row, from_row + count)
+    out_ref[rows] = (chunks_ref[index, rows].astype(F32) + got_ref[:count].astype(F32)).astype(BF16)
+    put_squares(out_ref, square_ref[...] + get_squares(got_ref))
+
+
+def end_kernel(inner, right_ref, left_ref, chunks_ref, square_ref, out_ref):
     tokens, features = out_ref.shape
-    factor = lax.rsqrt(square_ref[...] * (1.0 / inner) + 1e-05)
+    squares = square_ref[...] + get_squares(right_ref) + get_squares(left_ref)
+    factor = lax.rsqrt(squares * (1.0 / inner) + 1e-05)
     factor = jnp.broadcast_to(factor, (128, tokens)).T
-    copy.wait()
     for i in range(features // 128):
         span = slice(i * 128, (i + 1) * 128)
-        out_ref[:, span] = (summed_ref[:, span].astype(F32) * factor).astype(BF16)
-
-
-def call(kernel, ins, outs, args, fetched=(), flops=0, moved=0, limit=None):
-    scratch = [pltpu.VMEM(a.shape, a.dtype) for a in fetched]
+        total = chunks_ref[len(NEAR) - 1, :, span].astype(F32)
+        total = total + right_ref[:tokens, span].astype(F32) + left_ref[:tokens, span].astype(F32)
+        out_ref[:, span] = (total * factor).astype(BF16)
+
+
+def call(kernel, ins, outs, args, scratch=(), flops=0, moved=0, limit=24):
     return pl.pallas_call(
         kernel,
         in_specs=ins,
         out_specs=[VMEM] * len(outs),
         out_shape=[jax.ShapeDtypeStruct(*o) for o in outs],
-        scratch_shapes=scratch + [pltpu.SemaphoreType.DMA((8,))] * 2 * (HBM in ins),
+        scratch_shapes=[pltpu.VMEM(a.shape, a.dtype) for a in scratch] + [pltpu.SemaphoreType.DMA((8,))] * (HBM in ins),
         cost_estimate=pl.CostEstimate(flops=flops, bytes_accessed=moved, transcendentals=0),
-        compiler_params=pltpu.CompilerParams(vmem_limit_bytes=limit or 16 * 2**20),
+        compiler_params=pltpu.CompilerParams(vmem_limit_bytes=limit * 2**20),
     )(*args)
 
 
@@ -203,7 +255,6 @@
     heads = log_rate.shape[0]
     width = channels // heads
     state_width = input_b.shape[1]
-    parts = lax.axis_size("head")
     planes = lax.axis_size("seq") // N_ROW
     in_plane = [[p * N_ROW + i for i in range(N_ROW)] for p in range(planes)]
     across = [[p * N_ROW + i for p in range(planes)] for i in range(N_ROW)]
@@ -222,8 +273,8 @@
         [HBM] * 6,
         [((heads, *sent), BF16), ((5 * heads, tokens), F32), ((tokens, 128), F32)],
         local,
-        fetched=local,
-        limit=60 * 2**20,
+        scratch=local,
+        limit=60,
         flops=2 * tokens * channels * state_width,
         moved=2 * tokens * channels,
     )
@@ -236,10 +287,10 @@
         [HBM] * 7,
         [((tokens, channels), F32)] * 2 + [((8, 128), F32)],
         near,
-        fetched=near,
+        scratch=near,
+        limit=60,
         flops=2 * tokens * tokens * channels,
         moved=8 * 2**20,
-        limit=60 * 2**20,
     )
     (totals,) = call(plane_kernel, [ANY, VMEM], [((planes, *sent), BF16)], (done, got), moved=2**19)
     got_planes = lax.all_to_all(totals, "seq", 0, 0, axis_index_groups=across)
@@ -247,27 +298,58 @@
     (entries,) = call(
         entry_kernel, [SMEM, VMEM, VMEM], [((N_ROW, width, state_width), BF16)], (plane, got, got_planes), moved=2**19
     )
+    needed = (input_c, own, opened, gain)
+    needed = call(
+        bring_kernel,
+        [ANY] + [HBM] * len(needed),
+        [(a.shape, a.dtype) for a in needed],
+        (entries, *needed),
+        moved=2**21,
+        limit=48,
+    )
     entries = lax.all_to_all(entries, "seq", 0, 0, axis_index_groups=in_plane)
-    last = (entries, input_c, own, opened, gain, out_weight)
-    partial, squares = call(
-        project_kernel,
-        [HBM] * 6,
-        [((parts, tokens, out_weight.shape[1] // parts), BF16), ((1, tokens), F32)],
-        last,
-        fetched=last,
-        flops=2 * tokens * channels * out_weight.shape[1],
-        moved=8 * 2**20,
-        limit=60 * 2**20,
-    )
-    summed = lax.psum_scatter(partial, "head", scatter_dimension=0, tiled=False)
-    squares = lax.psum(squares, "head")
+    me = lax.axis_index("head").reshape(1)
+    features = out_weight.shape[1] // N_PART
+    half_sent = ((tokens // 2 + PAD, features), BF16)
+    full_sent = ((tokens + PAD, features), BF16)
+    scaled, squares, right, left = call(
+        gate_kernel,
+        [SMEM] + [VMEM] * 5 + [HBM],
+        [((tokens, channels), BF16), ((1, tokens), F32), half_sent, half_sent],
+        (me, entries, *needed, out_weight),
+        scratch=[jax.ShapeDtypeStruct((channels, features), BF16)],
+        limit=50,
+        flops=2 * tokens * channels * features,
+        moved=2**21,
+    )
+    turn = [[(i, (i + step) % N_PART) for i in range(N_PART)] for step in (1, -1)]
+    right = lax.ppermute(right, "head", turn[0])
+    left = lax.ppermute(left, "head", turn[1])
+    (chunks,) = call(
+        chunks_kernel,
+        [SMEM, VMEM, HBM],
+        [((len(NEAR), tokens, features), BF16)],
+        (me, scaled, out_weight),
+        scratch=[jax.ShapeDtypeStruct((len(NEAR), channels, features), BF16)],
+        limit=50,
+        flops=2 * tokens * channels * features * len(NEAR),
+        moved=2**22,
+    )
+    for step in range(N_PART // 2 - 1):
+        begin = tokens // 2 if step == 0 else 0
+        (right,) = call(
+            functools.partial(join_kernel, 2 * step, 0), [VMEM] * 3, [full_sent], (right, chunks, squares), moved=2**19
+        )
+        right = lax.ppermute(right, "head", turn[0])
+        (left,) = call(
+            functools.partial(join_kernel, 2 * step + 1, begin), [VMEM] * 3, [full_sent], (left, chunks, squares), moved=2**19
+        )
+        left = lax.ppermute(left, "head", turn[1])
     (out,) = call(
-        lambda *refs: scale_kernel(channels * parts, *refs),
-        [HBM, VMEM],
-        [(summed.shape, BF16)],
-        (summed, squares),
-        fetched=(summed,),
-        limit=60 * 2**20,
+        functools.partial(end_kernel, channels * N_PART),
+        [VMEM] * 4,
+        [((tokens, features), BF16)],
+        (right, left, chunks, squares),
         moved=2**19,
     )
     return out

time: 106 us -> 94.1 us (0.89)
  the two profiles are of different devices: /device:TPU:4 before, /device:TPU:24 now
where the time goes in v4:
time: 94.1 us; the launch traced here: 93.3 us
  starting transfers between devices  46.7 us (50%)
  waiting for transfers between devices  27.3 us (29%)
  Pallas kernels  14.8 us (16%)
  local copies, waits for them, and re-layouts  4.27 us (5%)
    ppermute x4, starting transfers between devices, body(): right = lax.ppermute(right, 'head', turn[0])  21 us
    pallas_call x14, Pallas kernels, call(): pl.pallas_call(kernel, in_specs=ins, out_specs=[VMEM] * len(outs), out_sh...  14.8 us
    all_to_all x1, starting transfers between devices, body(): got_planes = lax.all_to_all(totals, 'seq', 0, 0, axis_index_groups=across)  10.3 us
    all_to_all x1, waiting for transfers between devices, body(): got_planes = lax.all_to_all(totals, 'seq', 0, 0, axis_index_groups=across)  9.54 us
    ppermute x4, starting transfers between devices, body(): left = lax.ppermute(left, 'head', turn[1])  7.67 us
    ppermute x4, waiting for transfers between devices, body(): right = lax.ppermute(right, 'head', turn[0])  7.32 us
    ppermute x4, waiting for transfers between devices, body(): left = lax.ppermute(left, 'head', turn[1])  5.72 us
    all_to_all x1, starting transfers between devices, body(): got = lax.all_to_all(pieces, 'seq', 0, 0, axis_index_groups=in_plane)  4.31 us
  transfers between devices with their start and end apart: 11, of which 7 were waited for; matrix products, arithmetic and copies ran while one was open for 0% of the time, Pallas kernels for 9%

profile of v4, /device:TPU:24, one launch (start us, length us, event | category | flops | bytes accessed | tf_op | source)
XLA Modules:
  0.0 93.3 jit_solution(4852617330063388056)
XLA Ops:
  0.0 2.9 %shard_map.109 = (bf16[8,80,128]{2,1,0:T(8,128)(2,1)}, f32[40,256]{1,0:T(8,128)}, f32[256,128]{1,0:T(8,128)}) custom-call(f32[1,8]{1,0:T(1,128)} %bitcast.11, f32[1,8]{1,0:T(1,128)} %bitcast.12, f32[8,256]{1,0:T(8,128)} %bitcast.9, s32[1,256]{1,0:T(1,128)} %bitcast.10, bf16[256,128]{1,0:T(8,128)(2,1)} %refs_1_.2, bf16[256,512]{1,0:T(8,128)(2,1)} %refs_5_.3), custom_call_target="tpu_custom_call" | custom-call | flops 33554432 | bytes 262144 | tf_op jit(solution)/shard_map/pallas_call | solution.py:240
  2.9 4.3 %all-to-all-start = ((bf16[8,80,128]{2,1,0:T(8,128)(2,1)}), bf16[8,80,128]{2,1,0:T(8,128)(2,1)S(1)}, u32[]{:S(2)}, u32[]{:S(2)}) async-start(bf16[8,80,128]{2,1,0:T(8,128)(2,1)} %get-tuple-element.19), calls=%async_computation | async-start | bytes 327680 | tf_op jit(solution)/shard_map/all_to_all | solution.py:281
  7.2 4.0 %shard_map.110 = (f32[256,512]{1,0:T(8,128)}, f32[256,512]{1,0:T(8,128)}, f32[8,128]{1,0:T(8,128)}) custom-call(bf16[256,128]{1,0:T(8,128)(2,1)} %refs_1_.3, bf16[256,128]{1,0:T(8,128)(2,1)} %refs_1_.2, f32[40,256]{1,0:T(8,128)} %get-tuple-element.20.refs_2_, f32[256,128]{1,0:T(8,128)} %get-tuple-element.21.refs_3_, f32[1,8]{1,0:T(1,128)} %bitcast.13, ...), custom_call_target="tpu_custom_call" | custom-call | flops 67108864 | bytes 8388608 | tf_op jit(solution)/shard_map/pallas_call | solution.py:240
  11.2 2.5 %all-to-all-done.got_ref = bf16[8,80,128]{2,1,0:T(8,128)(2,1)S(1)} async-done(((bf16[8,80,128]{2,1,0:T(8,128)(2,1)}), bf16[8,80,128]{2,1,0:T(8,128)(2,1)S(1)}, u32[]{:S(2)}, u32[]{:S(2)}) %all-to-all-start) | async-done | bytes 163872 | tf_op jit(solution)/shard_map/all_to_all | solution.py:281
  13.7 0.0 copy-start.3
  13.7 0.7 copy-done.3
  14.4 0.7 shard_map.111
  15.1 10.3 %all-to-all-start.1 = ((bf16[8,80,128]{2,1,0:T(8,128)(2,1)}), bf16[8,80,128]{2,1,0:T(8,128)(2,1)S(1)}, u32[]{:S(2)}, u32[]{:S(2)}) async-start(bf16[8,80,128]{2,1,0:T(8,128)(2,1)} %shard_map.111), calls=%async_computation.1 | async-start | bytes 327680 | tf_op jit(solution)/shard_map/all_to_all | solution.py:296
  25.4 9.5 %all-to-all-done.1.planes_ref = bf16[8,80,128]{2,1,0:T(8,128)(2,1)S(1)} async-done(((bf16[8,80,128]{2,1,0:T(8,128)(2,1)}), bf16[8,80,128]{2,1,0:T(8,128)(2,1)S(1)}, u32[]{:S(2)}, u32[]{:S(2)}) %all-to-all-start.1) | async-done | bytes 163872 | tf_op jit(solution)/shard_map/all_to_all | solution.py:296
  34.9 0.7 shard_map.112.refs_0_
  35.7 3.4 %all-to-all-start.2 = ((bf16[8,64,128]{2,1,0:T(8,128)(2,1)}), bf16[8,64,128]{2,1,0:T(8,128)(2,1)S(1)}, u32[]{:S(2)}, u32[]{:S(2)}) async-start(bf16[8,64,128]{2,1,0:T(8,128)(2,1)} %shard_map.112.refs_0_), calls=%async_computation.2 | async-start | bytes 262144 | tf_op jit(solution)/shard_map/all_to_all | solution.py:310
  39.0 0.0 copy-start
  39.0 1.0 %copy-done = f32[256,512]{1,0:T(8,128)S(1)} copy-done((f32[256,512]{1,0:T(8,128)S(1)}, f32[256,512]{1,0:T(8,128)}, u32[]{:S(2)}) %copy-start) | copy-done | bytes 524312
  40.1 0.0 copy-start.1
  40.1 1.0 %copy-done.1 = f32[256,512]{1,0:T(8,128)S(1)} copy-done((f32[256,512]{1,0:T(8,128)S(1)}, f32[256,512]{1,0:T(8,128)}, u32[]{:S(2)}) %copy-start.1) | copy-done | bytes 524312
  41.1 0.0 copy-start.2
  41.1 0.8 copy-done.2
  42.0 0.0 copy-start.4
  42.0 0.7 copy-done.4
  42.6 0.2 shard_map.113
  42.9 2.2 %all-to-all-done.2.entry_ref = bf16[8,64,128]{2,1,0:T(8,128)(2,1)S(1)} async-done(((bf16[8,64,128]{2,1,0:T(8,128)(2,1)}), bf16[8,64,128]{2,1,0:T(8,128)(2,1)S(1)}, u32[]{:S(2)}, u32[]{:S(2)}) %all-to-all-start.2) | async-done | bytes 131104 | tf_op jit(solution)/shard_map/all_to_all | solution.py:310
  45.1 1.7 %shard_map.114 = (bf16[256,512]{1,0:T(8,128)(2,1)S(1)}, f32[1,256]{1,0:T(1,128)S(1)}, bf16[144,512]{1,0:T(8,128)(2,1)S(1)}, bf16[144,512]{1,0:T(8,128)(2,1)S(1)}) custom-call(s32[1]{0:T(128)} %bitcast.me, bf16[8,64,128]{2,1,0:T(8,128)(2,1)S(1)} %all-to-all-done.2.entry_ref, bf16[256,128]{1,0:T(8,128)(2,1)S(1)} %get-tuple-element.25.c_ref, ...), custom_call_target="tpu_custom_call" | custom-call | flops 134217728 | bytes 2097152 | tf_op jit(solution)/shard_map/pallas_call | solution.py:240
  46.8 4.7 %collective-permute-start = (bf16[144,512]{1,0:T(8,128)(2,1)S(1)}, bf16[144,512]{1,0:T(8,128)(2,1)S(1)}, u32[]{:S(2)}, u32[]{:S(2)}) collective-permute-start(bf16[144,512]{1,0:T(8,128)(2,1)S(1)} %get-tuple-element.29), channel_id=1, source_target_pairs={{0,1},{1,2},{2,3},{3,4},{4,5},{5,6},{6,7},{7,0},{8,9},{9,10},{10,1... | collective-permute-start | bytes 442376 | tf_op jit(solution)/shard_map/ppermute | solution.py:326
  51.5 1.9 %collective-permute-start.4 = (bf16[144,512]{1,0:T(8,128)(2,1)S(1)}, bf16[144,512]{1,0:T(8,128)(2,1)S(1)}, u32[]{:S(2)}, u32[]{:S(2)}) collective-permute-start(bf16[144,512]{1,0:T(8,128)(2,1)S(1)} %get-tuple-element.32), channel_id=1, source_target_pairs={{0,7},{1,0},{2,1},{3,2},{4,3},{5,4},{6,5},{7,6},{8,15},{9,8},{10,9... | collective-permute-start | bytes 442376 | tf_op jit(solution)/shard_map/ppermute | solution.py:327
  53.4 3.3 %shard_map.115.chunks_ref = bf16[7,256,512]{2,1,0:T(8,128)(2,1)S(1)} custom-call(s32[1]{0:T(128)} %bitcast.me, bf16[256,512]{1,0:T(8,128)(2,1)S(1)} %get-tuple-element.30.scaled_ref, bf16[512,4096]{1,0:T(8,128)(2,1)} %w_hbm.3), custom_call_target="tpu_custom_call" | custom-call | flops 939524096 | bytes 4194304 | tf_op jit(solution)/shard_map/pallas_call | solution.py:240
  56.7 0.0 collective-permute-done.got_ref
  56.7 0.1 shard_map.116
  56.8 5.1 %collective-permute-start.1 = (bf16[272,512]{1,0:T(8,128)(2,1)S(1)}, bf16[272,512]{1,0:T(8,128)(2,1)S(1)}, u32[]{:S(2)}, u32[]{:S(2)}) collective-permute-start(bf16[272,512]{1,0:T(8,128)(2,1)S(1)} %shard_map.116), channel_id=1, source_target_pairs={{0,1},{1,2},{2,3},{3,4},{4,5},{5,6},{6,7},{7,0},{8,9},{9,10},{10,1... | collective-permute-start | bytes 835592 | tf_op jit(solution)/shard_map/ppermute | solution.py:343
  61.9 0.0 collective-permute-done.4.got_ref
  61.9 0.1 shard_map.119
  62.0 1.9 %collective-permute-start.5 = (bf16[272,512]{1,0:T(8,128)(2,1)S(1)}, bf16[272,512]{1,0:T(8,128)(2,1)S(1)}, u32[]{:S(2)}, u32[]{:S(2)}) collective-permute-start(bf16[272,512]{1,0:T(8,128)(2,1)S(1)} %shard_map.119), channel_id=1, source_target_pairs={{0,7},{1,0},{2,1},{3,2},{4,3},{5,4},{6,5},{7,6},{8,15},{9,8},{10,9... | collective-permute-start | bytes 835592 | tf_op jit(solution)/shard_map/ppermute | solution.py:347
  63.9 3.1 %collective-permute-done.1.got_ref = bf16[272,512]{1,0:T(8,128)(2,1)S(1)} collective-permute-done((bf16[272,512]{1,0:T(8,128)(2,1)S(1)}, bf16[272,512]{1,0:T(8,128)(2,1)S(1)}, u32[]{:S(2)}, u32[]{:S(2)}) %collective-permute-start.1) | collective-permute-done | bytes 278560 | tf_op jit(solution)/shard_map/ppermute | solution.py:343
  67.0 0.1 shard_map.117
  67.1 5.6 %collective-permute-start.2 = (bf16[272,512]{1,0:T(8,128)(2,1)S(1)}, bf16[272,512]{1,0:T(8,128)(2,1)S(1)}, u32[]{:S(2)}, u32[]{:S(2)}) collective-permute-start(bf16[272,512]{1,0:T(8,128)(2,1)S(1)} %shard_map.117), channel_id=1, source_target_pairs={{0,1},{1,2},{2,3},{3,4},{4,5},{5,6},{6,7},{7,0},{8,9},{9,10},{10,1... | collective-permute-start | bytes 835592 | tf_op jit(solution)/shard_map/ppermute | solution.py:343
  72.7 0.0 collective-permute-done.5.got_ref
  72.7 0.1 shard_map.120
  72.8 1.9 %collective-permute-start.6 = (bf16[272,512]{1,0:T(8,128)(2,1)S(1)}, bf16[272,512]{1,0:T(8,128)(2,1)S(1)}, u32[]{:S(2)}, u32[]{:S(2)}) collective-permute-start(bf16[272,512]{1,0:T(8,128)(2,1)S(1)} %shard_map.120), channel_id=1, source_target_pairs={{0,7},{1,0},{2,1},{3,2},{4,3},{5,4},{6,5},{7,6},{8,15},{9,8},{10,9... | collective-permute-start | bytes 835592 | tf_op jit(solution)/shard_map/ppermute | solution.py:347
  74.8 2.2 %collective-permute-done.2.got_ref = bf16[272,512]{1,0:T(8,128)(2,1)S(1)} collective-permute-done((bf16[272,512]{1,0:T(8,128)(2,1)S(1)}, bf16[272,512]{1,0:T(8,128)(2,1)S(1)}, u32[]{:S(2)}, u32[]{:S(2)}) %collective-permute-start.2) | collective-permute-done | bytes 278560 | tf_op jit(solution)/shard_map/ppermute | solution.py:343
  76.9 0.1 shard_map.118
  77.0 5.6 %collective-permute-start.3 = (bf16[272,512]{1,0:T(8,128)(2,1)S(1)}, bf16[272,512]{1,0:T(8,128)(2,1)S(1)}, u32[]{:S(2)}, u32[]{:S(2)}) collective-permute-start(bf16[272,512]{1,0:T(8,128)(2,1)S(1)} %shard_map.118), channel_id=1, source_target_pairs={{0,1},{1,2},{2,3},{3,4},{4,5},{5,6},{6,7},{7,0},{8,9},{9,10},{10,1... | collective-permute-start | bytes 835592 | tf_op jit(solution)/shard_map/ppermute | solution.py:343
  82.6 0.0 collective-permute-done.6.got_ref
  82.7 0.1 shard_map.121
  82.8 1.9 %collective-permute-start.7 = (bf16[272,512]{1,0:T(8,128)(2,1)S(1)}, bf16[272,512]{1,0:T(8,128)(2,1)S(1)}, u32[]{:S(2)}, u32[]{:S(2)}) collective-permute-start(bf16[272,512]{1,0:T(8,128)(2,1)S(1)} %shard_map.121), channel_id=1, source_target_pairs={{0,7},{1,0},{2,1},{3,2},{4,3},{5,4},{6,5},{7,6},{8,15},{9,8},{10,9... | collective-permute-start | bytes 835592 | tf_op jit(solution)/shard_map/ppermute | solution.py:347
  84.7 2.0 %collective-permute-done.3.right_ref = bf16[272,512]{1,0:T(8,128)(2,1)S(1)} collective-permute-done((bf16[272,512]{1,0:T(8,128)(2,1)S(1)}, bf16[272,512]{1,0:T(8,128)(2,1)S(1)}, u32[]{:S(2)}, u32[]{:S(2)}) %collective-permute-start.3) | collective-permute-done | bytes 278560 | tf_op jit(solution)/shard_map/ppermute | solution.py:343
  86.7 5.7 %collective-permute-done.7.left_ref = bf16[272,512]{1,0:T(8,128)(2,1)S(1)} collective-permute-done((bf16[272,512]{1,0:T(8,128)(2,1)S(1)}, bf16[272,512]{1,0:T(8,128)(2,1)S(1)}, u32[]{:S(2)}, u32[]{:S(2)}) %collective-permute-start.7) | collective-permute-done | bytes 278560 | tf_op jit(solution)/shard_map/ppermute | solution.py:347
  92.4 0.9 shard_map.122
Async XLA Ops:
  2.9 10.8 %all-to-all-start = ((bf16[8,80,128]{2,1,0:T(8,128)(2,1)}), bf16[8,80,128]{2,1,0:T(8,128)(2,1)S(1)}, u32[]{:S(2)}, u32[]{:S(2)}) async-start(bf16[8,80,128]{2,1,0:T(8,128)(2,1)} %get-tuple-element.19), calls=%async_computation | async-start | bytes 327680 | tf_op jit(solution)/shard_map/all_to_all | solution.py:281
  13.7 0.7 copy-start.3
  15.1 19.9 %all-to-all-start.1 = ((bf16[8,80,128]{2,1,0:T(8,128)(2,1)}), bf16[8,80,128]{2,1,0:T(8,128)(2,1)S(1)}, u32[]{:S(2)}, u32[]{:S(2)}) async-start(bf16[8,80,128]{2,1,0:T(8,128)(2,1)} %shard_map.111), calls=%async_computation.1 | async-start | bytes 327680 | tf_op jit(solution)/shard_map/all_to_all | solution.py:296
  35.7 9.4 %all-to-all-start.2 = ((bf16[8,64,128]{2,1,0:T(8,128)(2,1)}), bf16[8,64,128]{2,1,0:T(8,128)(2,1)S(1)}, u32[]{:S(2)}, u32[]{:S(2)}) async-start(bf16[8,64,128]{2,1,0:T(8,128)(2,1)} %shard_map.112.refs_0_), calls=%async_computation.2 | async-start | bytes 262144 | tf_op jit(solution)/shard_map/all_to_all | solution.py:310
  39.0 1.0 %copy-start = (f32[256,512]{1,0:T(8,128)S(1)}, f32[256,512]{1,0:T(8,128)}, u32[]{:S(2)}) copy-start(f32[256,512]{1,0:T(8,128)} %get-tuple-element.23.refs_2_) | copy-start | bytes 1572868
  40.1 1.0 %copy-start.1 = (f32[256,512]{1,0:T(8,128)S(1)}, f32[256,512]{1,0:T(8,128)}, u32[]{:S(2)}) copy-start(f32[256,512]{1,0:T(8,128)} %get-tuple-element.24.refs_3_) | copy-start | bytes 1572868
  41.1 0.8 copy-start.2
  42.0 0.7 copy-start.4
  46.8 9.9 %collective-permute-start = (bf16[144,512]{1,0:T(8,128)(2,1)S(1)}, bf16[144,512]{1,0:T(8,128)(2,1)S(1)}, u32[]{:S(2)}, u32[]{:S(2)}) collective-permute-start(bf16[144,512]{1,0:T(8,128)(2,1)S(1)} %get-tuple-element.29), channel_id=1, source_target_pairs={{0,1},{1,2},{2,3},{3,4},{4,5},{5,6},{6,7},{7,0},{8,9},{9,10},{10,1... | collective-permute-start | bytes 442376 | tf_op jit(solution)/shard_map/ppermute | solution.py:326
  51.5 10.4 %collective-permute-start.4 = (bf16[144,512]{1,0:T(8,128)(2,1)S(1)}, bf16[144,512]{1,0:T(8,128)(2,1)S(1)}, u32[]{:S(2)}, u32[]{:S(2)}) collective-permute-start(bf16[144,512]{1,0:T(8,128)(2,1)S(1)} %get-tuple-element.32), channel_id=1, source_target_pairs={{0,7},{1,0},{2,1},{3,2},{4,3},{5,4},{6,5},{7,6},{8,15},{9,8},{10,9... | collective-permute-start | bytes 442376 | tf_op jit(solution)/shard_map/ppermute | solution.py:327
  56.8 10.3 %collective-permute-start.1 = (bf16[272,512]{1,0:T(8,128)(2,1)S(1)}, bf16[272,512]{1,0:T(8,128)(2,1)S(1)}, u32[]{:S(2)}, u32[]{:S(2)}) collective-permute-start(bf16[272,512]{1,0:T(8,128)(2,1)S(1)} %shard_map.116), channel_id=1, source_target_pairs={{0,1},{1,2},{2,3},{3,4},{4,5},{5,6},{6,7},{7,0},{8,9},{9,10},{10,1... | collective-permute-start | bytes 835592 | tf_op jit(solution)/shard_map/ppermute | solution.py:343
  62.0 10.8 %collective-permute-start.5 = (bf16[272,512]{1,0:T(8,128)(2,1)S(1)}, bf16[272,512]{1,0:T(8,128)(2,1)S(1)}, u32[]{:S(2)}, u32[]{:S(2)}) collective-permute-start(bf16[272,512]{1,0:T(8,128)(2,1)S(1)} %shard_map.119), channel_id=1, source_target_pairs={{0,7},{1,0},{2,1},{3,2},{4,3},{5,4},{6,5},{7,6},{8,15},{9,8},{10,9... | collective-permute-start | bytes 835592 | tf_op jit(solution)/shard_map/ppermute | solution.py:347
  67.1 9.8 %collective-permute-start.2 = (bf16[272,512]{1,0:T(8,128)(2,1)S(1)}, bf16[272,512]{1,0:T(8,128)(2,1)S(1)}, u32[]{:S(2)}, u32[]{:S(2)}) collective-permute-start(bf16[272,512]{1,0:T(8,128)(2,1)S(1)} %shard_map.117), channel_id=1, source_target_pairs={{0,1},{1,2},{2,3},{3,4},{4,5},{5,6},{6,7},{7,0},{8,9},{9,10},{10,1... | collective-permute-start | bytes 835592 | tf_op jit(solution)/shard_map/ppermute | solution.py:343
  72.8 9.8 %collective-permute-start.6 = (bf16[272,512]{1,0:T(8,128)(2,1)S(1)}, bf16[272,512]{1,0:T(8,128)(2,1)S(1)}, u32[]{:S(2)}, u32[]{:S(2)}) collective-permute-start(bf16[272,512]{1,0:T(8,128)(2,1)S(1)} %shard_map.120), channel_id=1, source_target_pairs={{0,7},{1,0},{2,1},{3,2},{4,3},{5,4},{6,5},{7,6},{8,15},{9,8},{10,9... | collective-permute-start | bytes 835592 | tf_op jit(solution)/shard_map/ppermute | solution.py:347
  77.0 9.6 %collective-permute-start.3 = (bf16[272,512]{1,0:T(8,128)(2,1)S(1)}, bf16[272,512]{1,0:T(8,128)(2,1)S(1)}, u32[]{:S(2)}, u32[]{:S(2)}) collective-permute-start(bf16[272,512]{1,0:T(8,128)(2,1)S(1)} %shard_map.118), channel_id=1, source_target_pairs={{0,1},{1,2},{2,3},{3,4},{4,5},{5,6},{6,7},{7,0},{8,9},{9,10},{10,1... | collective-permute-start | bytes 835592 | tf_op jit(solution)/shard_map/ppermute | solution.py:343
  82.8 9.6 %collective-permute-start.7 = (bf16[272,512]{1,0:T(8,128)(2,1)S(1)}, bf16[272,512]{1,0:T(8,128)(2,1)S(1)}, u32[]{:S(2)}, u32[]{:S(2)}) collective-permute-start(bf16[272,512]{1,0:T(8,128)(2,1)S(1)} %shard_map.121), channel_id=1, source_target_pairs={{0,7},{1,0},{2,1},{3,2},{4,3},{5,4},{6,5},{7,6},{8,15},{9,8},{10,9... | collective-permute-start | bytes 835592 | tf_op jit(solution)/shard_map/ppermute | solution.py:347

commit v5 on v4

--- a/solution.py
+++ b/solution.py
@@ -10,7 +10,6 @@
 SPAN = 256
 N_ROW = 8
 N_PART = 8
-NEAR = (3, -3, 2, -2, 1, -1, 0)
 PAD = 16
 F32, BF16 = (jnp.float32, jnp.bfloat16)
 VMEM = pl.BlockSpec(memory_space=pltpu.VMEM)
@@ -183,56 +182,71 @@
     return w_hbm.at[:, pl.ds(pl.multiple_of(place * features, features), features)]
 
 
+def project(scaled_ref, w_ref, copy):
+    copy.wait()
+    return jnp.dot(scaled_ref[...], w_ref[...], preferred_element_type=F32).astype(BF16)
+
+
 def gate_kernel(me, entry_ref, c_ref, own_ref, open_ref, gain_ref, w_hbm, *refs):
-    scaled_ref, square_ref, right_ref, left_ref, w_ref, sems = refs
+    scaled_ref, square_ref, far_right_ref, far_left_ref, right_ref, left_ref, w_ref, sems = refs
     heads, width, lanes = entry_ref.shape
     tokens = own_ref.shape[0]
     half = tokens // 2
-    (copy,) = fetch([columns(w_hbm, me, N_PART // 2, w_ref.shape[1])], [w_ref], sems)
+    away = (N_PART // 2, 3, -3)
+    copies = fetch([columns(w_hbm, me, a, w_ref.shape[2]) for a in away], [w_ref.at[i] for i in range(3)], sems)
     entries = entry_ref[...].reshape(heads * width, lanes)
     carried = lax.dot_general(c_ref[...], entries, (((1,), (1,)), ((), ())), preferred_element_type=F32)
     gated = own_ref[...] + open_ref[...] * carried
-    scaled = (gated * gain_ref[...]).astype(BF16)
-    scaled_ref[...] = scaled
+    scaled_ref[...] = (gated * gain_ref[...]).astype(BF16)
     squares = jnp.sum(gated * gated, axis=1, keepdims=True)
     squares = jnp.broadcast_to(squares, (tokens, 128)).T[:1]
     square_ref[...] = squares
     first = lax.broadcasted_iota(jnp.int32, squares.shape, 1) < half
-    put_squares(right_ref, jnp.where(first, squares, 0.0))
-    put_squares(left_ref, jnp.where(first, 0.0, squares))
-    copy.wait()
-    far = jnp.dot(scaled, w_ref[...], preferred_element_type=F32).astype(BF16)
-    right_ref[:half] = far[:half]
-    left_ref[:half] = far[half:]
-
-
-def chunks_kernel(me, scaled_ref, w_hbm, out_ref, w_ref, sems):
-    features = out_ref.shape[2]
-    copies = fetch([columns(w_hbm, me, away, features) for away in NEAR], [w_ref.at[i] for i in range(len(NEAR))], sems)
-    for i, copy in enumerate(copies):
-        copy.wait()
-        out_ref[i] = jnp.dot(scaled_ref[...], w_ref[i], preferred_element_type=F32).astype(BF16)
-
-
-def join_kernel(index, from_row, got_ref, chunks_ref, square_ref, out_ref):
-    tokens = chunks_ref.shape[1]
-    count = got_ref.shape[0] - PAD
-    if count < tokens:
-        out_ref[:tokens] = chunks_ref[index]
-    rows = slice(from_row, from_row + count)
-    out_ref[rows] = (chunks_ref[index, rows].astype(F32) + got_ref[:count].astype(F32)).astype(BF16)
-    put_squares(out_ref, square_ref[...] + get_squares(got_ref))
-
-
-def end_kernel(inner, right_ref, left_ref, chunks_ref, square_ref, out_ref):
+    far = project(scaled_ref, w_ref.at[0], copies[0])
+    far_right_ref[:half] = far[:half]
+    far_left_ref[:half] = far[half:]
+    put_squares(far_right_ref, jnp.where(first, squares, 0.0))
+    put_squares(far_left_ref, jnp.where(first, 0.0, squares))
+    for i, ref in ((1, right_ref), (2, left_ref)):
+        ref[:tokens] = project(scaled_ref, w_ref.at[i], copies[i])
+        put_squares(ref, squares)
+
+
+def near_kernel(me, scaled_ref, square_ref, w_hbm, right_ref, left_ref, near_ref, w_ref, sems):
+    tokens, features = near_ref.shape[1:]
+    copies = fetch([columns(w_hbm, me, a, features) for a in (1, -1, 2, -2, 0)], [w_ref.at[i] for i in range(5)], sems)
+    for i, ref in enumerate((right_ref, left_ref)):
+        ref[:tokens] = project(scaled_ref, w_ref.at[i], copies[i])
+        put_squares(ref, square_ref[...])
+    for i in range(2, 5):
+        near_ref[i - 2] = project(scaled_ref, w_ref.at[i], copies[i])
+
+
+def join_kernel(index, far_row, near_ref, square_ref, far_ref, got_ref, out_ref):
+    tokens = near_ref.shape[1]
+    half = tokens // 2
+    for row in (0, half):
+        rows = slice(row, row + half)
+        total = near_ref[index, rows].astype(F32) + got_ref[rows].astype(F32)
+        if row == far_row:
+            total = total + far_ref[:half].astype(F32)
+        out_ref[rows] = total.astype(BF16)
+    put_squares(out_ref, square_ref[...] + get_squares(got_ref) + get_squares(far_ref))
+
+
+def end_kernel(inner, near_ref, square_ref, *refs):
+    got_refs, out_ref = refs[:-1], refs[-1]
     tokens, features = out_ref.shape
-    squares = square_ref[...] + get_squares(right_ref) + get_squares(left_ref)
+    squares = square_ref[...]
+    for ref in got_refs:
+        squares = squares + get_squares(ref)
     factor = lax.rsqrt(squares * (1.0 / inner) + 1e-05)
     factor = jnp.broadcast_to(factor, (128, tokens)).T
     for i in range(features // 128):
         span = slice(i * 128, (i + 1) * 128)
-        total = chunks_ref[len(NEAR) - 1, :, span].astype(F32)
-        total = total + right_ref[:tokens, span].astype(F32) + left_ref[:tokens, span].astype(F32)
+        total = near_ref[2, :, span].astype(F32)
+        for ref in got_refs:
+            total = total + ref[:tokens, span].astype(F32)
         out_ref[:, span] = (total * factor).astype(BF16)
 
 
@@ -312,45 +326,45 @@
     features = out_weight.shape[1] // N_PART
     half_sent = ((tokens // 2 + PAD, features), BF16)
     full_sent = ((tokens + PAD, features), BF16)
-    scaled, squares, right, left = call(
+    def turn(array, step):
+        return lax.ppermute(array, "head", [(i, (i + step) % N_PART) for i in range(N_PART)])
+
+    scaled, squares, far_right, far_left, right, left = call(
         gate_kernel,
         [SMEM] + [VMEM] * 5 + [HBM],
-        [((tokens, channels), BF16), ((1, tokens), F32), half_sent, half_sent],
+        [((tokens, channels), BF16), ((1, tokens), F32), half_sent, half_sent, full_sent, full_sent],
         (me, entries, *needed, out_weight),
-        scratch=[jax.ShapeDtypeStruct((channels, features), BF16)],
+        scratch=[jax.ShapeDtypeStruct((3, channels, features), BF16)],
+        flops=6 * tokens * channels * features,
+        moved=2**21,
         limit=50,
-        flops=2 * tokens * channels * features,
-        moved=2**21,
-    )
-    turn = [[(i, (i + step) % N_PART) for i in range(N_PART)] for step in (1, -1)]
-    right = lax.ppermute(right, "head", turn[0])
-    left = lax.ppermute(left, "head", turn[1])
-    (chunks,) = call(
-        chunks_kernel,
-        [SMEM, VMEM, HBM],
-        [((len(NEAR), tokens, features), BF16)],
-        (me, scaled, out_weight),
-        scratch=[jax.ShapeDtypeStruct((len(NEAR), channels, features), BF16)],
+    )
+    far_right, far_left = turn(far_right, 2), turn(far_left, -2)
+    right, left = turn(right, 1), turn(left, -1)
+    next_right, next_left, near = call(
+        near_kernel,
+        [SMEM, VMEM, VMEM, HBM],
+        [full_sent, full_sent, ((3, tokens, features), BF16)],
+        (me, scaled, squares, out_weight),
+        scratch=[jax.ShapeDtypeStruct((5, channels, features), BF16)],
+        flops=10 * tokens * channels * features,
+        moved=2**22,
         limit=50,
-        flops=2 * tokens * channels * features * len(NEAR),
-        moved=2**22,
-    )
-    for step in range(N_PART // 2 - 1):
-        begin = tokens // 2 if step == 0 else 0
-        (right,) = call(
-            functools.partial(join_kernel, 2 * step, 0), [VMEM] * 3, [full_sent], (right, chunks, squares), moved=2**19
-        )
-        right = lax.ppermute(right, "head", turn[0])
-        (left,) = call(
-            functools.partial(join_kernel, 2 * step + 1, begin), [VMEM] * 3, [full_sent], (left, chunks, squares), moved=2**19
-        )
-        left = lax.ppermute(left, "head", turn[1])
+    )
+    next_right, next_left = turn(next_right, 1), turn(next_left, -1)
+    (right,) = call(
+        functools.partial(join_kernel, 0, 0), [VMEM] * 4, [full_sent], (near, squares, far_right, right), moved=2**20
+    )
+    (left,) = call(
+        functools.partial(join_kernel, 1, tokens // 2), [VMEM] * 4, [full_sent], (near, squares, far_left, left), moved=2**20
+    )
+    right, left = turn(right, 2), turn(left, -2)
     (out,) = call(
         functools.partial(end_kernel, channels * N_PART),
-        [VMEM] * 4,
+        [VMEM] * 6,
         [((tokens, features), BF16)],
-        (right, left, chunks, squares),
-        moved=2**19,
+        (near, squares, next_right, next_left, right, left),
+        moved=2**20,
     )
     return out
 

time: 94.1 us -> 95.4 us (1.014)
  the two profiles are of different devices: /device:TPU:24 before, /device:TPU:1 now
where the time goes in v5:
time: 95.4 us; the launch traced here: 94.5 us
  starting transfers between devices  49.9 us (52%)
  waiting for transfers between devices  25.8 us (27%)
  Pallas kernels  14.4 us (15%)
  local copies, waits for them, and re-layouts  4.28 us (4%)
    ppermute x8, starting transfers between devices, turn(): lax.ppermute(array, 'head', [(i, (i + step) % N_PART) for i in range(N_PA...  28.1 us
    ppermute x8, waiting for transfers between devices, turn(): lax.ppermute(array, 'head', [(i, (i + step) % N_PART) for i in range(N_PA...  14.7 us
    pallas_call x10, Pallas kernels, call(): pl.pallas_call(kernel, in_specs=ins, out_specs=[VMEM] * len(outs), out_sh...  14.4 us
    all_to_all x1, starting transfers between devices, body(): got = lax.all_to_all(pieces, 'seq', 0, 0, axis_index_groups=in_plane)  10.2 us
    all_to_all x1, waiting for transfers between devices, body(): got_planes = lax.all_to_all(totals, 'seq', 0, 0, axis_index_groups=across)  8.07 us
    all_to_all x1, starting transfers between devices, body(): entries = lax.all_to_all(entries, 'seq', 0, 0, axis_index_groups=in_plane)  5.93 us
    all_to_all x1, starting transfers between devices, body(): got_planes = lax.all_to_all(totals, 'seq', 0, 0, axis_index_groups=across)  5.65 us
    unnamed x10, local copies, waits for them, and re-layouts  4.28 us
  transfers between devices with their start and end apart: 11, of which 6 were waited for; matrix products, arithmetic and copies ran while one was open for 0% of the time, Pallas kernels for 7%

profile of v5, /device:TPU:1, one launch (start us, length us, event | category | flops | bytes accessed | tf_op | source)
XLA Modules:
  0.0 94.5 jit_solution(13391284527459940326)
XLA Ops:
  0.0 2.9 %shard_map.109 = (bf16[8,80,128]{2,1,0:T(8,128)(2,1)}, f32[40,256]{1,0:T(8,128)}, f32[256,128]{1,0:T(8,128)}) custom-call(f32[1,8]{1,0:T(1,128)} %bitcast.11, f32[1,8]{1,0:T(1,128)} %bitcast.12, f32[8,256]{1,0:T(8,128)} %bitcast.9, s32[1,256]{1,0:T(1,128)} %bitcast.10, bf16[256,128]{1,0:T(8,128)(2,1)} %refs_1_.2, bf16[256,512]{1,0:T(8,128)(2,1)} %refs_5_.3), custom_call_target="tpu_custom_call" | custom-call | flops 33554432 | bytes 262144 | tf_op jit(solution)/shard_map/pallas_call | solution.py:254
  2.9 10.2 %all-to-all-start = ((bf16[8,80,128]{2,1,0:T(8,128)(2,1)}), bf16[8,80,128]{2,1,0:T(8,128)(2,1)S(1)}, u32[]{:S(2)}, u32[]{:S(2)}) async-start(bf16[8,80,128]{2,1,0:T(8,128)(2,1)} %get-tuple-element.24), calls=%async_computation | async-start | bytes 327680 | tf_op jit(solution)/shard_map/all_to_all | solution.py:295
  13.1 4.0 %shard_map.110 = (f32[256,512]{1,0:T(8,128)}, f32[256,512]{1,0:T(8,128)}, f32[8,128]{1,0:T(8,128)}) custom-call(bf16[256,128]{1,0:T(8,128)(2,1)} %refs_1_.3, bf16[256,128]{1,0:T(8,128)(2,1)} %refs_1_.2, f32[40,256]{1,0:T(8,128)} %get-tuple-element.25.refs_2_, f32[256,128]{1,0:T(8,128)} %get-tuple-element.26.refs_3_, f32[1,8]{1,0:T(1,128)} %bitcast.13, ...), custom_call_target="tpu_custom_call" | custom-call | flops 67108864 | bytes 8388608 | tf_op jit(solution)/shard_map/pallas_call | solution.py:254
  17.0 1.6 %all-to-all-done.got_ref = bf16[8,80,128]{2,1,0:T(8,128)(2,1)S(1)} async-done(((bf16[8,80,128]{2,1,0:T(8,128)(2,1)}), bf16[8,80,128]{2,1,0:T(8,128)(2,1)S(1)}, u32[]{:S(2)}, u32[]{:S(2)}) %all-to-all-start) | async-done | bytes 163872 | tf_op jit(solution)/shard_map/all_to_all | solution.py:295
  18.7 0.0 copy-start.3
  18.7 0.7 copy-done.3
  19.3 0.7 shard_map.111
  20.1 5.7 %all-to-all-start.1 = ((bf16[8,80,128]{2,1,0:T(8,128)(2,1)}), bf16[8,80,128]{2,1,0:T(8,128)(2,1)S(1)}, u32[]{:S(2)}, u32[]{:S(2)}) async-start(bf16[8,80,128]{2,1,0:T(8,128)(2,1)} %shard_map.111), calls=%async_computation.1 | async-start | bytes 327680 | tf_op jit(solution)/shard_map/all_to_all | solution.py:310
  25.7 8.1 %all-to-all-done.1.planes_ref = bf16[8,80,128]{2,1,0:T(8,128)(2,1)S(1)} async-done(((bf16[8,80,128]{2,1,0:T(8,128)(2,1)}), bf16[8,80,128]{2,1,0:T(8,128)(2,1)S(1)}, u32[]{:S(2)}, u32[]{:S(2)}) %all-to-all-start.1) | async-done | bytes 163872 | tf_op jit(solution)/shard_map/all_to_all | solution.py:310
  33.8 0.7 shard_map.112.refs_0_
  34.5 5.9 %all-to-all-start.2 = ((bf16[8,64,128]{2,1,0:T(8,128)(2,1)}), bf16[8,64,128]{2,1,0:T(8,128)(2,1)S(1)}, u32[]{:S(2)}, u32[]{:S(2)}) async-start(bf16[8,64,128]{2,1,0:T(8,128)(2,1)} %shard_map.112.refs_0_), calls=%async_computation.2 | async-start | bytes 262144 | tf_op jit(solution)/shard_map/all_to_all | solution.py:324
  40.4 0.0 copy-start
  40.4 1.0 %copy-done = f32[256,512]{1,0:T(8,128)S(1)} copy-done((f32[256,512]{1,0:T(8,128)S(1)}, f32[256,512]{1,0:T(8,128)}, u32[]{:S(2)}) %copy-start) | copy-done | bytes 524312
  41.5 0.0 copy-start.1
  41.5 1.0 %copy-done.1 = f32[256,512]{1,0:T(8,128)S(1)} copy-done((f32[256,512]{1,0:T(8,128)S(1)}, f32[256,512]{1,0:T(8,128)}, u32[]{:S(2)}) %copy-start.1) | copy-done | bytes 524312
  42.5 0.0 copy-start.2
  42.5 0.8 copy-done.2
  43.4 0.0 copy-start.4
  43.4 0.7 copy-done.4
  44.0 0.2 shard_map.113
  44.3 1.5 %all-to-all-done.2.entry_ref = bf16[8,64,128]{2,1,0:T(8,128)(2,1)S(1)} async-done(((bf16[8,64,128]{2,1,0:T(8,128)(2,1)}), bf16[8,64,128]{2,1,0:T(8,128)(2,1)S(1)}, u32[]{:S(2)}, u32[]{:S(2)}) %all-to-all-start.2) | async-done | bytes 131104 | tf_op jit(solution)/shard_map/all_to_all | solution.py:324
  45.7 2.0 %shard_map.114 = (bf16[256,512]{1,0:T(8,128)(2,1)S(1)}, f32[1,256]{1,0:T(1,128)S(1)}, bf16[144,512]{1,0:T(8,128)(2,1)S(1)}, bf16[144,512]{1,0:T(8,128)(2,1)S(1)}...) custom-call(s32[1]{0:T(128)} %bitcast.me, bf16[8,64,128]{2,1,0:T(8,128)(2,1)S(1)} %all-to-all-done.2.entry_ref, ...), custom_call_target="tpu_custom_call" | custom-call | flops 402653184 | bytes 2097152 | tf_op jit(solution)/shard_map/pallas_call | solution.py:254
  47.8 3.2 %collective-permute-start.3 = (bf16[272,512]{1,0:T(8,128)(2,1)S(1)}, bf16[272,512]{1,0:T(8,128)(2,1)S(1)}, u32[]{:S(2)}, u32[]{:S(2)}) collective-permute-start(bf16[272,512]{1,0:T(8,128)(2,1)S(1)} %get-tuple-element.40), channel_id=1, source_target_pairs={{0,1},{1,2},{2,3},{3,4},{4,5},{5,6},{6,7},{7,0},{8,9},{9,10},{10,1... | collective-permute-start | bytes 835592 | tf_op jit(solution)/shard_map/ppermute | solution.py:330
  51.0 3.8 %collective-permute-start.6 = (bf16[272,512]{1,0:T(8,128)(2,1)S(1)}, bf16[272,512]{1,0:T(8,128)(2,1)S(1)}, u32[]{:S(2)}, u32[]{:S(2)}) collective-permute-start(bf16[272,512]{1,0:T(8,128)(2,1)S(1)} %get-tuple-element.42), channel_id=1, source_target_pairs={{0,7},{1,0},{2,1},{3,2},{4,3},{5,4},{6,5},{7,6},{8,15},{9,8},{10,9... | collective-permute-start | bytes 835592 | tf_op jit(solution)/shard_map/ppermute | solution.py:330
  54.8 2.5 %collective-permute-start.2 = (bf16[144,512]{1,0:T(8,128)(2,1)S(1)}, bf16[144,512]{1,0:T(8,128)(2,1)S(1)}, u32[]{:S(2)}, u32[]{:S(2)}) collective-permute-start(bf16[144,512]{1,0:T(8,128)(2,1)S(1)} %get-tuple-element.39), channel_id=1, source_target_pairs={{0,2},{1,3},{2,4},{3,5},{4,6},{5,7},{6,0},{7,1},{8,10},{9,11},{10,... | collective-permute-start | bytes 442376 | tf_op jit(solution)/shard_map/ppermute | solution.py:330
  57.3 4.9 %collective-permute-start.5 = (bf16[144,512]{1,0:T(8,128)(2,1)S(1)}, bf16[144,512]{1,0:T(8,128)(2,1)S(1)}, u32[]{:S(2)}, u32[]{:S(2)}) collective-permute-start(bf16[144,512]{1,0:T(8,128)(2,1)S(1)} %get-tuple-element.41), channel_id=1, source_target_pairs={{0,6},{1,7},{2,0},{3,1},{4,2},{5,3},{6,4},{7,5},{8,14},{9,15},{10,... | collective-permute-start | bytes 442376 | tf_op jit(solution)/shard_map/ppermute | solution.py:330
  62.2 2.7 %shard_map.115 = (bf16[272,512]{1,0:T(8,128)(2,1)S(1)}, bf16[272,512]{1,0:T(8,128)(2,1)S(1)}, bf16[3,256,512]{2,1,0:T(8,128)(2,1)S(1)}) custom-call(s32[1]{0:T(128)} %bitcast.me, bf16[256,512]{1,0:T(8,128)(2,1)S(1)} %get-tuple-element.34.scaled_ref, f32[1,256]{1,0:T(1,128)S(1)} %get-tuple-element.35.square_ref, bf16[512,4096]{1,0:T(8,128)(2,1)} %w_hbm.3), custom_call_target="tpu_custom_call" | custom-call | flops 671088640 | bytes 4194304 | tf_op jit(solution)/shard_map/pallas_call | solution.py:254
  64.9 1.9 %collective-permute-start = (bf16[272,512]{1,0:T(8,128)(2,1)S(1)}, bf16[272,512]{1,0:T(8,128)(2,1)S(1)}, u32[]{:S(2)}, u32[]{:S(2)}) collective-permute-start(bf16[272,512]{1,0:T(8,128)(2,1)S(1)} %get-tuple-element.37), channel_id=1, source_target_pairs={{0,1},{1,2},{2,3},{3,4},{4,5},{5,6},{6,7},{7,0},{8,9},{9,10},{10,1... | collective-permute-start | bytes 835592 | tf_op jit(solution)/shard_map/ppermute | solution.py:330
  66.8 0.2 collective-permute-done.2.far_ref
  67.0 4.4 %collective-permute-start.1 = (bf16[272,512]{1,0:T(8,128)(2,1)S(1)}, bf16[272,512]{1,0:T(8,128)(2,1)S(1)}, u32[]{:S(2)}, u32[]{:S(2)}) collective-permute-start(bf16[272,512]{1,0:T(8,128)(2,1)S(1)} %get-tuple-element.38), channel_id=1, source_target_pairs={{0,7},{1,0},{2,1},{3,2},{4,3},{5,4},{6,5},{7,6},{8,15},{9,8},{10,9... | collective-permute-start | bytes 835592 | tf_op jit(solution)/shard_map/ppermute | solution.py:330
  71.4 0.0 collective-permute-done.3.got_ref
  71.4 0.1 shard_map.116
  71.5 2.4 %collective-permute-start.4 = (bf16[272,512]{1,0:T(8,128)(2,1)S(1)}, bf16[272,512]{1,0:T(8,128)(2,1)S(1)}, u32[]{:S(2)}, u32[]{:S(2)}) collective-permute-start(bf16[272,512]{1,0:T(8,128)(2,1)S(1)} %shard_map.116), channel_id=1, source_target_pairs={{0,2},{1,3},{2,4},{3,5},{4,6},{5,7},{6,0},{7,1},{8,10},{9,11},{10,... | collective-permute-start | bytes 835592 | tf_op jit(solution)/shard_map/ppermute | solution.py:330
  74.0 0.0 collective-permute-done.5.far_ref
  74.0 0.0 collective-permute-done.6.got_ref
  74.0 0.1 shard_map.117
  74.1 5.0 %collective-permute-start.7 = (bf16[272,512]{1,0:T(8,128)(2,1)S(1)}, bf16[272,512]{1,0:T(8,128)(2,1)S(1)}, u32[]{:S(2)}, u32[]{:S(2)}) collective-permute-start(bf16[272,512]{1,0:T(8,128)(2,1)S(1)} %shard_map.117), channel_id=1, source_target_pairs={{0,6},{1,7},{2,0},{3,1},{4,2},{5,3},{6,4},{7,5},{8,14},{9,15},{10,... | collective-permute-start | bytes 835592 | tf_op jit(solution)/shard_map/ppermute | solution.py:330
  79.1 0.0 collective-permute-done.refs_0_
  79.1 0.0 collective-permute-done.1.refs_1_
  79.1 9.0 %collective-permute-done.4.refs_2_ = bf16[272,512]{1,0:T(8,128)(2,1)S(1)} collective-permute-done((bf16[272,512]{1,0:T(8,128)(2,1)S(1)}, bf16[272,512]{1,0:T(8,128)(2,1)S(1)}, u32[]{:S(2)}, u32[]{:S(2)}) %collective-permute-start.4) | collective-permute-done | bytes 278560 | tf_op jit(solution)/shard_map/ppermute | solution.py:330
  88.1 5.5 %collective-permute-done.7.refs_3_ = bf16[272,512]{1,0:T(8,128)(2,1)S(1)} collective-permute-done((bf16[272,512]{1,0:T(8,128)(2,1)S(1)}, bf16[272,512]{1,0:T(8,128)(2,1)S(1)}, u32[]{:S(2)}, u32[]{:S(2)}) %collective-permute-start.7) | collective-permute-done | bytes 278560 | tf_op jit(solution)/shard_map/ppermute | solution.py:330
  93.6 0.9 shard_map.118
Async XLA Ops:
  2.9 15.8 %all-to-all-start = ((bf16[8,80,128]{2,1,0:T(8,128)(2,1)}), bf16[8,80,128]{2,1,0:T(8,128)(2,1)S(1)}, u32[]{:S(2)}, u32[]{:S(2)}) async-start(bf16[8,80,128]{2,1,0:T(8,128)(2,1)} %get-tuple-element.24), calls=%async_computation | async-start | bytes 327680 | tf_op jit(solution)/shard_map/all_to_all | solution.py:295
  18.7 0.7 copy-start.3
  20.1 13.7 %all-to-all-start.1 = ((bf16[8,80,128]{2,1,0:T(8,128)(2,1)}), bf16[8,80,128]{2,1,0:T(8,128)(2,1)S(1)}, u32[]{:S(2)}, u32[]{:S(2)}) async-start(bf16[8,80,128]{2,1,0:T(8,128)(2,1)} %shard_map.111), calls=%async_computation.1 | async-start | bytes 327680 | tf_op jit(solution)/shard_map/all_to_all | solution.py:310
  34.5 11.2 %all-to-all-start.2 = ((bf16[8,64,128]{2,1,0:T(8,128)(2,1)}), bf16[8,64,128]{2,1,0:T(8,128)(2,1)S(1)}, u32[]{:S(2)}, u32[]{:S(2)}) async-start(bf16[8,64,128]{2,1,0:T(8,128)(2,1)} %shard_map.112.refs_0_), calls=%async_computation.2 | async-start | bytes 262144 | tf_op jit(solution)/shard_map/all_to_all | solution.py:324
  40.4 1.0 %copy-start = (f32[256,512]{1,0:T(8,128)S(1)}, f32[256,512]{1,0:T(8,128)}, u32[]{:S(2)}) copy-start(f32[256,512]{1,0:T(8,128)} %get-tuple-element.28.refs_2_) | copy-start | bytes 1572868
  41.5 1.0 %copy-start.1 = (f32[256,512]{1,0:T(8,128)S(1)}, f32[256,512]{1,0:T(8,128)}, u32[]{:S(2)}) copy-start(f32[256,512]{1,0:T(8,128)} %get-tuple-element.29.refs_3_) | copy-start | bytes 1572868
  42.5 0.8 copy-start.2
  43.4 0.7 copy-start.4
  47.8 23.6 %collective-permute-start.3 = (bf16[272,512]{1,0:T(8,128)(2,1)S(1)}, bf16[272,512]{1,0:T(8,128)(2,1)S(1)}, u32[]{:S(2)}, u32[]{:S(2)}) collective-permute-start(bf16[272,512]{1,0:T(8,128)(2,1)S(1)} %get-tuple-element.40), channel_id=1, source_target_pairs={{0,1},{1,2},{2,3},{3,4},{4,5},{5,6},{6,7},{7,0},{8,9},{9,10},{10,1... | collective-permute-start | bytes 835592 | tf_op jit(solution)/shard_map/ppermute | solution.py:330
  51.0 23.0 %collective-permute-start.6 = (bf16[272,512]{1,0:T(8,128)(2,1)S(1)}, bf16[272,512]{1,0:T(8,128)(2,1)S(1)}, u32[]{:S(2)}, u32[]{:S(2)}) collective-permute-start(bf16[272,512]{1,0:T(8,128)(2,1)S(1)} %get-tuple-element.42), channel_id=1, source_target_pairs={{0,7},{1,0},{2,1},{3,2},{4,3},{5,4},{6,5},{7,6},{8,15},{9,8},{10,9... | collective-permute-start | bytes 835592 | tf_op jit(solution)/shard_map/ppermute | solution.py:330
  54.8 12.2 %collective-permute-start.2 = (bf16[144,512]{1,0:T(8,128)(2,1)S(1)}, bf16[144,512]{1,0:T(8,128)(2,1)S(1)}, u32[]{:S(2)}, u32[]{:S(2)}) collective-permute-start(bf16[144,512]{1,0:T(8,128)(2,1)S(1)} %get-tuple-element.39), channel_id=1, source_target_pairs={{0,2},{1,3},{2,4},{3,5},{4,6},{5,7},{6,0},{7,1},{8,10},{9,11},{10,... | collective-permute-start | bytes 442376 | tf_op jit(solution)/shard_map/ppermute | solution.py:330
  57.3 16.7 %collective-permute-start.5 = (bf16[144,512]{1,0:T(8,128)(2,1)S(1)}, bf16[144,512]{1,0:T(8,128)(2,1)S(1)}, u32[]{:S(2)}, u32[]{:S(2)}) collective-permute-start(bf16[144,512]{1,0:T(8,128)(2,1)S(1)} %get-tuple-element.41), channel_id=1, source_target_pairs={{0,6},{1,7},{2,0},{3,1},{4,2},{5,3},{6,4},{7,5},{8,14},{9,15},{10,... | collective-permute-start | bytes 442376 | tf_op jit(solution)/shard_map/ppermute | solution.py:330
  64.9 14.2 %collective-permute-start = (bf16[272,512]{1,0:T(8,128)(2,1)S(1)}, bf16[272,512]{1,0:T(8,128)(2,1)S(1)}, u32[]{:S(2)}, u32[]{:S(2)}) collective-permute-start(bf16[272,512]{1,0:T(8,128)(2,1)S(1)} %get-tuple-element.37), channel_id=1, source_target_pairs={{0,1},{1,2},{2,3},{3,4},{4,5},{5,6},{6,7},{7,0},{8,9},{9,10},{10,1... | collective-permute-start | bytes 835592 | tf_op jit(solution)/shard_map/ppermute | solution.py:330
  67.0 12.1 %collective-permute-start.1 = (bf16[272,512]{1,0:T(8,128)(2,1)S(1)}, bf16[272,512]{1,0:T(8,128)(2,1)S(1)}, u32[]{:S(2)}, u32[]{:S(2)}) collective-permute-start(bf16[272,512]{1,0:T(8,128)(2,1)S(1)} %get-tuple-element.38), channel_id=1, source_target_pairs={{0,7},{1,0},{2,1},{3,2},{4,3},{5,4},{6,5},{7,6},{8,15},{9,8},{10,9... | collective-permute-start | bytes 835592 | tf_op jit(solution)/shard_map/ppermute | solution.py:330
  71.5 16.5 %collective-permute-start.4 = (bf16[272,512]{1,0:T(8,128)(2,1)S(1)}, bf16[272,512]{1,0:T(8,128)(2,1)S(1)}, u32[]{:S(2)}, u32[]{:S(2)}) collective-permute-start(bf16[272,512]{1,0:T(8,128)(2,1)S(1)} %shard_map.116), channel_id=1, source_target_pairs={{0,2},{1,3},{2,4},{3,5},{4,6},{5,7},{6,0},{7,1},{8,10},{9,11},{10,... | collective-permute-start | bytes 835592 | tf_op jit(solution)/shard_map/ppermute | solution.py:330
  74.1 19.4 %collective-permute-start.7 = (bf16[272,512]{1,0:T(8,128)(2,1)S(1)}, bf16[272,512]{1,0:T(8,128)(2,1)S(1)}, u32[]{:S(2)}, u32[]{:S(2)}) collective-permute-start(bf16[272,512]{1,0:T(8,128)(2,1)S(1)} %shard_map.117), channel_id=1, source_target_pairs={{0,6},{1,7},{2,0},{3,1},{4,2},{5,3},{6,4},{7,5},{8,14},{9,15},{10,... | collective-permute-start | bytes 835592 | tf_op jit(solution)/shard_map/ppermute | solution.py:330

commit v6 on v4

--- a/solution.py
+++ b/solution.py
@@ -10,7 +10,6 @@
 SPAN = 256
 N_ROW = 8
 N_PART = 8
-NEAR = (3, -3, 2, -2, 1, -1, 0)
 PAD = 16
 F32, BF16 = (jnp.float32, jnp.bfloat16)
 VMEM = pl.BlockSpec(memory_space=pltpu.VMEM)
@@ -97,11 +96,10 @@
 
 
 def intra_kernel(*refs):
-    own_ref, open_ref, done_ref = refs[7:10]
+    own_ref, open_ref = refs[8:10]
     c_ref, b_ref, rows_ref, cols_ref, skip_ref, x_ref, z_ref = refs[10:17]
-    for copy in fetch(refs[:7], refs[10:17], refs[17]):
+    for copy in fetch(refs[1:8], refs[10:17], refs[17]):
         copy.wait()
-    done_ref[...] = jnp.zeros_like(done_ref)
     tokens = x_ref.shape[0]
     heads = skip_ref.shape[1]
     width = x_ref.shape[1] // heads
@@ -126,7 +124,7 @@
         open_ref[:, span] = gate * cols_ref[:, 3 * heads + h : 3 * heads + h + 1]
 
 
-def plane_kernel(after_ref, got_ref, out_ref):
+def plane_kernel(got_ref, out_ref):
     count, rows, lanes = got_ref.shape
     state_rows = rows - PAD
     total, keep = piece(got_ref, 0, state_rows)
@@ -179,59 +177,62 @@
 
 
 def columns(w_hbm, me, away, features):
-    place = (me[0] + away + N_PART) % N_PART
+    place = (me + away + N_PART) % N_PART
     return w_hbm.at[:, pl.ds(pl.multiple_of(place * features, features), features)]
 
 
-def gate_kernel(me, entry_ref, c_ref, own_ref, open_ref, gain_ref, w_hbm, *refs):
-    scaled_ref, square_ref, right_ref, left_ref, w_ref, sems = refs
+def gate_kernel(me, entry_ref, c_ref, own_ref, open_ref, gain_ref, w_hbm, gated_ref, far_ref, w_ref, sems):
     heads, width, lanes = entry_ref.shape
     tokens = own_ref.shape[0]
-    half = tokens // 2
-    (copy,) = fetch([columns(w_hbm, me, N_PART // 2, w_ref.shape[1])], [w_ref], sems)
+    (copy,) = fetch([columns(w_hbm, me[0], N_PART // 2, w_ref.shape[1])], [w_ref], sems)
     entries = entry_ref[...].reshape(heads * width, lanes)
     carried = lax.dot_general(c_ref[...], entries, (((1,), (1,)), ((), ())), preferred_element_type=F32)
     gated = own_ref[...] + open_ref[...] * carried
     scaled = (gated * gain_ref[...]).astype(BF16)
-    scaled_ref[...] = scaled
+    gated_ref[:tokens] = scaled
     squares = jnp.sum(gated * gated, axis=1, keepdims=True)
     squares = jnp.broadcast_to(squares, (tokens, 128)).T[:1]
-    square_ref[...] = squares
-    first = lax.broadcasted_iota(jnp.int32, squares.shape, 1) < half
-    put_squares(right_ref, jnp.where(first, squares, 0.0))
-    put_squares(left_ref, jnp.where(first, 0.0, squares))
+    put_squares(gated_ref, squares)
+    put_squares(far_ref, squares)
     copy.wait()
-    far = jnp.dot(scaled, w_ref[...], preferred_element_type=F32).astype(BF16)
-    right_ref[:half] = far[:half]
-    left_ref[:half] = far[half:]
-
-
-def chunks_kernel(me, scaled_ref, w_hbm, out_ref, w_ref, sems):
-    features = out_ref.shape[2]
-    copies = fetch([columns(w_hbm, me, away, features) for away in NEAR], [w_ref.at[i] for i in range(len(NEAR))], sems)
-    for i, copy in enumerate(copies):
-        copy.wait()
-        out_ref[i] = jnp.dot(scaled_ref[...], w_ref[i], preferred_element_type=F32).astype(BF16)
-
-
-def join_kernel(index, from_row, got_ref, chunks_ref, square_ref, out_ref):
-    tokens = chunks_ref.shape[1]
-    count = got_ref.shape[0] - PAD
-    if count < tokens:
-        out_ref[:tokens] = chunks_ref[index]
-    rows = slice(from_row, from_row + count)
-    out_ref[rows] = (chunks_ref[index, rows].astype(F32) + got_ref[:count].astype(F32)).astype(BF16)
-    put_squares(out_ref, square_ref[...] + get_squares(got_ref))
-
-
-def end_kernel(inner, right_ref, left_ref, chunks_ref, square_ref, out_ref):
+    far_ref[:tokens] = jnp.dot(scaled, w_ref[...], preferred_element_type=F32).astype(BF16)
+
+
+def chunks_kernel(me, way, own_ref, other_ref, w_hbm, out_ref, base_ref, w_ref, sems):
+    steps, _, tokens, features = out_ref.shape
+    away = [(steps - i) * way[0] for i in range(steps + 1)]
+    copies = fetch([columns(w_hbm, me[0], a, features) for a in away], [w_ref.at[i] for i in range(steps + 1)], sems)
+    for i in range(steps + 1):
+        copies[i].wait()
+        for j, ref in enumerate((own_ref, other_ref)):
+            if i < steps:
+                out_ref[i, j] = jnp.dot(ref[:tokens], w_ref[i], preferred_element_type=F32).astype(BF16)
+            elif j == 0:
+                base_ref[...] = jnp.dot(ref[:tokens], w_ref[i], preferred_element_type=F32).astype(BF16)
+
+
+def join_kernel(index, chunks_ref, own_ref, other_ref, got_ref, *out_refs):
+    tokens = chunks_ref.shape[2]
+    for j, ref in enumerate((own_ref, other_ref)):
+        out = out_refs[0].at[j] if len(out_refs) == 1 else out_refs[j]
+        squares = get_squares(ref)
+        total = chunks_ref[index, j]
+        if len(got_ref.shape) == 3 or j == 0:
+            got = got_ref.at[j] if len(got_ref.shape) == 3 else got_ref
+            squares = squares + get_squares(got)
+            total = (total.astype(F32) + got[:tokens].astype(F32)).astype(BF16)
+        out[:tokens] = total
+        put_squares(out, squares)
+
+
+def end_kernel(inner, base_ref, own_ref, right_ref, left_ref, out_ref):
     tokens, features = out_ref.shape
-    squares = square_ref[...] + get_squares(right_ref) + get_squares(left_ref)
+    squares = get_squares(own_ref) + get_squares(right_ref) + get_squares(left_ref)
     factor = lax.rsqrt(squares * (1.0 / inner) + 1e-05)
     factor = jnp.broadcast_to(factor, (128, tokens)).T
     for i in range(features // 128):
         span = slice(i * 128, (i + 1) * 128)
-        total = chunks_ref[len(NEAR) - 1, :, span].astype(F32)
+        total = base_ref[:, span].astype(F32)
         total = total + right_ref[:tokens, span].astype(F32) + left_ref[:tokens, span].astype(F32)
         out_ref[:, span] = (total * factor).astype(BF16)
 
@@ -255,7 +256,8 @@
     heads = log_rate.shape[0]
     width = channels // heads
     state_width = input_b.shape[1]
-    planes = lax.axis_size("seq") // N_ROW
+    devices = lax.axis_size("seq")
+    planes = devices // N_ROW
     in_plane = [[p * N_ROW + i for i in range(N_ROW)] for p in range(planes)]
     across = [[p * N_ROW + i for p in range(planes)] for i in range(N_ROW)]
     sent = (width + PAD, state_width)
@@ -281,19 +283,20 @@
     got = lax.all_to_all(pieces, "seq", 0, 0, axis_index_groups=in_plane)
     skip = skip_gain.reshape(1, heads)
     gain = norm_gain.reshape(1, channels)
+    (totals,) = call(plane_kernel, [VMEM], [((planes, *sent), BF16)], (got,), moved=2**19)
     near = (input_c, input_b, rows, cols, skip, input_x, input_z)
-    own, opened, done = call(
+    own, opened = call(
         intra_kernel,
-        [HBM] * 7,
-        [((tokens, channels), F32)] * 2 + [((8, 128), F32)],
-        near,
+        [ANY] + [HBM] * 7,
+        [((tokens, channels), F32)] * 2,
+        (totals, *near),
         scratch=near,
         limit=60,
         flops=2 * tokens * tokens * channels,
         moved=8 * 2**20,
     )
-    (totals,) = call(plane_kernel, [ANY, VMEM], [((planes, *sent), BF16)], (done, got), moved=2**19)
     got_planes = lax.all_to_all(totals, "seq", 0, 0, axis_index_groups=across)
+    got_planes, own = lax.optimization_barrier((got_planes, own))
     plane = lax.div(lax.axis_index("seq"), N_ROW).reshape(1)
     (entries,) = call(
         entry_kernel, [SMEM, VMEM, VMEM], [((N_ROW, width, state_width), BF16)], (plane, got, got_planes), moved=2**19
@@ -310,47 +313,57 @@
     entries = lax.all_to_all(entries, "seq", 0, 0, axis_index_groups=in_plane)
     me = lax.axis_index("head").reshape(1)
     features = out_weight.shape[1] // N_PART
-    half_sent = ((tokens // 2 + PAD, features), BF16)
-    full_sent = ((tokens + PAD, features), BF16)
-    scaled, squares, right, left = call(
+    slab = ((tokens + PAD, features), BF16)
+    slabs = ((2, tokens + PAD, features), BF16)
+    way = (1 - 2 * lax.rem(lax.axis_index("seq"), 2)).reshape(1)
+
+    def send(array, steps, swap):
+        pairs = []
+        for seq in range(devices):
+            for head in range(N_PART):
+                there = (head + steps * (1 - 2 * (seq % 2))) % N_PART
+                pairs.append((seq * N_PART + head, (seq ^ swap) * N_PART + there))
+        return lax.ppermute(array, ("seq", "head"), pairs)
+
+    gated, far = call(
         gate_kernel,
         [SMEM] + [VMEM] * 5 + [HBM],
-        [((tokens, channels), BF16), ((1, tokens), F32), half_sent, half_sent],
+        [slab, slab],
         (me, entries, *needed, out_weight),
         scratch=[jax.ShapeDtypeStruct((channels, features), BF16)],
-        limit=50,
         flops=2 * tokens * channels * features,
         moved=2**21,
-    )
-    turn = [[(i, (i + step) % N_PART) for i in range(N_PART)] for step in (1, -1)]
-    right = lax.ppermute(right, "head", turn[0])
-    left = lax.ppermute(left, "head", turn[1])
-    (chunks,) = call(
+        limit=50,
+    )
+    other = send(gated, 0, 1)
+    flow = send(far, 1, 0)
+    steps = N_PART // 2 - 1
+    chunks, base = call(
         chunks_kernel,
-        [SMEM, VMEM, HBM],
-        [((len(NEAR), tokens, features), BF16)],
-        (me, scaled, out_weight),
-        scratch=[jax.ShapeDtypeStruct((len(NEAR), channels, features), BF16)],
+        [SMEM, SMEM, VMEM, VMEM, HBM],
+        [((steps, 2, tokens, features), BF16), ((tokens, features), BF16)],
+        (me, way, gated, other, out_weight),
+        scratch=[jax.ShapeDtypeStruct((steps + 1, channels, features), BF16)],
+        flops=14 * tokens * channels * features,
+        moved=2**22,
         limit=50,
-        flops=2 * tokens * channels * features * len(NEAR),
-        moved=2**22,
-    )
-    for step in range(N_PART // 2 - 1):
-        begin = tokens // 2 if step == 0 else 0
-        (right,) = call(
-            functools.partial(join_kernel, 2 * step, 0), [VMEM] * 3, [full_sent], (right, chunks, squares), moved=2**19
+    )
+    for step in range(steps):
+        flow = call(
+            functools.partial(join_kernel, step),
+            [VMEM] * 4,
+            [slabs] if step < steps - 1 else [slab, slab],
+            (chunks, gated, other, flow),
+            moved=2**20,
         )
-        right = lax.ppermute(right, "head", turn[0])
-        (left,) = call(
-            functools.partial(join_kernel, 2 * step + 1, begin), [VMEM] * 3, [full_sent], (left, chunks, squares), moved=2**19
-        )
-        left = lax.ppermute(left, "head", turn[1])
+        if step < steps - 1:
+            flow = send(flow[0], 1, 0)
     (out,) = call(
         functools.partial(end_kernel, channels * N_PART),
         [VMEM] * 4,
         [((tokens, features), BF16)],
-        (right, left, chunks, squares),
-        moved=2**19,
+        (base, gated, send(flow[0], 1, 0), send(flow[1], 1, 1)),
+        moved=2**20,
     )
     return out
 

time: 94.1 us -> 98.8 us (1.050)
  blocking collectives: 0 us -> 10.8 us
  starting transfers between devices: 46.7 us -> 39 us
  waiting for transfers between devices: 27.3 us -> 30.3 us
    all_to_all x0 -> x1, blocking collectives: none -> 10.8 us  [body(): got = lax.all_to_all(pieces, 'seq', 0, 0, axis_index_groups=in_plane)]
    ppermute x8 -> x6, waiting for transfers between devices: 13 us -> 22.5 us  [send(): return lax.ppermute(array, ('seq', 'head'), pairs)]
    all_to_all x1 -> x0, starting transfers between devices: 4.31 us -> none  [body(): got = lax.all_to_all(pieces, 'seq', 0, 0, axis_index_groups=in_plane)]
    all_to_all x1, waiting for transfers between devices: 9.54 us -> 5.58 us  [body(): got_planes = lax.all_to_all(totals, 'seq', 0, 0, axis_index_groups=across)]
    ppermute x8 -> x6, starting transfers between devices: 28.7 us -> 25.3 us  [send(): return lax.ppermute(array, ('seq', 'head'), pairs)]
    all_to_all x1 -> x0, waiting for transfers between devices: 2.49 us -> none  [body(): got = lax.all_to_all(pieces, 'seq', 0, 0, axis_index_groups=in_plane)]
    unnamed x10 -> x8, local copies, waits for them, and re-layouts: 4.27 us -> 3.6 us
    pallas_call x14 -> x11, Pallas kernels: 14.8 us -> 14.2 us  [call(): pl.pallas_call(kernel, in_specs=ins, out_specs=[VMEM] * len(outs), out_sh...]
  transfers between devices with their start and end apart: 11 -> 8, of which waited for: 7 -> 7; matrix products, arithmetic and copies ran while one was open for 0% -> 0% of each run, Pallas kernels for 9% -> 7%
where the time goes in v6:
time: 98.8 us; the launch traced here: 98 us
  starting transfers between devices  39 us (39%)
  waiting for transfers between devices  30.3 us (31%)
  Pallas kernels  14.2 us (14%)
  blocking collectives  10.8 us (11%)
  local copies, waits for them, and re-layouts  3.6 us (4%)
    ppermute x6, starting transfers between devices, send(): return lax.ppermute(array, ('seq', 'head'), pairs)  25.3 us
    ppermute x6, waiting for transfers between devices, send(): return lax.ppermute(array, ('seq', 'head'), pairs)  22.5 us
    pallas_call x11, Pallas kernels, call(): pl.pallas_call(kernel, in_specs=ins, out_specs=[VMEM] * len(outs), out_sh...  14.2 us
    all_to_all x1, blocking collectives, body(): got = lax.all_to_all(pieces, 'seq', 0, 0, axis_index_groups=in_plane)  10.8 us
    all_to_all x1, starting transfers between devices, body(): got_planes = lax.all_to_all(totals, 'seq', 0, 0, axis_index_groups=across)  10.3 us
    all_to_all x1, waiting for transfers between devices, body(): got_planes = lax.all_to_all(totals, 'seq', 0, 0, axis_index_groups=across)  5.58 us
    unnamed x8, local copies, waits for them, and re-layouts  3.6 us
    all_to_all x1, starting transfers between devices, body(): entries = lax.all_to_all(entries, 'seq', 0, 0, axis_index_groups=in_plane)  3.37 us
  transfers between devices with their start and end apart: 8, of which 7 were waited for; matrix products, arithmetic and copies ran while one was open for 0% of the time, Pallas kernels for 7%

profile of v6, /device:TPU:24, one launch (start us, length us, event | category | flops | bytes accessed | tf_op | source)
XLA Modules:
  0.0 98.0 jit_solution(12769505937090072069)
XLA Ops:
  0.0 2.9 %shard_map.109 = (bf16[8,80,128]{2,1,0:T(8,128)(2,1)}, f32[40,256]{1,0:T(8,128)}, f32[256,128]{1,0:T(8,128)}) custom-call(f32[1,8]{1,0:T(1,128)} %bitcast.13, f32[1,8]{1,0:T(1,128)} %bitcast.14, f32[8,256]{1,0:T(8,128)} %bitcast.10, s32[1,256]{1,0:T(1,128)} %bitcast.11, bf16[256,128]{1,0:T(8,128)(2,1)} %refs_2_.1, bf16[256,512]{1,0:T(8,128)(2,1)} %refs_6_.1), custom_call_target="tpu_custom_call" | custom-call | flops 33554432 | bytes 262144 | tf_op jit(solution)/shard_map/pallas_call | solution.py:241
  2.9 10.8 %all_to_all.15.got_ref = bf16[8,80,128]{2,1,0:T(8,128)(2,1)S(1)} all-to-all(bf16[8,80,128]{2,1,0:T(8,128)(2,1)} %get-tuple-element.22), channel_id=1, replica_groups={{0,8,16,24,32,40,48,56},{64,72,80,88,96,104,112,120},{128,136,144,152,1..., dimensions={0} | all-to-all | bytes 327680 | tf_op jit(solution)/shard_map/all_to_all | solution.py:283
  13.7 0.7 shard_map.110.refs_0_
  14.4 10.3 %all-to-all-start.1 = ((bf16[8,80,128]{2,1,0:T(8,128)(2,1)}), bf16[8,80,128]{2,1,0:T(8,128)(2,1)S(1)}, u32[]{:S(2)}, u32[]{:S(2)}) async-start(bf16[8,80,128]{2,1,0:T(8,128)(2,1)} %shard_map.110.refs_0_), calls=%async_computation.1 | async-start | bytes 327680 | tf_op jit(solution)/shard_map/all_to_all | solution.py:298
  24.7 3.9 %shard_map.111 = (f32[256,512]{1,0:T(8,128)}, f32[256,512]{1,0:T(8,128)}) custom-call(bf16[8,80,128]{2,1,0:T(8,128)(2,1)} %shard_map.110.refs_0_, bf16[256,128]{1,0:T(8,128)(2,1)} %refs_1_.3, bf16[256,128]{1,0:T(8,128)(2,1)} %refs_2_.1, f32[40,256]{1,0:T(8,128)} %get-tuple-element.23.refs_3_, f32[256,128]{1,0:T(8,128)} %get-tuple-element.24.refs_4_, ...), custom_call_target="tpu_custom_call" | custom-call | flops 67108864 | bytes 8388608 | tf_op jit(solution)/shard_map/pallas_call | solution.py:241
  28.7 5.6 %all-to-all-done.1.planes_ref = bf16[8,80,128]{2,1,0:T(8,128)(2,1)S(1)} async-done(((bf16[8,80,128]{2,1,0:T(8,128)(2,1)}), bf16[8,80,128]{2,1,0:T(8,128)(2,1)S(1)}, u32[]{:S(2)}, u32[]{:S(2)}) %all-to-all-start.1) | async-done | bytes 163872 | tf_op jit(solution)/shard_map/all_to_all | solution.py:298
  34.2 0.7 shard_map.112.refs_0_
  35.0 3.4 %all-to-all-start.2 = ((bf16[8,64,128]{2,1,0:T(8,128)(2,1)}), bf16[8,64,128]{2,1,0:T(8,128)(2,1)S(1)}, u32[]{:S(2)}, u32[]{:S(2)}) async-start(bf16[8,64,128]{2,1,0:T(8,128)(2,1)} %shard_map.112.refs_0_), calls=%async_computation.2 | async-start | bytes 262144 | tf_op jit(solution)/shard_map/all_to_all | solution.py:313
  38.4 0.0 copy-start
  38.4 1.0 %copy-done = f32[256,512]{1,0:T(8,128)S(1)} copy-done((f32[256,512]{1,0:T(8,128)S(1)}, f32[256,512]{1,0:T(8,128)}, u32[]{:S(2)}) %copy-start) | copy-done | bytes 524312
  39.4 0.0 copy-start.1
  39.4 1.0 %copy-done.1 = f32[256,512]{1,0:T(8,128)S(1)} copy-done((f32[256,512]{1,0:T(8,128)S(1)}, f32[256,512]{1,0:T(8,128)}, u32[]{:S(2)}) %copy-start.1) | copy-done | bytes 524312
  40.4 0.0 copy-start.2
  40.5 0.8 copy-done.2
  41.3 0.0 copy-start.3
  41.3 0.7 copy-done.3
  42.0 0.2 shard_map.113
  42.2 2.2 %all-to-all-done.2.entry_ref = bf16[8,64,128]{2,1,0:T(8,128)(2,1)S(1)} async-done(((bf16[8,64,128]{2,1,0:T(8,128)(2,1)}), bf16[8,64,128]{2,1,0:T(8,128)(2,1)S(1)}, u32[]{:S(2)}, u32[]{:S(2)}) %all-to-all-start.2) | async-done | bytes 131104 | tf_op jit(solution)/shard_map/all_to_all | solution.py:313
  44.4 1.7 %shard_map.114 = (bf16[272,512]{1,0:T(8,128)(2,1)S(1)}, bf16[272,512]{1,0:T(8,128)(2,1)S(1)}) custom-call(s32[1]{0:T(128)} %bitcast.me, bf16[8,64,128]{2,1,0:T(8,128)(2,1)S(1)} %all-to-all-done.2.entry_ref, bf16[256,128]{1,0:T(8,128)(2,1)S(1)} %get-tuple-element.29.c_ref, f32[256,512]{1,0:T(8,128)S(1)} %get-tuple-element.30.own_ref, ...), custom_call_target="tpu_custom_call" | custom-call | flops 134217728 | bytes 2097152 | tf_op jit(solution)/shard_map/pallas_call | solution.py:241
  46.1 1.9 %collective-permute-start = (bf16[272,512]{1,0:T(8,128)(2,1)S(1)}, bf16[272,512]{1,0:T(8,128)(2,1)S(1)}, u32[]{:S(2)}, u32[]{:S(2)}) collective-permute-start(bf16[272,512]{1,0:T(8,128)(2,1)S(1)} %get-tuple-element.33.own_ref), channel_id=1, source_target_pairs={{0,8},{1,9},{2,10},{3,11},{4,12},{5,13},{6,14},{7,15},{8,0},{9,1},... | collective-permute-start | bytes 835592 | tf_op jit(solution)/shard_map/ppermute | solution.py:326
  48.0 4.7 %collective-permute-start.1 = (bf16[272,512]{1,0:T(8,128)(2,1)S(1)}, bf16[272,512]{1,0:T(8,128)(2,1)S(1)}, u32[]{:S(2)}, u32[]{:S(2)}) collective-permute-start(bf16[272,512]{1,0:T(8,128)(2,1)S(1)} %get-tuple-element.36), channel_id=1, source_target_pairs={{0,1},{1,2},{2,3},{3,4},{4,5},{5,6},{6,7},{7,0},{8,15},{9,8},{10,9... | collective-permute-start | bytes 835592 | tf_op jit(solution)/shard_map/ppermute | solution.py:326
  52.7 0.0 collective-permute-done.other_ref
  52.7 2.7 %shard_map.115 = (bf16[3,2,256,512]{3,2,1,0:T(8,128)(2,1)S(1)}, bf16[256,512]{1,0:T(8,128)(2,1)S(1)}) custom-call(s32[1]{0:T(128)} %bitcast.me, s32[1]{0:T(128)} %bitcast.1.way, bf16[272,512]{1,0:T(8,128)(2,1)S(1)} %get-tuple-element.33.own_ref, bf16[272,512]{1,0:T(8,128)(2,1)S(1)} %collective-permute-done.other_ref, bf16[512,4096]{1,0:T(8,128)(2,1)} %w_hbm.3), custom_call_target="tpu_custom_call" | custom-call | flops 939524096 | bytes 4194304 | tf_op jit(solution)/shard_map/pallas_call | solution.py:241
  55.5 1.3 %collective-permute-done.1.got_ref = bf16[272,512]{1,0:T(8,128)(2,1)S(1)} collective-permute-done((bf16[272,512]{1,0:T(8,128)(2,1)S(1)}, bf16[272,512]{1,0:T(8,128)(2,1)S(1)}, u32[]{:S(2)}, u32[]{:S(2)}) %collective-permute-start.1) | collective-permute-done | bytes 278560 | tf_op jit(solution)/shard_map/ppermute | solution.py:326
  56.8 0.1 shard_map.116
  56.9 5.6 %collective-permute-start.2 = (bf16[2,272,512]{2,1,0:T(8,128)(2,1)S(1)}, bf16[2,272,512]{2,1,0:T(8,128)(2,1)S(1)}, u32[]{:S(2)}, u32[]{:S(2)}) collective-permute-start(bf16[2,272,512]{2,1,0:T(8,128)(2,1)S(1)} %shard_map.116), channel_id=1, source_target_pairs={{0,1},{1,2},{2,3},{3,4},{4,5},{5,6},{6,7},{7,0},{8,15},{9,8},{10,9... | collective-permute-start | bytes 1671176 | tf_op jit(solution)/shard_map/ppermute | solution.py:326
  62.5 7.0 %collective-permute-done.2.got_ref = bf16[2,272,512]{2,1,0:T(8,128)(2,1)S(1)} collective-permute-done((bf16[2,272,512]{2,1,0:T(8,128)(2,1)S(1)}, bf16[2,272,512]{2,1,0:T(8,128)(2,1)S(1)}, u32[]{:S(2)}, u32[]{:S(2)}) %collective-permute-start.2) | collective-permute-done | bytes 557088 | tf_op jit(solution)/shard_map/ppermute | solution.py:326
  69.5 0.2 shard_map.117
  69.7 5.6 %collective-permute-start.3 = (bf16[2,272,512]{2,1,0:T(8,128)(2,1)S(1)}, bf16[2,272,512]{2,1,0:T(8,128)(2,1)S(1)}, u32[]{:S(2)}, u32[]{:S(2)}) collective-permute-start(bf16[2,272,512]{2,1,0:T(8,128)(2,1)S(1)} %shard_map.117), channel_id=1, source_target_pairs={{0,1},{1,2},{2,3},{3,4},{4,5},{5,6},{6,7},{7,0},{8,15},{9,8},{10,9... | collective-permute-start | bytes 1671176 | tf_op jit(solution)/shard_map/ppermute | solution.py:326
  75.3 7.0 %collective-permute-done.3.got_ref = bf16[2,272,512]{2,1,0:T(8,128)(2,1)S(1)} collective-permute-done((bf16[2,272,512]{2,1,0:T(8,128)(2,1)S(1)}, bf16[2,272,512]{2,1,0:T(8,128)(2,1)S(1)}, u32[]{:S(2)}, u32[]{:S(2)}) %collective-permute-start.3) | collective-permute-done | bytes 557088 | tf_op jit(solution)/shard_map/ppermute | solution.py:326
  82.3 0.2 shard_map.118
  82.5 5.6 %collective-permute-start.4 = (bf16[272,512]{1,0:T(8,128)(2,1)S(1)}, bf16[272,512]{1,0:T(8,128)(2,1)S(1)}, u32[]{:S(2)}, u32[]{:S(2)}) collective-permute-start(bf16[272,512]{1,0:T(8,128)(2,1)S(1)} %get-tuple-element.37), channel_id=1, source_target_pairs={{0,1},{1,2},{2,3},{3,4},{4,5},{5,6},{6,7},{7,0},{8,15},{9,8},{10,9... | collective-permute-start | bytes 835592 | tf_op jit(solution)/shard_map/ppermute | solution.py:326
  88.1 1.9 %collective-permute-start.5 = (bf16[272,512]{1,0:T(8,128)(2,1)S(1)}, bf16[272,512]{1,0:T(8,128)(2,1)S(1)}, u32[]{:S(2)}, u32[]{:S(2)}) collective-permute-start(bf16[272,512]{1,0:T(8,128)(2,1)S(1)} %get-tuple-element.38), channel_id=1, source_target_pairs={{0,9},{1,10},{2,11},{3,12},{4,13},{5,14},{6,15},{7,8},{8,7},{9,0},... | collective-permute-start | bytes 835592 | tf_op jit(solution)/shard_map/ppermute | solution.py:326
  90.0 2.1 %collective-permute-done.4.right_ref = bf16[272,512]{1,0:T(8,128)(2,1)S(1)} collective-permute-done((bf16[272,512]{1,0:T(8,128)(2,1)S(1)}, bf16[272,512]{1,0:T(8,128)(2,1)S(1)}, u32[]{:S(2)}, u32[]{:S(2)}) %collective-permute-start.4) | collective-permute-done | bytes 278560 | tf_op jit(solution)/shard_map/ppermute | solution.py:326
  92.1 5.0 %collective-permute-done.5.left_ref = bf16[272,512]{1,0:T(8,128)(2,1)S(1)} collective-permute-done((bf16[272,512]{1,0:T(8,128)(2,1)S(1)}, bf16[272,512]{1,0:T(8,128)(2,1)S(1)}, u32[]{:S(2)}, u32[]{:S(2)}) %collective-permute-start.5) | collective-permute-done | bytes 278560 | tf_op jit(solution)/shard_map/ppermute | solution.py:326
  97.2 0.9 shard_map.119
Async XLA Ops:
  14.4 19.9 %all-to-all-start.1 = ((bf16[8,80,128]{2,1,0:T(8,128)(2,1)}), bf16[8,80,128]{2,1,0:T(8,128)(2,1)S(1)}, u32[]{:S(2)}, u32[]{:S(2)}) async-start(bf16[8,80,128]{2,1,0:T(8,128)(2,1)} %shard_map.110.refs_0_), calls=%async_computation.1 | async-start | bytes 327680 | tf_op jit(solution)/shard_map/all_to_all | solution.py:298
  35.0 9.4 %all-to-all-start.2 = ((bf16[8,64,128]{2,1,0:T(8,128)(2,1)}), bf16[8,64,128]{2,1,0:T(8,128)(2,1)S(1)}, u32[]{:S(2)}, u32[]{:S(2)}) async-start(bf16[8,64,128]{2,1,0:T(8,128)(2,1)} %shard_map.112.refs_0_), calls=%async_computation.2 | async-start | bytes 262144 | tf_op jit(solution)/shard_map/all_to_all | solution.py:313
  38.4 1.0 %copy-start = (f32[256,512]{1,0:T(8,128)S(1)}, f32[256,512]{1,0:T(8,128)}, u32[]{:S(2)}) copy-start(f32[256,512]{1,0:T(8,128)} %get-tuple-element.27.refs_2_) | copy-start | bytes 1572868
  39.4 1.0 %copy-start.1 = (f32[256,512]{1,0:T(8,128)S(1)}, f32[256,512]{1,0:T(8,128)}, u32[]{:S(2)}) copy-start(f32[256,512]{1,0:T(8,128)} %get-tuple-element.28.refs_3_) | copy-start | bytes 1572868
  40.4 0.8 copy-start.2
  41.3 0.7 copy-start.3
  46.1 6.6 %collective-permute-start = (bf16[272,512]{1,0:T(8,128)(2,1)S(1)}, bf16[272,512]{1,0:T(8,128)(2,1)S(1)}, u32[]{:S(2)}, u32[]{:S(2)}) collective-permute-start(bf16[272,512]{1,0:T(8,128)(2,1)S(1)} %get-tuple-element.33.own_ref), channel_id=1, source_target_pairs={{0,8},{1,9},{2,10},{3,11},{4,12},{5,13},{6,14},{7,15},{8,0},{9,1},... | collective-permute-start | bytes 835592 | tf_op jit(solution)/shard_map/ppermute | solution.py:326
  48.0 8.7 %collective-permute-start.1 = (bf16[272,512]{1,0:T(8,128)(2,1)S(1)}, bf16[272,512]{1,0:T(8,128)(2,1)S(1)}, u32[]{:S(2)}, u32[]{:S(2)}) collective-permute-start(bf16[272,512]{1,0:T(8,128)(2,1)S(1)} %get-tuple-element.36), channel_id=1, source_target_pairs={{0,1},{1,2},{2,3},{3,4},{4,5},{5,6},{6,7},{7,0},{8,15},{9,8},{10,9... | collective-permute-start | bytes 835592 | tf_op jit(solution)/shard_map/ppermute | solution.py:326
  56.9 12.6 %collective-permute-start.2 = (bf16[2,272,512]{2,1,0:T(8,128)(2,1)S(1)}, bf16[2,272,512]{2,1,0:T(8,128)(2,1)S(1)}, u32[]{:S(2)}, u32[]{:S(2)}) collective-permute-start(bf16[2,272,512]{2,1,0:T(8,128)(2,1)S(1)} %shard_map.116), channel_id=1, source_target_pairs={{0,1},{1,2},{2,3},{3,4},{4,5},{5,6},{6,7},{7,0},{8,15},{9,8},{10,9... | collective-permute-start | bytes 1671176 | tf_op jit(solution)/shard_map/ppermute | solution.py:326
  69.7 12.6 %collective-permute-start.3 = (bf16[2,272,512]{2,1,0:T(8,128)(2,1)S(1)}, bf16[2,272,512]{2,1,0:T(8,128)(2,1)S(1)}, u32[]{:S(2)}, u32[]{:S(2)}) collective-permute-start(bf16[2,272,512]{2,1,0:T(8,128)(2,1)S(1)} %shard_map.117), channel_id=1, source_target_pairs={{0,1},{1,2},{2,3},{3,4},{4,5},{5,6},{6,7},{7,0},{8,15},{9,8},{10,9... | collective-permute-start | bytes 1671176 | tf_op jit(solution)/shard_map/ppermute | solution.py:326
  82.5 9.7 %collective-permute-start.4 = (bf16[272,512]{1,0:T(8,128)(2,1)S(1)}, bf16[272,512]{1,0:T(8,128)(2,1)S(1)}, u32[]{:S(2)}, u32[]{:S(2)}) collective-permute-start(bf16[272,512]{1,0:T(8,128)(2,1)S(1)} %get-tuple-element.37), channel_id=1, source_target_pairs={{0,1},{1,2},{2,3},{3,4},{4,5},{5,6},{6,7},{7,0},{8,15},{9,8},{10,9... | collective-permute-start | bytes 835592 | tf_op jit(solution)/shard_map/ppermute | solution.py:326
  88.1 9.1 %collective-permute-start.5 = (bf16[272,512]{1,0:T(8,128)(2,1)S(1)}, bf16[272,512]{1,0:T(8,128)(2,1)S(1)}, u32[]{:S(2)}, u32[]{:S(2)}) collective-permute-start(bf16[272,512]{1,0:T(8,128)(2,1)S(1)} %get-tuple-element.38), channel_id=1, source_target_pairs={{0,9},{1,10},{2,11},{3,12},{4,13},{5,14},{6,15},{7,8},{8,7},{9,0},... | collective-permute-start | bytes 835592 | tf_op jit(solution)/shard_map/ppermute | solution.py:326

commit v7 on v6

--- a/solution.py
+++ b/solution.py
@@ -211,18 +211,16 @@
                 base_ref[...] = jnp.dot(ref[:tokens], w_ref[i], preferred_element_type=F32).astype(BF16)
 
 
-def join_kernel(index, chunks_ref, own_ref, other_ref, got_ref, *out_refs):
+def join_kernel(index, slab, chunks_ref, gated_ref, *refs):
+    got_refs, out_ref = refs[:-1], refs[-1]
     tokens = chunks_ref.shape[2]
-    for j, ref in enumerate((own_ref, other_ref)):
-        out = out_refs[0].at[j] if len(out_refs) == 1 else out_refs[j]
-        squares = get_squares(ref)
-        total = chunks_ref[index, j]
-        if len(got_ref.shape) == 3 or j == 0:
-            got = got_ref.at[j] if len(got_ref.shape) == 3 else got_ref
-            squares = squares + get_squares(got)
-            total = (total.astype(F32) + got[:tokens].astype(F32)).astype(BF16)
-        out[:tokens] = total
-        put_squares(out, squares)
+    squares = get_squares(gated_ref)
+    total = chunks_ref[index, slab].astype(F32)
+    for ref in got_refs:
+        squares = squares + get_squares(ref)
+        total = total + ref[:tokens].astype(F32)
+    out_ref[:tokens] = total.astype(BF16)
+    put_squares(out_ref, squares)
 
 
 def end_kernel(inner, base_ref, own_ref, right_ref, left_ref, out_ref):
@@ -314,7 +312,6 @@
     me = lax.axis_index("head").reshape(1)
     features = out_weight.shape[1] // N_PART
     slab = ((tokens + PAD, features), BF16)
-    slabs = ((2, tokens + PAD, features), BF16)
     way = (1 - 2 * lax.rem(lax.axis_index("seq"), 2)).reshape(1)
 
     def send(array, steps, swap):
@@ -348,21 +345,23 @@
         moved=2**22,
         limit=50,
     )
+    flows = [[flow], []]
     for step in range(steps):
-        flow = call(
-            functools.partial(join_kernel, step),
-            [VMEM] * 4,
-            [slabs] if step < steps - 1 else [slab, slab],
-            (chunks, gated, other, flow),
-            moved=2**20,
-        )
-        if step < steps - 1:
-            flow = send(flow[0], 1, 0)
+        for slab_index in (1, 0):
+            got = flows[slab_index]
+            (joined,) = call(
+                functools.partial(join_kernel, step, slab_index),
+                [VMEM] * (2 + len(got)),
+                [slab],
+                (chunks, (gated, other)[slab_index], *got),
+                moved=2**19,
+            )
+            flows[slab_index] = [send(joined, 1, slab_index if step == steps - 1 else 0)]
     (out,) = call(
         functools.partial(end_kernel, channels * N_PART),
         [VMEM] * 4,
         [((tokens, features), BF16)],
-        (base, gated, send(flow[0], 1, 0), send(flow[1], 1, 1)),
+        (base, gated, *flows[0], *flows[1]),
         moved=2**20,
     )
     return out

time: 98.8 us -> 88.6 us (0.90)
  the two profiles are of different devices: /device:TPU:24 before, /device:TPU:32 now
where the time goes in v7:
time: 88.6 us; the launch traced here: 87.8 us
  starting transfers between devices  30.4 us (34%)
  waiting for transfers between devices  28.6 us (32%)
  Pallas kernels  14.2 us (16%)
  blocking collectives  10.8 us (12%)
  local copies, waits for them, and re-layouts  3.6 us (4%)
    ppermute x8, waiting for transfers between devices, send(): return lax.ppermute(array, ('seq', 'head'), pairs)  20.8 us
    ppermute x8, starting transfers between devices, send(): return lax.ppermute(array, ('seq', 'head'), pairs)  16.7 us
    pallas_call x14, Pallas kernels, call(): pl.pallas_call(kernel, in_specs=ins, out_specs=[VMEM] * len(outs), out_sh...  14.2 us
    all_to_all x1, blocking collectives, body(): got = lax.all_to_all(pieces, 'seq', 0, 0, axis_index_groups=in_plane)  10.8 us
    all_to_all x1, starting transfers between devices, body(): got_planes = lax.all_to_all(totals, 'seq', 0, 0, axis_index_groups=across)  10.3 us
    all_to_all x1, waiting for transfers between devices, body(): got_planes = lax.all_to_all(totals, 'seq', 0, 0, axis_index_groups=across)  5.57 us
    unnamed x8, local copies, waits for them, and re-layouts  3.6 us
    all_to_all x1, starting transfers between devices, body(): entries = lax.all_to_all(entries, 'seq', 0, 0, axis_index_groups=in_plane)  3.37 us
  transfers between devices with their start and end apart: 10, of which 9 were waited for; matrix products, arithmetic and copies ran while one was open for 0% of the time, Pallas kernels for 8%

profile of v7, /device:TPU:32, one launch (start us, length us, event | category | flops | bytes accessed | tf_op | source)
XLA Modules:
  0.0 87.8 jit_solution(7329911160180157814)
XLA Ops:
  0.0 2.9 %shard_map.109 = (bf16[8,80,128]{2,1,0:T(8,128)(2,1)}, f32[40,256]{1,0:T(8,128)}, f32[256,128]{1,0:T(8,128)}) custom-call(f32[1,8]{1,0:T(1,128)} %bitcast.13, f32[1,8]{1,0:T(1,128)} %bitcast.14, f32[8,256]{1,0:T(8,128)} %bitcast.10, s32[1,256]{1,0:T(1,128)} %bitcast.11, bf16[256,128]{1,0:T(8,128)(2,1)} %refs_2_.1, bf16[256,512]{1,0:T(8,128)(2,1)} %refs_6_.1), custom_call_target="tpu_custom_call" | custom-call | flops 33554432 | bytes 262144 | tf_op jit(solution)/shard_map/pallas_call | solution.py:239
  2.9 10.8 %all_to_all.15.got_ref = bf16[8,80,128]{2,1,0:T(8,128)(2,1)S(1)} all-to-all(bf16[8,80,128]{2,1,0:T(8,128)(2,1)} %get-tuple-element.20), channel_id=1, replica_groups={{0,8,16,24,32,40,48,56},{64,72,80,88,96,104,112,120},{128,136,144,152,1..., dimensions={0} | all-to-all | bytes 327680 | tf_op jit(solution)/shard_map/all_to_all | solution.py:281
  13.7 0.7 shard_map.110.refs_0_
  14.4 10.3 %all-to-all-start.1 = ((bf16[8,80,128]{2,1,0:T(8,128)(2,1)}), bf16[8,80,128]{2,1,0:T(8,128)(2,1)S(1)}, u32[]{:S(2)}, u32[]{:S(2)}) async-start(bf16[8,80,128]{2,1,0:T(8,128)(2,1)} %shard_map.110.refs_0_), calls=%async_computation.1 | async-start | bytes 327680 | tf_op jit(solution)/shard_map/all_to_all | solution.py:296
  24.7 4.0 %shard_map.111 = (f32[256,512]{1,0:T(8,128)}, f32[256,512]{1,0:T(8,128)}) custom-call(bf16[8,80,128]{2,1,0:T(8,128)(2,1)} %shard_map.110.refs_0_, bf16[256,128]{1,0:T(8,128)(2,1)} %refs_1_.3, bf16[256,128]{1,0:T(8,128)(2,1)} %refs_2_.1, f32[40,256]{1,0:T(8,128)} %get-tuple-element.21.refs_3_, f32[256,128]{1,0:T(8,128)} %get-tuple-element.22.refs_4_, ...), custom_call_target="tpu_custom_call" | custom-call | flops 67108864 | bytes 8388608 | tf_op jit(solution)/shard_map/pallas_call | solution.py:239
  28.7 5.6 %all-to-all-done.1.planes_ref = bf16[8,80,128]{2,1,0:T(8,128)(2,1)S(1)} async-done(((bf16[8,80,128]{2,1,0:T(8,128)(2,1)}), bf16[8,80,128]{2,1,0:T(8,128)(2,1)S(1)}, u32[]{:S(2)}, u32[]{:S(2)}) %all-to-all-start.1) | async-done | bytes 163872 | tf_op jit(solution)/shard_map/all_to_all | solution.py:296
  34.2 0.7 shard_map.112.refs_0_
  35.0 3.4 %all-to-all-start.2 = ((bf16[8,64,128]{2,1,0:T(8,128)(2,1)}), bf16[8,64,128]{2,1,0:T(8,128)(2,1)S(1)}, u32[]{:S(2)}, u32[]{:S(2)}) async-start(bf16[8,64,128]{2,1,0:T(8,128)(2,1)} %shard_map.112.refs_0_), calls=%async_computation.2 | async-start | bytes 262144 | tf_op jit(solution)/shard_map/all_to_all | solution.py:311
  38.4 0.0 copy-start
  38.4 1.0 %copy-done = f32[256,512]{1,0:T(8,128)S(1)} copy-done((f32[256,512]{1,0:T(8,128)S(1)}, f32[256,512]{1,0:T(8,128)}, u32[]{:S(2)}) %copy-start) | copy-done | bytes 524312
  39.4 0.0 copy-start.1
  39.4 1.0 %copy-done.1 = f32[256,512]{1,0:T(8,128)S(1)} copy-done((f32[256,512]{1,0:T(8,128)S(1)}, f32[256,512]{1,0:T(8,128)}, u32[]{:S(2)}) %copy-start.1) | copy-done | bytes 524312
  40.4 0.0 copy-start.2
  40.4 0.8 copy-done.2
  41.3 0.0 copy-start.3
  41.3 0.7 copy-done.3
  42.0 0.2 shard_map.113
  42.2 2.2 %all-to-all-done.2.entry_ref = bf16[8,64,128]{2,1,0:T(8,128)(2,1)S(1)} async-done(((bf16[8,64,128]{2,1,0:T(8,128)(2,1)}), bf16[8,64,128]{2,1,0:T(8,128)(2,1)S(1)}, u32[]{:S(2)}, u32[]{:S(2)}) %all-to-all-start.2) | async-done | bytes 131104 | tf_op jit(solution)/shard_map/all_to_all | solution.py:311
  44.4 1.7 %shard_map.114 = (bf16[272,512]{1,0:T(8,128)(2,1)S(1)}, bf16[272,512]{1,0:T(8,128)(2,1)S(1)}) custom-call(s32[1]{0:T(128)} %bitcast.me, bf16[8,64,128]{2,1,0:T(8,128)(2,1)S(1)} %all-to-all-done.2.entry_ref, bf16[256,128]{1,0:T(8,128)(2,1)S(1)} %get-tuple-element.27.c_ref, f32[256,512]{1,0:T(8,128)S(1)} %get-tuple-element.28.own_ref, ...), custom_call_target="tpu_custom_call" | custom-call | flops 134217728 | bytes 2097152 | tf_op jit(solution)/shard_map/pallas_call | solution.py:239
  46.1 1.9 %collective-permute-start = (bf16[272,512]{1,0:T(8,128)(2,1)S(1)}, bf16[272,512]{1,0:T(8,128)(2,1)S(1)}, u32[]{:S(2)}, u32[]{:S(2)}) collective-permute-start(bf16[272,512]{1,0:T(8,128)(2,1)S(1)} %get-tuple-element.31.own_ref.gated_ref), channel_id=1, source_target_pairs={{0,8},{1,9},{2,10},{3,11},{4,12},{5,13},{6,14},{7,15},{8,0},{9,1},... | collective-permute-start | bytes 835592 | tf_op jit(solution)/shard_map/ppermute | solution.py:323
  48.0 2.6 %collective-permute-start.1 = (bf16[272,512]{1,0:T(8,128)(2,1)S(1)}, bf16[272,512]{1,0:T(8,128)(2,1)S(1)}, u32[]{:S(2)}, u32[]{:S(2)}) collective-permute-start(bf16[272,512]{1,0:T(8,128)(2,1)S(1)} %get-tuple-element.34), channel_id=1, source_target_pairs={{0,1},{1,2},{2,3},{3,4},{4,5},{5,6},{6,7},{7,0},{8,15},{9,8},{10,9... | collective-permute-start | bytes 835592 | tf_op jit(solution)/shard_map/ppermute | solution.py:323
  50.6 0.0 collective-permute-done.other_ref.gated_ref
  50.6 2.7 %shard_map.115 = (bf16[3,2,256,512]{3,2,1,0:T(8,128)(2,1)S(1)}, bf16[256,512]{1,0:T(8,128)(2,1)S(1)}) custom-call(s32[1]{0:T(128)} %bitcast.me, s32[1]{0:T(128)} %bitcast.1.way, bf16[272,512]{1,0:T(8,128)(2,1)S(1)} %get-tuple-element.31.own_ref.gated_ref, bf16[272,512]{1,0:T(8,128)(2,1)S(1)} %collective-permute-done.other_ref.gated_ref, bf16[512,4096]{1,0:T(8,128)(2,1)} %w_hbm.3), custom_call_target="tpu_custom_call" | custom-call | flops 939524096 | bytes 4194304 | tf_op jit(solution)/shard_map/pallas_call | solution.py:239
  53.4 2.6 %collective-permute-start.5 = (bf16[272,512]{1,0:T(8,128)(2,1)S(1)}, bf16[272,512]{1,0:T(8,128)(2,1)S(1)}, u32[]{:S(2)}, u32[]{:S(2)}) collective-permute-start(bf16[272,512]{1,0:T(8,128)(2,1)S(1)} %shard_map.119), channel_id=1, source_target_pairs={{0,1},{1,2},{2,3},{3,4},{4,5},{5,6},{6,7},{7,0},{8,15},{9,8},{10,9... | collective-permute-start | bytes 835592 | tf_op jit(solution)/shard_map/ppermute | solution.py:323
  56.0 1.7 %collective-permute-done.1.refs_0_ = bf16[272,512]{1,0:T(8,128)(2,1)S(1)} collective-permute-done((bf16[272,512]{1,0:T(8,128)(2,1)S(1)}, bf16[272,512]{1,0:T(8,128)(2,1)S(1)}, u32[]{:S(2)}, u32[]{:S(2)}) %collective-permute-start.1) | collective-permute-done | bytes 278560 | tf_op jit(solution)/shard_map/ppermute | solution.py:323
  57.7 0.1 shard_map.116
  57.8 1.9 %collective-permute-start.2 = (bf16[272,512]{1,0:T(8,128)(2,1)S(1)}, bf16[272,512]{1,0:T(8,128)(2,1)S(1)}, u32[]{:S(2)}, u32[]{:S(2)}) collective-permute-start(bf16[272,512]{1,0:T(8,128)(2,1)S(1)} %shard_map.116), channel_id=1, source_target_pairs={{0,1},{1,2},{2,3},{3,4},{4,5},{5,6},{6,7},{7,0},{8,15},{9,8},{10,9... | collective-permute-start | bytes 835592 | tf_op jit(solution)/shard_map/ppermute | solution.py:323
  59.7 3.4 %collective-permute-done.5.refs_0_ = bf16[272,512]{1,0:T(8,128)(2,1)S(1)} collective-permute-done((bf16[272,512]{1,0:T(8,128)(2,1)S(1)}, bf16[272,512]{1,0:T(8,128)(2,1)S(1)}, u32[]{:S(2)}, u32[]{:S(2)}) %collective-permute-start.5) | collective-permute-done | bytes 278560 | tf_op jit(solution)/shard_map/ppermute | solution.py:323
  63.1 0.1 shard_map.120
  63.2 1.9 %collective-permute-start.6 = (bf16[272,512]{1,0:T(8,128)(2,1)S(1)}, bf16[272,512]{1,0:T(8,128)(2,1)S(1)}, u32[]{:S(2)}, u32[]{:S(2)}) collective-permute-start(bf16[272,512]{1,0:T(8,128)(2,1)S(1)} %shard_map.120), channel_id=1, source_target_pairs={{0,1},{1,2},{2,3},{3,4},{4,5},{5,6},{6,7},{7,0},{8,15},{9,8},{10,9... | collective-permute-start | bytes 835592 | tf_op jit(solution)/shard_map/ppermute | solution.py:323
  65.1 2.3 %collective-permute-done.2.refs_0_ = bf16[272,512]{1,0:T(8,128)(2,1)S(1)} collective-permute-done((bf16[272,512]{1,0:T(8,128)(2,1)S(1)}, bf16[272,512]{1,0:T(8,128)(2,1)S(1)}, u32[]{:S(2)}, u32[]{:S(2)}) %collective-permute-start.2) | collective-permute-done | bytes 278560 | tf_op jit(solution)/shard_map/ppermute | solution.py:323
  67.4 0.1 shard_map.117
  67.5 1.9 %collective-permute-start.3 = (bf16[272,512]{1,0:T(8,128)(2,1)S(1)}, bf16[272,512]{1,0:T(8,128)(2,1)S(1)}, u32[]{:S(2)}, u32[]{:S(2)}) collective-permute-start(bf16[272,512]{1,0:T(8,128)(2,1)S(1)} %shard_map.117), channel_id=1, source_target_pairs={{0,1},{1,2},{2,3},{3,4},{4,5},{5,6},{6,7},{7,0},{8,15},{9,8},{10,9... | collective-permute-start | bytes 835592 | tf_op jit(solution)/shard_map/ppermute | solution.py:323
  69.4 3.4 %collective-permute-done.6.refs_0_ = bf16[272,512]{1,0:T(8,128)(2,1)S(1)} collective-permute-done((bf16[272,512]{1,0:T(8,128)(2,1)S(1)}, bf16[272,512]{1,0:T(8,128)(2,1)S(1)}, u32[]{:S(2)}, u32[]{:S(2)}) %collective-permute-start.6) | collective-permute-done | bytes 278560 | tf_op jit(solution)/shard_map/ppermute | solution.py:323
  72.8 0.1 shard_map.121
  72.9 1.9 %collective-permute-start.7 = (bf16[272,512]{1,0:T(8,128)(2,1)S(1)}, bf16[272,512]{1,0:T(8,128)(2,1)S(1)}, u32[]{:S(2)}, u32[]{:S(2)}) collective-permute-start(bf16[272,512]{1,0:T(8,128)(2,1)S(1)} %shard_map.121), channel_id=1, source_target_pairs={{0,9},{1,10},{2,11},{3,12},{4,13},{5,14},{6,15},{7,8},{8,7},{9,0},... | collective-permute-start | bytes 835592 | tf_op jit(solution)/shard_map/ppermute | solution.py:323
  74.8 2.3 %collective-permute-done.3.refs_0_ = bf16[272,512]{1,0:T(8,128)(2,1)S(1)} collective-permute-done((bf16[272,512]{1,0:T(8,128)(2,1)S(1)}, bf16[272,512]{1,0:T(8,128)(2,1)S(1)}, u32[]{:S(2)}, u32[]{:S(2)}) %collective-permute-start.3) | collective-permute-done | bytes 278560 | tf_op jit(solution)/shard_map/ppermute | solution.py:323
  77.2 0.1 shard_map.118
  77.2 1.9 %collective-permute-start.4 = (bf16[272,512]{1,0:T(8,128)(2,1)S(1)}, bf16[272,512]{1,0:T(8,128)(2,1)S(1)}, u32[]{:S(2)}, u32[]{:S(2)}) collective-permute-start(bf16[272,512]{1,0:T(8,128)(2,1)S(1)} %shard_map.118), channel_id=1, source_target_pairs={{0,1},{1,2},{2,3},{3,4},{4,5},{5,6},{6,7},{7,0},{8,15},{9,8},{10,9... | collective-permute-start | bytes 835592 | tf_op jit(solution)/shard_map/ppermute | solution.py:323
  79.2 1.6 %collective-permute-done.7.left_ref = bf16[272,512]{1,0:T(8,128)(2,1)S(1)} collective-permute-done((bf16[272,512]{1,0:T(8,128)(2,1)S(1)}, bf16[272,512]{1,0:T(8,128)(2,1)S(1)}, u32[]{:S(2)}, u32[]{:S(2)}) %collective-permute-start.7) | collective-permute-done | bytes 278560 | tf_op jit(solution)/shard_map/ppermute | solution.py:323
  80.8 6.1 %collective-permute-done.4.right_ref = bf16[272,512]{1,0:T(8,128)(2,1)S(1)} collective-permute-done((bf16[272,512]{1,0:T(8,128)(2,1)S(1)}, bf16[272,512]{1,0:T(8,128)(2,1)S(1)}, u32[]{:S(2)}, u32[]{:S(2)}) %collective-permute-start.4) | collective-permute-done | bytes 278560 | tf_op jit(solution)/shard_map/ppermute | solution.py:323
  86.9 0.9 shard_map.122
  (1 shorter events, 0.0 us)
Async XLA Ops:
  14.4 19.9 %all-to-all-start.1 = ((bf16[8,80,128]{2,1,0:T(8,128)(2,1)}), bf16[8,80,128]{2,1,0:T(8,128)(2,1)S(1)}, u32[]{:S(2)}, u32[]{:S(2)}) async-start(bf16[8,80,128]{2,1,0:T(8,128)(2,1)} %shard_map.110.refs_0_), calls=%async_computation.1 | async-start | bytes 327680 | tf_op jit(solution)/shard_map/all_to_all | solution.py:296
  35.0 9.4 %all-to-all-start.2 = ((bf16[8,64,128]{2,1,0:T(8,128)(2,1)}), bf16[8,64,128]{2,1,0:T(8,128)(2,1)S(1)}, u32[]{:S(2)}, u32[]{:S(2)}) async-start(bf16[8,64,128]{2,1,0:T(8,128)(2,1)} %shard_map.112.refs_0_), calls=%async_computation.2 | async-start | bytes 262144 | tf_op jit(solution)/shard_map/all_to_all | solution.py:311
  38.4 1.0 %copy-start = (f32[256,512]{1,0:T(8,128)S(1)}, f32[256,512]{1,0:T(8,128)}, u32[]{:S(2)}) copy-start(f32[256,512]{1,0:T(8,128)} %get-tuple-element.25.refs_2_) | copy-start | bytes 1572868
  39.4 1.0 %copy-start.1 = (f32[256,512]{1,0:T(8,128)S(1)}, f32[256,512]{1,0:T(8,128)}, u32[]{:S(2)}) copy-start(f32[256,512]{1,0:T(8,128)} %get-tuple-element.26.refs_3_) | copy-start | bytes 1572868
  40.4 0.8 copy-start.2
  41.3 0.7 copy-start.3
  46.1 4.5 %collective-permute-start = (bf16[272,512]{1,0:T(8,128)(2,1)S(1)}, bf16[272,512]{1,0:T(8,128)(2,1)S(1)}, u32[]{:S(2)}, u32[]{:S(2)}) collective-permute-start(bf16[272,512]{1,0:T(8,128)(2,1)S(1)} %get-tuple-element.31.own_ref.gated_ref), channel_id=1, source_target_pairs={{0,8},{1,9},{2,10},{3,11},{4,12},{5,13},{6,14},{7,15},{8,0},{9,1},... | collective-permute-start | bytes 835592 | tf_op jit(solution)/shard_map/ppermute | solution.py:323
  48.0 9.7 %collective-permute-start.1 = (bf16[272,512]{1,0:T(8,128)(2,1)S(1)}, bf16[272,512]{1,0:T(8,128)(2,1)S(1)}, u32[]{:S(2)}, u32[]{:S(2)}) collective-permute-start(bf16[272,512]{1,0:T(8,128)(2,1)S(1)} %get-tuple-element.34), channel_id=1, source_target_pairs={{0,1},{1,2},{2,3},{3,4},{4,5},{5,6},{6,7},{7,0},{8,15},{9,8},{10,9... | collective-permute-start | bytes 835592 | tf_op jit(solution)/shard_map/ppermute | solution.py:323
  53.4 9.7 %collective-permute-start.5 = (bf16[272,512]{1,0:T(8,128)(2,1)S(1)}, bf16[272,512]{1,0:T(8,128)(2,1)S(1)}, u32[]{:S(2)}, u32[]{:S(2)}) collective-permute-start(bf16[272,512]{1,0:T(8,128)(2,1)S(1)} %shard_map.119), channel_id=1, source_target_pairs={{0,1},{1,2},{2,3},{3,4},{4,5},{5,6},{6,7},{7,0},{8,15},{9,8},{10,9... | collective-permute-start | bytes 835592 | tf_op jit(solution)/shard_map/ppermute | solution.py:323
  57.8 9.7 %collective-permute-start.2 = (bf16[272,512]{1,0:T(8,128)(2,1)S(1)}, bf16[272,512]{1,0:T(8,128)(2,1)S(1)}, u32[]{:S(2)}, u32[]{:S(2)}) collective-permute-start(bf16[272,512]{1,0:T(8,128)(2,1)S(1)} %shard_map.116), channel_id=1, source_target_pairs={{0,1},{1,2},{2,3},{3,4},{4,5},{5,6},{6,7},{7,0},{8,15},{9,8},{10,9... | collective-permute-start | bytes 835592 | tf_op jit(solution)/shard_map/ppermute | solution.py:323
  63.2 9.7 %collective-permute-start.6 = (bf16[272,512]{1,0:T(8,128)(2,1)S(1)}, bf16[272,512]{1,0:T(8,128)(2,1)S(1)}, u32[]{:S(2)}, u32[]{:S(2)}) collective-permute-start(bf16[272,512]{1,0:T(8,128)(2,1)S(1)} %shard_map.120), channel_id=1, source_target_pairs={{0,1},{1,2},{2,3},{3,4},{4,5},{5,6},{6,7},{7,0},{8,15},{9,8},{10,9... | collective-permute-start | bytes 835592 | tf_op jit(solution)/shard_map/ppermute | solution.py:323
  67.5 9.7 %collective-permute-start.3 = (bf16[272,512]{1,0:T(8,128)(2,1)S(1)}, bf16[272,512]{1,0:T(8,128)(2,1)S(1)}, u32[]{:S(2)}, u32[]{:S(2)}) collective-permute-start(bf16[272,512]{1,0:T(8,128)(2,1)S(1)} %shard_map.117), channel_id=1, source_target_pairs={{0,1},{1,2},{2,3},{3,4},{4,5},{5,6},{6,7},{7,0},{8,15},{9,8},{10,9... | collective-permute-start | bytes 835592 | tf_op jit(solution)/shard_map/ppermute | solution.py:323
  72.9 7.9 %collective-permute-start.7 = (bf16[272,512]{1,0:T(8,128)(2,1)S(1)}, bf16[272,512]{1,0:T(8,128)(2,1)S(1)}, u32[]{:S(2)}, u32[]{:S(2)}) collective-permute-start(bf16[272,512]{1,0:T(8,128)(2,1)S(1)} %shard_map.121), channel_id=1, source_target_pairs={{0,9},{1,10},{2,11},{3,12},{4,13},{5,14},{6,15},{7,8},{8,7},{9,0},... | collective-permute-start | bytes 835592 | tf_op jit(solution)/shard_map/ppermute | solution.py:323
  77.2 9.7 %collective-permute-start.4 = (bf16[272,512]{1,0:T(8,128)(2,1)S(1)}, bf16[272,512]{1,0:T(8,128)(2,1)S(1)}, u32[]{:S(2)}, u32[]{:S(2)}) collective-permute-start(bf16[272,512]{1,0:T(8,128)(2,1)S(1)} %shard_map.118), channel_id=1, source_target_pairs={{0,1},{1,2},{2,3},{3,4},{4,5},{5,6},{6,7},{7,0},{8,15},{9,8},{10,9... | collective-permute-start | bytes 835592 | tf_op jit(solution)/shard_map/ppermute | solution.py:323

commit v8 on v7

--- a/solution.py
+++ b/solution.py
@@ -181,10 +181,21 @@
     return w_hbm.at[:, pl.ds(pl.multiple_of(place * features, features), features)]
 
 
-def gate_kernel(me, entry_ref, c_ref, own_ref, open_ref, gain_ref, w_hbm, gated_ref, far_ref, w_ref, sems):
+def put_halves(refs, total, squares):
+    half = total.shape[0] // 2
+    first = lax.broadcasted_iota(jnp.int32, squares.shape, 1) < half
+    for i, ref in enumerate(refs):
+        ref[:half] = total[i * half : (i + 1) * half]
+        put_squares(ref, jnp.where(first == (i == 0), squares, 0.0))
+
+
+def gate_kernel(me, way, entry_ref, c_ref, own_ref, open_ref, gain_ref, w_hbm, gated_ref, *refs):
+    next_ref, w_ref, sems = refs[2:]
     heads, width, lanes = entry_ref.shape
     tokens = own_ref.shape[0]
-    (copy,) = fetch([columns(w_hbm, me[0], N_PART // 2, w_ref.shape[1])], [w_ref], sems)
+    features = w_ref.shape[1]
+    wanted = [columns(w_hbm, me[0], away, features) for away in (N_PART // 2, (N_PART // 2 - 1) * way[0])]
+    copies = fetch(wanted, [w_ref, next_ref], sems)
     entries = entry_ref[...].reshape(heads * width, lanes)
     carried = lax.dot_general(c_ref[...], entries, (((1,), (1,)), ((), ())), preferred_element_type=F32)
     gated = own_ref[...] + open_ref[...] * carried
@@ -193,46 +204,63 @@
     squares = jnp.sum(gated * gated, axis=1, keepdims=True)
     squares = jnp.broadcast_to(squares, (tokens, 128)).T[:1]
     put_squares(gated_ref, squares)
-    put_squares(far_ref, squares)
-    copy.wait()
-    far_ref[:tokens] = jnp.dot(scaled, w_ref[...], preferred_element_type=F32).astype(BF16)
+    copies[0].wait()
+    put_halves(refs[:2], jnp.dot(scaled, w_ref[...], preferred_element_type=F32).astype(BF16), squares)
+    copies[1].wait()
+
+
+def begin_kernel(own_ref, other_ref, w_ref, chunk_ref, out_ref):
+    tokens = chunk_ref.shape[0]
+    out_ref[:tokens] = jnp.dot(other_ref[:tokens], w_ref[...], preferred_element_type=F32).astype(BF16)
+    out_ref[tokens:] = other_ref[tokens:]
+    chunk_ref[...] = jnp.dot(own_ref[:tokens], w_ref[...], preferred_element_type=F32).astype(BF16)
 
 
 def chunks_kernel(me, way, own_ref, other_ref, w_hbm, out_ref, base_ref, w_ref, sems):
     steps, _, tokens, features = out_ref.shape
-    away = [(steps - i) * way[0] for i in range(steps + 1)]
-    copies = fetch([columns(w_hbm, me[0], a, features) for a in away], [w_ref.at[i] for i in range(steps + 1)], sems)
-    for i in range(steps + 1):
-        copies[i].wait()
-        for j, ref in enumerate((own_ref, other_ref)):
-            if i < steps:
-                out_ref[i, j] = jnp.dot(ref[:tokens], w_ref[i], preferred_element_type=F32).astype(BF16)
-            elif j == 0:
-                base_ref[...] = jnp.dot(ref[:tokens], w_ref[i], preferred_element_type=F32).astype(BF16)
-
-
-def join_kernel(index, slab, chunks_ref, gated_ref, *refs):
-    got_refs, out_ref = refs[:-1], refs[-1]
-    tokens = chunks_ref.shape[2]
+    order = [*range(steps, 0, -1), 0]
+    copies = fetch([columns(w_hbm, me[0], a * way[0], features) for a in order], [w_ref.at[a] for a in order], sems)
+    for a, copy in zip(order, copies):
+        copy.wait()
+        if a == 0:
+            base_ref[...] = jnp.dot(own_ref[:tokens], w_ref[a], preferred_element_type=F32).astype(BF16)
+        else:
+            for j, ref in enumerate((own_ref, other_ref)):
+                out_ref[a - 1, j] = jnp.dot(ref[:tokens], w_ref[a], preferred_element_type=F32).astype(BF16)
+
+
+def join_kernel(place, chunks_ref, gated_ref, *refs):
+    tokens = gated_ref.shape[0] - PAD
+    half = tokens // 2
+    got_refs = [ref for ref in refs[:-2] if ref is not None]
     squares = get_squares(gated_ref)
-    total = chunks_ref[index, slab].astype(F32)
+    total = (chunks_ref if place is None else chunks_ref.at[place])[...].astype(F32)
     for ref in got_refs:
         squares = squares + get_squares(ref)
-        total = total + ref[:tokens].astype(F32)
-    out_ref[:tokens] = total.astype(BF16)
-    put_squares(out_ref, squares)
-
-
-def end_kernel(inner, base_ref, own_ref, right_ref, left_ref, out_ref):
+    if len(got_refs) == 2:
+        total = total + jnp.concatenate([ref[:half].astype(F32) for ref in got_refs], axis=0)
+    else:
+        total = total + got_refs[0][:tokens].astype(F32)
+    total = total.astype(BF16)
+    if refs[-1] is None:
+        refs[-2][:tokens] = total
+        put_squares(refs[-2], squares)
+    else:
+        put_halves(refs[-2:], total, squares)
+
+
+def end_kernel(inner, base_ref, own_ref, first_ref, second_ref, other_ref, out_ref):
     tokens, features = out_ref.shape
-    squares = get_squares(own_ref) + get_squares(right_ref) + get_squares(left_ref)
+    half = tokens // 2
+    squares = get_squares(own_ref) + get_squares(first_ref) + get_squares(second_ref) + get_squares(other_ref)
     factor = lax.rsqrt(squares * (1.0 / inner) + 1e-05)
     factor = jnp.broadcast_to(factor, (128, tokens)).T
-    for i in range(features // 128):
-        span = slice(i * 128, (i + 1) * 128)
-        total = base_ref[:, span].astype(F32)
-        total = total + right_ref[:tokens, span].astype(F32) + left_ref[:tokens, span].astype(F32)
-        out_ref[:, span] = (total * factor).astype(BF16)
+    for j, ref in enumerate((first_ref, second_ref)):
+        rows = slice(j * half, (j + 1) * half)
+        for i in range(features // 128):
+            span = slice(i * 128, (i + 1) * 128)
+            total = base_ref[rows, span].astype(F32) + ref[:half, span].astype(F32) + other_ref[rows, span].astype(F32)
+            out_ref[rows, span] = (total * factor[rows]).astype(BF16)
 
 
 def call(kernel, ins, outs, args, scratch=(), flops=0, moved=0, limit=24):
@@ -322,46 +350,59 @@
                 pairs.append((seq * N_PART + head, (seq ^ swap) * N_PART + there))
         return lax.ppermute(array, ("seq", "head"), pairs)
 
-    gated, far = call(
+    half_slab = ((tokens // 2 + PAD, features), BF16)
+    gated, far_first, far_second, w_next = call(
         gate_kernel,
-        [SMEM] + [VMEM] * 5 + [HBM],
-        [slab, slab],
-        (me, entries, *needed, out_weight),
+        [SMEM] * 2 + [VMEM] * 5 + [HBM],
+        [slab, half_slab, half_slab, ((channels, features), BF16)],
+        (me, way, entries, *needed, out_weight),
         scratch=[jax.ShapeDtypeStruct((channels, features), BF16)],
         flops=2 * tokens * channels * features,
         moved=2**21,
         limit=50,
     )
     other = send(gated, 0, 1)
-    flow = send(far, 1, 0)
-    steps = N_PART // 2 - 1
+    own_got = [send(far_first, 1, 0), send(far_second, 1, 0)]
+    begin, other_sent = call(
+        begin_kernel,
+        [VMEM] * 3,
+        [((tokens, features), BF16), slab],
+        (gated, other, w_next),
+        flops=4 * tokens * channels * features,
+        moved=2**20,
+    )
+    other_got = send(other_sent, 1, 0)
+    steps = N_PART // 2 - 2
     chunks, base = call(
         chunks_kernel,
         [SMEM, SMEM, VMEM, VMEM, HBM],
         [((steps, 2, tokens, features), BF16), ((tokens, features), BF16)],
         (me, way, gated, other, out_weight),
         scratch=[jax.ShapeDtypeStruct((steps + 1, channels, features), BF16)],
-        flops=14 * tokens * channels * features,
-        moved=2**22,
+        flops=10 * tokens * channels * features,
+        moved=2**21,
         limit=50,
     )
-    flows = [[flow], []]
-    for step in range(steps):
-        for slab_index in (1, 0):
-            got = flows[slab_index]
-            (joined,) = call(
-                functools.partial(join_kernel, step, slab_index),
-                [VMEM] * (2 + len(got)),
-                [slab],
-                (chunks, (gated, other)[slab_index], *got),
-                moved=2**19,
-            )
-            flows[slab_index] = [send(joined, 1, slab_index if step == steps - 1 else 0)]
+
+    def join(chunk, place, mine, got, halves):
+        def kernel(*refs):
+            outs = refs[2 + len(got) :]
+            join_kernel(place, *refs[: 2 + len(got)], *(outs if halves else (*outs, None)))
+
+        return call(
+            kernel, [VMEM] * (2 + len(got)), [half_slab] * 2 if halves else [slab], (chunk, mine, *got), moved=2**19
+        )
+
+    own_got = [send(*join(begin, None, gated, own_got, False), 1, 0)]
+    for away in range(steps, 0, -1):
+        last = away == 1
+        other_got = send(*join(chunks, (away - 1, 1), other, [other_got], False), 1, int(last))
+        own_got = [send(part, 1, 0) for part in join(chunks, (away - 1, 0), gated, own_got, last)]
     (out,) = call(
         functools.partial(end_kernel, channels * N_PART),
-        [VMEM] * 4,
+        [VMEM] * 5,
         [((tokens, features), BF16)],
-        (base, gated, *flows[0], *flows[1]),
+        (base, gated, *own_got, other_got),
         moved=2**20,
     )
     return out

time: 88.6 us -> 91.9 us (1.037)
  the two profiles are of different devices: /device:TPU:32 before, /device:TPU:24 now
where the time goes in v8:
time: 91.9 us; the launch traced here: 91.1 us
  starting transfers between devices  45.7 us (50%)
  waiting for transfers between devices  16.6 us (18%)
  Pallas kernels  14.2 us (15%)
  blocking collectives  10.8 us (12%)
  local copies, waits for them, and re-layouts  3.6 us (4%)
    ppermute x10, starting transfers between devices, send(): return lax.ppermute(array, ('seq', 'head'), pairs)  32 us
    pallas_call x14, Pallas kernels, call(): pl.pallas_call(kernel, in_specs=ins, out_specs=[VMEM] * len(outs), out_sh...  14.2 us
    all_to_all x1, blocking collectives, body(): got = lax.all_to_all(pieces, 'seq', 0, 0, axis_index_groups=in_plane)  10.8 us
    all_to_all x1, starting transfers between devices, body(): got_planes = lax.all_to_all(totals, 'seq', 0, 0, axis_index_groups=across)  10.3 us
    ppermute x10, waiting for transfers between devices, send(): return lax.ppermute(array, ('seq', 'head'), pairs)  8.79 us
    all_to_all x1, waiting for transfers between devices, body(): got_planes = lax.all_to_all(totals, 'seq', 0, 0, axis_index_groups=across)  5.57 us
    unnamed x8, local copies, waits for them, and re-layouts  3.6 us
    all_to_all x1, starting transfers between devices, body(): entries = lax.all_to_all(entries, 'seq', 0, 0, axis_index_groups=in_plane)  3.37 us
  transfers between devices with their start and end apart: 12, of which 8 were waited for; matrix products, arithmetic and copies ran while one was open for 0% of the time, Pallas kernels for 8%

profile of v8, /device:TPU:24, one launch (start us, length us, event | category | flops | bytes accessed | tf_op | source)
XLA Modules:
  0.0 91.1 jit_solution(17424270616486358552)
XLA Ops:
  0.0 2.9 %shard_map.109 = (bf16[8,80,128]{2,1,0:T(8,128)(2,1)}, f32[40,256]{1,0:T(8,128)}, f32[256,128]{1,0:T(8,128)}) custom-call(f32[1,8]{1,0:T(1,128)} %bitcast.13, f32[1,8]{1,0:T(1,128)} %bitcast.14, f32[8,256]{1,0:T(8,128)} %bitcast.10, s32[1,256]{1,0:T(1,128)} %bitcast.11, bf16[256,128]{1,0:T(8,128)(2,1)} %refs_2_.1, bf16[256,512]{1,0:T(8,128)(2,1)} %refs_6_.1), custom_call_target="tpu_custom_call" | custom-call | flops 33554432 | bytes 262144 | tf_op jit(solution)/shard_map/pallas_call | solution.py:267
  2.9 10.8 %all_to_all.15.got_ref = bf16[8,80,128]{2,1,0:T(8,128)(2,1)S(1)} all-to-all(bf16[8,80,128]{2,1,0:T(8,128)(2,1)} %get-tuple-element.26), channel_id=1, replica_groups={{0,8,16,24,32,40,48,56},{64,72,80,88,96,104,112,120},{128,136,144,152,1..., dimensions={0} | all-to-all | bytes 327680 | tf_op jit(solution)/shard_map/all_to_all | solution.py:309
  13.7 0.7 shard_map.110.refs_0_
  14.4 10.3 %all-to-all-start.1 = ((bf16[8,80,128]{2,1,0:T(8,128)(2,1)}), bf16[8,80,128]{2,1,0:T(8,128)(2,1)S(1)}, u32[]{:S(2)}, u32[]{:S(2)}) async-start(bf16[8,80,128]{2,1,0:T(8,128)(2,1)} %shard_map.110.refs_0_), calls=%async_computation.1 | async-start | bytes 327680 | tf_op jit(solution)/shard_map/all_to_all | solution.py:324
  24.7 4.0 %shard_map.111 = (f32[256,512]{1,0:T(8,128)}, f32[256,512]{1,0:T(8,128)}) custom-call(bf16[8,80,128]{2,1,0:T(8,128)(2,1)} %shard_map.110.refs_0_, bf16[256,128]{1,0:T(8,128)(2,1)} %refs_1_.3, bf16[256,128]{1,0:T(8,128)(2,1)} %refs_2_.1, f32[40,256]{1,0:T(8,128)} %get-tuple-element.27.refs_3_, f32[256,128]{1,0:T(8,128)} %get-tuple-element.28.refs_4_, ...), custom_call_target="tpu_custom_call" | custom-call | flops 67108864 | bytes 8388608 | tf_op jit(solution)/shard_map/pallas_call | solution.py:267
  28.7 5.6 %all-to-all-done.1.planes_ref = bf16[8,80,128]{2,1,0:T(8,128)(2,1)S(1)} async-done(((bf16[8,80,128]{2,1,0:T(8,128)(2,1)}), bf16[8,80,128]{2,1,0:T(8,128)(2,1)S(1)}, u32[]{:S(2)}, u32[]{:S(2)}) %all-to-all-start.1) | async-done | bytes 163872 | tf_op jit(solution)/shard_map/all_to_all | solution.py:324
  34.2 0.7 shard_map.112.refs_0_
  35.0 3.4 %all-to-all-start.2 = ((bf16[8,64,128]{2,1,0:T(8,128)(2,1)}), bf16[8,64,128]{2,1,0:T(8,128)(2,1)S(1)}, u32[]{:S(2)}, u32[]{:S(2)}) async-start(bf16[8,64,128]{2,1,0:T(8,128)(2,1)} %shard_map.112.refs_0_), calls=%async_computation.2 | async-start | bytes 262144 | tf_op jit(solution)/shard_map/all_to_all | solution.py:339
  38.4 0.0 copy-start
  38.4 1.0 %copy-done = f32[256,512]{1,0:T(8,128)S(1)} copy-done((f32[256,512]{1,0:T(8,128)S(1)}, f32[256,512]{1,0:T(8,128)}, u32[]{:S(2)}) %copy-start) | copy-done | bytes 524312
  39.4 0.0 copy-start.1
  39.4 1.0 %copy-done.1 = f32[256,512]{1,0:T(8,128)S(1)} copy-done((f32[256,512]{1,0:T(8,128)S(1)}, f32[256,512]{1,0:T(8,128)}, u32[]{:S(2)}) %copy-start.1) | copy-done | bytes 524312
  40.5 0.0 copy-start.2
  40.5 0.8 copy-done.2
  41.3 0.0 copy-start.3
  41.3 0.7 copy-done.3
  42.0 0.2 shard_map.113
  42.2 2.2 %all-to-all-done.2.entry_ref = bf16[8,64,128]{2,1,0:T(8,128)(2,1)S(1)} async-done(((bf16[8,64,128]{2,1,0:T(8,128)(2,1)}), bf16[8,64,128]{2,1,0:T(8,128)(2,1)S(1)}, u32[]{:S(2)}, u32[]{:S(2)}) %all-to-all-start.2) | async-done | bytes 131104 | tf_op jit(solution)/shard_map/all_to_all | solution.py:339
  44.4 1.7 %shard_map.114 = (bf16[272,512]{1,0:T(8,128)(2,1)S(1)}, bf16[144,512]{1,0:T(8,128)(2,1)S(1)}, bf16[144,512]{1,0:T(8,128)(2,1)S(1)}, bf16[512,512]{1,0:T(8,128)(2,1)S(1)}) custom-call(s32[1]{0:T(128)} %bitcast.me, s32[1]{0:T(128)} %bitcast.1.way, bf16[8,64,128]{2,1,0:T(8,128)(2,1)S(1)} %all-to-all-done.2.entry_ref, ...), custom_call_target="tpu_custom_call" | custom-call | flops 134217728 | bytes 2097152 | tf_op jit(solution)/shard_map/pallas_call | solution.py:267
  46.1 1.9 %collective-permute-start = (bf16[272,512]{1,0:T(8,128)(2,1)S(1)}, bf16[272,512]{1,0:T(8,128)(2,1)S(1)}, u32[]{:S(2)}, u32[]{:S(2)}) collective-permute-start(bf16[272,512]{1,0:T(8,128)(2,1)S(1)} %get-tuple-element.37.own_ref.refs_1_), channel_id=1, source_target_pairs={{0,8},{1,9},{2,10},{3,11},{4,12},{5,13},{6,14},{7,15},{8,0},{9,1},... | collective-permute-start | bytes 835592 | tf_op jit(solution)/shard_map/ppermute | solution.py:351
  48.0 4.7 %collective-permute-start.1 = (bf16[144,512]{1,0:T(8,128)(2,1)S(1)}, bf16[144,512]{1,0:T(8,128)(2,1)S(1)}, u32[]{:S(2)}, u32[]{:S(2)}) collective-permute-start(bf16[144,512]{1,0:T(8,128)(2,1)S(1)} %get-tuple-element.42), channel_id=1, source_target_pairs={{0,1},{1,2},{2,3},{3,4},{4,5},{5,6},{6,7},{7,0},{8,15},{9,8},{10,9... | collective-permute-start | bytes 442376 | tf_op jit(solution)/shard_map/ppermute | solution.py:351
  52.7 2.6 %collective-permute-start.2 = (bf16[144,512]{1,0:T(8,128)(2,1)S(1)}, bf16[144,512]{1,0:T(8,128)(2,1)S(1)}, u32[]{:S(2)}, u32[]{:S(2)}) collective-permute-start(bf16[144,512]{1,0:T(8,128)(2,1)S(1)} %get-tuple-element.43), channel_id=1, source_target_pairs={{0,1},{1,2},{2,3},{3,4},{4,5},{5,6},{6,7},{7,0},{8,15},{9,8},{10,9... | collective-permute-start | bytes 442376 | tf_op jit(solution)/shard_map/ppermute | solution.py:351
  55.3 0.0 collective-permute-done.other_ref.refs_1_
  55.3 0.4 shard_map.116
  55.8 2.6 %collective-permute-start.7 = (bf16[272,512]{1,0:T(8,128)(2,1)S(1)}, bf16[272,512]{1,0:T(8,128)(2,1)S(1)}, u32[]{:S(2)}, u32[]{:S(2)}) collective-permute-start(bf16[272,512]{1,0:T(8,128)(2,1)S(1)} %get-tuple-element.46), channel_id=1, source_target_pairs={{0,1},{1,2},{2,3},{3,4},{4,5},{5,6},{6,7},{7,0},{8,15},{9,8},{10,9... | collective-permute-start | bytes 835592 | tf_op jit(solution)/shard_map/ppermute | solution.py:351
  58.4 0.0 collective-permute-done.1.refs_2_
  58.4 1.4 %collective-permute-done.2.refs_3_ = bf16[144,512]{1,0:T(8,128)(2,1)S(1)} collective-permute-done((bf16[144,512]{1,0:T(8,128)(2,1)S(1)}, bf16[144,512]{1,0:T(8,128)(2,1)S(1)}, u32[]{:S(2)}, u32[]{:S(2)}) %collective-permute-start.2) | collective-permute-done | bytes 147488 | tf_op jit(solution)/shard_map/ppermute | solution.py:351
  59.8 0.1 shard_map.117
  59.9 3.8 %collective-permute-start.3 = (bf16[272,512]{1,0:T(8,128)(2,1)S(1)}, bf16[272,512]{1,0:T(8,128)(2,1)S(1)}, u32[]{:S(2)}, u32[]{:S(2)}) collective-permute-start(bf16[272,512]{1,0:T(8,128)(2,1)S(1)} %shard_map.117), channel_id=1, source_target_pairs={{0,1},{1,2},{2,3},{3,4},{4,5},{5,6},{6,7},{7,0},{8,15},{9,8},{10,9... | collective-permute-start | bytes 835592 | tf_op jit(solution)/shard_map/ppermute | solution.py:351
  63.7 2.3 %shard_map.115 = (bf16[2,2,256,512]{3,2,1,0:T(8,128)(2,1)S(1)}, bf16[256,512]{1,0:T(8,128)(2,1)S(1)}) custom-call(s32[1]{0:T(128)} %bitcast.me, s32[1]{0:T(128)} %bitcast.1.way, bf16[272,512]{1,0:T(8,128)(2,1)S(1)} %get-tuple-element.37.own_ref.refs_1_, bf16[272,512]{1,0:T(8,128)(2,1)S(1)} %collective-permute-done.other_ref.refs_1_, bf16[512,4096]{1,0:T(8,128)(2,1)} %w_hbm.3), custom_call_target="tpu_custom_call" | custom-call | flops 671088640 | bytes 2097152 | tf_op jit(solution)/shard_map/pallas_call | solution.py:267
  66.0 0.0 collective-permute-done.7.refs_2_
  66.0 0.1 shard_map.120
  66.1 2.0 %collective-permute-start.8 = (bf16[272,512]{1,0:T(8,128)(2,1)S(1)}, bf16[272,512]{1,0:T(8,128)(2,1)S(1)}, u32[]{:S(2)}, u32[]{:S(2)}) collective-permute-start(bf16[272,512]{1,0:T(8,128)(2,1)S(1)} %shard_map.120), channel_id=1, source_target_pairs={{0,1},{1,2},{2,3},{3,4},{4,5},{5,6},{6,7},{7,0},{8,15},{9,8},{10,9... | collective-permute-start | bytes 835592 | tf_op jit(solution)/shard_map/ppermute | solution.py:351
  68.1 0.2 collective-permute-done.3.refs_2_
  68.3 0.1 shard_map.118
  68.4 5.0 %collective-permute-start.4 = (bf16[272,512]{1,0:T(8,128)(2,1)S(1)}, bf16[272,512]{1,0:T(8,128)(2,1)S(1)}, u32[]{:S(2)}, u32[]{:S(2)}) collective-permute-start(bf16[272,512]{1,0:T(8,128)(2,1)S(1)} %shard_map.118), channel_id=1, source_target_pairs={{0,1},{1,2},{2,3},{3,4},{4,5},{5,6},{6,7},{7,0},{8,15},{9,8},{10,9... | collective-permute-start | bytes 835592 | tf_op jit(solution)/shard_map/ppermute | solution.py:351
  73.4 1.1 %collective-permute-done.8.refs_2_ = bf16[272,512]{1,0:T(8,128)(2,1)S(1)} collective-permute-done((bf16[272,512]{1,0:T(8,128)(2,1)S(1)}, bf16[272,512]{1,0:T(8,128)(2,1)S(1)}, u32[]{:S(2)}, u32[]{:S(2)}) %collective-permute-start.8) | collective-permute-done | bytes 278560 | tf_op jit(solution)/shard_map/ppermute | solution.py:351
  74.5 0.1 shard_map.121
  74.6 1.9 %collective-permute-start.9 = (bf16[272,512]{1,0:T(8,128)(2,1)S(1)}, bf16[272,512]{1,0:T(8,128)(2,1)S(1)}, u32[]{:S(2)}, u32[]{:S(2)}) collective-permute-start(bf16[272,512]{1,0:T(8,128)(2,1)S(1)} %shard_map.121), channel_id=1, source_target_pairs={{0,9},{1,10},{2,11},{3,12},{4,13},{5,14},{6,15},{7,8},{8,7},{9,0},... | collective-permute-start | bytes 835592 | tf_op jit(solution)/shard_map/ppermute | solution.py:351
  76.5 1.0 %collective-permute-done.4.refs_2_ = bf16[272,512]{1,0:T(8,128)(2,1)S(1)} collective-permute-done((bf16[272,512]{1,0:T(8,128)(2,1)S(1)}, bf16[272,512]{1,0:T(8,128)(2,1)S(1)}, u32[]{:S(2)}, u32[]{:S(2)}) %collective-permute-start.4) | collective-permute-done | bytes 278560 | tf_op jit(solution)/shard_map/ppermute | solution.py:351
  77.5 0.1 shard_map.119
  77.6 5.5 %collective-permute-start.5 = (bf16[144,512]{1,0:T(8,128)(2,1)S(1)}, bf16[144,512]{1,0:T(8,128)(2,1)S(1)}, u32[]{:S(2)}, u32[]{:S(2)}) collective-permute-start(bf16[144,512]{1,0:T(8,128)(2,1)S(1)} %get-tuple-element.44), channel_id=1, source_target_pairs={{0,1},{1,2},{2,3},{3,4},{4,5},{5,6},{6,7},{7,0},{8,15},{9,8},{10,9... | collective-permute-start | bytes 442376 | tf_op jit(solution)/shard_map/ppermute | solution.py:351
  83.1 1.9 %collective-permute-start.6 = (bf16[144,512]{1,0:T(8,128)(2,1)S(1)}, bf16[144,512]{1,0:T(8,128)(2,1)S(1)}, u32[]{:S(2)}, u32[]{:S(2)}) collective-permute-start(bf16[144,512]{1,0:T(8,128)(2,1)S(1)} %get-tuple-element.45), channel_id=1, source_target_pairs={{0,1},{1,2},{2,3},{3,4},{4,5},{5,6},{6,7},{7,0},{8,15},{9,8},{10,9... | collective-permute-start | bytes 442376 | tf_op jit(solution)/shard_map/ppermute | solution.py:351
  85.1 0.7 collective-permute-done.5.first_ref
  85.8 4.4 %collective-permute-done.6.second_ref = bf16[144,512]{1,0:T(8,128)(2,1)S(1)} collective-permute-done((bf16[144,512]{1,0:T(8,128)(2,1)S(1)}, bf16[144,512]{1,0:T(8,128)(2,1)S(1)}, u32[]{:S(2)}, u32[]{:S(2)}) %collective-permute-start.6) | collective-permute-done | bytes 147488 | tf_op jit(solution)/shard_map/ppermute | solution.py:351
  90.2 0.0 collective-permute-done.9.other_ref
  90.2 0.9 shard_map.122
Async XLA Ops:
  14.4 19.9 %all-to-all-start.1 = ((bf16[8,80,128]{2,1,0:T(8,128)(2,1)}), bf16[8,80,128]{2,1,0:T(8,128)(2,1)S(1)}, u32[]{:S(2)}, u32[]{:S(2)}) async-start(bf16[8,80,128]{2,1,0:T(8,128)(2,1)} %shard_map.110.refs_0_), calls=%async_computation.1 | async-start | bytes 327680 | tf_op jit(solution)/shard_map/all_to_all | solution.py:324
  35.0 9.4 %all-to-all-start.2 = ((bf16[8,64,128]{2,1,0:T(8,128)(2,1)}), bf16[8,64,128]{2,1,0:T(8,128)(2,1)S(1)}, u32[]{:S(2)}, u32[]{:S(2)}) async-start(bf16[8,64,128]{2,1,0:T(8,128)(2,1)} %shard_map.112.refs_0_), calls=%async_computation.2 | async-start | bytes 262144 | tf_op jit(solution)/shard_map/all_to_all | solution.py:339
  38.4 1.0 %copy-start = (f32[256,512]{1,0:T(8,128)S(1)}, f32[256,512]{1,0:T(8,128)}, u32[]{:S(2)}) copy-start(f32[256,512]{1,0:T(8,128)} %get-tuple-element.31.refs_2_) | copy-start | bytes 1572868
  39.4 1.0 %copy-start.1 = (f32[256,512]{1,0:T(8,128)S(1)}, f32[256,512]{1,0:T(8,128)}, u32[]{:S(2)}) copy-start(f32[256,512]{1,0:T(8,128)} %get-tuple-element.32.refs_3_) | copy-start | bytes 1572868
  40.5 0.8 copy-start.2
  41.3 0.7 copy-start.3
  46.1 9.2 %collective-permute-start = (bf16[272,512]{1,0:T(8,128)(2,1)S(1)}, bf16[272,512]{1,0:T(8,128)(2,1)S(1)}, u32[]{:S(2)}, u32[]{:S(2)}) collective-permute-start(bf16[272,512]{1,0:T(8,128)(2,1)S(1)} %get-tuple-element.37.own_ref.refs_1_), channel_id=1, source_target_pairs={{0,8},{1,9},{2,10},{3,11},{4,12},{5,13},{6,14},{7,15},{8,0},{9,1},... | collective-permute-start | bytes 835592 | tf_op jit(solution)/shard_map/ppermute | solution.py:351
  48.0 10.3 %collective-permute-start.1 = (bf16[144,512]{1,0:T(8,128)(2,1)S(1)}, bf16[144,512]{1,0:T(8,128)(2,1)S(1)}, u32[]{:S(2)}, u32[]{:S(2)}) collective-permute-start(bf16[144,512]{1,0:T(8,128)(2,1)S(1)} %get-tuple-element.42), channel_id=1, source_target_pairs={{0,1},{1,2},{2,3},{3,4},{4,5},{5,6},{6,7},{7,0},{8,15},{9,8},{10,9... | collective-permute-start | bytes 442376 | tf_op jit(solution)/shard_map/ppermute | solution.py:351
  52.7 7.0 %collective-permute-start.2 = (bf16[144,512]{1,0:T(8,128)(2,1)S(1)}, bf16[144,512]{1,0:T(8,128)(2,1)S(1)}, u32[]{:S(2)}, u32[]{:S(2)}) collective-permute-start(bf16[144,512]{1,0:T(8,128)(2,1)S(1)} %get-tuple-element.43), channel_id=1, source_target_pairs={{0,1},{1,2},{2,3},{3,4},{4,5},{5,6},{6,7},{7,0},{8,15},{9,8},{10,9... | collective-permute-start | bytes 442376 | tf_op jit(solution)/shard_map/ppermute | solution.py:351
  55.8 10.2 %collective-permute-start.7 = (bf16[272,512]{1,0:T(8,128)(2,1)S(1)}, bf16[272,512]{1,0:T(8,128)(2,1)S(1)}, u32[]{:S(2)}, u32[]{:S(2)}) collective-permute-start(bf16[272,512]{1,0:T(8,128)(2,1)S(1)} %get-tuple-element.46), channel_id=1, source_target_pairs={{0,1},{1,2},{2,3},{3,4},{4,5},{5,6},{6,7},{7,0},{8,15},{9,8},{10,9... | collective-permute-start | bytes 835592 | tf_op jit(solution)/shard_map/ppermute | solution.py:351
  59.9 8.4 %collective-permute-start.3 = (bf16[272,512]{1,0:T(8,128)(2,1)S(1)}, bf16[272,512]{1,0:T(8,128)(2,1)S(1)}, u32[]{:S(2)}, u32[]{:S(2)}) collective-permute-start(bf16[272,512]{1,0:T(8,128)(2,1)S(1)} %shard_map.117), channel_id=1, source_target_pairs={{0,1},{1,2},{2,3},{3,4},{4,5},{5,6},{6,7},{7,0},{8,15},{9,8},{10,9... | collective-permute-start | bytes 835592 | tf_op jit(solution)/shard_map/ppermute | solution.py:351
  66.1 8.4 %collective-permute-start.8 = (bf16[272,512]{1,0:T(8,128)(2,1)S(1)}, bf16[272,512]{1,0:T(8,128)(2,1)S(1)}, u32[]{:S(2)}, u32[]{:S(2)}) collective-permute-start(bf16[272,512]{1,0:T(8,128)(2,1)S(1)} %shard_map.120), channel_id=1, source_target_pairs={{0,1},{1,2},{2,3},{3,4},{4,5},{5,6},{6,7},{7,0},{8,15},{9,8},{10,9... | collective-permute-start | bytes 835592 | tf_op jit(solution)/shard_map/ppermute | solution.py:351
  68.4 9.1 %collective-permute-start.4 = (bf16[272,512]{1,0:T(8,128)(2,1)S(1)}, bf16[272,512]{1,0:T(8,128)(2,1)S(1)}, u32[]{:S(2)}, u32[]{:S(2)}) collective-permute-start(bf16[272,512]{1,0:T(8,128)(2,1)S(1)} %shard_map.118), channel_id=1, source_target_pairs={{0,1},{1,2},{2,3},{3,4},{4,5},{5,6},{6,7},{7,0},{8,15},{9,8},{10,9... | collective-permute-start | bytes 835592 | tf_op jit(solution)/shard_map/ppermute | solution.py:351
  74.6 15.6 %collective-permute-start.9 = (bf16[272,512]{1,0:T(8,128)(2,1)S(1)}, bf16[272,512]{1,0:T(8,128)(2,1)S(1)}, u32[]{:S(2)}, u32[]{:S(2)}) collective-permute-start(bf16[272,512]{1,0:T(8,128)(2,1)S(1)} %shard_map.121), channel_id=1, source_target_pairs={{0,9},{1,10},{2,11},{3,12},{4,13},{5,14},{6,15},{7,8},{8,7},{9,0},... | collective-permute-start | bytes 835592 | tf_op jit(solution)/shard_map/ppermute | solution.py:351
  77.6 8.2 %collective-permute-start.5 = (bf16[144,512]{1,0:T(8,128)(2,1)S(1)}, bf16[144,512]{1,0:T(8,128)(2,1)S(1)}, u32[]{:S(2)}, u32[]{:S(2)}) collective-permute-start(bf16[144,512]{1,0:T(8,128)(2,1)S(1)} %get-tuple-element.44), channel_id=1, source_target_pairs={{0,1},{1,2},{2,3},{3,4},{4,5},{5,6},{6,7},{7,0},{8,15},{9,8},{10,9... | collective-permute-start | bytes 442376 | tf_op jit(solution)/shard_map/ppermute | solution.py:351
  83.1 7.0 %collective-permute-start.6 = (bf16[144,512]{1,0:T(8,128)(2,1)S(1)}, bf16[144,512]{1,0:T(8,128)(2,1)S(1)}, u32[]{:S(2)}, u32[]{:S(2)}) collective-permute-start(bf16[144,512]{1,0:T(8,128)(2,1)S(1)} %get-tuple-element.45), channel_id=1, source_target_pairs={{0,1},{1,2},{2,3},{3,4},{4,5},{5,6},{6,7},{7,0},{8,15},{9,8},{10,9... | collective-permute-start | bytes 442376 | tf_op jit(solution)/shard_map/ppermute | solution.py:351

commit v9 on v8

--- a/solution.py
+++ b/solution.py
@@ -181,16 +181,8 @@
     return w_hbm.at[:, pl.ds(pl.multiple_of(place * features, features), features)]
 
 
-def put_halves(refs, total, squares):
-    half = total.shape[0] // 2
-    first = lax.broadcasted_iota(jnp.int32, squares.shape, 1) < half
-    for i, ref in enumerate(refs):
-        ref[:half] = total[i * half : (i + 1) * half]
-        put_squares(ref, jnp.where(first == (i == 0), squares, 0.0))
-
-
-def gate_kernel(me, way, entry_ref, c_ref, own_ref, open_ref, gain_ref, w_hbm, gated_ref, *refs):
-    next_ref, w_ref, sems = refs[2:]
+def gate_kernel(me, way, entry_ref, c_ref, own_ref, open_ref, gain_ref, w_hbm, *refs):
+    gated_ref, far_ref, next_ref, w_ref, sems = refs
     heads, width, lanes = entry_ref.shape
     tokens = own_ref.shape[0]
     features = w_ref.shape[1]
@@ -204,8 +196,9 @@
     squares = jnp.sum(gated * gated, axis=1, keepdims=True)
     squares = jnp.broadcast_to(squares, (tokens, 128)).T[:1]
     put_squares(gated_ref, squares)
+    put_squares(far_ref, squares)
     copies[0].wait()
-    put_halves(refs[:2], jnp.dot(scaled, w_ref[...], preferred_element_type=F32).astype(BF16), squares)
+    far_ref[:tokens] = jnp.dot(scaled, w_ref[...], preferred_element_type=F32).astype(BF16)
     copies[1].wait()
 
 
@@ -229,38 +222,23 @@
                 out_ref[a - 1, j] = jnp.dot(ref[:tokens], w_ref[a], preferred_element_type=F32).astype(BF16)
 
 
-def join_kernel(place, chunks_ref, gated_ref, *refs):
+def join_kernel(place, chunk_ref, gated_ref, got_ref, out_ref):
     tokens = gated_ref.shape[0] - PAD
-    half = tokens // 2
-    got_refs = [ref for ref in refs[:-2] if ref is not None]
-    squares = get_squares(gated_ref)
-    total = (chunks_ref if place is None else chunks_ref.at[place])[...].astype(F32)
-    for ref in got_refs:
-        squares = squares + get_squares(ref)
-    if len(got_refs) == 2:
-        total = total + jnp.concatenate([ref[:half].astype(F32) for ref in got_refs], axis=0)
-    else:
-        total = total + got_refs[0][:tokens].astype(F32)
-    total = total.astype(BF16)
-    if refs[-1] is None:
-        refs[-2][:tokens] = total
-        put_squares(refs[-2], squares)
-    else:
-        put_halves(refs[-2:], total, squares)
-
-
-def end_kernel(inner, base_ref, own_ref, first_ref, second_ref, other_ref, out_ref):
+    chunk = (chunk_ref if place is None else chunk_ref.at[place])[...]
+    out_ref[:tokens] = (chunk.astype(F32) + got_ref[:tokens].astype(F32)).astype(BF16)
+    put_squares(out_ref, get_squares(gated_ref) + get_squares(got_ref))
+
+
+def end_kernel(inner, base_ref, own_ref, right_ref, left_ref, out_ref):
     tokens, features = out_ref.shape
-    half = tokens // 2
-    squares = get_squares(own_ref) + get_squares(first_ref) + get_squares(second_ref) + get_squares(other_ref)
+    squares = get_squares(own_ref) + get_squares(right_ref) + get_squares(left_ref)
     factor = lax.rsqrt(squares * (1.0 / inner) + 1e-05)
     factor = jnp.broadcast_to(factor, (128, tokens)).T
-    for j, ref in enumerate((first_ref, second_ref)):
-        rows = slice(j * half, (j + 1) * half)
-        for i in range(features // 128):
-            span = slice(i * 128, (i + 1) * 128)
-            total = base_ref[rows, span].astype(F32) + ref[:half, span].astype(F32) + other_ref[rows, span].astype(F32)
-            out_ref[rows, span] = (total * factor[rows]).astype(BF16)
+    for i in range(features // 128):
+        span = slice(i * 128, (i + 1) * 128)
+        total = base_ref[:, span].astype(F32)
+        total = total + right_ref[:tokens, span].astype(F32) + left_ref[:tokens, span].astype(F32)
+        out_ref[:, span] = (total * factor).astype(BF16)
 
 
 def call(kernel, ins, outs, args, scratch=(), flops=0, moved=0, limit=24):
@@ -350,11 +328,10 @@
                 pairs.append((seq * N_PART + head, (seq ^ swap) * N_PART + there))
         return lax.ppermute(array, ("seq", "head"), pairs)
 
-    half_slab = ((tokens // 2 + PAD, features), BF16)
-    gated, far_first, far_second, w_next = call(
+    gated, far, w_next = call(
         gate_kernel,
         [SMEM] * 2 + [VMEM] * 5 + [HBM],
-        [slab, half_slab, half_slab, ((channels, features), BF16)],
+        [slab, slab, ((channels, features), BF16)],
         (me, way, entries, *needed, out_weight),
         scratch=[jax.ShapeDtypeStruct((channels, features), BF16)],
         flops=2 * tokens * channels * features,
@@ -362,7 +339,7 @@
         limit=50,
     )
     other = send(gated, 0, 1)
-    own_got = [send(far_first, 1, 0), send(far_second, 1, 0)]
+    own_got = send(far, 1, 0)
     begin, other_sent = call(
         begin_kernel,
         [VMEM] * 3,
@@ -372,6 +349,7 @@
         moved=2**20,
     )
     other_got = send(other_sent, 1, 0)
+
     steps = N_PART // 2 - 2
     chunks, base = call(
         chunks_kernel,
@@ -384,25 +362,18 @@
         limit=50,
     )
 
-    def join(chunk, place, mine, got, halves):
-        def kernel(*refs):
-            outs = refs[2 + len(got) :]
-            join_kernel(place, *refs[: 2 + len(got)], *(outs if halves else (*outs, None)))
-
-        return call(
-            kernel, [VMEM] * (2 + len(got)), [half_slab] * 2 if halves else [slab], (chunk, mine, *got), moved=2**19
-        )
-
-    own_got = [send(*join(begin, None, gated, own_got, False), 1, 0)]
+    def join(place, chunk, mine, got):
+        return call(functools.partial(join_kernel, place), [VMEM] * 3, [slab], (chunk, mine, got), moved=2**19)[0]
+
+    own_got = send(join(None, begin, gated, own_got), 1, 0)
     for away in range(steps, 0, -1):
-        last = away == 1
-        other_got = send(*join(chunks, (away - 1, 1), other, [other_got], False), 1, int(last))
-        own_got = [send(part, 1, 0) for part in join(chunks, (away - 1, 0), gated, own_got, last)]
+        other_got = send(join((away - 1, 1), chunks, other, other_got), 1, int(away == 1))
+        own_got = send(join((away - 1, 0), chunks, gated, own_got), 1, 0)
     (out,) = call(
         functools.partial(end_kernel, channels * N_PART),
-        [VMEM] * 5,
+        [VMEM] * 4,
         [((tokens, features), BF16)],
-        (base, gated, *own_got, other_got),
+        (base, gated, own_got, other_got),
         moved=2**20,
     )
     return out

time: 91.9 us -> 92.8 us (level)
  waiting for transfers between devices: 16.6 us -> 19.6 us
  starting transfers between devices: 45.7 us -> 43.6 us
    ppermute x10 -> x8, waiting for transfers between devices: 8.79 us -> 11.8 us  [send(): return lax.ppermute(array, ('seq', 'head'), pairs)]
    ppermute x10 -> x8, starting transfers between devices: 32 us -> 29.9 us  [send(): return lax.ppermute(array, ('seq', 'head'), pairs)]
  transfers between devices with their start and end apart: 12 -> 10, of which waited for: 8 -> 6; matrix products, arithmetic and copies ran while one was open for 0% -> 0% of each run, Pallas kernels for 8% -> 8%
where the time goes in v9:
time: 92.8 us; the launch traced here: 92 us
  starting transfers between devices  43.6 us (47%)
  waiting for transfers between devices  19.6 us (21%)
  Pallas kernels  14.2 us (15%)
  blocking collectives  10.8 us (12%)
  local copies, waits for them, and re-layouts  3.6 us (4%)
    ppermute x8, starting transfers between devices, send(): return lax.ppermute(array, ('seq', 'head'), pairs)  29.9 us
    pallas_call x14, Pallas kernels, call(): pl.pallas_call(kernel, in_specs=ins, out_specs=[VMEM] * len(outs), out_sh...  14.2 us
    ppermute x8, waiting for transfers between devices, send(): return lax.ppermute(array, ('seq', 'head'), pairs)  11.8 us
    all_to_all x1, blocking collectives, body(): got = lax.all_to_all(pieces, 'seq', 0, 0, axis_index_groups=in_plane)  10.8 us
    all_to_all x1, starting transfers between devices, body(): got_planes = lax.all_to_all(totals, 'seq', 0, 0, axis_index_groups=across)  10.3 us
    all_to_all x1, waiting for transfers between devices, body(): got_planes = lax.all_to_all(totals, 'seq', 0, 0, axis_index_groups=across)  5.57 us
    unnamed x8, local copies, waits for them, and re-layouts  3.6 us
    all_to_all x1, starting transfers between devices, body(): entries = lax.all_to_all(entries, 'seq', 0, 0, axis_index_groups=in_plane)  3.37 us
  transfers between devices with their start and end apart: 10, of which 6 were waited for; matrix products, arithmetic and copies ran while one was open for 0% of the time, Pallas kernels for 8%

profile of v9, /device:TPU:24, one launch (start us, length us, event | category | flops | bytes accessed | tf_op | source)
XLA Modules:
  0.0 92.0 jit_solution(12582934897370588210)
XLA Ops:
  0.0 2.9 %shard_map.109 = (bf16[8,80,128]{2,1,0:T(8,128)(2,1)}, f32[40,256]{1,0:T(8,128)}, f32[256,128]{1,0:T(8,128)}) custom-call(f32[1,8]{1,0:T(1,128)} %bitcast.13, f32[1,8]{1,0:T(1,128)} %bitcast.14, f32[8,256]{1,0:T(8,128)} %bitcast.10, s32[1,256]{1,0:T(1,128)} %bitcast.11, bf16[256,128]{1,0:T(8,128)(2,1)} %refs_2_.1, bf16[256,512]{1,0:T(8,128)(2,1)} %refs_6_.1), custom_call_target="tpu_custom_call" | custom-call | flops 33554432 | bytes 262144 | tf_op jit(solution)/shard_map/pallas_call | solution.py:245
  2.9 10.8 %all_to_all.15.got_ref = bf16[8,80,128]{2,1,0:T(8,128)(2,1)S(1)} all-to-all(bf16[8,80,128]{2,1,0:T(8,128)(2,1)} %get-tuple-element.23), channel_id=1, replica_groups={{0,8,16,24,32,40,48,56},{64,72,80,88,96,104,112,120},{128,136,144,152,1..., dimensions={0} | all-to-all | bytes 327680 | tf_op jit(solution)/shard_map/all_to_all | solution.py:287
  13.7 0.7 shard_map.110.refs_0_
  14.4 10.3 %all-to-all-start.1 = ((bf16[8,80,128]{2,1,0:T(8,128)(2,1)}), bf16[8,80,128]{2,1,0:T(8,128)(2,1)S(1)}, u32[]{:S(2)}, u32[]{:S(2)}) async-start(bf16[8,80,128]{2,1,0:T(8,128)(2,1)} %shard_map.110.refs_0_), calls=%async_computation.1 | async-start | bytes 327680 | tf_op jit(solution)/shard_map/all_to_all | solution.py:302
  24.7 4.0 %shard_map.111 = (f32[256,512]{1,0:T(8,128)}, f32[256,512]{1,0:T(8,128)}) custom-call(bf16[8,80,128]{2,1,0:T(8,128)(2,1)} %shard_map.110.refs_0_, bf16[256,128]{1,0:T(8,128)(2,1)} %refs_1_.3, bf16[256,128]{1,0:T(8,128)(2,1)} %refs_2_.1, f32[40,256]{1,0:T(8,128)} %get-tuple-element.24.refs_3_, f32[256,128]{1,0:T(8,128)} %get-tuple-element.25.refs_4_, ...), custom_call_target="tpu_custom_call" | custom-call | flops 67108864 | bytes 8388608 | tf_op jit(solution)/shard_map/pallas_call | solution.py:245
  28.7 5.6 %all-to-all-done.1.planes_ref = bf16[8,80,128]{2,1,0:T(8,128)(2,1)S(1)} async-done(((bf16[8,80,128]{2,1,0:T(8,128)(2,1)}), bf16[8,80,128]{2,1,0:T(8,128)(2,1)S(1)}, u32[]{:S(2)}, u32[]{:S(2)}) %all-to-all-start.1) | async-done | bytes 163872 | tf_op jit(solution)/shard_map/all_to_all | solution.py:302
  34.2 0.7 shard_map.112.refs_0_
  35.0 3.4 %all-to-all-start.2 = ((bf16[8,64,128]{2,1,0:T(8,128)(2,1)}), bf16[8,64,128]{2,1,0:T(8,128)(2,1)S(1)}, u32[]{:S(2)}, u32[]{:S(2)}) async-start(bf16[8,64,128]{2,1,0:T(8,128)(2,1)} %shard_map.112.refs_0_), calls=%async_computation.2 | async-start | bytes 262144 | tf_op jit(solution)/shard_map/all_to_all | solution.py:317
  38.4 0.0 copy-start
  38.4 1.0 %copy-done = f32[256,512]{1,0:T(8,128)S(1)} copy-done((f32[256,512]{1,0:T(8,128)S(1)}, f32[256,512]{1,0:T(8,128)}, u32[]{:S(2)}) %copy-start) | copy-done | bytes 524312
  39.4 0.0 copy-start.1
  39.4 1.0 %copy-done.1 = f32[256,512]{1,0:T(8,128)S(1)} copy-done((f32[256,512]{1,0:T(8,128)S(1)}, f32[256,512]{1,0:T(8,128)}, u32[]{:S(2)}) %copy-start.1) | copy-done | bytes 524312
  40.5 0.0 copy-start.2
  40.5 0.8 copy-done.2
  41.3 0.0 copy-start.3
  41.3 0.7 copy-done.3
  42.0 0.2 shard_map.113
  42.2 2.2 %all-to-all-done.2.entry_ref = bf16[8,64,128]{2,1,0:T(8,128)(2,1)S(1)} async-done(((bf16[8,64,128]{2,1,0:T(8,128)(2,1)}), bf16[8,64,128]{2,1,0:T(8,128)(2,1)S(1)}, u32[]{:S(2)}, u32[]{:S(2)}) %all-to-all-start.2) | async-done | bytes 131104 | tf_op jit(solution)/shard_map/all_to_all | solution.py:317
  44.4 1.7 %shard_map.114 = (bf16[272,512]{1,0:T(8,128)(2,1)S(1)}, bf16[272,512]{1,0:T(8,128)(2,1)S(1)}, bf16[512,512]{1,0:T(8,128)(2,1)S(1)}) custom-call(s32[1]{0:T(128)} %bitcast.me, s32[1]{0:T(128)} %bitcast.1.way, bf16[8,64,128]{2,1,0:T(8,128)(2,1)S(1)} %all-to-all-done.2.entry_ref, bf16[256,128]{1,0:T(8,128)(2,1)S(1)} %get-tuple-element.30.c_ref, ...), custom_call_target="tpu_custom_call" | custom-call | flops 134217728 | bytes 2097152 | tf_op jit(solution)/shard_map/pallas_call | solution.py:245
  46.1 1.9 %collective-permute-start = (bf16[272,512]{1,0:T(8,128)(2,1)S(1)}, bf16[272,512]{1,0:T(8,128)(2,1)S(1)}, u32[]{:S(2)}, u32[]{:S(2)}) collective-permute-start(bf16[272,512]{1,0:T(8,128)(2,1)S(1)} %get-tuple-element.34.own_ref.gated_ref), channel_id=1, source_target_pairs={{0,8},{1,9},{2,10},{3,11},{4,12},{5,13},{6,14},{7,15},{8,0},{9,1},... | collective-permute-start | bytes 835592 | tf_op jit(solution)/shard_map/ppermute | solution.py:329
  48.0 4.7 %collective-permute-start.1 = (bf16[272,512]{1,0:T(8,128)(2,1)S(1)}, bf16[272,512]{1,0:T(8,128)(2,1)S(1)}, u32[]{:S(2)}, u32[]{:S(2)}) collective-permute-start(bf16[272,512]{1,0:T(8,128)(2,1)S(1)} %get-tuple-element.39), channel_id=1, source_target_pairs={{0,1},{1,2},{2,3},{3,4},{4,5},{5,6},{6,7},{7,0},{8,15},{9,8},{10,9... | collective-permute-start | bytes 835592 | tf_op jit(solution)/shard_map/ppermute | solution.py:329
  52.7 0.0 collective-permute-done.other_ref.gated_ref
  52.7 0.4 shard_map.116
  53.2 3.6 %collective-permute-done.1.got_ref = bf16[272,512]{1,0:T(8,128)(2,1)S(1)} collective-permute-done((bf16[272,512]{1,0:T(8,128)(2,1)S(1)}, bf16[272,512]{1,0:T(8,128)(2,1)S(1)}, u32[]{:S(2)}, u32[]{:S(2)}) %collective-permute-start.1) | collective-permute-done | bytes 278560 | tf_op jit(solution)/shard_map/ppermute | solution.py:329
  56.8 0.1 shard_map.117
  56.9 5.6 %collective-permute-start.2 = (bf16[272,512]{1,0:T(8,128)(2,1)S(1)}, bf16[272,512]{1,0:T(8,128)(2,1)S(1)}, u32[]{:S(2)}, u32[]{:S(2)}) collective-permute-start(bf16[272,512]{1,0:T(8,128)(2,1)S(1)} %shard_map.117), channel_id=1, source_target_pairs={{0,1},{1,2},{2,3},{3,4},{4,5},{5,6},{6,7},{7,0},{8,15},{9,8},{10,9... | collective-permute-start | bytes 835592 | tf_op jit(solution)/shard_map/ppermute | solution.py:329
  62.5 1.9 %collective-permute-start.5 = (bf16[272,512]{1,0:T(8,128)(2,1)S(1)}, bf16[272,512]{1,0:T(8,128)(2,1)S(1)}, u32[]{:S(2)}, u32[]{:S(2)}) collective-permute-start(bf16[272,512]{1,0:T(8,128)(2,1)S(1)} %get-tuple-element.40), channel_id=1, source_target_pairs={{0,1},{1,2},{2,3},{3,4},{4,5},{5,6},{6,7},{7,0},{8,15},{9,8},{10,9... | collective-permute-start | bytes 835592 | tf_op jit(solution)/shard_map/ppermute | solution.py:329
  64.4 2.3 %shard_map.115 = (bf16[2,2,256,512]{3,2,1,0:T(8,128)(2,1)S(1)}, bf16[256,512]{1,0:T(8,128)(2,1)S(1)}) custom-call(s32[1]{0:T(128)} %bitcast.me, s32[1]{0:T(128)} %bitcast.1.way, bf16[272,512]{1,0:T(8,128)(2,1)S(1)} %get-tuple-element.34.own_ref.gated_ref, bf16[272,512]{1,0:T(8,128)(2,1)S(1)} %collective-permute-done.other_ref.gated_ref, bf16[512,4096]{1,0:T(8,128)(2,1)} %w_hbm.3), custom_call_target="tpu_custom_call" | custom-call | flops 671088640 | bytes 2097152 | tf_op jit(solution)/shard_map/pallas_call | solution.py:245
  66.7 0.0 collective-permute-done.2.got_ref
  66.7 0.1 shard_map.118
  66.8 5.4 %collective-permute-start.3 = (bf16[272,512]{1,0:T(8,128)(2,1)S(1)}, bf16[272,512]{1,0:T(8,128)(2,1)S(1)}, u32[]{:S(2)}, u32[]{:S(2)}) collective-permute-start(bf16[272,512]{1,0:T(8,128)(2,1)S(1)} %shard_map.118), channel_id=1, source_target_pairs={{0,1},{1,2},{2,3},{3,4},{4,5},{5,6},{6,7},{7,0},{8,15},{9,8},{10,9... | collective-permute-start | bytes 835592 | tf_op jit(solution)/shard_map/ppermute | solution.py:329
  72.2 0.0 collective-permute-done.5.got_ref
  72.2 0.1 shard_map.120
  72.3 2.9 %collective-permute-start.6 = (bf16[272,512]{1,0:T(8,128)(2,1)S(1)}, bf16[272,512]{1,0:T(8,128)(2,1)S(1)}, u32[]{:S(2)}, u32[]{:S(2)}) collective-permute-start(bf16[272,512]{1,0:T(8,128)(2,1)S(1)} %shard_map.120), channel_id=1, source_target_pairs={{0,1},{1,2},{2,3},{3,4},{4,5},{5,6},{6,7},{7,0},{8,15},{9,8},{10,9... | collective-permute-start | bytes 835592 | tf_op jit(solution)/shard_map/ppermute | solution.py:329
  75.2 1.1 %collective-permute-done.3.got_ref = bf16[272,512]{1,0:T(8,128)(2,1)S(1)} collective-permute-done((bf16[272,512]{1,0:T(8,128)(2,1)S(1)}, bf16[272,512]{1,0:T(8,128)(2,1)S(1)}, u32[]{:S(2)}, u32[]{:S(2)}) %collective-permute-start.3) | collective-permute-done | bytes 278560 | tf_op jit(solution)/shard_map/ppermute | solution.py:329
  76.3 0.1 shard_map.119
  76.3 5.6 %collective-permute-start.4 = (bf16[272,512]{1,0:T(8,128)(2,1)S(1)}, bf16[272,512]{1,0:T(8,128)(2,1)S(1)}, u32[]{:S(2)}, u32[]{:S(2)}) collective-permute-start(bf16[272,512]{1,0:T(8,128)(2,1)S(1)} %shard_map.119), channel_id=1, source_target_pairs={{0,1},{1,2},{2,3},{3,4},{4,5},{5,6},{6,7},{7,0},{8,15},{9,8},{10,9... | collective-permute-start | bytes 835592 | tf_op jit(solution)/shard_map/ppermute | solution.py:329
  82.0 0.0 collective-permute-done.6.got_ref
  82.0 0.1 shard_map.121
  82.1 1.9 %collective-permute-start.7 = (bf16[272,512]{1,0:T(8,128)(2,1)S(1)}, bf16[272,512]{1,0:T(8,128)(2,1)S(1)}, u32[]{:S(2)}, u32[]{:S(2)}) collective-permute-start(bf16[272,512]{1,0:T(8,128)(2,1)S(1)} %shard_map.121), channel_id=1, source_target_pairs={{0,9},{1,10},{2,11},{3,12},{4,13},{5,14},{6,15},{7,8},{8,7},{9,0},... | collective-permute-start | bytes 835592 | tf_op jit(solution)/shard_map/ppermute | solution.py:329
  84.0 2.0 %collective-permute-done.4.right_ref = bf16[272,512]{1,0:T(8,128)(2,1)S(1)} collective-permute-done((bf16[272,512]{1,0:T(8,128)(2,1)S(1)}, bf16[272,512]{1,0:T(8,128)(2,1)S(1)}, u32[]{:S(2)}, u32[]{:S(2)}) %collective-permute-start.4) | collective-permute-done | bytes 278560 | tf_op jit(solution)/shard_map/ppermute | solution.py:329
  86.0 5.1 %collective-permute-done.7.left_ref = bf16[272,512]{1,0:T(8,128)(2,1)S(1)} collective-permute-done((bf16[272,512]{1,0:T(8,128)(2,1)S(1)}, bf16[272,512]{1,0:T(8,128)(2,1)S(1)}, u32[]{:S(2)}, u32[]{:S(2)}) %collective-permute-start.7) | collective-permute-done | bytes 278560 | tf_op jit(solution)/shard_map/ppermute | solution.py:329
  91.1 0.9 shard_map.122
Async XLA Ops:
  14.4 19.9 %all-to-all-start.1 = ((bf16[8,80,128]{2,1,0:T(8,128)(2,1)}), bf16[8,80,128]{2,1,0:T(8,128)(2,1)S(1)}, u32[]{:S(2)}, u32[]{:S(2)}) async-start(bf16[8,80,128]{2,1,0:T(8,128)(2,1)} %shard_map.110.refs_0_), calls=%async_computation.1 | async-start | bytes 327680 | tf_op jit(solution)/shard_map/all_to_all | solution.py:302
  35.0 9.4 %all-to-all-start.2 = ((bf16[8,64,128]{2,1,0:T(8,128)(2,1)}), bf16[8,64,128]{2,1,0:T(8,128)(2,1)S(1)}, u32[]{:S(2)}, u32[]{:S(2)}) async-start(bf16[8,64,128]{2,1,0:T(8,128)(2,1)} %shard_map.112.refs_0_), calls=%async_computation.2 | async-start | bytes 262144 | tf_op jit(solution)/shard_map/all_to_all | solution.py:317
  38.4 1.0 %copy-start = (f32[256,512]{1,0:T(8,128)S(1)}, f32[256,512]{1,0:T(8,128)}, u32[]{:S(2)}) copy-start(f32[256,512]{1,0:T(8,128)} %get-tuple-element.28.refs_2_) | copy-start | bytes 1572868
  39.4 1.0 %copy-start.1 = (f32[256,512]{1,0:T(8,128)S(1)}, f32[256,512]{1,0:T(8,128)}, u32[]{:S(2)}) copy-start(f32[256,512]{1,0:T(8,128)} %get-tuple-element.29.refs_3_) | copy-start | bytes 1572868
  40.5 0.8 copy-start.2
  41.3 0.7 copy-start.3
  46.1 6.6 %collective-permute-start = (bf16[272,512]{1,0:T(8,128)(2,1)S(1)}, bf16[272,512]{1,0:T(8,128)(2,1)S(1)}, u32[]{:S(2)}, u32[]{:S(2)}) collective-permute-start(bf16[272,512]{1,0:T(8,128)(2,1)S(1)} %get-tuple-element.34.own_ref.gated_ref), channel_id=1, source_target_pairs={{0,8},{1,9},{2,10},{3,11},{4,12},{5,13},{6,14},{7,15},{8,0},{9,1},... | collective-permute-start | bytes 835592 | tf_op jit(solution)/shard_map/ppermute | solution.py:329
  48.0 8.7 %collective-permute-start.1 = (bf16[272,512]{1,0:T(8,128)(2,1)S(1)}, bf16[272,512]{1,0:T(8,128)(2,1)S(1)}, u32[]{:S(2)}, u32[]{:S(2)}) collective-permute-start(bf16[272,512]{1,0:T(8,128)(2,1)S(1)} %get-tuple-element.39), channel_id=1, source_target_pairs={{0,1},{1,2},{2,3},{3,4},{4,5},{5,6},{6,7},{7,0},{8,15},{9,8},{10,9... | collective-permute-start | bytes 835592 | tf_op jit(solution)/shard_map/ppermute | solution.py:329
  56.9 9.9 %collective-permute-start.2 = (bf16[272,512]{1,0:T(8,128)(2,1)S(1)}, bf16[272,512]{1,0:T(8,128)(2,1)S(1)}, u32[]{:S(2)}, u32[]{:S(2)}) collective-permute-start(bf16[272,512]{1,0:T(8,128)(2,1)S(1)} %shard_map.117), channel_id=1, source_target_pairs={{0,1},{1,2},{2,3},{3,4},{4,5},{5,6},{6,7},{7,0},{8,15},{9,8},{10,9... | collective-permute-start | bytes 835592 | tf_op jit(solution)/shard_map/ppermute | solution.py:329
  62.5 9.7 %collective-permute-start.5 = (bf16[272,512]{1,0:T(8,128)(2,1)S(1)}, bf16[272,512]{1,0:T(8,128)(2,1)S(1)}, u32[]{:S(2)}, u32[]{:S(2)}) collective-permute-start(bf16[272,512]{1,0:T(8,128)(2,1)S(1)} %get-tuple-element.40), channel_id=1, source_target_pairs={{0,1},{1,2},{2,3},{3,4},{4,5},{5,6},{6,7},{7,0},{8,15},{9,8},{10,9... | collective-permute-start | bytes 835592 | tf_op jit(solution)/shard_map/ppermute | solution.py:329
  66.8 9.4 %collective-permute-start.3 = (bf16[272,512]{1,0:T(8,128)(2,1)S(1)}, bf16[272,512]{1,0:T(8,128)(2,1)S(1)}, u32[]{:S(2)}, u32[]{:S(2)}) collective-permute-start(bf16[272,512]{1,0:T(8,128)(2,1)S(1)} %shard_map.118), channel_id=1, source_target_pairs={{0,1},{1,2},{2,3},{3,4},{4,5},{5,6},{6,7},{7,0},{8,15},{9,8},{10,9... | collective-permute-start | bytes 835592 | tf_op jit(solution)/shard_map/ppermute | solution.py:329
  72.3 9.6 %collective-permute-start.6 = (bf16[272,512]{1,0:T(8,128)(2,1)S(1)}, bf16[272,512]{1,0:T(8,128)(2,1)S(1)}, u32[]{:S(2)}, u32[]{:S(2)}) collective-permute-start(bf16[272,512]{1,0:T(8,128)(2,1)S(1)} %shard_map.120), channel_id=1, source_target_pairs={{0,1},{1,2},{2,3},{3,4},{4,5},{5,6},{6,7},{7,0},{8,15},{9,8},{10,9... | collective-permute-start | bytes 835592 | tf_op jit(solution)/shard_map/ppermute | solution.py:329
  76.3 9.7 %collective-permute-start.4 = (bf16[272,512]{1,0:T(8,128)(2,1)S(1)}, bf16[272,512]{1,0:T(8,128)(2,1)S(1)}, u32[]{:S(2)}, u32[]{:S(2)}) collective-permute-start(bf16[272,512]{1,0:T(8,128)(2,1)S(1)} %shard_map.119), channel_id=1, source_target_pairs={{0,1},{1,2},{2,3},{3,4},{4,5},{5,6},{6,7},{7,0},{8,15},{9,8},{10,9... | collective-permute-start | bytes 835592 | tf_op jit(solution)/shard_map/ppermute | solution.py:329
  82.1 9.1 %collective-permute-start.7 = (bf16[272,512]{1,0:T(8,128)(2,1)S(1)}, bf16[272,512]{1,0:T(8,128)(2,1)S(1)}, u32[]{:S(2)}, u32[]{:S(2)}) collective-permute-start(bf16[272,512]{1,0:T(8,128)(2,1)S(1)} %shard_map.121), channel_id=1, source_target_pairs={{0,9},{1,10},{2,11},{3,12},{4,13},{5,14},{6,15},{7,8},{8,7},{9,0},... | collective-permute-start | bytes 835592 | tf_op jit(solution)/shard_map/ppermute | solution.py:329

commit v10 on v9

--- a/solution.py
+++ b/solution.py
@@ -202,11 +202,10 @@
     copies[1].wait()
 
 
-def begin_kernel(own_ref, other_ref, w_ref, chunk_ref, out_ref):
-    tokens = chunk_ref.shape[0]
-    out_ref[:tokens] = jnp.dot(other_ref[:tokens], w_ref[...], preferred_element_type=F32).astype(BF16)
-    out_ref[tokens:] = other_ref[tokens:]
-    chunk_ref[...] = jnp.dot(own_ref[:tokens], w_ref[...], preferred_element_type=F32).astype(BF16)
+def begin_kernel(own_ref, other_ref, w_ref, out_ref):
+    tokens = out_ref.shape[1]
+    for j, ref in enumerate((own_ref, other_ref)):
+        out_ref[j] = jnp.dot(ref[:tokens], w_ref[...], preferred_element_type=F32).astype(BF16)
 
 
 def chunks_kernel(me, way, own_ref, other_ref, w_hbm, out_ref, base_ref, w_ref, sems):
@@ -222,22 +221,32 @@
                 out_ref[a - 1, j] = jnp.dot(ref[:tokens], w_ref[a], preferred_element_type=F32).astype(BF16)
 
 
-def join_kernel(place, chunk_ref, gated_ref, got_ref, out_ref):
+def join_kernel(place, chunk_ref, gated_ref, *refs):
+    got_refs, out_ref = refs[:-1], refs[-1]
     tokens = gated_ref.shape[0] - PAD
-    chunk = (chunk_ref if place is None else chunk_ref.at[place])[...]
-    out_ref[:tokens] = (chunk.astype(F32) + got_ref[:tokens].astype(F32)).astype(BF16)
-    put_squares(out_ref, get_squares(gated_ref) + get_squares(got_ref))
-
-
-def end_kernel(inner, base_ref, own_ref, right_ref, left_ref, out_ref):
+    squares = get_squares(gated_ref)
+    total = chunk_ref[place].astype(F32)
+    for ref in got_refs:
+        squares = squares + get_squares(ref)
+        total = total + ref[:tokens].astype(F32)
+    out_ref[:tokens] = total.astype(BF16)
+    put_squares(out_ref, squares)
+
+
+def sum_kernel(base_ref, own_ref, got_ref, total_ref, square_ref):
+    tokens = base_ref.shape[0]
+    square_ref[...] = get_squares(own_ref) + get_squares(got_ref)
+    total_ref[...] = base_ref[...].astype(F32) + got_ref[:tokens].astype(F32)
+
+
+def end_kernel(inner, total_ref, square_ref, got_ref, out_ref):
     tokens, features = out_ref.shape
-    squares = get_squares(own_ref) + get_squares(right_ref) + get_squares(left_ref)
+    squares = square_ref[...] + get_squares(got_ref)
     factor = lax.rsqrt(squares * (1.0 / inner) + 1e-05)
     factor = jnp.broadcast_to(factor, (128, tokens)).T
     for i in range(features // 128):
         span = slice(i * 128, (i + 1) * 128)
-        total = base_ref[:, span].astype(F32)
-        total = total + right_ref[:tokens, span].astype(F32) + left_ref[:tokens, span].astype(F32)
+        total = total_ref[:, span] + got_ref[:tokens, span].astype(F32)
         out_ref[:, span] = (total * factor).astype(BF16)
 
 
@@ -340,40 +349,46 @@
     )
     other = send(gated, 0, 1)
     own_got = send(far, 1, 0)
-    begin, other_sent = call(
+    (begin,) = call(
         begin_kernel,
         [VMEM] * 3,
-        [((tokens, features), BF16), slab],
+        [((2, tokens, features), BF16)],
         (gated, other, w_next),
         flops=4 * tokens * channels * features,
-        moved=2**20,
-    )
+        moved=2**22,
+    )
+
+    def join(place, chunk, mine, *got):
+        kernel = functools.partial(join_kernel, place)
+        return call(kernel, [VMEM] * (2 + len(got)), [slab], (chunk, mine, *got), moved=2**19)[0]
+
+    other_sent = join(1, begin, other)
     other_got = send(other_sent, 1, 0)
-
+    own_sent = join(0, begin, gated, own_got)
+    own_got = send(own_sent, 1, 0)
     steps = N_PART // 2 - 2
+    gated_then, _ = lax.optimization_barrier((gated, own_sent))
     chunks, base = call(
         chunks_kernel,
         [SMEM, SMEM, VMEM, VMEM, HBM],
         [((steps, 2, tokens, features), BF16), ((tokens, features), BF16)],
-        (me, way, gated, other, out_weight),
+        (me, way, gated_then, other, out_weight),
         scratch=[jax.ShapeDtypeStruct((steps + 1, channels, features), BF16)],
         flops=10 * tokens * channels * features,
         moved=2**21,
         limit=50,
     )
-
-    def join(place, chunk, mine, got):
-        return call(functools.partial(join_kernel, place), [VMEM] * 3, [slab], (chunk, mine, got), moved=2**19)[0]
-
-    own_got = send(join(None, begin, gated, own_got), 1, 0)
     for away in range(steps, 0, -1):
         other_got = send(join((away - 1, 1), chunks, other, other_got), 1, int(away == 1))
         own_got = send(join((away - 1, 0), chunks, gated, own_got), 1, 0)
+    total, squares = call(
+        sum_kernel, [VMEM] * 3, [((tokens, features), F32), ((1, tokens), F32)], (base, gated, other_got), moved=2**20
+    )
     (out,) = call(
         functools.partial(end_kernel, channels * N_PART),
-        [VMEM] * 4,
+        [VMEM] * 3,
         [((tokens, features), BF16)],
-        (base, gated, own_got, other_got),
+        (total, squares, own_got),
         moved=2**20,
     )
     return out

time: 92.8 us -> 88.6 us (0.955)
  the two profiles are of different devices: /device:TPU:24 before, /device:TPU:32 now
where the time goes in v10:
time: 88.6 us; the launch traced here: 87.7 us
  starting transfers between devices  30.5 us (34%)
  waiting for transfers between devices  28.4 us (32%)
  Pallas kernels  14.3 us (16%)
  blocking collectives  10.8 us (12%)
  local copies, waits for them, and re-layouts  3.6 us (4%)
    ppermute x8, waiting for transfers between devices, send(): return lax.ppermute(array, ('seq', 'head'), pairs)  20.6 us
    ppermute x8, starting transfers between devices, send(): return lax.ppermute(array, ('seq', 'head'), pairs)  16.8 us
    pallas_call x16, Pallas kernels, call(): pl.pallas_call(kernel, in_specs=ins, out_specs=[VMEM] * len(outs), out_sh...  14.3 us
    all_to_all x1, blocking collectives, body(): got = lax.all_to_all(pieces, 'seq', 0, 0, axis_index_groups=in_plane)  10.8 us
    all_to_all x1, starting transfers between devices, body(): got_planes = lax.all_to_all(totals, 'seq', 0, 0, axis_index_groups=across)  10.3 us
    all_to_all x1, waiting for transfers between devices, body(): got_planes = lax.all_to_all(totals, 'seq', 0, 0, axis_index_groups=across)  5.57 us
    unnamed x8, local copies, waits for them, and re-layouts  3.6 us
    all_to_all x1, starting transfers between devices, body(): entries = lax.all_to_all(entries, 'seq', 0, 0, axis_index_groups=in_plane)  3.37 us
  transfers between devices with their start and end apart: 10, of which 8 were waited for; matrix products, arithmetic and copies ran while one was open for 0% of the time, Pallas kernels for 8%

profile of v10, /device:TPU:32, one launch (start us, length us, event | category | flops | bytes accessed | tf_op | source)
XLA Modules:
  0.0 87.7 jit_solution(15640853386962598038)
XLA Ops:
  0.0 2.9 %shard_map.109 = (bf16[8,80,128]{2,1,0:T(8,128)(2,1)}, f32[40,256]{1,0:T(8,128)}, f32[256,128]{1,0:T(8,128)}) custom-call(f32[1,8]{1,0:T(1,128)} %bitcast.13, f32[1,8]{1,0:T(1,128)} %bitcast.14, f32[8,256]{1,0:T(8,128)} %bitcast.10, s32[1,256]{1,0:T(1,128)} %bitcast.11, bf16[256,128]{1,0:T(8,128)(2,1)} %refs_2_.1, bf16[256,512]{1,0:T(8,128)(2,1)} %refs_6_.1), custom_call_target="tpu_custom_call" | custom-call | flops 33554432 | bytes 262144 | tf_op jit(solution)/shard_map/pallas_call | solution.py:254
  2.9 10.8 %all_to_all.15.got_ref = bf16[8,80,128]{2,1,0:T(8,128)(2,1)S(1)} all-to-all(bf16[8,80,128]{2,1,0:T(8,128)(2,1)} %get-tuple-element.24), channel_id=1, replica_groups={{0,8,16,24,32,40,48,56},{64,72,80,88,96,104,112,120},{128,136,144,152,1..., dimensions={0} | all-to-all | bytes 327680 | tf_op jit(solution)/shard_map/all_to_all | solution.py:296
  13.7 0.7 shard_map.110.refs_0_
  14.4 10.3 %all-to-all-start.1 = ((bf16[8,80,128]{2,1,0:T(8,128)(2,1)}), bf16[8,80,128]{2,1,0:T(8,128)(2,1)S(1)}, u32[]{:S(2)}, u32[]{:S(2)}) async-start(bf16[8,80,128]{2,1,0:T(8,128)(2,1)} %shard_map.110.refs_0_), calls=%async_computation.1 | async-start | bytes 327680 | tf_op jit(solution)/shard_map/all_to_all | solution.py:311
  24.7 4.0 %shard_map.111 = (f32[256,512]{1,0:T(8,128)}, f32[256,512]{1,0:T(8,128)}) custom-call(bf16[8,80,128]{2,1,0:T(8,128)(2,1)} %shard_map.110.refs_0_, bf16[256,128]{1,0:T(8,128)(2,1)} %refs_1_.3, bf16[256,128]{1,0:T(8,128)(2,1)} %refs_2_.1, f32[40,256]{1,0:T(8,128)} %get-tuple-element.25.refs_3_, f32[256,128]{1,0:T(8,128)} %get-tuple-element.26.refs_4_, ...), custom_call_target="tpu_custom_call" | custom-call | flops 67108864 | bytes 8388608 | tf_op jit(solution)/shard_map/pallas_call | solution.py:254
  28.7 5.6 %all-to-all-done.1.planes_ref = bf16[8,80,128]{2,1,0:T(8,128)(2,1)S(1)} async-done(((bf16[8,80,128]{2,1,0:T(8,128)(2,1)}), bf16[8,80,128]{2,1,0:T(8,128)(2,1)S(1)}, u32[]{:S(2)}, u32[]{:S(2)}) %all-to-all-start.1) | async-done | bytes 163872 | tf_op jit(solution)/shard_map/all_to_all | solution.py:311
  34.2 0.7 shard_map.112.refs_0_
  35.0 3.4 %all-to-all-start.2 = ((bf16[8,64,128]{2,1,0:T(8,128)(2,1)}), bf16[8,64,128]{2,1,0:T(8,128)(2,1)S(1)}, u32[]{:S(2)}, u32[]{:S(2)}) async-start(bf16[8,64,128]{2,1,0:T(8,128)(2,1)} %shard_map.112.refs_0_), calls=%async_computation.2 | async-start | bytes 262144 | tf_op jit(solution)/shard_map/all_to_all | solution.py:326
  38.4 0.0 copy-start
  38.4 1.0 %copy-done = f32[256,512]{1,0:T(8,128)S(1)} copy-done((f32[256,512]{1,0:T(8,128)S(1)}, f32[256,512]{1,0:T(8,128)}, u32[]{:S(2)}) %copy-start) | copy-done | bytes 524312
  39.4 0.0 copy-start.1
  39.4 1.0 %copy-done.1 = f32[256,512]{1,0:T(8,128)S(1)} copy-done((f32[256,512]{1,0:T(8,128)S(1)}, f32[256,512]{1,0:T(8,128)}, u32[]{:S(2)}) %copy-start.1) | copy-done | bytes 524312
  40.5 0.0 copy-start.2
  40.5 0.8 copy-done.2
  41.3 0.0 copy-start.3
  41.3 0.7 copy-done.3
  42.0 0.2 shard_map.113
  42.2 2.2 %all-to-all-done.2.entry_ref = bf16[8,64,128]{2,1,0:T(8,128)(2,1)S(1)} async-done(((bf16[8,64,128]{2,1,0:T(8,128)(2,1)}), bf16[8,64,128]{2,1,0:T(8,128)(2,1)S(1)}, u32[]{:S(2)}, u32[]{:S(2)}) %all-to-all-start.2) | async-done | bytes 131104 | tf_op jit(solution)/shard_map/all_to_all | solution.py:326
  44.4 1.7 %shard_map.114 = (bf16[272,512]{1,0:T(8,128)(2,1)S(1)}, bf16[272,512]{1,0:T(8,128)(2,1)S(1)}, bf16[512,512]{1,0:T(8,128)(2,1)S(1)}) custom-call(s32[1]{0:T(128)} %bitcast.me, s32[1]{0:T(128)} %bitcast.1.way, bf16[8,64,128]{2,1,0:T(8,128)(2,1)S(1)} %all-to-all-done.2.entry_ref, bf16[256,128]{1,0:T(8,128)(2,1)S(1)} %get-tuple-element.31.c_ref, ...), custom_call_target="tpu_custom_call" | custom-call | flops 134217728 | bytes 2097152 | tf_op jit(solution)/shard_map/pallas_call | solution.py:254
  46.1 1.9 %collective-permute-start = (bf16[272,512]{1,0:T(8,128)(2,1)S(1)}, bf16[272,512]{1,0:T(8,128)(2,1)S(1)}, u32[]{:S(2)}, u32[]{:S(2)}) collective-permute-start(bf16[272,512]{1,0:T(8,128)(2,1)S(1)} %get-tuple-element.38.own_ref.gated_ref), channel_id=1, source_target_pairs={{0,8},{1,9},{2,10},{3,11},{4,12},{5,13},{6,14},{7,15},{8,0},{9,1},... | collective-permute-start | bytes 835592 | tf_op jit(solution)/shard_map/ppermute | solution.py:338
  48.0 2.6 %collective-permute-start.1 = (bf16[272,512]{1,0:T(8,128)(2,1)S(1)}, bf16[272,512]{1,0:T(8,128)(2,1)S(1)}, u32[]{:S(2)}, u32[]{:S(2)}) collective-permute-start(bf16[272,512]{1,0:T(8,128)(2,1)S(1)} %get-tuple-element.37), channel_id=1, source_target_pairs={{0,1},{1,2},{2,3},{3,4},{4,5},{5,6},{6,7},{7,0},{8,15},{9,8},{10,9... | collective-permute-start | bytes 835592 | tf_op jit(solution)/shard_map/ppermute | solution.py:338
  50.6 0.0 collective-permute-done.other_ref.gated_ref
  50.6 0.4 shard_map.115.chunk_ref
  51.1 2.6 %collective-permute-start.2 = (bf16[272,512]{1,0:T(8,128)(2,1)S(1)}, bf16[272,512]{1,0:T(8,128)(2,1)S(1)}, u32[]{:S(2)}, u32[]{:S(2)}) collective-permute-start(bf16[272,512]{1,0:T(8,128)(2,1)S(1)} %shard_map.118), channel_id=1, source_target_pairs={{0,1},{1,2},{2,3},{3,4},{4,5},{5,6},{6,7},{7,0},{8,15},{9,8},{10,9... | collective-permute-start | bytes 835592 | tf_op jit(solution)/shard_map/ppermute | solution.py:338
  53.7 4.0 %collective-permute-done.1.refs_0_ = bf16[272,512]{1,0:T(8,128)(2,1)S(1)} collective-permute-done((bf16[272,512]{1,0:T(8,128)(2,1)S(1)}, bf16[272,512]{1,0:T(8,128)(2,1)S(1)}, u32[]{:S(2)}, u32[]{:S(2)}) %collective-permute-start.1) | collective-permute-done | bytes 278560 | tf_op jit(solution)/shard_map/ppermute | solution.py:338
  57.7 0.1 shard_map.116
  57.8 1.9 %collective-permute-start.5 = (bf16[272,512]{1,0:T(8,128)(2,1)S(1)}, bf16[272,512]{1,0:T(8,128)(2,1)S(1)}, u32[]{:S(2)}, u32[]{:S(2)}) collective-permute-start(bf16[272,512]{1,0:T(8,128)(2,1)S(1)} %shard_map.116), channel_id=1, source_target_pairs={{0,1},{1,2},{2,3},{3,4},{4,5},{5,6},{6,7},{7,0},{8,15},{9,8},{10,9... | collective-permute-start | bytes 835592 | tf_op jit(solution)/shard_map/ppermute | solution.py:338
  59.7 2.3 %shard_map.117 = (bf16[2,2,256,512]{3,2,1,0:T(8,128)(2,1)S(1)}, bf16[256,512]{1,0:T(8,128)(2,1)S(1)}) custom-call(s32[1]{0:T(128)} %bitcast.me, s32[1]{0:T(128)} %bitcast.1.way, bf16[272,512]{1,0:T(8,128)(2,1)S(1)} %get-tuple-element.38.own_ref.gated_ref, bf16[272,512]{1,0:T(8,128)(2,1)S(1)} %collective-permute-done.other_ref.gated_ref, bf16[512,4096]{1,0:T(8,128)(2,1)} %w_hbm.3), custom_call_target="tpu_custom_call" | custom-call | flops 671088640 | bytes 2097152 | tf_op jit(solution)/shard_map/pallas_call | solution.py:254
  62.0 0.0 collective-permute-done.2.refs_0_
  62.0 0.1 shard_map.119
  62.1 2.0 %collective-permute-start.3 = (bf16[272,512]{1,0:T(8,128)(2,1)S(1)}, bf16[272,512]{1,0:T(8,128)(2,1)S(1)}, u32[]{:S(2)}, u32[]{:S(2)}) collective-permute-start(bf16[272,512]{1,0:T(8,128)(2,1)S(1)} %shard_map.119), channel_id=1, source_target_pairs={{0,1},{1,2},{2,3},{3,4},{4,5},{5,6},{6,7},{7,0},{8,15},{9,8},{10,9... | collective-permute-start | bytes 835592 | tf_op jit(solution)/shard_map/ppermute | solution.py:338
  64.2 3.3 %collective-permute-done.5.refs_0_ = bf16[272,512]{1,0:T(8,128)(2,1)S(1)} collective-permute-done((bf16[272,512]{1,0:T(8,128)(2,1)S(1)}, bf16[272,512]{1,0:T(8,128)(2,1)S(1)}, u32[]{:S(2)}, u32[]{:S(2)}) %collective-permute-start.5) | collective-permute-done | bytes 278560 | tf_op jit(solution)/shard_map/ppermute | solution.py:338
  67.4 0.1 shard_map.122
  67.5 1.9 %collective-permute-start.6 = (bf16[272,512]{1,0:T(8,128)(2,1)S(1)}, bf16[272,512]{1,0:T(8,128)(2,1)S(1)}, u32[]{:S(2)}, u32[]{:S(2)}) collective-permute-start(bf16[272,512]{1,0:T(8,128)(2,1)S(1)} %shard_map.122), channel_id=1, source_target_pairs={{0,1},{1,2},{2,3},{3,4},{4,5},{5,6},{6,7},{7,0},{8,15},{9,8},{10,9... | collective-permute-start | bytes 835592 | tf_op jit(solution)/shard_map/ppermute | solution.py:338
  69.4 2.3 %collective-permute-done.3.refs_0_ = bf16[272,512]{1,0:T(8,128)(2,1)S(1)} collective-permute-done((bf16[272,512]{1,0:T(8,128)(2,1)S(1)}, bf16[272,512]{1,0:T(8,128)(2,1)S(1)}, u32[]{:S(2)}, u32[]{:S(2)}) %collective-permute-start.3) | collective-permute-done | bytes 278560 | tf_op jit(solution)/shard_map/ppermute | solution.py:338
  71.8 0.1 shard_map.120
  71.9 1.9 %collective-permute-start.4 = (bf16[272,512]{1,0:T(8,128)(2,1)S(1)}, bf16[272,512]{1,0:T(8,128)(2,1)S(1)}, u32[]{:S(2)}, u32[]{:S(2)}) collective-permute-start(bf16[272,512]{1,0:T(8,128)(2,1)S(1)} %shard_map.120), channel_id=1, source_target_pairs={{0,9},{1,10},{2,11},{3,12},{4,13},{5,14},{6,15},{7,8},{8,7},{9,0},... | collective-permute-start | bytes 835592 | tf_op jit(solution)/shard_map/ppermute | solution.py:338
  73.8 3.4 %collective-permute-done.6.refs_0_ = bf16[272,512]{1,0:T(8,128)(2,1)S(1)} collective-permute-done((bf16[272,512]{1,0:T(8,128)(2,1)S(1)}, bf16[272,512]{1,0:T(8,128)(2,1)S(1)}, u32[]{:S(2)}, u32[]{:S(2)}) %collective-permute-start.6) | collective-permute-done | bytes 278560 | tf_op jit(solution)/shard_map/ppermute | solution.py:338
  77.2 0.1 shard_map.123
  77.3 1.9 %collective-permute-start.7 = (bf16[272,512]{1,0:T(8,128)(2,1)S(1)}, bf16[272,512]{1,0:T(8,128)(2,1)S(1)}, u32[]{:S(2)}, u32[]{:S(2)}) collective-permute-start(bf16[272,512]{1,0:T(8,128)(2,1)S(1)} %shard_map.123), channel_id=1, source_target_pairs={{0,1},{1,2},{2,3},{3,4},{4,5},{5,6},{6,7},{7,0},{8,15},{9,8},{10,9... | collective-permute-start | bytes 835592 | tf_op jit(solution)/shard_map/ppermute | solution.py:338
  79.2 0.5 collective-permute-done.4.got_ref
  79.7 0.1 shard_map.121
  79.8 7.1 %collective-permute-done.7.got_ref = bf16[272,512]{1,0:T(8,128)(2,1)S(1)} collective-permute-done((bf16[272,512]{1,0:T(8,128)(2,1)S(1)}, bf16[272,512]{1,0:T(8,128)(2,1)S(1)}, u32[]{:S(2)}, u32[]{:S(2)}) %collective-permute-start.7) | collective-permute-done | bytes 278560 | tf_op jit(solution)/shard_map/ppermute | solution.py:338
  86.9 0.8 shard_map.124
  (1 shorter events, 0.0 us)
Async XLA Ops:
  14.4 19.9 %all-to-all-start.1 = ((bf16[8,80,128]{2,1,0:T(8,128)(2,1)}), bf16[8,80,128]{2,1,0:T(8,128)(2,1)S(1)}, u32[]{:S(2)}, u32[]{:S(2)}) async-start(bf16[8,80,128]{2,1,0:T(8,128)(2,1)} %shard_map.110.refs_0_), calls=%async_computation.1 | async-start | bytes 327680 | tf_op jit(solution)/shard_map/all_to_all | solution.py:311
  35.0 9.4 %all-to-all-start.2 = ((bf16[8,64,128]{2,1,0:T(8,128)(2,1)}), bf16[8,64,128]{2,1,0:T(8,128)(2,1)S(1)}, u32[]{:S(2)}, u32[]{:S(2)}) async-start(bf16[8,64,128]{2,1,0:T(8,128)(2,1)} %shard_map.112.refs_0_), calls=%async_computation.2 | async-start | bytes 262144 | tf_op jit(solution)/shard_map/all_to_all | solution.py:326
  38.4 1.0 %copy-start = (f32[256,512]{1,0:T(8,128)S(1)}, f32[256,512]{1,0:T(8,128)}, u32[]{:S(2)}) copy-start(f32[256,512]{1,0:T(8,128)} %get-tuple-element.29.refs_2_) | copy-start | bytes 1572868
  39.4 1.0 %copy-start.1 = (f32[256,512]{1,0:T(8,128)S(1)}, f32[256,512]{1,0:T(8,128)}, u32[]{:S(2)}) copy-start(f32[256,512]{1,0:T(8,128)} %get-tuple-element.30.refs_3_) | copy-start | bytes 1572868
  40.5 0.8 copy-start.2
  41.3 0.7 copy-start.3
  46.1 4.5 %collective-permute-start = (bf16[272,512]{1,0:T(8,128)(2,1)S(1)}, bf16[272,512]{1,0:T(8,128)(2,1)S(1)}, u32[]{:S(2)}, u32[]{:S(2)}) collective-permute-start(bf16[272,512]{1,0:T(8,128)(2,1)S(1)} %get-tuple-element.38.own_ref.gated_ref), channel_id=1, source_target_pairs={{0,8},{1,9},{2,10},{3,11},{4,12},{5,13},{6,14},{7,15},{8,0},{9,1},... | collective-permute-start | bytes 835592 | tf_op jit(solution)/shard_map/ppermute | solution.py:338
  48.0 9.7 %collective-permute-start.1 = (bf16[272,512]{1,0:T(8,128)(2,1)S(1)}, bf16[272,512]{1,0:T(8,128)(2,1)S(1)}, u32[]{:S(2)}, u32[]{:S(2)}) collective-permute-start(bf16[272,512]{1,0:T(8,128)(2,1)S(1)} %get-tuple-element.37), channel_id=1, source_target_pairs={{0,1},{1,2},{2,3},{3,4},{4,5},{5,6},{6,7},{7,0},{8,15},{9,8},{10,9... | collective-permute-start | bytes 835592 | tf_op jit(solution)/shard_map/ppermute | solution.py:338
  51.1 10.9 %collective-permute-start.2 = (bf16[272,512]{1,0:T(8,128)(2,1)S(1)}, bf16[272,512]{1,0:T(8,128)(2,1)S(1)}, u32[]{:S(2)}, u32[]{:S(2)}) collective-permute-start(bf16[272,512]{1,0:T(8,128)(2,1)S(1)} %shard_map.118), channel_id=1, source_target_pairs={{0,1},{1,2},{2,3},{3,4},{4,5},{5,6},{6,7},{7,0},{8,15},{9,8},{10,9... | collective-permute-start | bytes 835592 | tf_op jit(solution)/shard_map/ppermute | solution.py:338
  57.8 9.7 %collective-permute-start.5 = (bf16[272,512]{1,0:T(8,128)(2,1)S(1)}, bf16[272,512]{1,0:T(8,128)(2,1)S(1)}, u32[]{:S(2)}, u32[]{:S(2)}) collective-permute-start(bf16[272,512]{1,0:T(8,128)(2,1)S(1)} %shard_map.116), channel_id=1, source_target_pairs={{0,1},{1,2},{2,3},{3,4},{4,5},{5,6},{6,7},{7,0},{8,15},{9,8},{10,9... | collective-permute-start | bytes 835592 | tf_op jit(solution)/shard_map/ppermute | solution.py:338
  62.1 9.7 %collective-permute-start.3 = (bf16[272,512]{1,0:T(8,128)(2,1)S(1)}, bf16[272,512]{1,0:T(8,128)(2,1)S(1)}, u32[]{:S(2)}, u32[]{:S(2)}) collective-permute-start(bf16[272,512]{1,0:T(8,128)(2,1)S(1)} %shard_map.119), channel_id=1, source_target_pairs={{0,1},{1,2},{2,3},{3,4},{4,5},{5,6},{6,7},{7,0},{8,15},{9,8},{10,9... | collective-permute-start | bytes 835592 | tf_op jit(solution)/shard_map/ppermute | solution.py:338
  67.5 9.7 %collective-permute-start.6 = (bf16[272,512]{1,0:T(8,128)(2,1)S(1)}, bf16[272,512]{1,0:T(8,128)(2,1)S(1)}, u32[]{:S(2)}, u32[]{:S(2)}) collective-permute-start(bf16[272,512]{1,0:T(8,128)(2,1)S(1)} %shard_map.122), channel_id=1, source_target_pairs={{0,1},{1,2},{2,3},{3,4},{4,5},{5,6},{6,7},{7,0},{8,15},{9,8},{10,9... | collective-permute-start | bytes 835592 | tf_op jit(solution)/shard_map/ppermute | solution.py:338
  71.9 7.9 %collective-permute-start.4 = (bf16[272,512]{1,0:T(8,128)(2,1)S(1)}, bf16[272,512]{1,0:T(8,128)(2,1)S(1)}, u32[]{:S(2)}, u32[]{:S(2)}) collective-permute-start(bf16[272,512]{1,0:T(8,128)(2,1)S(1)} %shard_map.120), channel_id=1, source_target_pairs={{0,9},{1,10},{2,11},{3,12},{4,13},{5,14},{6,15},{7,8},{8,7},{9,0},... | collective-permute-start | bytes 835592 | tf_op jit(solution)/shard_map/ppermute | solution.py:338
  77.3 9.7 %collective-permute-start.7 = (bf16[272,512]{1,0:T(8,128)(2,1)S(1)}, bf16[272,512]{1,0:T(8,128)(2,1)S(1)}, u32[]{:S(2)}, u32[]{:S(2)}) collective-permute-start(bf16[272,512]{1,0:T(8,128)(2,1)S(1)} %shard_map.123), channel_id=1, source_target_pairs={{0,1},{1,2},{2,3},{3,4},{4,5},{5,6},{6,7},{7,0},{8,15},{9,8},{10,9... | collective-permute-start | bytes 835592 | tf_op jit(solution)/shard_map/ppermute | solution.py:338

commit v11 on v10

--- a/solution.py
+++ b/solution.py
@@ -32,13 +32,10 @@
     return copies
 
 
-def running_sum(rows):
-    lanes = lax.broadcasted_iota(jnp.int32, rows.shape, 1)
-    step = 1
-    while step < rows.shape[1]:
-        rows = rows + jnp.where(lanes >= step, pltpu.roll(rows, step, 1), 0.0)
-        step *= 2
-    return rows
+def parts_of(rows):
+    high = rows.astype(BF16).astype(F32)
+    middle = (rows - high).astype(BF16).astype(F32)
+    return [high, middle, rows - high - middle]
 
 
 def keep_rows(keep):
@@ -57,34 +54,40 @@
 
 
 def state_kernel(*refs):
-    (log_rate, bias, raw_ref, flag_ref, b_ref, x_ref) = refs[9:15]
-    out_ref, rows_ref, cols_ref = refs[6:9]
-    copies = fetch(refs[:6], refs[9:15], refs[15])
+    (log_rate, bias, raw_ref, flag_ref, b_ref, x_ref) = refs[8:14]
+    out_ref, rows_ref = refs[6:8]
+    copies = fetch(refs[:6], refs[8:14], refs[14])
     for copy in copies[:4]:
         copy.wait()
     heads, tokens = raw_ref.shape
-    width = x_ref.shape[1] // heads
+    channels = x_ref.shape[1]
+    width = channels // heads
     raw = raw_ref[...]
     dt = jax.nn.softplus(raw + column_of(bias[...], raw.shape))
     rate = -jnp.exp(column_of(log_rate[...], raw.shape))
     flags = jnp.broadcast_to(flag_ref[...].astype(F32), raw.shape)
-    sums = running_sum(jnp.concatenate([rate * dt, flags], axis=0))
-    running, resets = (sums[:heads], sums[heads:])
+    steps = jnp.concatenate([*parts_of(rate * dt), flags], axis=0).astype(BF16)
+    square = (tokens, tokens)
+    upto = lax.broadcasted_iota(jnp.int32, square, 0) <= lax.broadcasted_iota(jnp.int32, square, 1)
+    sums = jnp.dot(steps, jnp.where(upto, 1.0, 0.0).astype(BF16), preferred_element_type=F32)
+    running = sums[:heads] + sums[heads : 2 * heads] + sums[2 * heads : 3 * heads]
+    resets = sums[3 * heads :]
     run_last = jnp.broadcast_to(running[:, tokens - 1 :], raw.shape)
     reset_last = jnp.broadcast_to(resets[:, tokens - 1 :], raw.shape)
     weights = jnp.where(resets == reset_last, jnp.exp(run_last - running), 0.0) * dt
     opening = jnp.where(resets == 0.0, jnp.exp(running), 0.0)
-    rows = jnp.concatenate([running, dt, resets, opening, weights], axis=0)
-    rows_ref[...] = rows
-    cols = jnp.concatenate([rows, jnp.zeros((128 - rows.shape[0], tokens), F32)], axis=0).T
-    cols_ref[...] = cols
+    rows_ref[...] = jnp.concatenate([running, dt, resets, opening], axis=0)
     through = jnp.where(reset_last == 0.0, jnp.exp(run_last), 0.0)
-    spread = jnp.concatenate(
-        [
-            jnp.broadcast_to(cols[:, 4 * heads + h : 4 * heads + h + 1], (tokens, width))
-            for h in range(heads)
-        ],
-        axis=1,
+    shape = (4 * heads, channels)
+    row, first = lax.broadcasted_iota(jnp.int32, shape, 0), lax.broadcasted_iota(jnp.int32, shape, 1)
+    for i in range(3):
+        row = jnp.where(row >= heads, row - heads, row)
+    mine = (first >= row * width) & (first < (row + 1) * width)
+    spread = lax.dot_general(
+        jnp.concatenate([*parts_of(weights), jnp.zeros_like(weights)], axis=0).astype(BF16),
+        jnp.where(mine, 1.0, 0.0).astype(BF16),
+        (((0,), (0,)), ((), ())),
+        preferred_element_type=F32,
     )
     for copy in copies[4:]:
         copy.wait()
@@ -96,10 +99,12 @@
 
 
 def intra_kernel(*refs):
-    own_ref, open_ref = refs[8:10]
-    c_ref, b_ref, rows_ref, cols_ref, skip_ref, x_ref, z_ref = refs[10:17]
-    for copy in fetch(refs[1:8], refs[10:17], refs[17]):
+    own_ref, open_ref = refs[7:9]
+    c_ref, b_ref, rows_ref, skip_ref, x_ref, z_ref, cols_ref = refs[9:16]
+    for copy in fetch(refs[1:7], refs[9:15], refs[16]):
         copy.wait()
+    rows = rows_ref[...]
+    cols_ref[...] = jnp.concatenate([rows, jnp.zeros((128 - rows.shape[0], rows.shape[1]), F32)], axis=0).T
     tokens = x_ref.shape[0]
     heads = skip_ref.shape[1]
     width = x_ref.shape[1] // heads
@@ -283,10 +288,10 @@
         input_b,
         input_x,
     )
-    pieces, rows, cols = call(
+    pieces, rows = call(
         state_kernel,
         [HBM] * 6,
-        [((heads, *sent), BF16), ((5 * heads, tokens), F32), ((tokens, 128), F32)],
+        [((heads, *sent), BF16), ((4 * heads, tokens), F32)],
         local,
         scratch=local,
         limit=60,
@@ -297,13 +302,13 @@
     skip = skip_gain.reshape(1, heads)
     gain = norm_gain.reshape(1, channels)
     (totals,) = call(plane_kernel, [VMEM], [((planes, *sent), BF16)], (got,), moved=2**19)
-    near = (input_c, input_b, rows, cols, skip, input_x, input_z)
+    near = (input_c, input_b, rows, skip, input_x, input_z)
     own, opened = call(
         intra_kernel,
-        [ANY] + [HBM] * 7,
+        [ANY] + [HBM] * 6,
         [((tokens, channels), F32)] * 2,
         (totals, *near),
-        scratch=near,
+        scratch=(*near, jax.ShapeDtypeStruct((tokens, 128), F32)),
         limit=60,
         flops=2 * tokens * tokens * channels,
         moved=8 * 2**20,

time: 88.6 us -> 88 us (level)
  transfers between devices with their start and end apart: 10 -> 10, of which waited for: 8 -> 8; matrix products, arithmetic and copies ran while one was open for 0% -> 0% of each run, Pallas kernels for 8% -> 9%
where the time goes in v11:
time: 88 us; the launch traced here: 87.2 us
  starting transfers between devices  30.5 us (35%)
  waiting for transfers between devices  28.3 us (32%)
  Pallas kernels  13.7 us (16%)
  blocking collectives  10.8 us (12%)
  local copies, waits for them, and re-layouts  3.6 us (4%)
    ppermute x8, waiting for transfers between devices, send(): return lax.ppermute(array, ('seq', 'head'), pairs)  20.6 us
    ppermute x8, starting transfers between devices, send(): return lax.ppermute(array, ('seq', 'head'), pairs)  16.8 us
    pallas_call x16, Pallas kernels, call(): pl.pallas_call(kernel, in_specs=ins, out_specs=[VMEM] * len(outs), out_sh...  13.7 us
    all_to_all x1, blocking collectives, body(): got = lax.all_to_all(pieces, 'seq', 0, 0, axis_index_groups=in_plane)  10.8 us
    all_to_all x1, starting transfers between devices, body(): got_planes = lax.all_to_all(totals, 'seq', 0, 0, axis_index_groups=across)  10.3 us
    all_to_all x1, waiting for transfers between devices, body(): got_planes = lax.all_to_all(totals, 'seq', 0, 0, axis_index_groups=across)  5.54 us
    unnamed x8, local copies, waits for them, and re-layouts  3.6 us
    all_to_all x1, starting transfers between devices, body(): entries = lax.all_to_all(entries, 'seq', 0, 0, axis_index_groups=in_plane)  3.37 us
  transfers between devices with their start and end apart: 10, of which 8 were waited for; matrix products, arithmetic and copies ran while one was open for 0% of the time, Pallas kernels for 9%

profile of v11, /device:TPU:32, one launch (start us, length us, event | category | flops | bytes accessed | tf_op | source)
XLA Modules:
  0.0 87.2 jit_solution(7129296039952171732)
XLA Ops:
  0.0 2.3 %shard_map.109 = (bf16[8,80,128]{2,1,0:T(8,128)(2,1)}, f32[32,256]{1,0:T(8,128)}) custom-call(f32[1,8]{1,0:T(1,128)} %bitcast.12, f32[1,8]{1,0:T(1,128)} %bitcast.13, f32[8,256]{1,0:T(8,128)} %bitcast.10, s32[1,256]{1,0:T(1,128)} %bitcast.11, bf16[256,128]{1,0:T(8,128)(2,1)} %refs_2_.1, bf16[256,512]{1,0:T(8,128)(2,1)} %refs_5_.3), custom_call_target="tpu_custom_call" | custom-call | flops 33554432 | bytes 262144 | tf_op jit(solution)/shard_map/pallas_call | solution.py:259
  2.3 10.8 %all_to_all.15.got_ref = bf16[8,80,128]{2,1,0:T(8,128)(2,1)S(1)} all-to-all(bf16[8,80,128]{2,1,0:T(8,128)(2,1)} %get-tuple-element.23), channel_id=1, replica_groups={{0,8,16,24,32,40,48,56},{64,72,80,88,96,104,112,120},{128,136,144,152,1..., dimensions={0} | all-to-all | bytes 327680 | tf_op jit(solution)/shard_map/all_to_all | solution.py:301
  13.1 0.7 shard_map.110.refs_0_
  13.8 10.3 %all-to-all-start.1 = ((bf16[8,80,128]{2,1,0:T(8,128)(2,1)}), bf16[8,80,128]{2,1,0:T(8,128)(2,1)S(1)}, u32[]{:S(2)}, u32[]{:S(2)}) async-start(bf16[8,80,128]{2,1,0:T(8,128)(2,1)} %shard_map.110.refs_0_), calls=%async_computation.1 | async-start | bytes 327680 | tf_op jit(solution)/shard_map/all_to_all | solution.py:316
  24.1 4.0 %shard_map.111 = (f32[256,512]{1,0:T(8,128)}, f32[256,512]{1,0:T(8,128)}) custom-call(bf16[8,80,128]{2,1,0:T(8,128)(2,1)} %shard_map.110.refs_0_, bf16[256,128]{1,0:T(8,128)(2,1)} %refs_1_.3, bf16[256,128]{1,0:T(8,128)(2,1)} %refs_2_.1, f32[32,256]{1,0:T(8,128)} %get-tuple-element.24.refs_3_, f32[1,8]{1,0:T(1,128)} %bitcast.14, bf16[256,512]{1,0:T(8,128)(2,1)} %refs_5_.3, ...), custom_call_target="tpu_custom_call" | custom-call | flops 67108864 | bytes 8388608 | tf_op jit(solution)/shard_map/pallas_call | solution.py:259
  28.1 5.5 %all-to-all-done.1.planes_ref = bf16[8,80,128]{2,1,0:T(8,128)(2,1)S(1)} async-done(((bf16[8,80,128]{2,1,0:T(8,128)(2,1)}), bf16[8,80,128]{2,1,0:T(8,128)(2,1)S(1)}, u32[]{:S(2)}, u32[]{:S(2)}) %all-to-all-start.1) | async-done | bytes 163872 | tf_op jit(solution)/shard_map/all_to_all | solution.py:316
  33.7 0.7 shard_map.112.refs_0_
  34.4 3.4 %all-to-all-start.2 = ((bf16[8,64,128]{2,1,0:T(8,128)(2,1)}), bf16[8,64,128]{2,1,0:T(8,128)(2,1)S(1)}, u32[]{:S(2)}, u32[]{:S(2)}) async-start(bf16[8,64,128]{2,1,0:T(8,128)(2,1)} %shard_map.112.refs_0_), calls=%async_computation.2 | async-start | bytes 262144 | tf_op jit(solution)/shard_map/all_to_all | solution.py:331
  37.8 0.0 copy-start
  37.8 1.0 %copy-done = f32[256,512]{1,0:T(8,128)S(1)} copy-done((f32[256,512]{1,0:T(8,128)S(1)}, f32[256,512]{1,0:T(8,128)}, u32[]{:S(2)}) %copy-start) | copy-done | bytes 524312
  38.8 0.0 copy-start.1
  38.8 1.0 %copy-done.1 = f32[256,512]{1,0:T(8,128)S(1)} copy-done((f32[256,512]{1,0:T(8,128)S(1)}, f32[256,512]{1,0:T(8,128)}, u32[]{:S(2)}) %copy-start.1) | copy-done | bytes 524312
  39.9 0.0 copy-start.2
  39.9 0.8 copy-done.2
  40.7 0.0 copy-start.3
  40.7 0.7 copy-done.3
  41.4 0.2 shard_map.113
  41.6 2.2 %all-to-all-done.2.entry_ref = bf16[8,64,128]{2,1,0:T(8,128)(2,1)S(1)} async-done(((bf16[8,64,128]{2,1,0:T(8,128)(2,1)}), bf16[8,64,128]{2,1,0:T(8,128)(2,1)S(1)}, u32[]{:S(2)}, u32[]{:S(2)}) %all-to-all-start.2) | async-done | bytes 131104 | tf_op jit(solution)/shard_map/all_to_all | solution.py:331
  43.8 1.7 %shard_map.114 = (bf16[272,512]{1,0:T(8,128)(2,1)S(1)}, bf16[272,512]{1,0:T(8,128)(2,1)S(1)}, bf16[512,512]{1,0:T(8,128)(2,1)S(1)}) custom-call(s32[1]{0:T(128)} %bitcast.me, s32[1]{0:T(128)} %bitcast.1.way, bf16[8,64,128]{2,1,0:T(8,128)(2,1)S(1)} %all-to-all-done.2.entry_ref, bf16[256,128]{1,0:T(8,128)(2,1)S(1)} %get-tuple-element.29.c_ref, ...), custom_call_target="tpu_custom_call" | custom-call | flops 134217728 | bytes 2097152 | tf_op jit(solution)/shard_map/pallas_call | solution.py:259
  45.5 1.9 %collective-permute-start = (bf16[272,512]{1,0:T(8,128)(2,1)S(1)}, bf16[272,512]{1,0:T(8,128)(2,1)S(1)}, u32[]{:S(2)}, u32[]{:S(2)}) collective-permute-start(bf16[272,512]{1,0:T(8,128)(2,1)S(1)} %get-tuple-element.36.own_ref.gated_ref), channel_id=1, source_target_pairs={{0,8},{1,9},{2,10},{3,11},{4,12},{5,13},{6,14},{7,15},{8,0},{9,1},... | collective-permute-start | bytes 835592 | tf_op jit(solution)/shard_map/ppermute | solution.py:343
  47.5 2.6 %collective-permute-start.1 = (bf16[272,512]{1,0:T(8,128)(2,1)S(1)}, bf16[272,512]{1,0:T(8,128)(2,1)S(1)}, u32[]{:S(2)}, u32[]{:S(2)}) collective-permute-start(bf16[272,512]{1,0:T(8,128)(2,1)S(1)} %get-tuple-element.35), channel_id=1, source_target_pairs={{0,1},{1,2},{2,3},{3,4},{4,5},{5,6},{6,7},{7,0},{8,15},{9,8},{10,9... | collective-permute-start | bytes 835592 | tf_op jit(solution)/shard_map/ppermute | solution.py:343
  50.1 0.0 collective-permute-done.other_ref.gated_ref
  50.1 0.4 shard_map.115.chunk_ref
  50.5 2.6 %collective-permute-start.2 = (bf16[272,512]{1,0:T(8,128)(2,1)S(1)}, bf16[272,512]{1,0:T(8,128)(2,1)S(1)}, u32[]{:S(2)}, u32[]{:S(2)}) collective-permute-start(bf16[272,512]{1,0:T(8,128)(2,1)S(1)} %shard_map.118), channel_id=1, source_target_pairs={{0,1},{1,2},{2,3},{3,4},{4,5},{5,6},{6,7},{7,0},{8,15},{9,8},{10,9... | collective-permute-start | bytes 835592 | tf_op jit(solution)/shard_map/ppermute | solution.py:343
  53.2 4.0 %collective-permute-done.1.refs_0_ = bf16[272,512]{1,0:T(8,128)(2,1)S(1)} collective-permute-done((bf16[272,512]{1,0:T(8,128)(2,1)S(1)}, bf16[272,512]{1,0:T(8,128)(2,1)S(1)}, u32[]{:S(2)}, u32[]{:S(2)}) %collective-permute-start.1) | collective-permute-done | bytes 278560 | tf_op jit(solution)/shard_map/ppermute | solution.py:343
  57.1 0.1 shard_map.116
  57.2 1.9 %collective-permute-start.5 = (bf16[272,512]{1,0:T(8,128)(2,1)S(1)}, bf16[272,512]{1,0:T(8,128)(2,1)S(1)}, u32[]{:S(2)}, u32[]{:S(2)}) collective-permute-start(bf16[272,512]{1,0:T(8,128)(2,1)S(1)} %shard_map.116), channel_id=1, source_target_pairs={{0,1},{1,2},{2,3},{3,4},{4,5},{5,6},{6,7},{7,0},{8,15},{9,8},{10,9... | collective-permute-start | bytes 835592 | tf_op jit(solution)/shard_map/ppermute | solution.py:343
  59.1 2.3 %shard_map.117 = (bf16[2,2,256,512]{3,2,1,0:T(8,128)(2,1)S(1)}, bf16[256,512]{1,0:T(8,128)(2,1)S(1)}) custom-call(s32[1]{0:T(128)} %bitcast.me, s32[1]{0:T(128)} %bitcast.1.way, bf16[272,512]{1,0:T(8,128)(2,1)S(1)} %get-tuple-element.36.own_ref.gated_ref, bf16[272,512]{1,0:T(8,128)(2,1)S(1)} %collective-permute-done.other_ref.gated_ref, bf16[512,4096]{1,0:T(8,128)(2,1)} %w_hbm.3), custom_call_target="tpu_custom_call" | custom-call | flops 671088640 | bytes 2097152 | tf_op jit(solution)/shard_map/pallas_call | solution.py:259
  61.4 0.0 collective-permute-done.2.refs_0_
  61.5 0.1 shard_map.119
  61.5 2.0 %collective-permute-start.3 = (bf16[272,512]{1,0:T(8,128)(2,1)S(1)}, bf16[272,512]{1,0:T(8,128)(2,1)S(1)}, u32[]{:S(2)}, u32[]{:S(2)}) collective-permute-start(bf16[272,512]{1,0:T(8,128)(2,1)S(1)} %shard_map.119), channel_id=1, source_target_pairs={{0,1},{1,2},{2,3},{3,4},{4,5},{5,6},{6,7},{7,0},{8,15},{9,8},{10,9... | collective-permute-start | bytes 835592 | tf_op jit(solution)/shard_map/ppermute | solution.py:343
  63.6 3.2 %collective-permute-done.5.refs_0_ = bf16[272,512]{1,0:T(8,128)(2,1)S(1)} collective-permute-done((bf16[272,512]{1,0:T(8,128)(2,1)S(1)}, bf16[272,512]{1,0:T(8,128)(2,1)S(1)}, u32[]{:S(2)}, u32[]{:S(2)}) %collective-permute-start.5) | collective-permute-done | bytes 278560 | tf_op jit(solution)/shard_map/ppermute | solution.py:343
  66.9 0.1 shard_map.122
  66.9 1.9 %collective-permute-start.6 = (bf16[272,512]{1,0:T(8,128)(2,1)S(1)}, bf16[272,512]{1,0:T(8,128)(2,1)S(1)}, u32[]{:S(2)}, u32[]{:S(2)}) collective-permute-start(bf16[272,512]{1,0:T(8,128)(2,1)S(1)} %shard_map.122), channel_id=1, source_target_pairs={{0,1},{1,2},{2,3},{3,4},{4,5},{5,6},{6,7},{7,0},{8,15},{9,8},{10,9... | collective-permute-start | bytes 835592 | tf_op jit(solution)/shard_map/ppermute | solution.py:343
  68.9 2.3 %collective-permute-done.3.refs_0_ = bf16[272,512]{1,0:T(8,128)(2,1)S(1)} collective-permute-done((bf16[272,512]{1,0:T(8,128)(2,1)S(1)}, bf16[272,512]{1,0:T(8,128)(2,1)S(1)}, u32[]{:S(2)}, u32[]{:S(2)}) %collective-permute-start.3) | collective-permute-done | bytes 278560 | tf_op jit(solution)/shard_map/ppermute | solution.py:343
  71.2 0.1 shard_map.120
  71.3 1.9 %collective-permute-start.4 = (bf16[272,512]{1,0:T(8,128)(2,1)S(1)}, bf16[272,512]{1,0:T(8,128)(2,1)S(1)}, u32[]{:S(2)}, u32[]{:S(2)}) collective-permute-start(bf16[272,512]{1,0:T(8,128)(2,1)S(1)} %shard_map.120), channel_id=1, source_target_pairs={{0,9},{1,10},{2,11},{3,12},{4,13},{5,14},{6,15},{7,8},{8,7},{9,0},... | collective-permute-start | bytes 835592 | tf_op jit(solution)/shard_map/ppermute | solution.py:343
  73.2 3.4 %collective-permute-done.6.refs_0_ = bf16[272,512]{1,0:T(8,128)(2,1)S(1)} collective-permute-done((bf16[272,512]{1,0:T(8,128)(2,1)S(1)}, bf16[272,512]{1,0:T(8,128)(2,1)S(1)}, u32[]{:S(2)}, u32[]{:S(2)}) %collective-permute-start.6) | collective-permute-done | bytes 278560 | tf_op jit(solution)/shard_map/ppermute | solution.py:343
  76.6 0.1 shard_map.123
  76.7 1.9 %collective-permute-start.7 = (bf16[272,512]{1,0:T(8,128)(2,1)S(1)}, bf16[272,512]{1,0:T(8,128)(2,1)S(1)}, u32[]{:S(2)}, u32[]{:S(2)}) collective-permute-start(bf16[272,512]{1,0:T(8,128)(2,1)S(1)} %shard_map.123), channel_id=1, source_target_pairs={{0,1},{1,2},{2,3},{3,4},{4,5},{5,6},{6,7},{7,0},{8,15},{9,8},{10,9... | collective-permute-start | bytes 835592 | tf_op jit(solution)/shard_map/ppermute | solution.py:343
  78.6 0.6 collective-permute-done.4.got_ref
  79.2 0.1 shard_map.121
  79.2 7.1 %collective-permute-done.7.got_ref = bf16[272,512]{1,0:T(8,128)(2,1)S(1)} collective-permute-done((bf16[272,512]{1,0:T(8,128)(2,1)S(1)}, bf16[272,512]{1,0:T(8,128)(2,1)S(1)}, u32[]{:S(2)}, u32[]{:S(2)}) %collective-permute-start.7) | collective-permute-done | bytes 278560 | tf_op jit(solution)/shard_map/ppermute | solution.py:343
  86.3 0.8 shard_map.124
  (1 shorter events, 0.0 us)
Async XLA Ops:
  13.8 19.9 %all-to-all-start.1 = ((bf16[8,80,128]{2,1,0:T(8,128)(2,1)}), bf16[8,80,128]{2,1,0:T(8,128)(2,1)S(1)}, u32[]{:S(2)}, u32[]{:S(2)}) async-start(bf16[8,80,128]{2,1,0:T(8,128)(2,1)} %shard_map.110.refs_0_), calls=%async_computation.1 | async-start | bytes 327680 | tf_op jit(solution)/shard_map/all_to_all | solution.py:316
  34.4 9.4 %all-to-all-start.2 = ((bf16[8,64,128]{2,1,0:T(8,128)(2,1)}), bf16[8,64,128]{2,1,0:T(8,128)(2,1)S(1)}, u32[]{:S(2)}, u32[]{:S(2)}) async-start(bf16[8,64,128]{2,1,0:T(8,128)(2,1)} %shard_map.112.refs_0_), calls=%async_computation.2 | async-start | bytes 262144 | tf_op jit(solution)/shard_map/all_to_all | solution.py:331
  37.8 1.0 %copy-start = (f32[256,512]{1,0:T(8,128)S(1)}, f32[256,512]{1,0:T(8,128)}, u32[]{:S(2)}) copy-start(f32[256,512]{1,0:T(8,128)} %get-tuple-element.27.refs_2_) | copy-start | bytes 1572868
  38.8 1.0 %copy-start.1 = (f32[256,512]{1,0:T(8,128)S(1)}, f32[256,512]{1,0:T(8,128)}, u32[]{:S(2)}) copy-start(f32[256,512]{1,0:T(8,128)} %get-tuple-element.28.refs_3_) | copy-start | bytes 1572868
  39.9 0.8 copy-start.2
  40.7 0.7 copy-start.3
  45.5 4.5 %collective-permute-start = (bf16[272,512]{1,0:T(8,128)(2,1)S(1)}, bf16[272,512]{1,0:T(8,128)(2,1)S(1)}, u32[]{:S(2)}, u32[]{:S(2)}) collective-permute-start(bf16[272,512]{1,0:T(8,128)(2,1)S(1)} %get-tuple-element.36.own_ref.gated_ref), channel_id=1, source_target_pairs={{0,8},{1,9},{2,10},{3,11},{4,12},{5,13},{6,14},{7,15},{8,0},{9,1},... | collective-permute-start | bytes 835592 | tf_op jit(solution)/shard_map/ppermute | solution.py:343
  47.5 9.7 %collective-permute-start.1 = (bf16[272,512]{1,0:T(8,128)(2,1)S(1)}, bf16[272,512]{1,0:T(8,128)(2,1)S(1)}, u32[]{:S(2)}, u32[]{:S(2)}) collective-permute-start(bf16[272,512]{1,0:T(8,128)(2,1)S(1)} %get-tuple-element.35), channel_id=1, source_target_pairs={{0,1},{1,2},{2,3},{3,4},{4,5},{5,6},{6,7},{7,0},{8,15},{9,8},{10,9... | collective-permute-start | bytes 835592 | tf_op jit(solution)/shard_map/ppermute | solution.py:343
  50.5 10.9 %collective-permute-start.2 = (bf16[272,512]{1,0:T(8,128)(2,1)S(1)}, bf16[272,512]{1,0:T(8,128)(2,1)S(1)}, u32[]{:S(2)}, u32[]{:S(2)}) collective-permute-start(bf16[272,512]{1,0:T(8,128)(2,1)S(1)} %shard_map.118), channel_id=1, source_target_pairs={{0,1},{1,2},{2,3},{3,4},{4,5},{5,6},{6,7},{7,0},{8,15},{9,8},{10,9... | collective-permute-start | bytes 835592 | tf_op jit(solution)/shard_map/ppermute | solution.py:343
  57.2 9.7 %collective-permute-start.5 = (bf16[272,512]{1,0:T(8,128)(2,1)S(1)}, bf16[272,512]{1,0:T(8,128)(2,1)S(1)}, u32[]{:S(2)}, u32[]{:S(2)}) collective-permute-start(bf16[272,512]{1,0:T(8,128)(2,1)S(1)} %shard_map.116), channel_id=1, source_target_pairs={{0,1},{1,2},{2,3},{3,4},{4,5},{5,6},{6,7},{7,0},{8,15},{9,8},{10,9... | collective-permute-start | bytes 835592 | tf_op jit(solution)/shard_map/ppermute | solution.py:343
  61.5 9.7 %collective-permute-start.3 = (bf16[272,512]{1,0:T(8,128)(2,1)S(1)}, bf16[272,512]{1,0:T(8,128)(2,1)S(1)}, u32[]{:S(2)}, u32[]{:S(2)}) collective-permute-start(bf16[272,512]{1,0:T(8,128)(2,1)S(1)} %shard_map.119), channel_id=1, source_target_pairs={{0,1},{1,2},{2,3},{3,4},{4,5},{5,6},{6,7},{7,0},{8,15},{9,8},{10,9... | collective-permute-start | bytes 835592 | tf_op jit(solution)/shard_map/ppermute | solution.py:343
  66.9 9.7 %collective-permute-start.6 = (bf16[272,512]{1,0:T(8,128)(2,1)S(1)}, bf16[272,512]{1,0:T(8,128)(2,1)S(1)}, u32[]{:S(2)}, u32[]{:S(2)}) collective-permute-start(bf16[272,512]{1,0:T(8,128)(2,1)S(1)} %shard_map.122), channel_id=1, source_target_pairs={{0,1},{1,2},{2,3},{3,4},{4,5},{5,6},{6,7},{7,0},{8,15},{9,8},{10,9... | collective-permute-start | bytes 835592 | tf_op jit(solution)/shard_map/ppermute | solution.py:343
  71.3 7.9 %collective-permute-start.4 = (bf16[272,512]{1,0:T(8,128)(2,1)S(1)}, bf16[272,512]{1,0:T(8,128)(2,1)S(1)}, u32[]{:S(2)}, u32[]{:S(2)}) collective-permute-start(bf16[272,512]{1,0:T(8,128)(2,1)S(1)} %shard_map.120), channel_id=1, source_target_pairs={{0,9},{1,10},{2,11},{3,12},{4,13},{5,14},{6,15},{7,8},{8,7},{9,0},... | collective-permute-start | bytes 835592 | tf_op jit(solution)/shard_map/ppermute | solution.py:343
  76.7 9.7 %collective-permute-start.7 = (bf16[272,512]{1,0:T(8,128)(2,1)S(1)}, bf16[272,512]{1,0:T(8,128)(2,1)S(1)}, u32[]{:S(2)}, u32[]{:S(2)}) collective-permute-start(bf16[272,512]{1,0:T(8,128)(2,1)S(1)} %shard_map.123), channel_id=1, source_target_pairs={{0,1},{1,2},{2,3},{3,4},{4,5},{5,6},{6,7},{7,0},{8,15},{9,8},{10,9... | collective-permute-start | bytes 835592 | tf_op jit(solution)/shard_map/ppermute | solution.py:343

commit v12 on v11

--- a/solution.py
+++ b/solution.py
@@ -187,12 +187,12 @@
 
 
 def gate_kernel(me, way, entry_ref, c_ref, own_ref, open_ref, gain_ref, w_hbm, *refs):
-    gated_ref, far_ref, next_ref, w_ref, sems = refs
+    gated_ref, far_ref, chunk_ref, w_ref, sems = refs
     heads, width, lanes = entry_ref.shape
     tokens = own_ref.shape[0]
-    features = w_ref.shape[1]
+    features = w_ref.shape[2]
     wanted = [columns(w_hbm, me[0], away, features) for away in (N_PART // 2, (N_PART // 2 - 1) * way[0])]
-    copies = fetch(wanted, [w_ref, next_ref], sems)
+    copies = fetch(wanted, [w_ref.at[0], w_ref.at[1]], sems)
     entries = entry_ref[...].reshape(heads * width, lanes)
     carried = lax.dot_general(c_ref[...], entries, (((1,), (1,)), ((), ())), preferred_element_type=F32)
     gated = own_ref[...] + open_ref[...] * carried
@@ -203,23 +203,21 @@
     put_squares(gated_ref, squares)
     put_squares(far_ref, squares)
     copies[0].wait()
-    far_ref[:tokens] = jnp.dot(scaled, w_ref[...], preferred_element_type=F32).astype(BF16)
+    far_ref[:tokens] = jnp.dot(scaled, w_ref[0], preferred_element_type=F32).astype(BF16)
     copies[1].wait()
-
-
-def begin_kernel(own_ref, other_ref, w_ref, out_ref):
-    tokens = out_ref.shape[1]
-    for j, ref in enumerate((own_ref, other_ref)):
-        out_ref[j] = jnp.dot(ref[:tokens], w_ref[...], preferred_element_type=F32).astype(BF16)
-
-
-def chunks_kernel(me, way, own_ref, other_ref, w_hbm, out_ref, base_ref, w_ref, sems):
+    chunk_ref[0] = jnp.dot(scaled, w_ref[1], preferred_element_type=F32).astype(BF16)
+
+
+def chunks_kernel(me, way, own_ref, other_ref, w_hbm, sent_ref, out_ref, base_ref, w_ref, sems):
     steps, _, tokens, features = out_ref.shape
-    order = [*range(steps, 0, -1), 0]
+    order = [*range(steps + 1, 0, -1), 0]
     copies = fetch([columns(w_hbm, me[0], a * way[0], features) for a in order], [w_ref.at[a] for a in order], sems)
     for a, copy in zip(order, copies):
         copy.wait()
-        if a == 0:
+        if a == steps + 1:
+            sent_ref[:tokens] = jnp.dot(other_ref[:tokens], w_ref[a], preferred_element_type=F32).astype(BF16)
+            sent_ref[tokens:] = other_ref[tokens:]
+        elif a == 0:
             base_ref[...] = jnp.dot(own_ref[:tokens], w_ref[a], preferred_element_type=F32).astype(BF16)
         else:
             for j, ref in enumerate((own_ref, other_ref)):
@@ -342,58 +340,49 @@
                 pairs.append((seq * N_PART + head, (seq ^ swap) * N_PART + there))
         return lax.ppermute(array, ("seq", "head"), pairs)
 
-    gated, far, w_next = call(
+    gated, far, first_chunk = call(
         gate_kernel,
         [SMEM] * 2 + [VMEM] * 5 + [HBM],
-        [slab, slab, ((channels, features), BF16)],
+        [slab, slab, ((1, tokens, features), BF16)],
         (me, way, entries, *needed, out_weight),
-        scratch=[jax.ShapeDtypeStruct((channels, features), BF16)],
-        flops=2 * tokens * channels * features,
+        scratch=[jax.ShapeDtypeStruct((2, channels, features), BF16)],
+        flops=4 * tokens * channels * features,
         moved=2**21,
         limit=50,
     )
+
+    def join(place, chunk, mine, got):
+        kernel = functools.partial(join_kernel, place)
+        return call(kernel, [VMEM] * 3, [slab], (chunk, mine, got), moved=2**19)[0]
+
+    own_got = send(far, 1, 0)
     other = send(gated, 0, 1)
-    own_got = send(far, 1, 0)
-    (begin,) = call(
-        begin_kernel,
-        [VMEM] * 3,
-        [((2, tokens, features), BF16)],
-        (gated, other, w_next),
-        flops=4 * tokens * channels * features,
-        moved=2**22,
-    )
-
-    def join(place, chunk, mine, *got):
-        kernel = functools.partial(join_kernel, place)
-        return call(kernel, [VMEM] * (2 + len(got)), [slab], (chunk, mine, *got), moved=2**19)[0]
-
-    other_sent = join(1, begin, other)
-    other_got = send(other_sent, 1, 0)
-    own_sent = join(0, begin, gated, own_got)
+    own_sent = join(0, first_chunk, gated, own_got)
     own_got = send(own_sent, 1, 0)
     steps = N_PART // 2 - 2
-    gated_then, _ = lax.optimization_barrier((gated, own_sent))
-    chunks, base = call(
+    gated_then, own_sent = lax.optimization_barrier((gated, own_sent))
+    other_sent, chunks, base = call(
         chunks_kernel,
         [SMEM, SMEM, VMEM, VMEM, HBM],
-        [((steps, 2, tokens, features), BF16), ((tokens, features), BF16)],
+        [slab, ((steps, 2, tokens, features), BF16), ((tokens, features), BF16)],
         (me, way, gated_then, other, out_weight),
-        scratch=[jax.ShapeDtypeStruct((steps + 1, channels, features), BF16)],
-        flops=10 * tokens * channels * features,
-        moved=2**21,
+        scratch=[jax.ShapeDtypeStruct((steps + 2, channels, features), BF16)],
+        flops=12 * tokens * channels * features,
+        moved=2**22,
         limit=50,
     )
+    other_got = send(other_sent, 1, 0)
     for away in range(steps, 0, -1):
+        own_got = send(join((away - 1, 0), chunks, gated, own_got), 1, 0)
         other_got = send(join((away - 1, 1), chunks, other, other_got), 1, int(away == 1))
-        own_got = send(join((away - 1, 0), chunks, gated, own_got), 1, 0)
     total, squares = call(
-        sum_kernel, [VMEM] * 3, [((tokens, features), F32), ((1, tokens), F32)], (base, gated, other_got), moved=2**20
+        sum_kernel, [VMEM] * 3, [((tokens, features), F32), ((1, tokens), F32)], (base, gated, own_got), moved=2**20
     )
     (out,) = call(
         functools.partial(end_kernel, channels * N_PART),
         [VMEM] * 3,
         [((tokens, features), BF16)],
-        (total, squares, own_got),
+        (total, squares, other_got),
         moved=2**20,
     )
     return out

time: 88 us -> 90.7 us (1.031)
  the two profiles are of different devices: /device:TPU:32 before, /device:TPU:24 now
where the time goes in v12:
time: 90.7 us; the launch traced here: 89.9 us
  starting transfers between devices  43 us (47%)
  waiting for transfers between devices  18.4 us (20%)
  Pallas kernels  13.9 us (15%)
  blocking collectives  10.8 us (12%)
  local copies, waits for them, and re-layouts  3.6 us (4%)
    ppermute x8, starting transfers between devices, send(): return lax.ppermute(array, ('seq', 'head'), pairs)  29.3 us
    pallas_call x14, Pallas kernels, call(): pl.pallas_call(kernel, in_specs=ins, out_specs=[VMEM] * len(outs), out_sh...  13.9 us
    all_to_all x1, blocking collectives, body(): got = lax.all_to_all(pieces, 'seq', 0, 0, axis_index_groups=in_plane)  10.8 us
    ppermute x8, waiting for transfers between devices, send(): return lax.ppermute(array, ('seq', 'head'), pairs)  10.7 us
    all_to_all x1, starting transfers between devices, body(): got_planes = lax.all_to_all(totals, 'seq', 0, 0, axis_index_groups=across)  10.3 us
    all_to_all x1, waiting for transfers between devices, body(): got_planes = lax.all_to_all(totals, 'seq', 0, 0, axis_index_groups=across)  5.54 us
    unnamed x8, local copies, waits for them, and re-layouts  3.6 us
    all_to_all x1, starting transfers between devices, body(): entries = lax.all_to_all(entries, 'seq', 0, 0, axis_index_groups=in_plane)  3.37 us
  transfers between devices with their start and end apart: 10, of which 7 were waited for; matrix products, arithmetic and copies ran while one was open for 0% of the time, Pallas kernels for 8%

profile of v12, /device:TPU:24, one launch (start us, length us, event | category | flops | bytes accessed | tf_op | source)
XLA Modules:
  0.0 89.9 jit_solution(12484105219569523503)
XLA Ops:
  0.0 2.3 %shard_map.109 = (bf16[8,80,128]{2,1,0:T(8,128)(2,1)}, f32[32,256]{1,0:T(8,128)}) custom-call(f32[1,8]{1,0:T(1,128)} %bitcast.12, f32[1,8]{1,0:T(1,128)} %bitcast.13, f32[8,256]{1,0:T(8,128)} %bitcast.10, s32[1,256]{1,0:T(1,128)} %bitcast.11, bf16[256,128]{1,0:T(8,128)(2,1)} %refs_2_.1, bf16[256,512]{1,0:T(8,128)(2,1)} %refs_5_.3), custom_call_target="tpu_custom_call" | custom-call | flops 33554432 | bytes 262144 | tf_op jit(solution)/shard_map/pallas_call | solution.py:257
  2.3 10.8 %all_to_all.15.got_ref = bf16[8,80,128]{2,1,0:T(8,128)(2,1)S(1)} all-to-all(bf16[8,80,128]{2,1,0:T(8,128)(2,1)} %get-tuple-element.24), channel_id=1, replica_groups={{0,8,16,24,32,40,48,56},{64,72,80,88,96,104,112,120},{128,136,144,152,1..., dimensions={0} | all-to-all | bytes 327680 | tf_op jit(solution)/shard_map/all_to_all | solution.py:299
  13.1 0.7 shard_map.110.refs_0_
  13.8 10.3 %all-to-all-start.1 = ((bf16[8,80,128]{2,1,0:T(8,128)(2,1)}), bf16[8,80,128]{2,1,0:T(8,128)(2,1)S(1)}, u32[]{:S(2)}, u32[]{:S(2)}) async-start(bf16[8,80,128]{2,1,0:T(8,128)(2,1)} %shard_map.110.refs_0_), calls=%async_computation.1 | async-start | bytes 327680 | tf_op jit(solution)/shard_map/all_to_all | solution.py:314
  24.1 4.0 %shard_map.111 = (f32[256,512]{1,0:T(8,128)}, f32[256,512]{1,0:T(8,128)}) custom-call(bf16[8,80,128]{2,1,0:T(8,128)(2,1)} %shard_map.110.refs_0_, bf16[256,128]{1,0:T(8,128)(2,1)} %refs_1_.3, bf16[256,128]{1,0:T(8,128)(2,1)} %refs_2_.1, f32[32,256]{1,0:T(8,128)} %get-tuple-element.25.refs_3_, f32[1,8]{1,0:T(1,128)} %bitcast.14, bf16[256,512]{1,0:T(8,128)(2,1)} %refs_5_.3, ...), custom_call_target="tpu_custom_call" | custom-call | flops 67108864 | bytes 8388608 | tf_op jit(solution)/shard_map/pallas_call | solution.py:257
  28.1 5.5 %all-to-all-done.1.planes_ref = bf16[8,80,128]{2,1,0:T(8,128)(2,1)S(1)} async-done(((bf16[8,80,128]{2,1,0:T(8,128)(2,1)}), bf16[8,80,128]{2,1,0:T(8,128)(2,1)S(1)}, u32[]{:S(2)}, u32[]{:S(2)}) %all-to-all-start.1) | async-done | bytes 163872 | tf_op jit(solution)/shard_map/all_to_all | solution.py:314
  33.7 0.7 shard_map.112.refs_0_
  34.4 3.4 %all-to-all-start.2 = ((bf16[8,64,128]{2,1,0:T(8,128)(2,1)}), bf16[8,64,128]{2,1,0:T(8,128)(2,1)S(1)}, u32[]{:S(2)}, u32[]{:S(2)}) async-start(bf16[8,64,128]{2,1,0:T(8,128)(2,1)} %shard_map.112.refs_0_), calls=%async_computation.2 | async-start | bytes 262144 | tf_op jit(solution)/shard_map/all_to_all | solution.py:329
  37.8 0.0 copy-start
  37.8 1.0 %copy-done = f32[256,512]{1,0:T(8,128)S(1)} copy-done((f32[256,512]{1,0:T(8,128)S(1)}, f32[256,512]{1,0:T(8,128)}, u32[]{:S(2)}) %copy-start) | copy-done | bytes 524312
  38.8 0.0 copy-start.1
  38.8 1.0 %copy-done.1 = f32[256,512]{1,0:T(8,128)S(1)} copy-done((f32[256,512]{1,0:T(8,128)S(1)}, f32[256,512]{1,0:T(8,128)}, u32[]{:S(2)}) %copy-start.1) | copy-done | bytes 524312
  39.9 0.0 copy-start.2
  39.9 0.8 copy-done.2
  40.7 0.0 copy-start.3
  40.7 0.7 copy-done.3
  41.4 0.2 shard_map.113
  41.6 2.2 %all-to-all-done.2.entry_ref = bf16[8,64,128]{2,1,0:T(8,128)(2,1)S(1)} async-done(((bf16[8,64,128]{2,1,0:T(8,128)(2,1)}), bf16[8,64,128]{2,1,0:T(8,128)(2,1)S(1)}, u32[]{:S(2)}, u32[]{:S(2)}) %all-to-all-start.2) | async-done | bytes 131104 | tf_op jit(solution)/shard_map/all_to_all | solution.py:329
  43.8 2.0 %shard_map.114 = (bf16[272,512]{1,0:T(8,128)(2,1)S(1)}, bf16[272,512]{1,0:T(8,128)(2,1)S(1)}, bf16[1,256,512]{2,1,0:T(8,128)(2,1)S(1)}) custom-call(s32[1]{0:T(128)} %bitcast.me, s32[1]{0:T(128)} %bitcast.1.way, bf16[8,64,128]{2,1,0:T(8,128)(2,1)S(1)} %all-to-all-done.2.entry_ref, bf16[256,128]{1,0:T(8,128)(2,1)S(1)} %get-tuple-element.30.c_ref, ...), custom_call_target="tpu_custom_call" | custom-call | flops 268435456 | bytes 2097152 | tf_op jit(solution)/shard_map/pallas_call | solution.py:257
  45.8 4.7 %collective-permute-start = (bf16[272,512]{1,0:T(8,128)(2,1)S(1)}, bf16[272,512]{1,0:T(8,128)(2,1)S(1)}, u32[]{:S(2)}, u32[]{:S(2)}) collective-permute-start(bf16[272,512]{1,0:T(8,128)(2,1)S(1)} %get-tuple-element.36), channel_id=1, source_target_pairs={{0,1},{1,2},{2,3},{3,4},{4,5},{5,6},{6,7},{7,0},{8,15},{9,8},{10,9... | collective-permute-start | bytes 835592 | tf_op jit(solution)/shard_map/ppermute | solution.py:341
  50.5 1.9 %collective-permute-start.1 = (bf16[272,512]{1,0:T(8,128)(2,1)S(1)}, bf16[272,512]{1,0:T(8,128)(2,1)S(1)}, u32[]{:S(2)}, u32[]{:S(2)}) collective-permute-start(bf16[272,512]{1,0:T(8,128)(2,1)S(1)} %get-tuple-element.37.gated_ref.own_ref), channel_id=1, source_target_pairs={{0,8},{1,9},{2,10},{3,11},{4,12},{5,13},{6,14},{7,15},{8,0},{9,1},... | collective-permute-start | bytes 835592 | tf_op jit(solution)/shard_map/ppermute | solution.py:341
  52.5 2.1 %collective-permute-done.refs_0_ = bf16[272,512]{1,0:T(8,128)(2,1)S(1)} collective-permute-done((bf16[272,512]{1,0:T(8,128)(2,1)S(1)}, bf16[272,512]{1,0:T(8,128)(2,1)S(1)}, u32[]{:S(2)}, u32[]{:S(2)}) %collective-permute-start) | collective-permute-done | bytes 278560 | tf_op jit(solution)/shard_map/ppermute | solution.py:341
  54.6 0.1 shard_map.115
  54.7 5.6 %collective-permute-start.2 = (bf16[272,512]{1,0:T(8,128)(2,1)S(1)}, bf16[272,512]{1,0:T(8,128)(2,1)S(1)}, u32[]{:S(2)}, u32[]{:S(2)}) collective-permute-start(bf16[272,512]{1,0:T(8,128)(2,1)S(1)} %shard_map.115), channel_id=1, source_target_pairs={{0,1},{1,2},{2,3},{3,4},{4,5},{5,6},{6,7},{7,0},{8,15},{9,8},{10,9... | collective-permute-start | bytes 835592 | tf_op jit(solution)/shard_map/ppermute | solution.py:341
  60.3 0.0 collective-permute-done.1.other_ref.gated_ref
  60.3 2.6 %shard_map.116 = (bf16[272,512]{1,0:T(8,128)(2,1)S(1)}, bf16[2,2,256,512]{3,2,1,0:T(8,128)(2,1)S(1)}, bf16[256,512]{1,0:T(8,128)(2,1)S(1)}) custom-call(s32[1]{0:T(128)} %bitcast.me, s32[1]{0:T(128)} %bitcast.1.way, bf16[272,512]{1,0:T(8,128)(2,1)S(1)} %get-tuple-element.37.gated_ref.own_ref, ...), custom_call_target="tpu_custom_call" | custom-call | flops 805306368 | bytes 4194304 | tf_op jit(solution)/shard_map/pallas_call | solution.py:257
  62.9 1.9 %collective-permute-start.5 = (bf16[272,512]{1,0:T(8,128)(2,1)S(1)}, bf16[272,512]{1,0:T(8,128)(2,1)S(1)}, u32[]{:S(2)}, u32[]{:S(2)}) collective-permute-start(bf16[272,512]{1,0:T(8,128)(2,1)S(1)} %get-tuple-element.42), channel_id=1, source_target_pairs={{0,1},{1,2},{2,3},{3,4},{4,5},{5,6},{6,7},{7,0},{8,15},{9,8},{10,9... | collective-permute-start | bytes 835592 | tf_op jit(solution)/shard_map/ppermute | solution.py:341
  64.8 0.0 collective-permute-done.2.refs_0_
  64.9 0.1 shard_map.117
  64.9 5.1 %collective-permute-start.3 = (bf16[272,512]{1,0:T(8,128)(2,1)S(1)}, bf16[272,512]{1,0:T(8,128)(2,1)S(1)}, u32[]{:S(2)}, u32[]{:S(2)}) collective-permute-start(bf16[272,512]{1,0:T(8,128)(2,1)S(1)} %shard_map.117), channel_id=1, source_target_pairs={{0,1},{1,2},{2,3},{3,4},{4,5},{5,6},{6,7},{7,0},{8,15},{9,8},{10,9... | collective-permute-start | bytes 835592 | tf_op jit(solution)/shard_map/ppermute | solution.py:341
  70.0 1.3 %collective-permute-done.5.refs_0_ = bf16[272,512]{1,0:T(8,128)(2,1)S(1)} collective-permute-done((bf16[272,512]{1,0:T(8,128)(2,1)S(1)}, bf16[272,512]{1,0:T(8,128)(2,1)S(1)}, u32[]{:S(2)}, u32[]{:S(2)}) %collective-permute-start.5) | collective-permute-done | bytes 278560 | tf_op jit(solution)/shard_map/ppermute | solution.py:341
  71.4 0.1 shard_map.120
  71.4 3.1 %collective-permute-start.6 = (bf16[272,512]{1,0:T(8,128)(2,1)S(1)}, bf16[272,512]{1,0:T(8,128)(2,1)S(1)}, u32[]{:S(2)}, u32[]{:S(2)}) collective-permute-start(bf16[272,512]{1,0:T(8,128)(2,1)S(1)} %shard_map.120), channel_id=1, source_target_pairs={{0,1},{1,2},{2,3},{3,4},{4,5},{5,6},{6,7},{7,0},{8,15},{9,8},{10,9... | collective-permute-start | bytes 835592 | tf_op jit(solution)/shard_map/ppermute | solution.py:341
  74.6 0.0 collective-permute-done.3.refs_0_
  74.6 0.1 shard_map.118
  74.7 5.1 %collective-permute-start.4 = (bf16[272,512]{1,0:T(8,128)(2,1)S(1)}, bf16[272,512]{1,0:T(8,128)(2,1)S(1)}, u32[]{:S(2)}, u32[]{:S(2)}) collective-permute-start(bf16[272,512]{1,0:T(8,128)(2,1)S(1)} %shard_map.118), channel_id=1, source_target_pairs={{0,1},{1,2},{2,3},{3,4},{4,5},{5,6},{6,7},{7,0},{8,15},{9,8},{10,9... | collective-permute-start | bytes 835592 | tf_op jit(solution)/shard_map/ppermute | solution.py:341
  79.8 0.1 collective-permute-done.6.refs_0_
  79.9 0.1 shard_map.121
  80.0 1.9 %collective-permute-start.7 = (bf16[272,512]{1,0:T(8,128)(2,1)S(1)}, bf16[272,512]{1,0:T(8,128)(2,1)S(1)}, u32[]{:S(2)}, u32[]{:S(2)}) collective-permute-start(bf16[272,512]{1,0:T(8,128)(2,1)S(1)} %shard_map.121), channel_id=1, source_target_pairs={{0,9},{1,10},{2,11},{3,12},{4,13},{5,14},{6,15},{7,8},{8,7},{9,0},... | collective-permute-start | bytes 835592 | tf_op jit(solution)/shard_map/ppermute | solution.py:341
  81.9 1.9 %collective-permute-done.4.got_ref = bf16[272,512]{1,0:T(8,128)(2,1)S(1)} collective-permute-done((bf16[272,512]{1,0:T(8,128)(2,1)S(1)}, bf16[272,512]{1,0:T(8,128)(2,1)S(1)}, u32[]{:S(2)}, u32[]{:S(2)}) %collective-permute-start.4) | collective-permute-done | bytes 278560 | tf_op jit(solution)/shard_map/ppermute | solution.py:341
  83.8 0.1 shard_map.119
  83.9 5.2 %collective-permute-done.7.got_ref = bf16[272,512]{1,0:T(8,128)(2,1)S(1)} collective-permute-done((bf16[272,512]{1,0:T(8,128)(2,1)S(1)}, bf16[272,512]{1,0:T(8,128)(2,1)S(1)}, u32[]{:S(2)}, u32[]{:S(2)}) %collective-permute-start.7) | collective-permute-done | bytes 278560 | tf_op jit(solution)/shard_map/ppermute | solution.py:341
  89.0 0.8 shard_map.122
Async XLA Ops:
  13.8 19.9 %all-to-all-start.1 = ((bf16[8,80,128]{2,1,0:T(8,128)(2,1)}), bf16[8,80,128]{2,1,0:T(8,128)(2,1)S(1)}, u32[]{:S(2)}, u32[]{:S(2)}) async-start(bf16[8,80,128]{2,1,0:T(8,128)(2,1)} %shard_map.110.refs_0_), calls=%async_computation.1 | async-start | bytes 327680 | tf_op jit(solution)/shard_map/all_to_all | solution.py:314
  34.4 9.4 %all-to-all-start.2 = ((bf16[8,64,128]{2,1,0:T(8,128)(2,1)}), bf16[8,64,128]{2,1,0:T(8,128)(2,1)S(1)}, u32[]{:S(2)}, u32[]{:S(2)}) async-start(bf16[8,64,128]{2,1,0:T(8,128)(2,1)} %shard_map.112.refs_0_), calls=%async_computation.2 | async-start | bytes 262144 | tf_op jit(solution)/shard_map/all_to_all | solution.py:329
  37.8 1.0 %copy-start = (f32[256,512]{1,0:T(8,128)S(1)}, f32[256,512]{1,0:T(8,128)}, u32[]{:S(2)}) copy-start(f32[256,512]{1,0:T(8,128)} %get-tuple-element.28.refs_2_) | copy-start | bytes 1572868
  38.8 1.0 %copy-start.1 = (f32[256,512]{1,0:T(8,128)S(1)}, f32[256,512]{1,0:T(8,128)}, u32[]{:S(2)}) copy-start(f32[256,512]{1,0:T(8,128)} %get-tuple-element.29.refs_3_) | copy-start | bytes 1572868
  39.9 0.8 copy-start.2
  40.7 0.7 copy-start.3
  45.8 8.7 %collective-permute-start = (bf16[272,512]{1,0:T(8,128)(2,1)S(1)}, bf16[272,512]{1,0:T(8,128)(2,1)S(1)}, u32[]{:S(2)}, u32[]{:S(2)}) collective-permute-start(bf16[272,512]{1,0:T(8,128)(2,1)S(1)} %get-tuple-element.36), channel_id=1, source_target_pairs={{0,1},{1,2},{2,3},{3,4},{4,5},{5,6},{6,7},{7,0},{8,15},{9,8},{10,9... | collective-permute-start | bytes 835592 | tf_op jit(solution)/shard_map/ppermute | solution.py:341
  50.5 9.7 %collective-permute-start.1 = (bf16[272,512]{1,0:T(8,128)(2,1)S(1)}, bf16[272,512]{1,0:T(8,128)(2,1)S(1)}, u32[]{:S(2)}, u32[]{:S(2)}) collective-permute-start(bf16[272,512]{1,0:T(8,128)(2,1)S(1)} %get-tuple-element.37.gated_ref.own_ref), channel_id=1, source_target_pairs={{0,8},{1,9},{2,10},{3,11},{4,12},{5,13},{6,14},{7,15},{8,0},{9,1},... | collective-permute-start | bytes 835592 | tf_op jit(solution)/shard_map/ppermute | solution.py:341
  54.7 10.2 %collective-permute-start.2 = (bf16[272,512]{1,0:T(8,128)(2,1)S(1)}, bf16[272,512]{1,0:T(8,128)(2,1)S(1)}, u32[]{:S(2)}, u32[]{:S(2)}) collective-permute-start(bf16[272,512]{1,0:T(8,128)(2,1)S(1)} %shard_map.115), channel_id=1, source_target_pairs={{0,1},{1,2},{2,3},{3,4},{4,5},{5,6},{6,7},{7,0},{8,15},{9,8},{10,9... | collective-permute-start | bytes 835592 | tf_op jit(solution)/shard_map/ppermute | solution.py:341
  62.9 8.4 %collective-permute-start.5 = (bf16[272,512]{1,0:T(8,128)(2,1)S(1)}, bf16[272,512]{1,0:T(8,128)(2,1)S(1)}, u32[]{:S(2)}, u32[]{:S(2)}) collective-permute-start(bf16[272,512]{1,0:T(8,128)(2,1)S(1)} %get-tuple-element.42), channel_id=1, source_target_pairs={{0,1},{1,2},{2,3},{3,4},{4,5},{5,6},{6,7},{7,0},{8,15},{9,8},{10,9... | collective-permute-start | bytes 835592 | tf_op jit(solution)/shard_map/ppermute | solution.py:341
  64.9 9.6 %collective-permute-start.3 = (bf16[272,512]{1,0:T(8,128)(2,1)S(1)}, bf16[272,512]{1,0:T(8,128)(2,1)S(1)}, u32[]{:S(2)}, u32[]{:S(2)}) collective-permute-start(bf16[272,512]{1,0:T(8,128)(2,1)S(1)} %shard_map.117), channel_id=1, source_target_pairs={{0,1},{1,2},{2,3},{3,4},{4,5},{5,6},{6,7},{7,0},{8,15},{9,8},{10,9... | collective-permute-start | bytes 835592 | tf_op jit(solution)/shard_map/ppermute | solution.py:341
  71.4 8.4 %collective-permute-start.6 = (bf16[272,512]{1,0:T(8,128)(2,1)S(1)}, bf16[272,512]{1,0:T(8,128)(2,1)S(1)}, u32[]{:S(2)}, u32[]{:S(2)}) collective-permute-start(bf16[272,512]{1,0:T(8,128)(2,1)S(1)} %shard_map.120), channel_id=1, source_target_pairs={{0,1},{1,2},{2,3},{3,4},{4,5},{5,6},{6,7},{7,0},{8,15},{9,8},{10,9... | collective-permute-start | bytes 835592 | tf_op jit(solution)/shard_map/ppermute | solution.py:341
  74.7 9.1 %collective-permute-start.4 = (bf16[272,512]{1,0:T(8,128)(2,1)S(1)}, bf16[272,512]{1,0:T(8,128)(2,1)S(1)}, u32[]{:S(2)}, u32[]{:S(2)}) collective-permute-start(bf16[272,512]{1,0:T(8,128)(2,1)S(1)} %shard_map.118), channel_id=1, source_target_pairs={{0,1},{1,2},{2,3},{3,4},{4,5},{5,6},{6,7},{7,0},{8,15},{9,8},{10,9... | collective-permute-start | bytes 835592 | tf_op jit(solution)/shard_map/ppermute | solution.py:341
  80.0 9.1 %collective-permute-start.7 = (bf16[272,512]{1,0:T(8,128)(2,1)S(1)}, bf16[272,512]{1,0:T(8,128)(2,1)S(1)}, u32[]{:S(2)}, u32[]{:S(2)}) collective-permute-start(bf16[272,512]{1,0:T(8,128)(2,1)S(1)} %shard_map.121), channel_id=1, source_target_pairs={{0,9},{1,10},{2,11},{3,12},{4,13},{5,14},{6,15},{7,8},{8,7},{9,0},... | collective-permute-start | bytes 835592 | tf_op jit(solution)/shard_map/ppermute | solution.py:341

commit v13 on v11

--- a/solution.py
+++ b/solution.py
@@ -99,9 +99,9 @@
 
 
 def intra_kernel(*refs):
-    own_ref, open_ref = refs[7:9]
-    c_ref, b_ref, rows_ref, skip_ref, x_ref, z_ref, cols_ref = refs[9:16]
-    for copy in fetch(refs[1:7], refs[9:15], refs[16]):
+    out_ref = refs[8]
+    c_ref, b_ref, rows_ref, skip_ref, x_ref, z_ref, gain_ref, cols_ref = refs[9:17]
+    for copy in fetch(refs[1:8], refs[9:16], refs[17]):
         copy.wait()
     rows = rows_ref[...]
     cols_ref[...] = jnp.concatenate([rows, jnp.zeros((128 - rows.shape[0], rows.shape[1]), F32)], axis=0).T
@@ -125,8 +125,9 @@
         out = jnp.dot(mixing, x_h, preferred_element_type=F32) + skip[:, h : h + 1] * x_h.astype(F32)
         v = z_ref[:, span].astype(F32)
         gate = v / (1.0 + jnp.exp(-v))
-        own_ref[:, span] = out * gate
-        open_ref[:, span] = gate * cols_ref[:, 3 * heads + h : 3 * heads + h + 1]
+        out_ref[:tokens, span] = out * gate
+        out_ref[tokens : 2 * tokens, span] = gate * cols_ref[:, 3 * heads + h : 3 * heads + h + 1]
+    out_ref[2 * tokens :] = jnp.broadcast_to(gain_ref[...], (8, x_ref.shape[1]))
 
 
 def plane_kernel(got_ref, out_ref):
@@ -186,17 +187,17 @@
     return w_hbm.at[:, pl.ds(pl.multiple_of(place * features, features), features)]
 
 
-def gate_kernel(me, way, entry_ref, c_ref, own_ref, open_ref, gain_ref, w_hbm, *refs):
+def gate_kernel(me, way, entry_ref, c_ref, gates_ref, w_hbm, *refs):
     gated_ref, far_ref, next_ref, w_ref, sems = refs
     heads, width, lanes = entry_ref.shape
-    tokens = own_ref.shape[0]
+    tokens = c_ref.shape[0]
     features = w_ref.shape[1]
     wanted = [columns(w_hbm, me[0], away, features) for away in (N_PART // 2, (N_PART // 2 - 1) * way[0])]
     copies = fetch(wanted, [w_ref, next_ref], sems)
     entries = entry_ref[...].reshape(heads * width, lanes)
     carried = lax.dot_general(c_ref[...], entries, (((1,), (1,)), ((), ())), preferred_element_type=F32)
-    gated = own_ref[...] + open_ref[...] * carried
-    scaled = (gated * gain_ref[...]).astype(BF16)
+    gated = gates_ref[:tokens] + gates_ref[tokens : 2 * tokens] * carried
+    scaled = (gated * gates_ref[2 * tokens : 2 * tokens + 1]).astype(BF16)
     gated_ref[:tokens] = scaled
     squares = jnp.sum(gated * gated, axis=1, keepdims=True)
     squares = jnp.broadcast_to(squares, (tokens, 128)).T[:1]
@@ -302,11 +303,11 @@
     skip = skip_gain.reshape(1, heads)
     gain = norm_gain.reshape(1, channels)
     (totals,) = call(plane_kernel, [VMEM], [((planes, *sent), BF16)], (got,), moved=2**19)
-    near = (input_c, input_b, rows, skip, input_x, input_z)
-    own, opened = call(
+    near = (input_c, input_b, rows, skip, input_x, input_z, gain)
+    (gates,) = call(
         intra_kernel,
-        [ANY] + [HBM] * 6,
-        [((tokens, channels), F32)] * 2,
+        [ANY] + [HBM] * 7,
+        [((2 * tokens + 8, channels), F32)],
         (totals, *near),
         scratch=(*near, jax.ShapeDtypeStruct((tokens, 128), F32)),
         limit=60,
@@ -314,12 +315,12 @@
         moved=8 * 2**20,
     )
     got_planes = lax.all_to_all(totals, "seq", 0, 0, axis_index_groups=across)
-    got_planes, own = lax.optimization_barrier((got_planes, own))
+    got_planes, gates = lax.optimization_barrier((got_planes, gates))
     plane = lax.div(lax.axis_index("seq"), N_ROW).reshape(1)
     (entries,) = call(
         entry_kernel, [SMEM, VMEM, VMEM], [((N_ROW, width, state_width), BF16)], (plane, got, got_planes), moved=2**19
     )
-    needed = (input_c, own, opened, gain)
+    needed = (input_c, gates)
     needed = call(
         bring_kernel,
         [ANY] + [HBM] * len(needed),
@@ -344,7 +345,7 @@
 
     gated, far, w_next = call(
         gate_kernel,
-        [SMEM] * 2 + [VMEM] * 5 + [HBM],
+        [SMEM] * 2 + [VMEM] * 3 + [HBM],
         [slab, slab, ((channels, features), BF16)],
         (me, way, entries, *needed, out_weight),
         scratch=[jax.ShapeDtypeStruct((channels, features), BF16)],

time: 88 us -> 87.9 us (level)
  local copies, waits for them, and re-layouts: 3.6 us -> 1.23 us
  waiting for transfers between devices: 28.3 us -> 30.6 us
    unnamed x8 -> x4, local copies, waits for them, and re-layouts: 3.6 us -> 1.23 us
    all_to_all x1, waiting for transfers between devices: 2.23 us -> 4.58 us  [body(): entries = lax.all_to_all(entries, 'seq', 0, 0, axis_index_groups=in_plane)]
where the time goes in v13:
time: 87.9 us; the launch traced here: 87.2 us
  waiting for transfers between devices  30.6 us (35%)
  starting transfers between devices  30.5 us (35%)
  Pallas kernels  13.8 us (16%)
  blocking collectives  10.8 us (12%)
  local copies, waits for them, and re-layouts  1.23 us (1%)
    ppermute x8, waiting for transfers between devices, send(): return lax.ppermute(array, ('seq', 'head'), pairs)  20.6 us
    ppermute x8, starting transfers between devices, send(): return lax.ppermute(array, ('seq', 'head'), pairs)  16.8 us
    pallas_call x16, Pallas kernels, call(): pl.pallas_call(kernel, in_specs=ins, out_specs=[VMEM] * len(outs), out_sh...  13.8 us
    all_to_all x1, blocking collectives, body(): got = lax.all_to_all(pieces, 'seq', 0, 0, axis_index_groups=in_plane)  10.8 us
    all_to_all x1, starting transfers between devices, body(): got_planes = lax.all_to_all(totals, 'seq', 0, 0, axis_index_groups=across)  10.3 us
    all_to_all x1, waiting for transfers between devices, body(): got_planes = lax.all_to_all(totals, 'seq', 0, 0, axis_index_groups=across)  5.48 us
    all_to_all x1, waiting for transfers between devices, body(): entries = lax.all_to_all(entries, 'seq', 0, 0, axis_index_groups=in_plane)  4.58 us
    all_to_all x1, starting transfers between devices, body(): entries = lax.all_to_all(entries, 'seq', 0, 0, axis_index_groups=in_plane)  3.37 us
  transfers between devices with their start and end apart: 10, of which 8 were waited for; matrix products, arithmetic and copies ran while one was open for 0% of the time, Pallas kernels for 9%

profile of v13, /device:TPU:32, one launch (start us, length us, event | category | flops | bytes accessed | tf_op | source)
XLA Modules:
  0.0 87.2 jit_solution(7530738153134921008)
XLA Ops:
  0.0 2.3 %shard_map.109 = (bf16[8,80,128]{2,1,0:T(8,128)(2,1)}, f32[32,256]{1,0:T(8,128)}) custom-call(f32[1,8]{1,0:T(1,128)} %bitcast.12, f32[1,8]{1,0:T(1,128)} %bitcast.13, f32[8,256]{1,0:T(8,128)} %bitcast.9, s32[1,256]{1,0:T(1,128)} %bitcast.11, bf16[256,128]{1,0:T(8,128)(2,1)} %refs_2_.1, bf16[256,512]{1,0:T(8,128)(2,1)} %refs_5_.3), custom_call_target="tpu_custom_call" | custom-call | flops 33554432 | bytes 262144 | tf_op jit(solution)/shard_map/pallas_call | solution.py:260
  2.3 10.8 %all_to_all.15.got_ref = bf16[8,80,128]{2,1,0:T(8,128)(2,1)S(1)} all-to-all(bf16[8,80,128]{2,1,0:T(8,128)(2,1)} %get-tuple-element.19), channel_id=1, replica_groups={{0,8,16,24,32,40,48,56},{64,72,80,88,96,104,112,120},{128,136,144,152,1..., dimensions={0} | all-to-all | bytes 327680 | tf_op jit(solution)/shard_map/all_to_all | solution.py:302
  13.1 0.7 shard_map.110.refs_0_
  13.8 10.3 %all-to-all-start.1 = ((bf16[8,80,128]{2,1,0:T(8,128)(2,1)}), bf16[8,80,128]{2,1,0:T(8,128)(2,1)S(1)}, u32[]{:S(2)}, u32[]{:S(2)}) async-start(bf16[8,80,128]{2,1,0:T(8,128)(2,1)} %shard_map.110.refs_0_), calls=%async_computation.1 | async-start | bytes 327680 | tf_op jit(solution)/shard_map/all_to_all | solution.py:317
  24.1 0.0 copy-start.1
  24.1 4.0 %shard_map.111.refs_2_ = f32[520,512]{1,0:T(8,128)} custom-call(bf16[8,80,128]{2,1,0:T(8,128)(2,1)} %shard_map.110.refs_0_, bf16[256,128]{1,0:T(8,128)(2,1)} %refs_1_.3, bf16[256,128]{1,0:T(8,128)(2,1)} %refs_2_.1, f32[32,256]{1,0:T(8,128)} %get-tuple-element.20.refs_3_, f32[1,8]{1,0:T(1,128)} %bitcast.14, bf16[256,512]{1,0:T(8,128)(2,1)} %refs_5_.3, ...), custom_call_target="tpu_custom_call" | custom-call | flops 67108864 | bytes 8388608 | tf_op jit(solution)/shard_map/pallas_call | solution.py:260
  28.2 5.5 %all-to-all-done.1.planes_ref = bf16[8,80,128]{2,1,0:T(8,128)(2,1)S(1)} async-done(((bf16[8,80,128]{2,1,0:T(8,128)(2,1)}), bf16[8,80,128]{2,1,0:T(8,128)(2,1)S(1)}, u32[]{:S(2)}, u32[]{:S(2)}) %all-to-all-start.1) | async-done | bytes 163872 | tf_op jit(solution)/shard_map/all_to_all | solution.py:317
  33.7 0.7 shard_map.112.refs_0_
  34.4 3.4 %all-to-all-start.2 = ((bf16[8,64,128]{2,1,0:T(8,128)(2,1)}), bf16[8,64,128]{2,1,0:T(8,128)(2,1)S(1)}, u32[]{:S(2)}, u32[]{:S(2)}) async-start(bf16[8,64,128]{2,1,0:T(8,128)(2,1)} %shard_map.112.refs_0_), calls=%async_computation.2 | async-start | bytes 262144 | tf_op jit(solution)/shard_map/all_to_all | solution.py:332
  37.8 0.0 copy-done.1
  37.8 0.0 copy-start
  37.8 1.2 %copy-done = f32[520,512]{1,0:T(8,128)S(1)} copy-done((f32[520,512]{1,0:T(8,128)S(1)}, f32[520,512]{1,0:T(8,128)}, u32[]{:S(2)}) %copy-start) | copy-done | bytes 1064984
  39.0 0.2 shard_map.113
  39.3 4.6 %all-to-all-done.2.entry_ref = bf16[8,64,128]{2,1,0:T(8,128)(2,1)S(1)} async-done(((bf16[8,64,128]{2,1,0:T(8,128)(2,1)}), bf16[8,64,128]{2,1,0:T(8,128)(2,1)S(1)}, u32[]{:S(2)}, u32[]{:S(2)}) %all-to-all-start.2) | async-done | bytes 131104 | tf_op jit(solution)/shard_map/all_to_all | solution.py:332
  43.8 1.7 %shard_map.114 = (bf16[272,512]{1,0:T(8,128)(2,1)S(1)}, bf16[272,512]{1,0:T(8,128)(2,1)S(1)}, bf16[512,512]{1,0:T(8,128)(2,1)S(1)}) custom-call(s32[1]{0:T(128)} %bitcast.me, s32[1]{0:T(128)} %bitcast.1.way, bf16[8,64,128]{2,1,0:T(8,128)(2,1)S(1)} %all-to-all-done.2.entry_ref, bf16[256,128]{1,0:T(8,128)(2,1)S(1)} %get-tuple-element.23.c_ref, ...), custom_call_target="tpu_custom_call" | custom-call | flops 134217728 | bytes 2097152 | tf_op jit(solution)/shard_map/pallas_call | solution.py:260
  45.5 1.9 %collective-permute-start = (bf16[272,512]{1,0:T(8,128)(2,1)S(1)}, bf16[272,512]{1,0:T(8,128)(2,1)S(1)}, u32[]{:S(2)}, u32[]{:S(2)}) collective-permute-start(bf16[272,512]{1,0:T(8,128)(2,1)S(1)} %get-tuple-element.28.own_ref.gated_ref), channel_id=1, source_target_pairs={{0,8},{1,9},{2,10},{3,11},{4,12},{5,13},{6,14},{7,15},{8,0},{9,1},... | collective-permute-start | bytes 835592 | tf_op jit(solution)/shard_map/ppermute | solution.py:344
  47.5 2.6 %collective-permute-start.1 = (bf16[272,512]{1,0:T(8,128)(2,1)S(1)}, bf16[272,512]{1,0:T(8,128)(2,1)S(1)}, u32[]{:S(2)}, u32[]{:S(2)}) collective-permute-start(bf16[272,512]{1,0:T(8,128)(2,1)S(1)} %get-tuple-element.27), channel_id=1, source_target_pairs={{0,1},{1,2},{2,3},{3,4},{4,5},{5,6},{6,7},{7,0},{8,15},{9,8},{10,9... | collective-permute-start | bytes 835592 | tf_op jit(solution)/shard_map/ppermute | solution.py:344
  50.1 0.0 collective-permute-done.other_ref.gated_ref
  50.1 0.4 shard_map.115.chunk_ref
  50.5 2.6 %collective-permute-start.2 = (bf16[272,512]{1,0:T(8,128)(2,1)S(1)}, bf16[272,512]{1,0:T(8,128)(2,1)S(1)}, u32[]{:S(2)}, u32[]{:S(2)}) collective-permute-start(bf16[272,512]{1,0:T(8,128)(2,1)S(1)} %shard_map.118), channel_id=1, source_target_pairs={{0,1},{1,2},{2,3},{3,4},{4,5},{5,6},{6,7},{7,0},{8,15},{9,8},{10,9... | collective-permute-start | bytes 835592 | tf_op jit(solution)/shard_map/ppermute | solution.py:344
  53.2 4.0 %collective-permute-done.1.refs_0_ = bf16[272,512]{1,0:T(8,128)(2,1)S(1)} collective-permute-done((bf16[272,512]{1,0:T(8,128)(2,1)S(1)}, bf16[272,512]{1,0:T(8,128)(2,1)S(1)}, u32[]{:S(2)}, u32[]{:S(2)}) %collective-permute-start.1) | collective-permute-done | bytes 278560 | tf_op jit(solution)/shard_map/ppermute | solution.py:344
  57.1 0.1 shard_map.116
  57.2 1.9 %collective-permute-start.5 = (bf16[272,512]{1,0:T(8,128)(2,1)S(1)}, bf16[272,512]{1,0:T(8,128)(2,1)S(1)}, u32[]{:S(2)}, u32[]{:S(2)}) collective-permute-start(bf16[272,512]{1,0:T(8,128)(2,1)S(1)} %shard_map.116), channel_id=1, source_target_pairs={{0,1},{1,2},{2,3},{3,4},{4,5},{5,6},{6,7},{7,0},{8,15},{9,8},{10,9... | collective-permute-start | bytes 835592 | tf_op jit(solution)/shard_map/ppermute | solution.py:344
  59.1 2.3 %shard_map.117 = (bf16[2,2,256,512]{3,2,1,0:T(8,128)(2,1)S(1)}, bf16[256,512]{1,0:T(8,128)(2,1)S(1)}) custom-call(s32[1]{0:T(128)} %bitcast.me, s32[1]{0:T(128)} %bitcast.1.way, bf16[272,512]{1,0:T(8,128)(2,1)S(1)} %get-tuple-element.28.own_ref.gated_ref, bf16[272,512]{1,0:T(8,128)(2,1)S(1)} %collective-permute-done.other_ref.gated_ref, bf16[512,4096]{1,0:T(8,128)(2,1)} %w_hbm.3), custom_call_target="tpu_custom_call" | custom-call | flops 671088640 | bytes 2097152 | tf_op jit(solution)/shard_map/pallas_call | solution.py:260
  61.4 0.0 collective-permute-done.2.refs_0_
  61.5 0.1 shard_map.119
  61.5 2.0 %collective-permute-start.3 = (bf16[272,512]{1,0:T(8,128)(2,1)S(1)}, bf16[272,512]{1,0:T(8,128)(2,1)S(1)}, u32[]{:S(2)}, u32[]{:S(2)}) collective-permute-start(bf16[272,512]{1,0:T(8,128)(2,1)S(1)} %shard_map.119), channel_id=1, source_target_pairs={{0,1},{1,2},{2,3},{3,4},{4,5},{5,6},{6,7},{7,0},{8,15},{9,8},{10,9... | collective-permute-start | bytes 835592 | tf_op jit(solution)/shard_map/ppermute | solution.py:344
  63.6 3.2 %collective-permute-done.5.refs_0_ = bf16[272,512]{1,0:T(8,128)(2,1)S(1)} collective-permute-done((bf16[272,512]{1,0:T(8,128)(2,1)S(1)}, bf16[272,512]{1,0:T(8,128)(2,1)S(1)}, u32[]{:S(2)}, u32[]{:S(2)}) %collective-permute-start.5) | collective-permute-done | bytes 278560 | tf_op jit(solution)/shard_map/ppermute | solution.py:344
  66.9 0.1 shard_map.122
  66.9 1.9 %collective-permute-start.6 = (bf16[272,512]{1,0:T(8,128)(2,1)S(1)}, bf16[272,512]{1,0:T(8,128)(2,1)S(1)}, u32[]{:S(2)}, u32[]{:S(2)}) collective-permute-start(bf16[272,512]{1,0:T(8,128)(2,1)S(1)} %shard_map.122), channel_id=1, source_target_pairs={{0,1},{1,2},{2,3},{3,4},{4,5},{5,6},{6,7},{7,0},{8,15},{9,8},{10,9... | collective-permute-start | bytes 835592 | tf_op jit(solution)/shard_map/ppermute | solution.py:344
  68.9 2.3 %collective-permute-done.3.refs_0_ = bf16[272,512]{1,0:T(8,128)(2,1)S(1)} collective-permute-done((bf16[272,512]{1,0:T(8,128)(2,1)S(1)}, bf16[272,512]{1,0:T(8,128)(2,1)S(1)}, u32[]{:S(2)}, u32[]{:S(2)}) %collective-permute-start.3) | collective-permute-done | bytes 278560 | tf_op jit(solution)/shard_map/ppermute | solution.py:344
  71.2 0.1 shard_map.120
  71.3 1.9 %collective-permute-start.4 = (bf16[272,512]{1,0:T(8,128)(2,1)S(1)}, bf16[272,512]{1,0:T(8,128)(2,1)S(1)}, u32[]{:S(2)}, u32[]{:S(2)}) collective-permute-start(bf16[272,512]{1,0:T(8,128)(2,1)S(1)} %shard_map.120), channel_id=1, source_target_pairs={{0,9},{1,10},{2,11},{3,12},{4,13},{5,14},{6,15},{7,8},{8,7},{9,0},... | collective-permute-start | bytes 835592 | tf_op jit(solution)/shard_map/ppermute | solution.py:344
  73.2 3.4 %collective-permute-done.6.refs_0_ = bf16[272,512]{1,0:T(8,128)(2,1)S(1)} collective-permute-done((bf16[272,512]{1,0:T(8,128)(2,1)S(1)}, bf16[272,512]{1,0:T(8,128)(2,1)S(1)}, u32[]{:S(2)}, u32[]{:S(2)}) %collective-permute-start.6) | collective-permute-done | bytes 278560 | tf_op jit(solution)/shard_map/ppermute | solution.py:344
  76.6 0.1 shard_map.123
  76.7 1.9 %collective-permute-start.7 = (bf16[272,512]{1,0:T(8,128)(2,1)S(1)}, bf16[272,512]{1,0:T(8,128)(2,1)S(1)}, u32[]{:S(2)}, u32[]{:S(2)}) collective-permute-start(bf16[272,512]{1,0:T(8,128)(2,1)S(1)} %shard_map.123), channel_id=1, source_target_pairs={{0,1},{1,2},{2,3},{3,4},{4,5},{5,6},{6,7},{7,0},{8,15},{9,8},{10,9... | collective-permute-start | bytes 835592 | tf_op jit(solution)/shard_map/ppermute | solution.py:344
  78.6 0.5 collective-permute-done.4.got_ref
  79.2 0.1 shard_map.121
  79.2 7.1 %collective-permute-done.7.got_ref = bf16[272,512]{1,0:T(8,128)(2,1)S(1)} collective-permute-done((bf16[272,512]{1,0:T(8,128)(2,1)S(1)}, bf16[272,512]{1,0:T(8,128)(2,1)S(1)}, u32[]{:S(2)}, u32[]{:S(2)}) %collective-permute-start.7) | collective-permute-done | bytes 278560 | tf_op jit(solution)/shard_map/ppermute | solution.py:344
  86.3 0.8 shard_map.124
  (1 shorter events, 0.0 us)
Async XLA Ops:
  13.8 19.9 %all-to-all-start.1 = ((bf16[8,80,128]{2,1,0:T(8,128)(2,1)}), bf16[8,80,128]{2,1,0:T(8,128)(2,1)S(1)}, u32[]{:S(2)}, u32[]{:S(2)}) async-start(bf16[8,80,128]{2,1,0:T(8,128)(2,1)} %shard_map.110.refs_0_), calls=%async_computation.1 | async-start | bytes 327680 | tf_op jit(solution)/shard_map/all_to_all | solution.py:317
  24.1 13.7 %copy-start.1 = (bf16[256,128]{1,0:T(8,128)(2,1)S(1)}, bf16[256,128]{1,0:T(8,128)(2,1)}, u32[]{:S(2)}) copy-start(bf16[256,128]{1,0:T(8,128)(2,1)} %refs_1_.3) | copy-start | bytes 196612
  34.4 9.4 %all-to-all-start.2 = ((bf16[8,64,128]{2,1,0:T(8,128)(2,1)}), bf16[8,64,128]{2,1,0:T(8,128)(2,1)S(1)}, u32[]{:S(2)}, u32[]{:S(2)}) async-start(bf16[8,64,128]{2,1,0:T(8,128)(2,1)} %shard_map.112.refs_0_), calls=%async_computation.2 | async-start | bytes 262144 | tf_op jit(solution)/shard_map/all_to_all | solution.py:332
  37.8 1.2 %copy-start = (f32[520,512]{1,0:T(8,128)S(1)}, f32[520,512]{1,0:T(8,128)}, u32[]{:S(2)}) copy-start(f32[520,512]{1,0:T(8,128)} %shard_map.111.refs_2_) | copy-start | bytes 3194884
  45.5 4.5 %collective-permute-start = (bf16[272,512]{1,0:T(8,128)(2,1)S(1)}, bf16[272,512]{1,0:T(8,128)(2,1)S(1)}, u32[]{:S(2)}, u32[]{:S(2)}) collective-permute-start(bf16[272,512]{1,0:T(8,128)(2,1)S(1)} %get-tuple-element.28.own_ref.gated_ref), channel_id=1, source_target_pairs={{0,8},{1,9},{2,10},{3,11},{4,12},{5,13},{6,14},{7,15},{8,0},{9,1},... | collective-permute-start | bytes 835592 | tf_op jit(solution)/shard_map/ppermute | solution.py:344
  47.5 9.7 %collective-permute-start.1 = (bf16[272,512]{1,0:T(8,128)(2,1)S(1)}, bf16[272,512]{1,0:T(8,128)(2,1)S(1)}, u32[]{:S(2)}, u32[]{:S(2)}) collective-permute-start(bf16[272,512]{1,0:T(8,128)(2,1)S(1)} %get-tuple-element.27), channel_id=1, source_target_pairs={{0,1},{1,2},{2,3},{3,4},{4,5},{5,6},{6,7},{7,0},{8,15},{9,8},{10,9... | collective-permute-start | bytes 835592 | tf_op jit(solution)/shard_map/ppermute | solution.py:344
  50.5 10.9 %collective-permute-start.2 = (bf16[272,512]{1,0:T(8,128)(2,1)S(1)}, bf16[272,512]{1,0:T(8,128)(2,1)S(1)}, u32[]{:S(2)}, u32[]{:S(2)}) collective-permute-start(bf16[272,512]{1,0:T(8,128)(2,1)S(1)} %shard_map.118), channel_id=1, source_target_pairs={{0,1},{1,2},{2,3},{3,4},{4,5},{5,6},{6,7},{7,0},{8,15},{9,8},{10,9... | collective-permute-start | bytes 835592 | tf_op jit(solution)/shard_map/ppermute | solution.py:344
  57.2 9.7 %collective-permute-start.5 = (bf16[272,512]{1,0:T(8,128)(2,1)S(1)}, bf16[272,512]{1,0:T(8,128)(2,1)S(1)}, u32[]{:S(2)}, u32[]{:S(2)}) collective-permute-start(bf16[272,512]{1,0:T(8,128)(2,1)S(1)} %shard_map.116), channel_id=1, source_target_pairs={{0,1},{1,2},{2,3},{3,4},{4,5},{5,6},{6,7},{7,0},{8,15},{9,8},{10,9... | collective-permute-start | bytes 835592 | tf_op jit(solution)/shard_map/ppermute | solution.py:344
  61.5 9.7 %collective-permute-start.3 = (bf16[272,512]{1,0:T(8,128)(2,1)S(1)}, bf16[272,512]{1,0:T(8,128)(2,1)S(1)}, u32[]{:S(2)}, u32[]{:S(2)}) collective-permute-start(bf16[272,512]{1,0:T(8,128)(2,1)S(1)} %shard_map.119), channel_id=1, source_target_pairs={{0,1},{1,2},{2,3},{3,4},{4,5},{5,6},{6,7},{7,0},{8,15},{9,8},{10,9... | collective-permute-start | bytes 835592 | tf_op jit(solution)/shard_map/ppermute | solution.py:344
  66.9 9.7 %collective-permute-start.6 = (bf16[272,512]{1,0:T(8,128)(2,1)S(1)}, bf16[272,512]{1,0:T(8,128)(2,1)S(1)}, u32[]{:S(2)}, u32[]{:S(2)}) collective-permute-start(bf16[272,512]{1,0:T(8,128)(2,1)S(1)} %shard_map.122), channel_id=1, source_target_pairs={{0,1},{1,2},{2,3},{3,4},{4,5},{5,6},{6,7},{7,0},{8,15},{9,8},{10,9... | collective-permute-start | bytes 835592 | tf_op jit(solution)/shard_map/ppermute | solution.py:344
  71.3 7.9 %collective-permute-start.4 = (bf16[272,512]{1,0:T(8,128)(2,1)S(1)}, bf16[272,512]{1,0:T(8,128)(2,1)S(1)}, u32[]{:S(2)}, u32[]{:S(2)}) collective-permute-start(bf16[272,512]{1,0:T(8,128)(2,1)S(1)} %shard_map.120), channel_id=1, source_target_pairs={{0,9},{1,10},{2,11},{3,12},{4,13},{5,14},{6,15},{7,8},{8,7},{9,0},... | collective-permute-start | bytes 835592 | tf_op jit(solution)/shard_map/ppermute | solution.py:344
  76.7 9.7 %collective-permute-start.7 = (bf16[272,512]{1,0:T(8,128)(2,1)S(1)}, bf16[272,512]{1,0:T(8,128)(2,1)S(1)}, u32[]{:S(2)}, u32[]{:S(2)}) collective-permute-start(bf16[272,512]{1,0:T(8,128)(2,1)S(1)} %shard_map.123), channel_id=1, source_target_pairs={{0,1},{1,2},{2,3},{3,4},{4,5},{5,6},{6,7},{7,0},{8,15},{9,8},{10,9... | collective-permute-start | bytes 835592 | tf_op jit(solution)/shard_map/ppermute | solution.py:344

commit v14 on v13

--- a/solution.py
+++ b/solution.py
@@ -159,9 +159,10 @@
         out_ref[i + 1] = entry.astype(BF16)
 
 
-def bring_kernel(*refs):
-    count = len(refs) // 2 - 1
-    for copy in fetch(refs[1 : count + 1], refs[count + 1 : -1], refs[-1]):
+def bring_kernel(me, way, after_ref, c_hbm, gates_hbm, w_hbm, c_ref, gates_ref, w_ref, sems):
+    count, _, features = w_ref.shape
+    sources = [c_hbm, gates_hbm] + [columns(w_hbm, me[0], a * way[0], features) for a in range(count)]
+    for copy in fetch(sources, [c_ref, gates_ref] + [w_ref.at[a] for a in range(count)], sems):
         copy.wait()
 
 
@@ -214,17 +215,12 @@
         out_ref[j] = jnp.dot(ref[:tokens], w_ref[...], preferred_element_type=F32).astype(BF16)
 
 
-def chunks_kernel(me, way, own_ref, other_ref, w_hbm, out_ref, base_ref, w_ref, sems):
+def chunks_kernel(own_ref, other_ref, w_ref, out_ref, base_ref):
     steps, _, tokens, features = out_ref.shape
-    order = [*range(steps, 0, -1), 0]
-    copies = fetch([columns(w_hbm, me[0], a * way[0], features) for a in order], [w_ref.at[a] for a in order], sems)
-    for a, copy in zip(order, copies):
-        copy.wait()
-        if a == 0:
-            base_ref[...] = jnp.dot(own_ref[:tokens], w_ref[a], preferred_element_type=F32).astype(BF16)
-        else:
-            for j, ref in enumerate((own_ref, other_ref)):
-                out_ref[a - 1, j] = jnp.dot(ref[:tokens], w_ref[a], preferred_element_type=F32).astype(BF16)
+    for a in range(steps, 0, -1):
+        for j, ref in enumerate((own_ref, other_ref)):
+            out_ref[a - 1, j] = jnp.dot(ref[:tokens], w_ref[a], preferred_element_type=F32).astype(BF16)
+    base_ref[...] = jnp.dot(own_ref[:tokens], w_ref[0], preferred_element_type=F32).astype(BF16)
 
 
 def join_kernel(place, chunk_ref, gated_ref, *refs):
@@ -320,20 +316,20 @@
     (entries,) = call(
         entry_kernel, [SMEM, VMEM, VMEM], [((N_ROW, width, state_width), BF16)], (plane, got, got_planes), moved=2**19
     )
-    needed = (input_c, gates)
-    needed = call(
+    me = lax.axis_index("head").reshape(1)
+    way = (1 - 2 * lax.rem(lax.axis_index("seq"), 2)).reshape(1)
+    features = out_weight.shape[1] // N_PART
+    steps = N_PART // 2 - 2
+    *needed, w_near = call(
         bring_kernel,
-        [ANY] + [HBM] * len(needed),
-        [(a.shape, a.dtype) for a in needed],
-        (entries, *needed),
+        [SMEM] * 2 + [ANY] + [HBM] * 3,
+        [(a.shape, a.dtype) for a in (input_c, gates)] + [((steps + 1, channels, features), BF16)],
+        (me, way, entries, input_c, gates, out_weight),
         moved=2**21,
         limit=48,
     )
     entries = lax.all_to_all(entries, "seq", 0, 0, axis_index_groups=in_plane)
-    me = lax.axis_index("head").reshape(1)
-    features = out_weight.shape[1] // N_PART
     slab = ((tokens + PAD, features), BF16)
-    way = (1 - 2 * lax.rem(lax.axis_index("seq"), 2)).reshape(1)
 
     def send(array, steps, swap):
         pairs = []
@@ -372,17 +368,14 @@
     other_got = send(other_sent, 1, 0)
     own_sent = join(0, begin, gated, own_got)
     own_got = send(own_sent, 1, 0)
-    steps = N_PART // 2 - 2
     gated_then, _ = lax.optimization_barrier((gated, own_sent))
     chunks, base = call(
         chunks_kernel,
-        [SMEM, SMEM, VMEM, VMEM, HBM],
+        [VMEM] * 3,
         [((steps, 2, tokens, features), BF16), ((tokens, features), BF16)],
-        (me, way, gated_then, other, out_weight),
-        scratch=[jax.ShapeDtypeStruct((steps + 1, channels, features), BF16)],
+        (gated_then, other, w_near),
         flops=10 * tokens * channels * features,
         moved=2**21,
-        limit=50,
     )
     for away in range(steps, 0, -1):
         other_got = send(join((away - 1, 1), chunks, other, other_got), 1, int(away == 1))

time: 87.9 us -> 88 us (level)
    ppermute x8, waiting for transfers between devices: 20.6 us -> 22.2 us  [send(): return lax.ppermute(array, ('seq', 'head'), pairs)]
    all_to_all x1, waiting for transfers between devices: 4.58 us -> 3.22 us  [body(): entries = lax.all_to_all(entries, 'seq', 0, 0, axis_index_groups=in_plane)]
  transfers between devices with their start and end apart: 10 -> 10, of which waited for: 8 -> 8; matrix products, arithmetic and copies ran while one was open for 0% -> 0% of each run, Pallas kernels for 9% -> 8%
where the time goes in v14:
time: 88 us; the launch traced here: 87.3 us
  waiting for transfers between devices  30.9 us (35%)
  starting transfers between devices  30.5 us (35%)
  Pallas kernels  13.7 us (16%)
  blocking collectives  10.8 us (12%)
  local copies, waits for them, and re-layouts  1.23 us (1%)
    ppermute x8, waiting for transfers between devices, send(): return lax.ppermute(array, ('seq', 'head'), pairs)  22.2 us
    ppermute x8, starting transfers between devices, send(): return lax.ppermute(array, ('seq', 'head'), pairs)  16.7 us
    pallas_call x16, Pallas kernels, call(): pl.pallas_call(kernel, in_specs=ins, out_specs=[VMEM] * len(outs), out_sh...  13.7 us
    all_to_all x1, blocking collectives, body(): got = lax.all_to_all(pieces, 'seq', 0, 0, axis_index_groups=in_plane)  10.8 us
    all_to_all x1, starting transfers between devices, body(): got_planes = lax.all_to_all(totals, 'seq', 0, 0, axis_index_groups=across)  10.4 us
    all_to_all x1, waiting for transfers between devices, body(): got_planes = lax.all_to_all(totals, 'seq', 0, 0, axis_index_groups=across)  5.51 us
    all_to_all x1, starting transfers between devices, body(): entries = lax.all_to_all(entries, 'seq', 0, 0, axis_index_groups=in_plane)  3.37 us
    all_to_all x1, waiting for transfers between devices, body(): entries = lax.all_to_all(entries, 'seq', 0, 0, axis_index_groups=in_plane)  3.22 us
  transfers between devices with their start and end apart: 10, of which 8 were waited for; matrix products, arithmetic and copies ran while one was open for 0% of the time, Pallas kernels for 8%

profile of v14, /device:TPU:32, one launch (start us, length us, event | category | flops | bytes accessed | tf_op | source)
XLA Modules:
  0.0 87.3 jit_solution(7245611438145264251)
XLA Ops:
  0.0 2.3 %shard_map.109 = (bf16[8,80,128]{2,1,0:T(8,128)(2,1)}, f32[32,256]{1,0:T(8,128)}) custom-call(f32[1,8]{1,0:T(1,128)} %bitcast.12, f32[1,8]{1,0:T(1,128)} %bitcast.13, f32[8,256]{1,0:T(8,128)} %bitcast.9, s32[1,256]{1,0:T(1,128)} %bitcast.11, bf16[256,128]{1,0:T(8,128)(2,1)} %refs_2_.1, bf16[256,512]{1,0:T(8,128)(2,1)} %refs_5_.3), custom_call_target="tpu_custom_call" | custom-call | flops 33554432 | bytes 262144 | tf_op jit(solution)/shard_map/pallas_call | solution.py:256
  2.3 10.8 %all_to_all.15.got_ref = bf16[8,80,128]{2,1,0:T(8,128)(2,1)S(1)} all-to-all(bf16[8,80,128]{2,1,0:T(8,128)(2,1)} %get-tuple-element.20), channel_id=1, replica_groups={{0,8,16,24,32,40,48,56},{64,72,80,88,96,104,112,120},{128,136,144,152,1..., dimensions={0} | all-to-all | bytes 327680 | tf_op jit(solution)/shard_map/all_to_all | solution.py:298
  13.1 0.7 shard_map.110.refs_0_
  13.8 0.0 copy-start.1
  13.8 10.4 %all-to-all-start.1 = ((bf16[8,80,128]{2,1,0:T(8,128)(2,1)}), bf16[8,80,128]{2,1,0:T(8,128)(2,1)S(1)}, u32[]{:S(2)}, u32[]{:S(2)}) async-start(bf16[8,80,128]{2,1,0:T(8,128)(2,1)} %shard_map.110.refs_0_), calls=%async_computation.1 | async-start | bytes 327680 | tf_op jit(solution)/shard_map/all_to_all | solution.py:313
  24.3 4.0 %shard_map.111.gates_hbm = f32[520,512]{1,0:T(8,128)} custom-call(bf16[8,80,128]{2,1,0:T(8,128)(2,1)} %shard_map.110.refs_0_, bf16[256,128]{1,0:T(8,128)(2,1)} %c_hbm.1, bf16[256,128]{1,0:T(8,128)(2,1)} %refs_2_.1, f32[32,256]{1,0:T(8,128)} %get-tuple-element.21.refs_3_, f32[1,8]{1,0:T(1,128)} %bitcast.14, bf16[256,512]{1,0:T(8,128)(2,1)} %refs_5_.3, ...), custom_call_target="tpu_custom_call" | custom-call | flops 67108864 | bytes 8388608 | tf_op jit(solution)/shard_map/pallas_call | solution.py:256
  28.3 5.5 %all-to-all-done.1.planes_ref = bf16[8,80,128]{2,1,0:T(8,128)(2,1)S(1)} async-done(((bf16[8,80,128]{2,1,0:T(8,128)(2,1)}), bf16[8,80,128]{2,1,0:T(8,128)(2,1)S(1)}, u32[]{:S(2)}, u32[]{:S(2)}) %all-to-all-start.1) | async-done | bytes 163872 | tf_op jit(solution)/shard_map/all_to_all | solution.py:313
  33.8 0.7 shard_map.112.after_ref
  34.5 3.4 %all-to-all-start.2 = ((bf16[8,64,128]{2,1,0:T(8,128)(2,1)}), bf16[8,64,128]{2,1,0:T(8,128)(2,1)S(1)}, u32[]{:S(2)}, u32[]{:S(2)}) async-start(bf16[8,64,128]{2,1,0:T(8,128)(2,1)} %shard_map.112.after_ref), calls=%async_computation.2 | async-start | bytes 262144 | tf_op jit(solution)/shard_map/all_to_all | solution.py:331
  37.9 0.0 copy-done.1
  37.9 0.0 copy-start
  37.9 1.2 %copy-done = f32[520,512]{1,0:T(8,128)S(1)} copy-done((f32[520,512]{1,0:T(8,128)S(1)}, f32[520,512]{1,0:T(8,128)}, u32[]{:S(2)}) %copy-start) | copy-done | bytes 1064984
  39.2 1.6 %shard_map.113 = (bf16[256,128]{1,0:T(8,128)(2,1)S(1)}, f32[520,512]{1,0:T(8,128)S(1)}, bf16[3,512,512]{2,1,0:T(8,128)(2,1)S(1)}) custom-call(s32[1]{0:T(128)} %bitcast.me, s32[1]{0:T(128)} %bitcast.1.way, bf16[8,64,128]{2,1,0:T(8,128)(2,1)} %shard_map.112.after_ref, bf16[256,128]{1,0:T(8,128)(2,1)S(1)} %copy-done.1, f32[520,512]{1,0:T(8,128)S(1)} %copy-done, ...), custom_call_target="tpu_custom_call" | custom-call | bytes 2097152 | tf_op jit(solution)/shard_map/pallas_call | solution.py:256
  40.8 3.2 %all-to-all-done.2.entry_ref = bf16[8,64,128]{2,1,0:T(8,128)(2,1)S(1)} async-done(((bf16[8,64,128]{2,1,0:T(8,128)(2,1)}), bf16[8,64,128]{2,1,0:T(8,128)(2,1)S(1)}, u32[]{:S(2)}, u32[]{:S(2)}) %all-to-all-start.2) | async-done | bytes 131104 | tf_op jit(solution)/shard_map/all_to_all | solution.py:331
  44.0 1.7 %shard_map.114 = (bf16[272,512]{1,0:T(8,128)(2,1)S(1)}, bf16[272,512]{1,0:T(8,128)(2,1)S(1)}, bf16[512,512]{1,0:T(8,128)(2,1)S(1)}) custom-call(s32[1]{0:T(128)} %bitcast.me, s32[1]{0:T(128)} %bitcast.1.way, bf16[8,64,128]{2,1,0:T(8,128)(2,1)S(1)} %all-to-all-done.2.entry_ref, bf16[256,128]{1,0:T(8,128)(2,1)S(1)} %get-tuple-element.24.c_ref, ...), custom_call_target="tpu_custom_call" | custom-call | flops 134217728 | bytes 2097152 | tf_op jit(solution)/shard_map/pallas_call | solution.py:256
  45.7 1.9 %collective-permute-start = (bf16[272,512]{1,0:T(8,128)(2,1)S(1)}, bf16[272,512]{1,0:T(8,128)(2,1)S(1)}, u32[]{:S(2)}, u32[]{:S(2)}) collective-permute-start(bf16[272,512]{1,0:T(8,128)(2,1)S(1)} %get-tuple-element.29.own_ref.gated_ref), channel_id=1, source_target_pairs={{0,8},{1,9},{2,10},{3,11},{4,12},{5,13},{6,14},{7,15},{8,0},{9,1},... | collective-permute-start | bytes 835592 | tf_op jit(solution)/shard_map/ppermute | solution.py:340
  47.6 2.6 %collective-permute-start.1 = (bf16[272,512]{1,0:T(8,128)(2,1)S(1)}, bf16[272,512]{1,0:T(8,128)(2,1)S(1)}, u32[]{:S(2)}, u32[]{:S(2)}) collective-permute-start(bf16[272,512]{1,0:T(8,128)(2,1)S(1)} %get-tuple-element.28), channel_id=1, source_target_pairs={{0,1},{1,2},{2,3},{3,4},{4,5},{5,6},{6,7},{7,0},{8,15},{9,8},{10,9... | collective-permute-start | bytes 835592 | tf_op jit(solution)/shard_map/ppermute | solution.py:340
  50.2 0.0 collective-permute-done.other_ref.gated_ref
  50.2 0.4 shard_map.115.chunk_ref
  50.7 2.6 %collective-permute-start.2 = (bf16[272,512]{1,0:T(8,128)(2,1)S(1)}, bf16[272,512]{1,0:T(8,128)(2,1)S(1)}, u32[]{:S(2)}, u32[]{:S(2)}) collective-permute-start(bf16[272,512]{1,0:T(8,128)(2,1)S(1)} %shard_map.118), channel_id=1, source_target_pairs={{0,1},{1,2},{2,3},{3,4},{4,5},{5,6},{6,7},{7,0},{8,15},{9,8},{10,9... | collective-permute-start | bytes 835592 | tf_op jit(solution)/shard_map/ppermute | solution.py:340
  53.3 4.0 %collective-permute-done.1.refs_0_ = bf16[272,512]{1,0:T(8,128)(2,1)S(1)} collective-permute-done((bf16[272,512]{1,0:T(8,128)(2,1)S(1)}, bf16[272,512]{1,0:T(8,128)(2,1)S(1)}, u32[]{:S(2)}, u32[]{:S(2)}) %collective-permute-start.1) | collective-permute-done | bytes 278560 | tf_op jit(solution)/shard_map/ppermute | solution.py:340
  57.2 0.1 shard_map.116
  57.3 1.9 %collective-permute-start.5 = (bf16[272,512]{1,0:T(8,128)(2,1)S(1)}, bf16[272,512]{1,0:T(8,128)(2,1)S(1)}, u32[]{:S(2)}, u32[]{:S(2)}) collective-permute-start(bf16[272,512]{1,0:T(8,128)(2,1)S(1)} %shard_map.116), channel_id=1, source_target_pairs={{0,1},{1,2},{2,3},{3,4},{4,5},{5,6},{6,7},{7,0},{8,15},{9,8},{10,9... | collective-permute-start | bytes 835592 | tf_op jit(solution)/shard_map/ppermute | solution.py:340
  59.3 0.8 shard_map.117
  60.1 0.2 collective-permute-done.2.refs_0_
  60.3 0.1 shard_map.119
  60.4 1.9 %collective-permute-start.3 = (bf16[272,512]{1,0:T(8,128)(2,1)S(1)}, bf16[272,512]{1,0:T(8,128)(2,1)S(1)}, u32[]{:S(2)}, u32[]{:S(2)}) collective-permute-start(bf16[272,512]{1,0:T(8,128)(2,1)S(1)} %shard_map.119), channel_id=1, source_target_pairs={{0,1},{1,2},{2,3},{3,4},{4,5},{5,6},{6,7},{7,0},{8,15},{9,8},{10,9... | collective-permute-start | bytes 835592 | tf_op jit(solution)/shard_map/ppermute | solution.py:340
  62.3 4.6 %collective-permute-done.5.refs_0_ = bf16[272,512]{1,0:T(8,128)(2,1)S(1)} collective-permute-done((bf16[272,512]{1,0:T(8,128)(2,1)S(1)}, bf16[272,512]{1,0:T(8,128)(2,1)S(1)}, u32[]{:S(2)}, u32[]{:S(2)}) %collective-permute-start.5) | collective-permute-done | bytes 278560 | tf_op jit(solution)/shard_map/ppermute | solution.py:340
  67.0 0.1 shard_map.122
  67.1 1.9 %collective-permute-start.6 = (bf16[272,512]{1,0:T(8,128)(2,1)S(1)}, bf16[272,512]{1,0:T(8,128)(2,1)S(1)}, u32[]{:S(2)}, u32[]{:S(2)}) collective-permute-start(bf16[272,512]{1,0:T(8,128)(2,1)S(1)} %shard_map.122), channel_id=1, source_target_pairs={{0,1},{1,2},{2,3},{3,4},{4,5},{5,6},{6,7},{7,0},{8,15},{9,8},{10,9... | collective-permute-start | bytes 835592 | tf_op jit(solution)/shard_map/ppermute | solution.py:340
  69.0 1.1 %collective-permute-done.3.refs_0_ = bf16[272,512]{1,0:T(8,128)(2,1)S(1)} collective-permute-done((bf16[272,512]{1,0:T(8,128)(2,1)S(1)}, bf16[272,512]{1,0:T(8,128)(2,1)S(1)}, u32[]{:S(2)}, u32[]{:S(2)}) %collective-permute-start.3) | collective-permute-done | bytes 278560 | tf_op jit(solution)/shard_map/ppermute | solution.py:340
  70.1 0.1 shard_map.120
  70.2 1.9 %collective-permute-start.4 = (bf16[272,512]{1,0:T(8,128)(2,1)S(1)}, bf16[272,512]{1,0:T(8,128)(2,1)S(1)}, u32[]{:S(2)}, u32[]{:S(2)}) collective-permute-start(bf16[272,512]{1,0:T(8,128)(2,1)S(1)} %shard_map.120), channel_id=1, source_target_pairs={{0,9},{1,10},{2,11},{3,12},{4,13},{5,14},{6,15},{7,8},{8,7},{9,0},... | collective-permute-start | bytes 835592 | tf_op jit(solution)/shard_map/ppermute | solution.py:340
  72.1 4.6 %collective-permute-done.6.refs_0_ = bf16[272,512]{1,0:T(8,128)(2,1)S(1)} collective-permute-done((bf16[272,512]{1,0:T(8,128)(2,1)S(1)}, bf16[272,512]{1,0:T(8,128)(2,1)S(1)}, u32[]{:S(2)}, u32[]{:S(2)}) %collective-permute-start.6) | collective-permute-done | bytes 278560 | tf_op jit(solution)/shard_map/ppermute | solution.py:340
  76.7 0.1 shard_map.123
  76.8 1.9 %collective-permute-start.7 = (bf16[272,512]{1,0:T(8,128)(2,1)S(1)}, bf16[272,512]{1,0:T(8,128)(2,1)S(1)}, u32[]{:S(2)}, u32[]{:S(2)}) collective-permute-start(bf16[272,512]{1,0:T(8,128)(2,1)S(1)} %shard_map.123), channel_id=1, source_target_pairs={{0,1},{1,2},{2,3},{3,4},{4,5},{5,6},{6,7},{7,0},{8,15},{9,8},{10,9... | collective-permute-start | bytes 835592 | tf_op jit(solution)/shard_map/ppermute | solution.py:340
  78.7 0.0 collective-permute-done.4.got_ref
  78.7 0.1 shard_map.121
  78.8 7.6 %collective-permute-done.7.got_ref = bf16[272,512]{1,0:T(8,128)(2,1)S(1)} collective-permute-done((bf16[272,512]{1,0:T(8,128)(2,1)S(1)}, bf16[272,512]{1,0:T(8,128)(2,1)S(1)}, u32[]{:S(2)}, u32[]{:S(2)}) %collective-permute-start.7) | collective-permute-done | bytes 278560 | tf_op jit(solution)/shard_map/ppermute | solution.py:340
  86.5 0.8 shard_map.124
  (1 shorter events, 0.0 us)
Async XLA Ops:
  13.8 24.1 %copy-start.1 = (bf16[256,128]{1,0:T(8,128)(2,1)S(1)}, bf16[256,128]{1,0:T(8,128)(2,1)}, u32[]{:S(2)}) copy-start(bf16[256,128]{1,0:T(8,128)(2,1)} %c_hbm.1) | copy-start | bytes 196612
  13.8 20.0 %all-to-all-start.1 = ((bf16[8,80,128]{2,1,0:T(8,128)(2,1)}), bf16[8,80,128]{2,1,0:T(8,128)(2,1)S(1)}, u32[]{:S(2)}, u32[]{:S(2)}) async-start(bf16[8,80,128]{2,1,0:T(8,128)(2,1)} %shard_map.110.refs_0_), calls=%async_computation.1 | async-start | bytes 327680 | tf_op jit(solution)/shard_map/all_to_all | solution.py:313
  34.5 9.4 %all-to-all-start.2 = ((bf16[8,64,128]{2,1,0:T(8,128)(2,1)}), bf16[8,64,128]{2,1,0:T(8,128)(2,1)S(1)}, u32[]{:S(2)}, u32[]{:S(2)}) async-start(bf16[8,64,128]{2,1,0:T(8,128)(2,1)} %shard_map.112.after_ref), calls=%async_computation.2 | async-start | bytes 262144 | tf_op jit(solution)/shard_map/all_to_all | solution.py:331
  37.9 1.2 %copy-start = (f32[520,512]{1,0:T(8,128)S(1)}, f32[520,512]{1,0:T(8,128)}, u32[]{:S(2)}) copy-start(f32[520,512]{1,0:T(8,128)} %shard_map.111.gates_hbm) | copy-start | bytes 3194884
  45.7 4.5 %collective-permute-start = (bf16[272,512]{1,0:T(8,128)(2,1)S(1)}, bf16[272,512]{1,0:T(8,128)(2,1)S(1)}, u32[]{:S(2)}, u32[]{:S(2)}) collective-permute-start(bf16[272,512]{1,0:T(8,128)(2,1)S(1)} %get-tuple-element.29.own_ref.gated_ref), channel_id=1, source_target_pairs={{0,8},{1,9},{2,10},{3,11},{4,12},{5,13},{6,14},{7,15},{8,0},{9,1},... | collective-permute-start | bytes 835592 | tf_op jit(solution)/shard_map/ppermute | solution.py:340
  47.6 9.7 %collective-permute-start.1 = (bf16[272,512]{1,0:T(8,128)(2,1)S(1)}, bf16[272,512]{1,0:T(8,128)(2,1)S(1)}, u32[]{:S(2)}, u32[]{:S(2)}) collective-permute-start(bf16[272,512]{1,0:T(8,128)(2,1)S(1)} %get-tuple-element.28), channel_id=1, source_target_pairs={{0,1},{1,2},{2,3},{3,4},{4,5},{5,6},{6,7},{7,0},{8,15},{9,8},{10,9... | collective-permute-start | bytes 835592 | tf_op jit(solution)/shard_map/ppermute | solution.py:340
  50.7 9.7 %collective-permute-start.2 = (bf16[272,512]{1,0:T(8,128)(2,1)S(1)}, bf16[272,512]{1,0:T(8,128)(2,1)S(1)}, u32[]{:S(2)}, u32[]{:S(2)}) collective-permute-start(bf16[272,512]{1,0:T(8,128)(2,1)S(1)} %shard_map.118), channel_id=1, source_target_pairs={{0,1},{1,2},{2,3},{3,4},{4,5},{5,6},{6,7},{7,0},{8,15},{9,8},{10,9... | collective-permute-start | bytes 835592 | tf_op jit(solution)/shard_map/ppermute | solution.py:340
  57.3 9.7 %collective-permute-start.5 = (bf16[272,512]{1,0:T(8,128)(2,1)S(1)}, bf16[272,512]{1,0:T(8,128)(2,1)S(1)}, u32[]{:S(2)}, u32[]{:S(2)}) collective-permute-start(bf16[272,512]{1,0:T(8,128)(2,1)S(1)} %shard_map.116), channel_id=1, source_target_pairs={{0,1},{1,2},{2,3},{3,4},{4,5},{5,6},{6,7},{7,0},{8,15},{9,8},{10,9... | collective-permute-start | bytes 835592 | tf_op jit(solution)/shard_map/ppermute | solution.py:340
  60.4 9.7 %collective-permute-start.3 = (bf16[272,512]{1,0:T(8,128)(2,1)S(1)}, bf16[272,512]{1,0:T(8,128)(2,1)S(1)}, u32[]{:S(2)}, u32[]{:S(2)}) collective-permute-start(bf16[272,512]{1,0:T(8,128)(2,1)S(1)} %shard_map.119), channel_id=1, source_target_pairs={{0,1},{1,2},{2,3},{3,4},{4,5},{5,6},{6,7},{7,0},{8,15},{9,8},{10,9... | collective-permute-start | bytes 835592 | tf_op jit(solution)/shard_map/ppermute | solution.py:340
  67.1 9.7 %collective-permute-start.6 = (bf16[272,512]{1,0:T(8,128)(2,1)S(1)}, bf16[272,512]{1,0:T(8,128)(2,1)S(1)}, u32[]{:S(2)}, u32[]{:S(2)}) collective-permute-start(bf16[272,512]{1,0:T(8,128)(2,1)S(1)} %shard_map.122), channel_id=1, source_target_pairs={{0,1},{1,2},{2,3},{3,4},{4,5},{5,6},{6,7},{7,0},{8,15},{9,8},{10,9... | collective-permute-start | bytes 835592 | tf_op jit(solution)/shard_map/ppermute | solution.py:340
  70.2 8.6 %collective-permute-start.4 = (bf16[272,512]{1,0:T(8,128)(2,1)S(1)}, bf16[272,512]{1,0:T(8,128)(2,1)S(1)}, u32[]{:S(2)}, u32[]{:S(2)}) collective-permute-start(bf16[272,512]{1,0:T(8,128)(2,1)S(1)} %shard_map.120), channel_id=1, source_target_pairs={{0,9},{1,10},{2,11},{3,12},{4,13},{5,14},{6,15},{7,8},{8,7},{9,0},... | collective-permute-start | bytes 835592 | tf_op jit(solution)/shard_map/ppermute | solution.py:340
  76.8 9.7 %collective-permute-start.7 = (bf16[272,512]{1,0:T(8,128)(2,1)S(1)}, bf16[272,512]{1,0:T(8,128)(2,1)S(1)}, u32[]{:S(2)}, u32[]{:S(2)}) collective-permute-start(bf16[272,512]{1,0:T(8,128)(2,1)S(1)} %shard_map.123), channel_id=1, source_target_pairs={{0,1},{1,2},{2,3},{3,4},{4,5},{5,6},{6,7},{7,0},{8,15},{9,8},{10,9... | collective-permute-start | bytes 835592 | tf_op jit(solution)/shard_map/ppermute | solution.py:340
